TPU v7x, 32 devices: a whole 2x2x4 slice. The times are simulated.
32 devices in a mesh: space: 8 (over y, x, core), wave: 4 (over z).
Axes of the slice: x: 2, y: 2, z: 4, core: 2. Of those that a mesh axis runs over, the one named last changes fastest.
Arguments:
- noise: float32 [8, 3, 8192], P(None, None, 'space'), may hold values from -6 to 6
- positions: float32 [3, 8192], P(None, 'space'), may hold values from 0 to 8, as said below
- wave_index: int32 [3, 4096], P(None, 'wave'), may hold values from -16 to 16, as said below
- tile_lists: int32 [64, 8], P('space'), may hold values from 0 to 23, as said below
- tile_counts: int32 [64], P('space'), may hold values from 0 to 8, as said below
Outputs:
- displacement: float32 [8, 3, 8192], P(None, None, 'space')
Inputs may be any that keep to these rules, and one draw needn't show every extreme that they name: `positions`: particle j has x between j // 1024 and j // 1024 + 1, and y and z between 0 and 8. `wave_index`: row 0 holds n_1 from 1 to 16; rows 1 and 2 hold values from -16 to 15. `tile_lists`: A tile's 8 entries are distinct; window indices below 8 name tiles of the slab before, the next 8 tiles of the own slab, the rest tiles of the slab after. `tile_counts`: the counts of the 8 tiles of one slab add up to exactly 32, and in every slab one tile has 8.
All inputs are finite; a program needn't handle non-finite values.
Results may differ from a plain program's by a relative error of at most 0.0003.
Values sent between devices are 32-bit elements; how exact they have to be, the bound alone decides.
No kernel may reach another device: no remote copies, remote signals or barrier semaphores. Data moves between devices by JAX's collectives and lax.ppermute only.
A program may use at most 64 MiB of HBM per device.

v0:
```python
import math

import jax
import jax.numpy as jnp
from jax import lax
from jax.sharding import PartitionSpec as P

TILE = 128
KW = 4096
NB_MOST = 8
DEGREE = 3
PAIR_MOST = 32


PRECISE = lax.Precision.HIGHEST
SIDE_CROSS = 8.0
NEAR_SQUARE = 0.36
NEAR_AMP = 0.15
FAR_AMP = 8.0
SPLIT_SQUARE = 64.0
SCREEN = 4.0
SAFETY = 1.25
SPREAD = 100.0
EPSILON = 1e-06


def padded(x, sides, width):
    for axis, dim in sides:
        size, length = (lax.axis_size(axis), x.shape[dim])
        up = [(i, (i + 1) % size) for i in range(size)]
        down = [(j, i) for i, j in up]
        last = lax.slice_in_dim(x, length - width, length, axis=dim)
        initial = lax.slice_in_dim(x, 0, width, axis=dim)
        before = lax.ppermute(last, axis, up)
        after = lax.ppermute(initial, axis, down)
        x = jnp.concatenate([before, x, after], axis=dim)
    return x


def pair_block(target, source, self_flag, live_weight, length_x):
    box_sides = jnp.array([length_x, SIDE_CROSS, SIDE_CROSS], jnp.float32)[:, None, None]
    offset = target[:, None, :] - source[:, :, None]
    offset = offset - box_sides * jnp.floor(offset / box_sides + 0.5)
    distance_sq = jnp.sum(offset * offset, axis=0)
    tile_width = target.shape[1]
    diagonal_mask = jnp.arange(tile_width)[:, None] == jnp.arange(tile_width)[None, :]
    keep_mask = jnp.where(diagonal_mask & self_flag, 0.0, 1.0) * live_weight
    envelope = NEAR_AMP * jnp.exp(-distance_sq / NEAR_SQUARE) * keep_mask
    outer_product = offset[None, :, :, :] * offset[:, None, :, :]
    identity = jnp.eye(3, dtype=jnp.float32)[:, :, None, None]
    pair_matrix = (identity + outer_product / NEAR_SQUARE) * envelope[None, None]
    return jnp.transpose(pair_matrix, (0, 2, 1, 3)).reshape(3 * tile_width, 3 * tile_width)


def wave_terms(indices, length_x):
    box_sides = jnp.array([length_x, SIDE_CROSS, SIDE_CROSS], jnp.float32)[:, None]
    wave_vectors = 2.0 * math.pi * indices.astype(jnp.float32) / box_sides
    wave_square = jnp.sum(wave_vectors * wave_vectors, axis=0)
    scaled_square = wave_square / SPLIT_SQUARE
    weight = (
        FAR_AMP * (1.0 + scaled_square) * jnp.exp(-scaled_square) / (KW * (wave_square + SCREEN))
    )
    unit_waves = wave_vectors / jnp.sqrt(wave_square)
    return (wave_vectors, weight, unit_waves)


def make_phases(positions, wave_vectors):
    phase_angles = (
        positions[0][:, None] * wave_vectors[0][None, :]
        + positions[1][:, None] * wave_vectors[1][None, :]
        + positions[2][:, None] * wave_vectors[2][None, :]
    )
    return jnp.concatenate([jnp.cos(phase_angles), jnp.sin(phase_angles)], axis=1)


def project(factors, weight, unit_waves):
    along_wave = jnp.sum(factors * unit_waves[None, :, None, :], axis=1)
    return weight * (factors - unit_waves[None, :, None, :] * along_wave[:, None])


def chebyshev(lower_bound, upper_bound):
    node_count = DEGREE + 1
    node_angles = (jnp.arange(node_count, dtype=jnp.float32) + 0.5) * (math.pi / node_count)
    samples = jnp.sqrt(
        0.5 * (upper_bound - lower_bound) * jnp.cos(node_angles) + 0.5 * (upper_bound + lower_bound)
    )
    orders = jnp.arange(node_count, dtype=jnp.float32)
    coeffs = (
        2.0
        / node_count
        * jnp.sum(samples[None, :] * jnp.cos(orders[:, None] * node_angles[None, :]), axis=1)
    )
    return coeffs * jnp.where(orders == 0.0, 0.5, 1.0)


def body(noise, positions, wave_index, tile_lists, tile_counts):
    length_x = float(lax.axis_size("space"))
    vectors = noise.shape[0]
    particle_count = positions.shape[1]
    tile_count = particle_count // TILE
    local_waves = wave_index.shape[1]
    window_positions = padded(positions, (("space", 1),), particle_count)
    own_tiles = positions.reshape(3, tile_count, TILE)
    window_tiles = window_positions.reshape(3, 3 * tile_count, TILE)
    wave_vectors, weight, unit_waves = wave_terms(wave_index, length_x)
    phases = make_phases(positions, wave_vectors)
    wave_count = lax.axis_size("wave")
    wave_rank = lax.axis_index("wave")
    pair_share = PAIR_MOST // wave_count
    flat_live = (jnp.arange(NB_MOST, dtype=jnp.int32)[None, :] < tile_counts[:, None]).reshape(-1)
    ranking = jnp.cumsum(flat_live.astype(jnp.int32)) - 1
    wanted = wave_rank + wave_count * jnp.arange(pair_share, dtype=jnp.int32)
    chosen = flat_live[None, :] & (ranking[None, :] == wanted[:, None])
    sources = jnp.sum(jnp.where(chosen, tile_lists.reshape(-1)[None, :], 0), axis=1)
    owners = jnp.repeat(jnp.arange(tile_count, dtype=jnp.int32), NB_MOST)
    targets = jnp.sum(jnp.where(chosen, owners[None, :], 0), axis=1)
    live_mask = jnp.any(chosen, axis=1).astype(jnp.float32)
    pair_count = sources.shape[0]
    target_pos = jnp.transpose(jnp.take(own_tiles, targets, axis=1), (1, 0, 2))
    source_pos = jnp.transpose(jnp.take(window_tiles, sources, axis=1), (1, 0, 2))
    self_flags = sources == tile_count + targets
    matrices = jax.vmap(pair_block, in_axes=(0, 0, 0, 0, None))(
        target_pos, source_pos, self_flags, live_mask, length_x
    )
    target_hot = (targets[:, None] == jnp.arange(tile_count, dtype=jnp.int32)[None, :]).astype(
        jnp.float32
    )

    def mobility(forces):
        window_forces = padded(forces, (("space", 2),), particle_count)
        window_split = window_forces.reshape(vectors, 3, 3 * tile_count, TILE)
        gathered = jnp.take(window_split, sources, axis=2)
        gathered = jnp.transpose(gathered, (2, 0, 1, 3)).reshape(pair_count, vectors, 3 * TILE)
        pushed = jnp.einsum("pvx,pxy->pvy", gathered, matrices, precision=PRECISE)
        near_part = jnp.einsum("pt,pvy->tvy", target_hot, pushed, precision=PRECISE)
        near_part = jnp.transpose(
            near_part.reshape(tile_count, vectors, 3, TILE), (1, 2, 0, 3)
        ).reshape(vectors, 3, particle_count)
        factors = jnp.dot(
            forces.reshape(vectors * 3, particle_count),
            phases,
            precision=PRECISE,
            preferred_element_type=jnp.float32,
        ).reshape(vectors, 3, 2, local_waves)
        weighted = project(lax.psum(factors, "space"), weight, unit_waves)
        far_part = lax.dot_general(
            weighted.reshape(vectors * 3, 2 * local_waves),
            phases,
            (((1,), (1,)), ((), ())),
            precision=PRECISE,
            preferred_element_type=jnp.float32,
        )
        wave_share = near_part + far_part.reshape(vectors, 3, particle_count)
        return forces + lax.psum(wave_share, "wave")

    first_image = mobility(noise)
    first_sum = lax.psum(jnp.sum(first_image * first_image, axis=(1, 2)), "space")
    first_scale = jnp.sqrt(first_sum + EPSILON)
    unit_image = mobility(first_image / first_scale[:, None, None])
    second_sum = lax.psum(jnp.sum(unit_image * unit_image, axis=(1, 2)), "space")
    upper_bound = SAFETY * jnp.max(jnp.sqrt(second_sum))
    second = unit_image * first_scale[:, None, None]
    lower_bound = upper_bound / SPREAD
    coeffs = chebyshev(lower_bound, upper_bound)
    bound_sum = upper_bound + lower_bound
    bound_span = upper_bound - lower_bound
    previous = noise
    current = (2.0 * first_image - bound_sum * noise) / bound_span
    mapped = (2.0 * second - bound_sum * first_image) / bound_span
    running_sum = coeffs[0] * previous + coeffs[1] * current
    for degree_step in range(2, DEGREE + 1):
        following = 2.0 * (2.0 * mapped - bound_sum * current) / bound_span - previous
        running_sum = running_sum + coeffs[degree_step] * following
        if degree_step < DEGREE:
            mapped = mobility(following)
        previous, current = (current, following)
    return running_sum


def solution(mesh):
    in_specs = (
        P(None, None, "space"),
        P(None, "space"),
        P(None, "wave"),
        P("space", None),
        P("space"),
    )
    out_specs = P(None, None, "space")
    return jax.shard_map(body, mesh=mesh, in_specs=in_specs, out_specs=out_specs, check_vma=False)
```

profile of v0, /device:TPU:0, one launch (start us, length us, event | category | flops | bytes accessed | tf_op | source)
XLA Modules:
  0.0 403.5 jit_solution(8890615899971515394)
XLA Ops:
  6.5 3.3 collective-permute-start.3
  9.9 2.6 collective-permute-start.1
  12.5 1.0 copy.32
  13.5 0.8 fusion.68
  14.4 0.7 multiply_reduce_fusion.6
  15.2 0.7 multiply_divide_fusion
  15.9 16.0 %fusion.7 = (f32[1024,1024]{1,0:T(8,128)S(1)}, f32[1024,1024]{1,0:T(8,128)S(1)}) fusion(f32[1024]{0:T(1024)S(1)} %bitcast.131, f32[1024]{0:T(1024)S(1)} %bitcast.127, f32[1024]{0:T(1024)S(1)} %bitcast.130, f32[1024]{0:T(1024)S(1)} %bitcast.128, f32[1024]{0:T(1024)S(1)} %bitcast.129, f32[1024]{0:T(1024)S(1)} %bitcast.126), kind=kLoop, calls=%fused_computation.16 | loop fusion | flops 5242880 | bytes 8413184 | tf_op jit(solution)/shard_map/cos | solution.py:73
  32.0 2.0 copy-done
  34.0 1.3 copy-done.1
  35.3 4.5 %fusion.10 = f32[24,2048]{1,0:T(8,128)S(1)} fusion(f32[24,1024]{1,0:T(8,128)S(1)} %reshape.291, f32[1024,1024]{1,0:T(8,128)S(1)} %get-tuple-element.13, f32[1024,1024]{1,0:T(8,128)S(1)} %get-tuple-element.12), kind=kOutput, calls=%fused_computation.23 | convolution fusion | flops 606076928 | bytes 8683520 | tf_op jit(solution)/shard_map/dot_general | solution.py:139
  39.9 0.7 copy.33
  44.1 4.0 %mul.389 = f32[8,3,128,3,128]{4,3,2,1,0:T(4,128)} broadcast(f32[8,128,128]{2,1,0:T(8,128)S(1)} %multiply_multiply_fusion.1), dimensions={0,2,4} | broadcast | bytes 5242880 | tf_op jit(solution)/shard_map/vmap()/mul | solution.py:51
  48.2 8.7 %mul.390 = f32[8,384,384]{2,1,0:T(8,128)} reshape(f32[8,3,128,3,128]{4,3,2,1,0:T(4,128)} %mul.389) | data formatting | bytes 9437184 | tf_op jit(solution)/shard_map/vmap()/mul | solution.py:51
  57.1 1.4 subtract_subtract_fusion
  58.4 4.6 %multiply_multiply_fusion = f32[8,3,128,3,128]{4,3,2,1,0:T(4,128)} fusion(f32[8,3,128,128]{3,2,1,0:T(8,128)S(1)} %get-tuple-element.10, f32[8,128,3,128]{3,2,1,0:T(4,128)S(1)} %subtract_subtract_fusion), kind=kLoop, calls=%fused_computation.12 | loop fusion | flops 2359296 | bytes 7864320 | tf_op jit(solution)/shard_map/vmap()/div | solution.py:51
  63.0 8.5 %div.93 = f32[8,384,384]{2,1,0:T(8,128)} reshape(f32[8,3,128,3,128]{4,3,2,1,0:T(4,128)} %multiply_multiply_fusion) | data formatting | bytes 9437184 | tf_op jit(solution)/shard_map/vmap()/div | solution.py:51
  71.5 6.5 %add_multiply_fusion = f32[8,384,384]{2,1,0:T(8,128)} fusion(f32[8,384,384]{2,1,0:T(8,128)} %mul.390, f32[8,384,384]{2,1,0:T(8,128)} %div.93, f32[384,384]{1,0:T(8,128)S(1)} %bitcast.120), kind=kLoop, calls=%fused_computation.13 | loop fusion | flops 2359296 | bytes 14745600 | tf_op jit(solution)/shard_map/vmap()/mul | solution.py:51
  78.6 4.3 %fusion.34 = f32[8,8,384]{2,1,0:T(8,128)S(1)} fusion(f32[8,384,384]{2,1,0:T(8,128)} %add_multiply_fusion, f32[8,8,3,128]{3,1,2,0:T(8,128)S(1)} %gather_fusion.2, pred[8]{0:T(512)(128)(4,1)S(1)} %get-tuple-element.30), kind=kOutput, calls=%fused_computation.56 | convolution fusion | flops 113270784 | bytes 4915208 | tf_op jit(solution)/shard_map/pvx,pxy->pvy/dot_general | solution.py:134
  83.0 12.7 %all-reduce.7.cloned.1.call-done = f32[8,3,2,1024]{3,0,2,1:T(8,128)} async-done(((f32[8,3,2,1024]{3,0,2,1:T(8,128)}), f32[8,3,2,1024]{3,0,2,1:T(8,128)}) %all-reduce.7.cloned.1.call-update) | async-done | bytes 196624 | tf_op jit(solution)/shard_map/psum | solution.py:145
  95.7 0.9 multiply_reduce_fusion.3
  96.7 1.0 subtract_multiply_fusion.4
  97.6 11.0 %fusion.17 = f32[8,3,1024]{2,0,1:T(8,128)} fusion(f32[8,3,2048]{2,0,1:T(8,128)S(1)} %bitcast.122, f32[1024,1024]{1,0:T(8,128)} %copy-done.1, f32[1024,1024]{1,0:T(8,128)} %copy-done, f32[8,3,8,128]{3,2,1,0:T(8,128)S(1)} %convolution_bitcast_fusion.2), kind=kOutput, calls=%fused_computation.34 | convolution fusion | flops 606101504 | bytes 8781824 | tf_op jit(solution)/shard_map/dot_general | solution.py:146
  108.7 7.8 %fusion.8 = f32[2048,1024]{0,1:T(8,128)} fusion(f32[1024,1024]{1,0:T(8,128)} %copy-done.1, f32[1024,1024]{1,0:T(8,128)} %copy-done), kind=kLoop, calls=%fused_computation.19 | loop fusion | flops 2097152 | bytes 16777216 | tf_op jit(solution)/shard_map/dot_general | solution.py:139
  116.4 9.5 %copy.42 = f32[2048,1024]{1,0:T(8,128)} copy(f32[2048,1024]{0,1:T(8,128)} %fusion.8) | data formatting | bytes 16777216 | tf_op jit(solution)/shard_map/dot_general | solution.py:139
  125.9 16.5 %all-reduce.9.cloned.1.call-done = f32[8,3,1024]{2,0,1:T(8,128)} async-done(((f32[8,3,1024]{2,0,1:T(8,128)}), f32[8,3,1024]{2,0,1:T(8,128)}) %all-reduce.9.cloned.1.call-update) | async-done | bytes 98320 | tf_op jit(solution)/shard_map/psum | solution.py:154
  142.4 1.0 multiply_reduce_fusion.5
  143.5 11.8 %psum.58 = f32[8]{0:T(128)S(1)} all-reduce(f32[8]{0:T(128)S(1)} %get-tuple-element.8), channel_id=1, replica_groups=mesh['space'=8,'wave'=4] {'space'}, use_global_device_ids=true, to_apply=%region_10.12 | all-reduce | flops 8 | bytes 64 | tf_op jit(solution)/shard_map/psum | solution.py:157
  155.9 10.1 %fusion.28 = f32[8,3,2,1024]{3,0,2,1:T(8,128)} fusion(f32[2,1024,1024,1]{2,1,0,3:T(8,128)} %bitcast.117, f32[8,3,1024]{2,0,1:T(8,128)S(1)} %get-tuple-element.9, f32[8]{0:T(128)S(1)} %add_sqrt_fusion.1), kind=kOutput, calls=%fused_computation.50 | convolution fusion | flops 604004352 | bytes 8683552 | tf_op jit(solution)/shard_map/dot_general | solution.py:139
  166.7 4.3 %fusion.32 = f32[8,8,384]{2,1,0:T(8,128)S(1)} fusion(f32[8,384,384]{2,1,0:T(8,128)} %add_multiply_fusion, f32[8,8,3,128]{3,1,2,0:T(8,128)S(1)} %gather_fusion.3, pred[8]{0:T(512)(128)(4,1)S(1)} %get-tuple-element.30), kind=kOutput, calls=%fused_computation.54 | convolution fusion | flops 113270784 | bytes 4915208 | tf_op jit(solution)/shard_map/pvx,pxy->pvy/dot_general | solution.py:134
  171.1 48.0 %all-reduce.11.cloned.1.call-done = f32[8,3,2,1024]{3,0,2,1:T(8,128)} async-done(((f32[8,3,2,1024]{3,0,2,1:T(8,128)}), f32[8,3,2,1024]{3,0,2,1:T(8,128)}) %all-reduce.11.cloned.1.call-update) | async-done | bytes 196624 | tf_op jit(solution)/shard_map/psum | solution.py:145
  219.1 0.9 multiply_reduce_fusion.2
  220.1 1.0 subtract_multiply_fusion.3
  221.0 11.0 %fusion.20 = f32[8,3,1024]{2,0,1:T(8,128)} fusion(f32[8,3,2048]{2,0,1:T(8,128)S(1)} %bitcast.123, f32[1024,1024]{1,0:T(8,128)} %copy-done.1, f32[1024,1024]{1,0:T(8,128)} %copy-done, f32[8,8,3,128]{3,0,2,1:T(8,128)S(1)} %convolution_bitcast_fusion.1), kind=kOutput, calls=%fused_computation.35 | convolution fusion | flops 606101504 | bytes 8781824 | tf_op jit(solution)/shard_map/dot_general | solution.py:146
  232.1 33.8 %all-reduce.13.cloned.1.call-done = f32[8,3,1024]{2,0,1:T(8,128)} async-done(((f32[8,3,1024]{2,0,1:T(8,128)}), f32[8,3,1024]{2,0,1:T(8,128)}) %all-reduce.13.cloned.1.call-update) | async-done | bytes 98320 | tf_op jit(solution)/shard_map/psum | solution.py:154
  265.8 1.1 multiply_reduce_fusion.4
  266.9 12.1 %psum.61 = f32[8]{0:T(128)S(1)} all-reduce(f32[8]{0:T(128)S(1)} %multiply_reduce_fusion.4), channel_id=1, replica_groups=mesh['space'=8,'wave'=4] {'space'}, use_global_device_ids=true, to_apply=%region_15.17 | all-reduce | flops 8 | bytes 64 | tf_op jit(solution)/shard_map/psum | solution.py:160
  280.9 1.0 divide_subtract_fusion
  281.9 9.9 %fusion.26 = f32[8,3,2,1024]{3,0,2,1:T(8,128)} fusion(f32[2,1024,1024,1]{2,1,0,3:T(8,128)} %bitcast.118, f32[8,3,1024]{2,0,1:T(8,128)S(1)} %divide_subtract_fusion), kind=kOutput, calls=%fused_computation.48 | convolution fusion | flops 603979776 | bytes 8683520 | tf_op jit(solution)/shard_map/dot_general | solution.py:139
  292.6 1.5 collective-permute-done.7
  294.1 3.7 collective-permute-done.6
  298.4 4.3 %fusion.30 = f32[8,8,384]{2,1,0:T(8,128)S(1)} fusion(f32[8,384,384]{2,1,0:T(8,128)} %add_multiply_fusion, f32[8,8,3,128]{3,1,2,0:T(8,128)S(1)} %gather_fusion.4, pred[8]{0:T(512)(128)(4,1)S(1)} %get-tuple-element.30), kind=kOutput, calls=%fused_computation.52 | convolution fusion | flops 113270784 | bytes 4915208 | tf_op jit(solution)/shard_map/pvx,pxy->pvy/dot_general | solution.py:134
  302.9 42.6 %all-reduce.15.cloned.1.call-done = f32[8,3,2,1024]{3,0,2,1:T(8,128)} async-done(((f32[8,3,2,1024]{3,0,2,1:T(8,128)}), f32[8,3,2,1024]{3,0,2,1:T(8,128)}) %all-reduce.15.cloned.1.call-update) | async-done | bytes 196624 | tf_op jit(solution)/shard_map/psum | solution.py:145
  345.4 0.9 multiply_reduce_fusion.1
  346.4 1.0 subtract_multiply_fusion.2
  347.4 11.0 %fusion.23 = f32[8,3,1024]{2,0,1:T(8,128)} fusion(f32[8,3,2048]{2,0,1:T(8,128)S(1)} %bitcast.121, f32[1024,1024]{1,0:T(8,128)} %copy-done.1, f32[1024,1024]{1,0:T(8,128)} %copy-done, f32[8,8,3,128]{3,0,2,1:T(8,128)S(1)} %convolution_bitcast_fusion), kind=kOutput, calls=%fused_computation.36 | convolution fusion | flops 606101504 | bytes 8781824 | tf_op jit(solution)/shard_map/dot_general | solution.py:146
  358.3 0.7 fusion.70
  359.0 33.2 %all-reduce.17.cloned.1.call-done = f32[8,3,1024]{2,0,1:T(8,128)} async-done(((f32[8,3,1024]{2,0,1:T(8,128)}), f32[8,3,1024]{2,0,1:T(8,128)}) %all-reduce.17.cloned.1.call-update) | async-done | bytes 98320 | tf_op jit(solution)/shard_map/psum | solution.py:154
  392.1 4.1 %multiply_add_fusion.1 = f32[8,3,1024]{2,0,1:T(8,128)} fusion(f32[8,3,1024]{2,0,1:T(8,128)S(1)} %divide_subtract_fusion, f32[8,3,1024]{2,0,1:T(8,128)} %all-reduce.17.cloned.1.call-done, f32[8,3,1024]{2,0,1:T(8,128)S(1)} %copy-done.2, f32[8,3,1024]{2,0,1:T(8,128)S(1)} %get-tuple-element.9, f32[]{:T(128)} %bitcast.39, f32[]{:T(128)} %bitcast.38, f32[]{:T(128)S(6)} %sub.91, ...), kind=kLoop, calls=%fused_computation.64 | loop fusion | flops 442368 | bytes 491544 | tf_op jit(solution)/shard_map/add | solution.py:173
  (84 shorter events, 8.3 us)
Async XLA Ops:
  6.5 89.2 %all-reduce.7.cloned.1.call-start = ((), (), s32[]{:S(2)}) async-start(), calls=%async_computation | async-start | bytes 393216 | tf_op jit(solution)/shard_map/psum | solution.py:145
  6.5 36.2 %collective-permute-start.3 = (f32[3,1024]{1,0:T(4,128)}, f32[3,1024]{1,0:T(4,128)S(1)}, u32[]{:S(2)}, u32[]{:S(2)}) collective-permute-start(f32[3,1024]{1,0:T(4,128)} %param.10), channel_id=1, source_target_pairs={{4,0},{8,4},{12,8},{16,12},{20,16},{24,20},{28,24},{0,28},{5,1},{9... | collective-permute-start | bytes 36872 | tf_op jit(solution)/shard_map/ppermute | solution.py:35
  9.9 32.9 %collective-permute-start.2 = (f32[3,1024]{1,0:T(4,128)}, f32[3,1024]{1,0:T(4,128)S(1)}, u32[]{:S(2)}, u32[]{:S(2)}) collective-permute-start(f32[3,1024]{1,0:T(4,128)} %param.10), channel_id=1, source_target_pairs={{0,4},{4,8},{8,12},{12,16},{16,20},{20,24},{24,28},{28,0},{1,5},{5... | collective-permute-start | bytes 36872 | tf_op jit(solution)/shard_map/ppermute | solution.py:34
  9.9 68.1 %collective-permute-start.1 = (f32[8,3,1024]{2,0,1:T(8,128)}, f32[8,3,1024]{2,0,1:T(8,128)S(1)}, u32[]{:S(2)}, u32[]{:S(2)}) collective-permute-start(f32[8,3,1024]{2,0,1:T(8,128)} %param.9), channel_id=1, source_target_pairs={{4,0},{8,4},{12,8},{16,12},{20,16},{24,20},{28,24},{0,28},{5,1},{9... | collective-permute-start | bytes 294920 | tf_op jit(solution)/shard_map/ppermute | solution.py:35
  12.5 65.5 %collective-permute-start = (f32[8,3,1024]{2,0,1:T(8,128)}, f32[8,3,1024]{2,0,1:T(8,128)S(1)}, u32[]{:S(2)}, u32[]{:S(2)}) collective-permute-start(f32[8,3,1024]{2,0,1:T(8,128)} %param.9), channel_id=1, source_target_pairs={{0,4},{4,8},{8,12},{12,16},{16,20},{20,24},{24,28},{28,0},{1,5},{5... | collective-permute-start | bytes 294920 | tf_op jit(solution)/shard_map/ppermute | solution.py:34
  32.0 2.0 copy-start
  32.0 3.3 copy-start.1
  35.3 5.6 %copy-start.5 = (s32[8]{0:T(128)S(1)}, s32[8]{0:T(128)}, u32[]{:S(2)}) copy-start(s32[8]{0:T(128)} %param.13) | copy-start | bytes 100
  35.3 6.0 %copy-start.4 = (s32[8,8]{1,0:T(8,128)S(1)}, s32[8,8]{1,0:T(8,128)}, u32[]{:S(2)}) copy-start(s32[8,8]{1,0:T(8,128)} %param.12) | copy-start | bytes 772
  35.3 6.9 %copy-start.3 = (f32[3,1024]{1,0:T(4,128)S(1)}, f32[3,1024]{1,0:T(4,128)}, u32[]{:S(2)}) copy-start(f32[3,1024]{1,0:T(4,128)} %param.10) | copy-start | bytes 36868
  40.7 101.7 %all-reduce.9.cloned.1.call-start = ((), (), s32[]{:S(2)}) async-start(), calls=%async_computation.1 | async-start | bytes 196608 | tf_op jit(solution)/shard_map/psum | solution.py:154
  71.5 6.5 %copy-start.2 = (f32[8,3,1024]{2,0,1:T(8,128)S(1)}, f32[8,3,1024]{2,0,1:T(8,128)}, u32[]{:S(2)}) copy-start(f32[8,3,1024]{2,0,1:T(8,128)} %param.9) | copy-start | bytes 294916
  108.6 110.5 %all-reduce.11.cloned.1.call-start = ((), (), s32[]{:S(2)}) async-start(), calls=%async_computation.2 | async-start | bytes 393216 | tf_op jit(solution)/shard_map/psum | solution.py:145
  155.3 10.7 %collective-permute-start.5 = (f32[8,3,1024]{2,0,1:T(8,128)S(1)}, f32[8,3,1024]{2,0,1:T(8,128)S(1)}, u32[]{:S(2)}, u32[]{:S(2)}) collective-permute-start(f32[8,3,1024]{2,0,1:T(8,128)S(1)} %broadcast_divide_fusion), channel_id=1, source_target_pairs={{4,0},{8,4},{12,8},{16,12},{20,16},{24,20},{28,24},{0,28},{5,1},{9... | collective-permute-start | bytes 294920 | tf_op jit(solution)/shard_map/ppermute | solution.py:35
  155.4 10.6 %collective-permute-start.4 = (f32[8,3,1024]{2,0,1:T(8,128)S(1)}, f32[8,3,1024]{2,0,1:T(8,128)S(1)}, u32[]{:S(2)}, u32[]{:S(2)}) collective-permute-start(f32[8,3,1024]{2,0,1:T(8,128)S(1)} %broadcast_divide_fusion), channel_id=1, source_target_pairs={{0,4},{4,8},{8,12},{12,16},{16,20},{20,24},{24,28},{28,0},{1,5},{5... | collective-permute-start | bytes 294920 | tf_op jit(solution)/shard_map/ppermute | solution.py:34
  166.0 99.8 %all-reduce.13.cloned.1.call-start = ((), (), s32[]{:S(2)}) async-start(), calls=%async_computation.3 | async-start | bytes 196608 | tf_op jit(solution)/shard_map/psum | solution.py:154
  232.0 113.4 %all-reduce.15.cloned.1.call-start = ((), (), s32[]{:S(2)}) async-start(), calls=%async_computation.4 | async-start | bytes 393216 | tf_op jit(solution)/shard_map/psum | solution.py:145
  291.8 2.3 collective-permute-start.7
  291.8 6.0 %collective-permute-start.6 = (f32[8,3,1024]{2,0,1:T(8,128)S(1)}, f32[8,3,1024]{2,0,1:T(8,128)S(1)}, u32[]{:S(2)}, u32[]{:S(2)}) collective-permute-start(f32[8,3,1024]{2,0,1:T(8,128)S(1)} %divide_subtract_fusion), channel_id=1, source_target_pairs={{0,4},{4,8},{8,12},{12,16},{16,20},{20,24},{24,28},{28,0},{1,5},{5... | collective-permute-start | bytes 294920 | tf_op jit(solution)/shard_map/ppermute | solution.py:34
  292.3 99.8 %all-reduce.17.cloned.1.call-start = ((), (), s32[]{:S(2)}) async-start(), calls=%async_computation.5 | async-start | bytes 196608 | tf_op jit(solution)/shard_map/psum | solution.py:154
Sparse Core Ops, SparseCore 0:
  40.8 54.8 all-reduce.6
  108.7 33.6 all-reduce.8
  166.1 52.9 all-reduce.10
  232.1 33.6 all-reduce.12
  292.4 52.9 all-reduce.14
  358.5 33.6 all-reduce.16
where the time goes:
time: 411 us; the launch traced here: 404 us
  waiting for transfers between devices  192 us (47%)
  matrix products  70.7 us (17%)
  other arithmetic  53.1 us (13%)
  local copies, waits for them, and re-layouts  41 us (10%)
  blocking collectives  23.8 us (6%)
  between operations  15.6 us (4%)
  starting transfers between devices  7.25 us (2%)
    psum x3, waiting for transfers between devices, mobility(): weighted = project(lax.psum(factors, 'space'), weight, unit_waves)  103 us
    psum x3, waiting for transfers between devices, mobility(): return forces + lax.psum(wave_share, 'wave')  83.4 us
    dot_general x3, matrix products, mobility(): lax.dot_general(weighted.reshape(vectors * 3, 2 * local_waves), phases, (...  32.9 us
    dot_general x3, matrix products, mobility(): jnp.dot(forces.reshape(vectors * 3, particle_count), phases, precision=PR...  24.5 us
    cos x1, other arithmetic, make_phases(): jnp.cos(phase_angles)  16 us
    dot_general x3, matrix products, mobility(): pushed = jnp.einsum('pvx,pxy->pvy', gathered, matrices, precision=PRECISE)  12.8 us
    mul x2, local copies, waits for them, and re-layouts, pair_block(): (identity + outer_product / NEAR_SQUARE) * envelope[None, None]  12.7 us
    psum x1, blocking collectives, body(): lax.psum(jnp.sum(unit_image * unit_image, axis=(1, 2)), 'space')  12.1 us
  transfers between devices with their start and end apart: 14, of which 8 were waited for; matrix products, arithmetic and copies ran while one was open for 26% of the time, Pallas kernels for 0%

commit v1 on v0

v1 whole, which is shorter than its diff:
```python
import functools
import math

import jax
import jax.numpy as jnp
from jax import lax
from jax.experimental import pallas as pl
from jax.experimental.pallas import tpu as pltpu
from jax.sharding import PartitionSpec as P

TILE = 128
KW = 4096
NB_MOST = 8
DEGREE = 3
PAIR_MOST = 32

SIDE_CROSS = 8.0
NEAR_SQUARE = 0.36
NEAR_AMP = 0.15
FAR_AMP = 8.0
SPLIT_SQUARE = 64.0
SCREEN = 4.0
SAFETY = 1.25
SPREAD = 100.0
EPSILON = 1e-06

F32 = jnp.float32
BF16 = jnp.bfloat16
VMEM_LIMIT = 24 << 20

SINE = (4.44287968, -7.30781651, 3.59777427, -0.791199386)
COSINE = (1.41421354, -6.97885084, 5.73946047, -1.88355792, 0.310688019)


def split(x):
    high = x.astype(BF16)
    return high, (x - high.astype(F32)).astype(BF16)


def poly(coeffs, x):
    acc = coeffs[-1]
    for c in coeffs[-2::-1]:
        acc = acc * x + c
    return acc


def forward(rows, cos_hi, sin_hi, cos_lo, sin_lo, terms, msg_ref):
    waves = cos_hi.shape[1]
    both = jnp.concatenate(split(rows), axis=0)
    high = both[:24]
    step = min(512, waves)
    for at in range(0, waves, step):
        cols = slice(at, at + step)
        pieces = []
        for hi_ref, lo_ref in ((cos_hi, cos_lo), (sin_hi, sin_lo)):
            first = jnp.dot(both, hi_ref[:, cols], preferred_element_type=F32)
            second = jnp.dot(high, lo_ref[:, cols], preferred_element_type=F32)
            full = first[:24] + (first[24:] + second)
            fx, fy, fz = full[0:8], full[8:16], full[16:24]
            t = terms[:, cols]
            pieces.append(t[1:2] * fx + t[2:3] * fy)
            pieces.append(t[3:4] * fx + t[4:5] * fy + t[5:6] * fz)
        stacked = jnp.concatenate(pieces, axis=0)
        for k in range(step // TILE):
            row = (at // TILE + k) * 32
            msg_ref[row : row + 32, :] = stacked[:, k * TILE : (k + 1) * TILE]


def start_kernel(
    length_x,
    pos_ref,
    noise_ref,
    index_ref,
    cos_hi,
    sin_hi,
    cos_lo,
    sin_lo,
    terms_ref,
    rows_ref,
    msg_ref,
    pack_ref,
    turn_ref,
):
    particles = pos_ref.shape[1]
    waves = index_ref.shape[1]
    tiles = particles // TILE
    sides = (length_x, SIDE_CROSS, SIDE_CROSS)
    counts = [index_ref[a : a + 1, :].astype(F32) for a in range(3)]
    k1, k2, k3 = [2.0 * math.pi * counts[a] / sides[a] for a in range(3)]
    square = k1 * k1 + k2 * k2 + k3 * k3
    scaled = square / SPLIT_SQUARE
    weight = FAR_AMP * (1.0 + scaled) * jnp.exp(-scaled) / (KW * (square + SCREEN))
    flat_square = k1 * k1 + k2 * k2
    flat = 1.0 / jnp.sqrt(flat_square)
    both = 1.0 / jnp.sqrt(square * flat_square)
    zero = jnp.zeros_like(k1)
    terms_ref[...] = jnp.concatenate(
        [weight, -k2 * flat, k1 * flat, -k1 * k3 * both, -k2 * k3 * both, flat_square * both, zero, zero],
        axis=0,
    )
    for a in range(3):
        rows_ref[8 * a : 8 * a + 8, :] = noise_ref[:, a, :]
    filler = jnp.zeros((5, TILE), F32)
    for i in range(tiles):
        lanes = slice(i * TILE, (i + 1) * TILE)
        pack_ref[32 * i : 32 * i + 24, :] = rows_ref[:, lanes]
        place = jnp.concatenate([pos_ref[:, lanes], filler], axis=0)
        pack_ref[32 * i + 24 : 32 * i + 32, :] = place
        for a in range(3):
            line = jnp.broadcast_to(place[a : a + 1] / sides[a], (TILE, TILE))
            turn_ref[a, i * TILE : (i + 1) * TILE, :] = line.T

    def block(at, carry):
        mine = pl.ds(pl.multiple_of(at * 16, 16), 16)
        u1, u2, u3 = [turn_ref[a, mine, :] for a in range(3)]
        for j in range(waves // TILE):
            cols = slice(j * TILE, (j + 1) * TILE)
            turns = u1 * counts[0][:, cols] + u2 * counts[1][:, cols] + u3 * counts[2][:, cols]
            r = turns - jnp.round(turns)
            x = r * r
            s = r * poly(SINE, x)
            c = poly(COSINE, x)
            cos_hi[mine, cols], cos_lo[mine, cols] = split(1.0 - s * s)
            sin_hi[mine, cols], sin_lo[mine, cols] = split(s * c)
        return carry

    lax.fori_loop(0, particles // 16, block, 0)
    forward(rows_ref[...], cos_hi, sin_hi, cos_lo, sin_lo, terms_ref[...], msg_ref)


def pair_kernel(
    length_x, share, meta_ref, lists_ref, counts_ref, own_ref, near_ref, away_ref, out_ref, plan_ref, place_ref
):
    tiles = lists_ref.shape[0]
    rank, ranks, odd = meta_ref[0], meta_ref[1], meta_ref[2]
    for p in range(share):
        for q in range(4):
            plan_ref[q, p] = 0

    def slot(at, seen):
        target, k = at // NB_MOST, at % NB_MOST
        live = k < counts_ref[target]
        at_p = seen // ranks

        @pl.when(live & (seen % ranks == rank) & (at_p < share))
        def _():
            window = lists_ref[target, k]
            side = window // tiles
            tile = window % tiles
            which = jnp.where(side == 1, 0, jnp.where((side == 0) == (odd == 1), 1, 2))
            plan_ref[0, at_p] = target
            plan_ref[1, at_p] = which * tiles + tile
            plan_ref[2, at_p] = jnp.where((side == 1) & (tile == target), 1, 0)
            plan_ref[3, at_p] = 1

        return seen + jnp.where(live, 1, 0)

    lax.fori_loop(0, tiles * NB_MOST, slot, 0)
    for slab, ref in enumerate((own_ref, near_ref, away_ref)):
        for i in range(tiles):
            place_ref[slab * tiles + i] = ref[32 * i + 24 : 32 * i + 32, :]
    sides = (length_x, SIDE_CROSS, SIDE_CROSS)
    off_diagonal = (
        lax.broadcasted_iota(jnp.int32, (TILE, TILE), 0) != lax.broadcasted_iota(jnp.int32, (TILE, TILE), 1)
    ).astype(F32)

    def pair(p, carry):
        target = place_ref[plan_ref[0, p]]
        source = place_ref[plan_ref[1, p]]
        own = plan_ref[2, p].astype(F32)
        keep = (1.0 - own * (1.0 - off_diagonal)) * plan_ref[3, p].astype(F32)
        d = []
        for a in range(3):
            line = jnp.broadcast_to(source[a : a + 1], (TILE, TILE)).T
            offset = target[a : a + 1] - line
            d.append(offset - sides[a] * jnp.floor(offset / sides[a] + 0.5))
        square = d[0] * d[0] + d[1] * d[1] + d[2] * d[2]
        envelope = NEAR_AMP * jnp.exp(-square / NEAR_SQUARE) * keep
        scaled = [envelope * d[a] * (1.0 / NEAR_SQUARE) for a in range(3)]
        at = 0
        for a in range(3):
            for b in range(a, 3):
                value = scaled[a] * d[b]
                if a == b:
                    value = value + envelope
                high, low = split(value)
                out_ref[p, 0:TILE, at * TILE : (at + 1) * TILE] = high
                out_ref[p, TILE : 2 * TILE, at * TILE : (at + 1) * TILE] = low
                at += 1
        return carry

    lax.fori_loop(0, share, pair, 0)


def near_kernel(stride, base, plan_ref, own_ref, near_ref, away_ref, pair_ref, out_ref, window_ref, sum_ref):
    tiles = sum_ref.shape[0]
    share = pair_ref.shape[0]
    for slab, ref in enumerate((own_ref, near_ref, away_ref)):
        for i in range(tiles):
            row = (base if slab < 2 else 0) + stride * i
            window_ref[slab * tiles + i] = ref[row : row + 24, :]
    sum_ref[...] = jnp.zeros_like(sum_ref)
    for p in range(share):
        target = plan_ref[0, p]
        high, low = split(window_ref[plan_ref[1, p]])
        left = jnp.concatenate(
            [jnp.concatenate([high, high], axis=1), jnp.concatenate([low, jnp.zeros_like(low)], axis=1)], axis=0
        )
        both = jnp.dot(left, pair_ref[p], preferred_element_type=F32)
        full = both[:24] + both[24:]
        x, y, z = full[0:8], full[8:16], full[16:24]

        def part(rows, at):
            return rows[:, at * TILE : (at + 1) * TILE]

        sum_ref[target] += jnp.concatenate(
            [
                part(x, 0) + part(y, 1) + part(z, 2),
                part(x, 1) + part(y, 3) + part(z, 4),
                part(x, 2) + part(y, 4) + part(z, 5),
            ],
            axis=0,
        )
    for i in range(tiles):
        out_ref[:, i * TILE : (i + 1) * TILE] = sum_ref[i]


def back_kernel(parts, *refs):
    ins, (terms_ref, cos_hi, sin_hi, cos_lo, sin_lo, near_ref, out_ref, norm_ref, left_ref) = (
        refs[:parts],
        refs[parts:],
    )
    waves = terms_ref.shape[1]
    particles = out_ref.shape[1]
    tiles = waves // TILE
    norm = ins[0][32 * tiles :, :]
    for ref in ins[1:]:
        norm = norm + ref[32 * tiles :, :]
    norm_ref[...] = norm
    for i in range(tiles):
        block = ins[0][32 * i : 32 * i + 32, :]
        for ref in ins[1:]:
            block = block + ref[32 * i : 32 * i + 32, :]
        t = terms_ref[:, i * TILE : (i + 1) * TILE]
        block = block * t[0:1]
        for kind in range(2):
            one, two = block[16 * kind : 16 * kind + 8], block[16 * kind + 8 : 16 * kind + 16]
            rows = jnp.concatenate(
                [t[1:2] * one + t[3:4] * two, t[2:3] * one + t[4:5] * two, t[5:6] * two], axis=0
            )
            left_ref[kind, :, i * TILE : (i + 1) * TILE] = jnp.concatenate(split(rows), axis=0)
    dims = (((1,), (1,)), ((), ()))
    step = min(256, particles)
    for at in range(0, particles, step):
        rows = slice(at, at + step)
        first = lax.dot_general(left_ref[0], cos_hi[rows, :], dims, preferred_element_type=F32)
        first += lax.dot_general(left_ref[1], sin_hi[rows, :], dims, preferred_element_type=F32)
        second = lax.dot_general(left_ref[0, 0:24], cos_lo[rows, :], dims, preferred_element_type=F32)
        second += lax.dot_general(left_ref[1, 0:24], sin_lo[rows, :], dims, preferred_element_type=F32)
        out_ref[:, rows] = first[:24] + (first[24:] + second) + near_ref[:, rows]


def step_kernel(parts, *refs):
    ins, (force_ref, terms_ref, cos_hi, sin_hi, cos_lo, sin_lo, rows_ref, msg_ref) = refs[:parts], refs[parts:]
    particles = force_ref.shape[1]
    waves = terms_ref.shape[1]
    total = ins[0][...]
    for ref in ins[1:]:
        total = total + ref[...]
    rows = force_ref[...] + total
    rows_ref[...] = rows
    squares = rows * rows
    squares = squares[0:8] + squares[8:16] + squares[16:24]
    tiles = particles // TILE
    norm = squares[:, 0:TILE]
    for i in range(1, tiles):
        norm = norm + squares[:, i * TILE : (i + 1) * TILE]
    base = waves // TILE * 32
    msg_ref[base : base + 8, :] = norm
    for i in range(tiles):
        msg_ref[base + 8 + 24 * i : base + 32 + 24 * i, :] = rows[:, i * TILE : (i + 1) * TILE]
    forward(rows, cos_hi, sin_hi, cos_lo, sin_lo, terms_ref[...], msg_ref)


def final_kernel(parts, *refs):
    ins, (noise_ref, one_ref, two_ref, first_ref, second_ref, out_ref) = refs[:parts], refs[parts:]
    total = ins[0][...]
    for ref in ins[1:]:
        total = total + ref[...]
    u0, u1, u2 = noise_ref[...], one_ref[...], two_ref[...]
    u3 = u2 + total
    first = jnp.sum(first_ref[...], axis=1, keepdims=True)
    second = jnp.sum(second_ref[...], axis=1, keepdims=True)
    ratio = jnp.max(second / (first + EPSILON), axis=0, keepdims=True)
    high = SAFETY * jnp.sqrt(ratio)
    low = high / SPREAD
    nodes = DEGREE + 1
    angles = [math.pi * (j + 0.5) / nodes for j in range(nodes)]
    samples = [jnp.sqrt(0.5 * (high - low) * math.cos(t) + 0.5 * (high + low)) for t in angles]
    coeffs = []
    for k in range(nodes):
        acc = samples[0] * math.cos(k * angles[0])
        for j in range(1, nodes):
            acc = acc + samples[j] * math.cos(k * angles[j])
        coeffs.append(acc * (2.0 / nodes) * (0.5 if k == 0 else 1.0))
    p = 2.0 / (high - low)
    q = (high + low) / (high - low)
    v0, v1, v2 = p * u1 - q * u0, p * u2 - q * u1, p * u3 - q * u2
    t2 = 2.0 * (p * v1 - q * v0) - u0
    m2 = 2.0 * (p * v2 - q * v1) - u1
    t3 = 2.0 * (p * m2 - q * t2) - v0
    out = coeffs[0] * u0 + coeffs[1] * v0 + coeffs[2] * t2 + coeffs[3] * t3
    for a in range(3):
        out_ref[:, a, :] = out[8 * a : 8 * a + 8]


def call(kernel, outs, args, scratch=(), smem_in=0, smem_out=()):
    vmem = pl.BlockSpec(memory_space=pltpu.VMEM)
    smem = pl.BlockSpec(memory_space=pltpu.SMEM)
    return pl.pallas_call(
        kernel,
        out_shape=[jax.ShapeDtypeStruct(*o) for o in outs],
        in_specs=[smem] * smem_in + [vmem] * (len(args) - smem_in),
        out_specs=[smem if i in smem_out else vmem for i in range(len(outs))],
        scratch_shapes=list(scratch),
        compiler_params=pltpu.CompilerParams(vmem_limit_bytes=VMEM_LIMIT),
    )(*args)


def exchange(x, axis, lowest):
    size = lax.axis_size(axis)
    bit = lowest
    parts = [x]
    while bit < size:
        if len(parts) > 1:
            x = functools.reduce(jnp.add, parts)
        radix = min(4, size // bit)
        parts = [x] + [
            lax.ppermute(x, axis, [(i, i ^ (d * bit)) for i in range(size)]) for d in range(1, radix)
        ]
        bit *= radix
    return parts


def body(noise, positions, wave_index, tile_lists, tile_counts):
    slabs, wave_count = lax.axis_size("space"), lax.axis_size("wave")
    length_x = float(slabs)
    vectors = noise.shape[0]
    particles = positions.shape[1]
    waves = wave_index.shape[1]
    tiles = particles // TILE
    share = PAIR_MOST // wave_count
    meta = jnp.stack(
        [lax.axis_index("wave"), jnp.int32(wave_count), lax.axis_index("space") % 2]
    ).astype(jnp.int32)
    core = [(i, i ^ 1) for i in range(slabs)]
    third = [(i, (i + 1 if i % 2 else i - 1) % slabs) for i in range(slabs)]
    table = ((particles, waves), BF16)
    rows_shape = ((3 * vectors, particles), F32)
    factor_rows = waves // TILE * 32

    cos_hi, sin_hi, cos_lo, sin_lo, terms, rows, msg, pack = call(
        functools.partial(start_kernel, length_x),
        [table] * 4 + [((8, waves), F32), rows_shape, ((factor_rows, TILE), F32), ((32 * tiles, TILE), F32)],
        (positions, noise, wave_index),
        [pltpu.VMEM((3, particles, TILE), F32)],
    )
    phases = (cos_hi, sin_hi, cos_lo, sin_lo)
    msg = jnp.concatenate([msg, jnp.zeros((8, TILE), F32), pack], axis=0)
    noise_rows = rows
    away = lax.ppermute(pack, "space", third)
    images, norms = [], []
    pairs = plan = None
    for step in range(DEGREE):
        other = lax.ppermute(msg, "space", core)
        chip = msg[: factor_rows + 8] + other[: factor_rows + 8]
        factors = exchange(chip, "space", 2)
        base, stride = factor_rows + 8, 32 if step == 0 else 24
        if step == 0:
            own, near = pack, other[base:]
            pairs, plan = call(
                functools.partial(pair_kernel, length_x, share),
                [((share, 2 * TILE, 6 * TILE), BF16), ((4, share), jnp.int32)],
                (meta, tile_lists, tile_counts, pack, other[base:], away),
                [pltpu.VMEM((3 * tiles, 8, TILE), F32)],
                smem_in=3,
                smem_out=(1,),
            )
        near_part = call(
            functools.partial(near_kernel, stride, base),
            [rows_shape],
            (plan, msg, other, away, pairs),
            [pltpu.VMEM((3 * tiles, 24, TILE), F32), pltpu.VMEM((tiles, 24, TILE), F32)],
            smem_in=1,
        )[0]
        part, norm = call(
            functools.partial(back_kernel, len(factors)),
            [rows_shape, ((8, TILE), F32)],
            (*factors, terms, *phases, near_part),
            [pltpu.VMEM((2, 48, waves), BF16)],
        )
        norms.append(norm)
        sums = exchange(part, "wave", 1)
        if step < DEGREE - 1:
            rows, msg = call(
                functools.partial(step_kernel, len(sums)),
                [rows_shape, ((factor_rows + 8 + 24 * tiles, TILE), F32)],
                (*sums, rows, terms, *phases),
            )
            images.append(rows)
            away = lax.ppermute(msg[factor_rows + 8 :], "space", third)
    return call(
        functools.partial(final_kernel, len(sums)),
        [((vectors, 3, particles), F32)],
        (*sums, noise_rows, *images, norms[1], norms[2]),
    )[0]


def solution(mesh):
    in_specs = (
        P(None, None, "space"),
        P(None, "space"),
        P(None, "wave"),
        P("space", None),
        P("space"),
    )
    out_specs = P(None, None, "space")
    return jax.shard_map(body, mesh=mesh, in_specs=in_specs, out_specs=out_specs, check_vma=False)
```

time: 411 us -> 118 us (0.29); the launches traced: 404 us -> 117 us
  waiting for transfers between devices: 192 us -> 47.6 us
  matrix products: 70.7 us -> 0 us
  other arithmetic: 53.1 us -> 0.26 us
  local copies, waits for them, and re-layouts: 41 us -> 10.1 us
  Pallas kernels: 0 us -> 30 us
  blocking collectives: 23.8 us -> 0 us
  starting transfers between devices: 7.25 us -> 28.9 us
  between operations: 15.6 us -> 0.3 us
    psum x6 -> x0, waiting for transfers between devices: 187 us -> none  [the longest x3 103 us: mobility(): weighted = project(lax.psum(factors, 'space'), weight, unit_waves)]
    dot_general x12 -> x0, matrix products: 70.7 us -> none  [the longest x3 32.9 us: mobility(): lax.dot_general(weighted.reshape(vectors * 3, 2 * local_waves), phases, (...]
    ppermute x8 -> x24, waiting for transfers between devices: 5.21 us -> 47.6 us  [the longest x18 24.2 us: exchange(): lax.ppermute(x, axis, [(i, i ^ d * bit) for i in range(size)])]
    pallas_call x0 -> x11, Pallas kernels: none -> 30 us  [call(): pl.pallas_call(kernel, out_shape=[jax.ShapeDtypeStruct(*o) for o in outs]...]
    psum x2 -> x0, blocking collectives: 23.8 us -> none  [the longest x1 12.1 us: body(): lax.psum(jnp.sum(unit_image * unit_image, axis=(1, 2)), 'space')]
    ppermute x8 -> x24, starting transfers between devices: 7.04 us -> 28.9 us  [the longest x18 25.4 us: exchange(): lax.ppermute(x, axis, [(i, i ^ d * bit) for i in range(size)])]
    cos x1 -> x0, other arithmetic: 16 us -> none  [make_phases(): jnp.cos(phase_angles)]
    mul x2 -> x0, local copies, waits for them, and re-layouts: 12.7 us -> none  [pair_block(): (identity + outer_product / NEAR_SQUARE) * envelope[None, None]]
  transfers between devices with their start and end apart: 14 -> 24, of which waited for: 8 -> 12; matrix products, arithmetic and copies ran while one was open for 26% -> 0% of each run, Pallas kernels for 0% -> 8%
where the time goes in v1:
time: 118 us; the launch traced here: 117 us
  waiting for transfers between devices  47.6 us (40%)
  Pallas kernels  30 us (25%)
  starting transfers between devices  28.9 us (24%)
  local copies, waits for them, and re-layouts  10.1 us (9%)
    pallas_call x11, Pallas kernels, call(): pl.pallas_call(kernel, out_shape=[jax.ShapeDtypeStruct(*o) for o in outs]...  30 us
    ppermute x18, starting transfers between devices, exchange(): lax.ppermute(x, axis, [(i, i ^ d * bit) for i in range(size)])  25.4 us
    ppermute x18, waiting for transfers between devices, exchange(): lax.ppermute(x, axis, [(i, i ^ d * bit) for i in range(size)])  24.2 us
    ppermute x2, waiting for transfers between devices, body(): away = lax.ppermute(msg[factor_rows + 8:], 'space', third)  12.9 us
    unnamed x23, local copies, waits for them, and re-layouts  9.39 us
    ppermute x1, waiting for transfers between devices, body(): away = lax.ppermute(pack, 'space', third)  6.44 us
    ppermute x3, waiting for transfers between devices, body(): other = lax.ppermute(msg, 'space', core)  4.13 us
  transfers between devices with their start and end apart: 24, of which 12 were waited for; matrix products, arithmetic and copies ran while one was open for 0% of the time, Pallas kernels for 8%

profile of v1, /device:TPU:0, one launch (start us, length us, event | category | flops | bytes accessed | tf_op | source)
XLA Modules:
  0.0 117.2 jit_solution(800039212246826837)
XLA Ops:
  0.0 1.0 copy.6.noise_ref
  1.0 0.7 copy-done.7
  1.7 0.7 copy-done.8
  2.4 7.6 %shard_map.55 = (bf16[1024,1024]{1,0:T(8,128)(2,1)S(1)}, bf16[1024,1024]{1,0:T(8,128)(2,1)S(1)}, bf16[1024,1024]{1,0:T(8,128)(2,1)S(1)}, bf16[1024,1024]{1,0:T(8...) custom-call(f32[3,1024]{1,0:T(4,128)S(1)} %copy-done.7, ...), custom_call_target="tpu_custom_call" | custom-call | tf_op jit(solution)/shard_map/pallas_call | solution.py:320
  10.1 1.3 %copy-done = bf16[1024,1024]{1,0:T(8,128)(2,1)} copy-done((bf16[1024,1024]{1,0:T(8,128)(2,1)}, bf16[1024,1024]{1,0:T(8,128)(2,1)S(1)}, u32[]{:S(2)}) %copy-start) | copy-done | bytes 2097176
  11.4 1.4 %copy-done.2 = bf16[1024,1024]{1,0:T(8,128)(2,1)} copy-done((bf16[1024,1024]{1,0:T(8,128)(2,1)}, bf16[1024,1024]{1,0:T(8,128)(2,1)S(1)}, u32[]{:S(2)}) %copy-start.2) | copy-done | bytes 2097176
  12.8 1.4 %copy-done.4 = bf16[1024,1024]{1,0:T(8,128)(2,1)} copy-done((bf16[1024,1024]{1,0:T(8,128)(2,1)}, bf16[1024,1024]{1,0:T(8,128)(2,1)S(1)}, u32[]{:S(2)}) %copy-start.4) | copy-done | bytes 2097176
  14.8 1.2 collective-permute-done.near_ref
  16.0 2.9 %collective-permute-start.1 = (f32[264,128]{1,0:T(8,128)S(1)}, f32[264,128]{1,0:T(8,128)S(1)}, u32[]{:S(2)}, u32[]{:S(2)}) collective-permute-start(f32[264,128]{1,0:T(8,128)S(1)} %slice_add_fusion.2.refs_0_), channel_id=1, source_target_pairs={{0,8},{4,12},{8,0},{12,4},{16,24},{20,28},{24,16},{28,20},{1,9},{5... | collective-permute-start | bytes 405512 | tf_op jit(solution)/shard_map/ppermute | solution.py:339
  18.9 1.5 %collective-permute-start.2 = (f32[264,128]{1,0:T(8,128)S(1)}, f32[264,128]{1,0:T(8,128)S(1)}, u32[]{:S(2)}, u32[]{:S(2)}) collective-permute-start(f32[264,128]{1,0:T(8,128)S(1)} %slice_add_fusion.2.refs_0_), channel_id=1, source_target_pairs={{0,16},{4,20},{8,24},{12,28},{16,0},{20,4},{24,8},{28,12},{1,17},{... | collective-permute-start | bytes 405512 | tf_op jit(solution)/shard_map/ppermute | solution.py:339
  20.4 1.8 %collective-permute-start.4 = (f32[256,128]{1,0:T(8,128)S(1)}, f32[256,128]{1,0:T(8,128)S(1)}, u32[]{:S(2)}, u32[]{:S(2)}) collective-permute-start(f32[256,128]{1,0:T(8,128)S(1)} %get-tuple-element.25.own_ref), channel_id=1, source_target_pairs={{0,28},{4,8},{8,4},{12,16},{16,12},{20,24},{24,20},{28,0},{1,29},{... | collective-permute-start | bytes 393224 | tf_op jit(solution)/shard_map/ppermute | solution.py:371
  22.4 6.4 %collective-permute-done.4.away_ref = f32[256,128]{1,0:T(8,128)S(1)} collective-permute-done((f32[256,128]{1,0:T(8,128)S(1)}, f32[256,128]{1,0:T(8,128)S(1)}, u32[]{:S(2)}, u32[]{:S(2)}) %collective-permute-start.4) | collective-permute-done | bytes 131104 | tf_op jit(solution)/shard_map/ppermute | solution.py:371
  28.8 0.7 copy-done.9
  29.5 0.7 copy-done.10
  30.1 6.0 %shard_map.56 = (bf16[8,256,768]{2,1,0:T(8,128)(2,1)S(1)}, s32[4,8]{1,0:T(4,128)S(1)}) custom-call(s32[3]{0:T(128)S(1)} %pad_add_fusion.meta_ref, s32[8,8]{1,0:T(8,128)S(1)} %copy-done.9, s32[8]{0:T(128)S(1)} %copy-done.10, f32[256,128]{1,0:T(8,128)S(1)} %get-tuple-element.25.own_ref, f32[256,128]{1,0:T(8,128)S(1)} %slice.35.near_ref, ...), custom_call_target="tpu_custom_call" | custom-call | tf_op jit(solution)/shard_map/pallas_call | solution.py:320
  36.1 1.2 %shard_map.57.refs_9_ = f32[24,1024]{1,0:T(8,128)S(1)} custom-call(s32[4,8]{1,0:T(4,128)S(1)} %get-tuple-element.31.plan_ref, f32[520,128]{1,0:T(8,128)S(1)} %pad_maximum_fusion.own_ref, f32[520,128]{1,0:T(8,128)S(1)} %collective-permute-done.near_ref, f32[256,128]{1,0:T(8,128)S(1)} %collective-permute-done.4.away_ref, ...), custom_call_target="tpu_custom_call" | custom-call | tf_op jit(solution)/shard_map/pallas_call | solution.py:320
  37.4 1.6 %copy-done.5 = bf16[1024,1024]{1,0:T(8,128)(2,1)S(1)} copy-done((bf16[1024,1024]{1,0:T(8,128)(2,1)S(1)}, bf16[1024,1024]{1,0:T(8,128)(2,1)}, u32[]{:S(2)}) %copy-start.5) | copy-done | bytes 2097176
  39.0 4.0 %shard_map.58 = (f32[24,1024]{1,0:T(8,128)S(1)}, f32[8,128]{1,0:T(8,128)}) custom-call(f32[264,128]{1,0:T(8,128)S(1)} %slice_add_fusion.2.refs_0_, f32[264,128]{1,0:T(8,128)S(1)} %collective-permute-done.1.refs_1_, f32[264,128]{1,0:T(8,128)S(1)} %collective-permute-done.2.refs_2_, f32[264,128]{1,0:T(8,128)} %collective-permute-done.3.refs_3_, ...), custom_call_target="tpu_custom_call" | custom-call | tf_op jit(solution)/shard_map/pallas_call | solution.py:320
  43.0 1.6 %collective-permute-start.5 = (f32[24,1024]{1,0:T(8,128)S(1)}, f32[24,1024]{1,0:T(8,128)S(1)}, u32[]{:S(2)}, u32[]{:S(2)}) collective-permute-start(f32[24,1024]{1,0:T(8,128)S(1)} %get-tuple-element.33.refs_0_), channel_id=1, source_target_pairs={{0,1},{1,0},{2,3},{3,2},{4,5},{5,4},{6,7},{7,6},{8,9},{9,8},{10,11... | collective-permute-start | bytes 294920 | tf_op jit(solution)/shard_map/ppermute | solution.py:339
  44.6 2.6 %collective-permute-start.6 = (f32[24,1024]{1,0:T(8,128)S(1)}, f32[24,1024]{1,0:T(8,128)S(1)}, u32[]{:S(2)}, u32[]{:S(2)}) collective-permute-start(f32[24,1024]{1,0:T(8,128)S(1)} %get-tuple-element.33.refs_0_), channel_id=1, source_target_pairs={{0,2},{1,3},{2,0},{3,1},{4,6},{5,7},{6,4},{7,5},{8,10},{9,11},{10,... | collective-permute-start | bytes 294920 | tf_op jit(solution)/shard_map/ppermute | solution.py:339
  47.6 7.6 %collective-permute-done.6.refs_2_ = f32[24,1024]{1,0:T(8,128)S(1)} collective-permute-done((f32[24,1024]{1,0:T(8,128)S(1)}, f32[24,1024]{1,0:T(8,128)S(1)}, u32[]{:S(2)}, u32[]{:S(2)}) %collective-permute-start.6) | collective-permute-done | bytes 98336 | tf_op jit(solution)/shard_map/ppermute | solution.py:339
  55.3 1.6 %shard_map.59 = (f32[24,1024]{1,0:T(8,128)S(1)}, f32[456,128]{1,0:T(8,128)S(1)}) custom-call(f32[24,1024]{1,0:T(8,128)S(1)} %get-tuple-element.33.refs_0_, f32[24,1024]{1,0:T(8,128)S(1)} %collective-permute-done.5.refs_1_, f32[24,1024]{1,0:T(8,128)S(1)} %collective-permute-done.6.refs_2_, f32[24,1024]{1,0:T(8,128)S(1)} %collective-permute-done.7.refs_3_, ...), custom_call_target="tpu_custom_call" | custom-call | tf_op jit(solution)/shard_map/pallas_call | solution.py:320
  56.9 1.5 %collective-permute-done.8.near_ref = f32[456,128]{1,0:T(8,128)S(1)} collective-permute-done((f32[456,128]{1,0:T(8,128)S(1)}, f32[456,128]{1,0:T(8,128)S(1)}, u32[]{:S(2)}, u32[]{:S(2)}) %collective-permute-start.8) | collective-permute-done | bytes 233504 | tf_op jit(solution)/shard_map/ppermute | solution.py:375
  59.0 1.5 %collective-permute-start.11 = (f32[264,128]{1,0:T(8,128)S(1)}, f32[264,128]{1,0:T(8,128)S(1)}, u32[]{:S(2)}, u32[]{:S(2)}) collective-permute-start(f32[264,128]{1,0:T(8,128)S(1)} %slice_add_fusion.1.refs_0_), channel_id=1, source_target_pairs={{0,24},{4,28},{8,16},{12,20},{16,8},{20,12},{24,0},{28,4},{1,25},{... | collective-permute-start | bytes 405512 | tf_op jit(solution)/shard_map/ppermute | solution.py:339
  60.5 1.5 %collective-permute-start.9 = (f32[264,128]{1,0:T(8,128)S(1)}, f32[264,128]{1,0:T(8,128)S(1)}, u32[]{:S(2)}, u32[]{:S(2)}) collective-permute-start(f32[264,128]{1,0:T(8,128)S(1)} %slice_add_fusion.1.refs_0_), channel_id=1, source_target_pairs={{0,8},{4,12},{8,0},{12,4},{16,24},{20,28},{24,16},{28,20},{1,9},{5... | collective-permute-start | bytes 405512 | tf_op jit(solution)/shard_map/ppermute | solution.py:339
  62.0 0.6 collective-permute-start.12
  62.6 6.6 %collective-permute-done.12.away_ref = f32[192,128]{1,0:T(8,128)S(1)} collective-permute-done((f32[192,128]{1,0:T(8,128)S(1)}, f32[192,128]{1,0:T(8,128)S(1)}, u32[]{:S(2)}, u32[]{:S(2)}) %collective-permute-start.12) | collective-permute-done | bytes 98336 | tf_op jit(solution)/shard_map/ppermute | solution.py:411
  69.2 1.2 %shard_map.60.refs_9_ = f32[24,1024]{1,0:T(8,128)S(1)} custom-call(s32[4,8]{1,0:T(4,128)S(1)} %get-tuple-element.31.plan_ref, f32[456,128]{1,0:T(8,128)S(1)} %get-tuple-element.35.own_ref, f32[456,128]{1,0:T(8,128)S(1)} %collective-permute-done.8.near_ref, f32[192,128]{1,0:T(8,128)S(1)} %collective-permute-done.12.away_ref, ...), custom_call_target="tpu_custom_call" | custom-call | tf_op jit(solution)/shard_map/pallas_call | solution.py:320
  70.5 2.6 %shard_map.61 = (f32[24,1024]{1,0:T(8,128)S(1)}, f32[8,128]{1,0:T(8,128)S(1)}) custom-call(f32[264,128]{1,0:T(8,128)S(1)} %slice_add_fusion.1.refs_0_, f32[264,128]{1,0:T(8,128)S(1)} %collective-permute-done.9.refs_1_, f32[264,128]{1,0:T(8,128)S(1)} %collective-permute-done.10.refs_2_, f32[264,128]{1,0:T(8,128)S(1)} %collective-permute-done.11.refs_3_, ...), custom_call_target="tpu_custom_call" | custom-call | tf_op jit(solution)/shard_map/pallas_call | solution.py:320
  73.1 2.5 %collective-permute-start.13 = (f32[24,1024]{1,0:T(8,128)S(1)}, f32[24,1024]{1,0:T(8,128)S(1)}, u32[]{:S(2)}, u32[]{:S(2)}) collective-permute-start(f32[24,1024]{1,0:T(8,128)S(1)} %get-tuple-element.36.refs_0_), channel_id=1, source_target_pairs={{0,1},{1,0},{2,3},{3,2},{4,5},{5,4},{6,7},{7,6},{8,9},{9,8},{10,11... | collective-permute-start | bytes 294920 | tf_op jit(solution)/shard_map/ppermute | solution.py:339
  75.6 1.1 collective-permute-start.14
  76.7 1.4 %collective-permute-start.15 = (f32[24,1024]{1,0:T(8,128)S(1)}, f32[24,1024]{1,0:T(8,128)S(1)}, u32[]{:S(2)}, u32[]{:S(2)}) collective-permute-start(f32[24,1024]{1,0:T(8,128)S(1)} %get-tuple-element.36.refs_0_), channel_id=1, source_target_pairs={{0,3},{1,2},{2,1},{3,0},{4,7},{5,6},{6,5},{7,4},{8,11},{9,10},{10,... | collective-permute-start | bytes 294920 | tf_op jit(solution)/shard_map/ppermute | solution.py:339
  78.1 0.7 collective-permute-done.13.refs_1_
  78.8 7.4 %collective-permute-done.14.refs_2_ = f32[24,1024]{1,0:T(8,128)S(1)} collective-permute-done((f32[24,1024]{1,0:T(8,128)S(1)}, f32[24,1024]{1,0:T(8,128)S(1)}, u32[]{:S(2)}, u32[]{:S(2)}) %collective-permute-start.14) | collective-permute-done | bytes 98336 | tf_op jit(solution)/shard_map/ppermute | solution.py:339
  86.3 1.6 %shard_map.62 = (f32[24,1024]{1,0:T(8,128)S(1)}, f32[456,128]{1,0:T(8,128)S(1)}) custom-call(f32[24,1024]{1,0:T(8,128)S(1)} %get-tuple-element.36.refs_0_, f32[24,1024]{1,0:T(8,128)S(1)} %collective-permute-done.13.refs_1_, f32[24,1024]{1,0:T(8,128)S(1)} %collective-permute-done.14.refs_2_, f32[24,1024]{1,0:T(8,128)S(1)} %collective-permute-done.15.refs_3_, ...), custom_call_target="tpu_custom_call" | custom-call | tf_op jit(solution)/shard_map/pallas_call | solution.py:320
  87.9 1.5 %collective-permute-done.16.near_ref = f32[456,128]{1,0:T(8,128)S(1)} collective-permute-done((f32[456,128]{1,0:T(8,128)S(1)}, f32[456,128]{1,0:T(8,128)S(1)}, u32[]{:S(2)}, u32[]{:S(2)}) %collective-permute-start.16) | collective-permute-done | bytes 233504 | tf_op jit(solution)/shard_map/ppermute | solution.py:375
  89.4 0.8 collective-permute-start.17
  90.2 1.4 %collective-permute-start.18 = (f32[264,128]{1,0:T(8,128)S(1)}, f32[264,128]{1,0:T(8,128)S(1)}, u32[]{:S(2)}, u32[]{:S(2)}) collective-permute-start(f32[264,128]{1,0:T(8,128)S(1)} %slice_add_fusion.refs_0_), channel_id=1, source_target_pairs={{0,16},{4,20},{8,24},{12,28},{16,0},{20,4},{24,8},{28,12},{1,17},{... | collective-permute-start | bytes 405512 | tf_op jit(solution)/shard_map/ppermute | solution.py:339
  91.6 1.4 %collective-permute-start.19 = (f32[264,128]{1,0:T(8,128)S(1)}, f32[264,128]{1,0:T(8,128)S(1)}, u32[]{:S(2)}, u32[]{:S(2)}) collective-permute-start(f32[264,128]{1,0:T(8,128)S(1)} %slice_add_fusion.refs_0_), channel_id=1, source_target_pairs={{0,24},{4,28},{8,16},{12,20},{16,8},{20,12},{24,0},{28,4},{1,25},{... | collective-permute-start | bytes 405512 | tf_op jit(solution)/shard_map/ppermute | solution.py:339
  93.4 6.2 %collective-permute-done.20.away_ref = f32[192,128]{1,0:T(8,128)S(1)} collective-permute-done((f32[192,128]{1,0:T(8,128)S(1)}, f32[192,128]{1,0:T(8,128)S(1)}, u32[]{:S(2)}, u32[]{:S(2)}) %collective-permute-start.20) | collective-permute-done | bytes 98336 | tf_op jit(solution)/shard_map/ppermute | solution.py:411
  99.7 1.2 %shard_map.63.refs_9_ = f32[24,1024]{1,0:T(8,128)S(1)} custom-call(s32[4,8]{1,0:T(4,128)S(1)} %get-tuple-element.31.plan_ref, f32[456,128]{1,0:T(8,128)S(1)} %get-tuple-element.38.own_ref, f32[456,128]{1,0:T(8,128)S(1)} %collective-permute-done.16.near_ref, f32[192,128]{1,0:T(8,128)S(1)} %collective-permute-done.20.away_ref, ...), custom_call_target="tpu_custom_call" | custom-call | tf_op jit(solution)/shard_map/pallas_call | solution.py:320
  101.0 2.6 %shard_map.64 = (f32[24,1024]{1,0:T(8,128)S(1)}, f32[8,128]{1,0:T(8,128)S(1)}) custom-call(f32[264,128]{1,0:T(8,128)S(1)} %slice_add_fusion.refs_0_, f32[264,128]{1,0:T(8,128)S(1)} %collective-permute-done.17.refs_1_, f32[264,128]{1,0:T(8,128)S(1)} %collective-permute-done.18.refs_2_, f32[264,128]{1,0:T(8,128)S(1)} %collective-permute-done.19.refs_3_, ...), custom_call_target="tpu_custom_call" | custom-call | tf_op jit(solution)/shard_map/pallas_call | solution.py:320
  103.6 1.9 %collective-permute-start.21 = (f32[24,1024]{1,0:T(8,128)S(1)}, f32[24,1024]{1,0:T(8,128)S(1)}, u32[]{:S(2)}, u32[]{:S(2)}) collective-permute-start(f32[24,1024]{1,0:T(8,128)S(1)} %get-tuple-element.39.refs_0_), channel_id=1, source_target_pairs={{0,1},{1,0},{2,3},{3,2},{4,5},{5,4},{6,7},{7,6},{8,9},{9,8},{10,11... | collective-permute-start | bytes 294920 | tf_op jit(solution)/shard_map/ppermute | solution.py:339
  105.5 1.2 %collective-permute-start.22 = (f32[24,1024]{1,0:T(8,128)S(1)}, f32[24,1024]{1,0:T(8,128)S(1)}, u32[]{:S(2)}, u32[]{:S(2)}) collective-permute-start(f32[24,1024]{1,0:T(8,128)S(1)} %get-tuple-element.39.refs_0_), channel_id=1, source_target_pairs={{0,2},{1,3},{2,0},{3,1},{4,6},{5,7},{6,4},{7,5},{8,10},{9,11},{10,... | collective-permute-start | bytes 294920 | tf_op jit(solution)/shard_map/ppermute | solution.py:339
  106.7 1.4 %collective-permute-start.23 = (f32[24,1024]{1,0:T(8,128)S(1)}, f32[24,1024]{1,0:T(8,128)S(1)}, u32[]{:S(2)}, u32[]{:S(2)}) collective-permute-start(f32[24,1024]{1,0:T(8,128)S(1)} %get-tuple-element.39.refs_0_), channel_id=1, source_target_pairs={{0,3},{1,2},{2,1},{3,0},{4,7},{5,6},{6,5},{7,4},{8,11},{9,10},{10,... | collective-permute-start | bytes 294920 | tf_op jit(solution)/shard_map/ppermute | solution.py:339
  108.0 1.0 collective-permute-done.21.refs_1_
  109.0 7.2 %collective-permute-done.22.refs_2_ = f32[24,1024]{1,0:T(8,128)S(1)} collective-permute-done((f32[24,1024]{1,0:T(8,128)S(1)}, f32[24,1024]{1,0:T(8,128)S(1)}, u32[]{:S(2)}, u32[]{:S(2)}) %collective-permute-start.22) | collective-permute-done | bytes 98336 | tf_op jit(solution)/shard_map/ppermute | solution.py:339
  116.5 0.7 copy.7
  (45 shorter events, 2.8 us)
Async XLA Ops:
  1.0 0.7 copy-start.7
  1.7 0.7 copy-start.8
  10.1 1.3 %copy-start = (bf16[1024,1024]{1,0:T(8,128)(2,1)}, bf16[1024,1024]{1,0:T(8,128)(2,1)S(1)}, u32[]{:S(2)}) copy-start(bf16[1024,1024]{1,0:T(8,128)(2,1)S(1)} %get-tuple-element.28.refs_6_.refs_7_) | copy-start | bytes 6291460
  11.4 1.4 %copy-start.2 = (bf16[1024,1024]{1,0:T(8,128)(2,1)}, bf16[1024,1024]{1,0:T(8,128)(2,1)S(1)}, u32[]{:S(2)}) copy-start(bf16[1024,1024]{1,0:T(8,128)(2,1)S(1)} %get-tuple-element.29.refs_7_.refs_8_) | copy-start | bytes 6291460
  12.8 1.4 %copy-start.4 = (bf16[1024,1024]{1,0:T(8,128)(2,1)}, bf16[1024,1024]{1,0:T(8,128)(2,1)S(1)}, u32[]{:S(2)}) copy-start(bf16[1024,1024]{1,0:T(8,128)(2,1)S(1)} %get-tuple-element.30.refs_8_.refs_9_) | copy-start | bytes 6291460
  14.3 1.7 %collective-permute-start = (f32[520,128]{1,0:T(8,128)S(1)}, f32[520,128]{1,0:T(8,128)S(1)}, u32[]{:S(2)}, u32[]{:S(2)}) collective-permute-start(f32[520,128]{1,0:T(8,128)S(1)} %pad_maximum_fusion.own_ref), channel_id=1, source_target_pairs={{0,4},{4,0},{8,12},{12,8},{16,20},{20,16},{24,28},{28,24},{1,5},{5... | collective-permute-start | bytes 798728 | tf_op jit(solution)/shard_map/ppermute | solution.py:375
  16.0 21.4 %collective-permute-start.1 = (f32[264,128]{1,0:T(8,128)S(1)}, f32[264,128]{1,0:T(8,128)S(1)}, u32[]{:S(2)}, u32[]{:S(2)}) collective-permute-start(f32[264,128]{1,0:T(8,128)S(1)} %slice_add_fusion.2.refs_0_), channel_id=1, source_target_pairs={{0,8},{4,12},{8,0},{12,4},{16,24},{20,28},{24,16},{28,20},{1,9},{5... | collective-permute-start | bytes 405512 | tf_op jit(solution)/shard_map/ppermute | solution.py:339
  18.9 18.5 %collective-permute-start.2 = (f32[264,128]{1,0:T(8,128)S(1)}, f32[264,128]{1,0:T(8,128)S(1)}, u32[]{:S(2)}, u32[]{:S(2)}) collective-permute-start(f32[264,128]{1,0:T(8,128)S(1)} %slice_add_fusion.2.refs_0_), channel_id=1, source_target_pairs={{0,16},{4,20},{8,24},{12,28},{16,0},{20,4},{24,8},{28,12},{1,17},{... | collective-permute-start | bytes 405512 | tf_op jit(solution)/shard_map/ppermute | solution.py:339
  20.4 17.0 %collective-permute-start.3 = (f32[264,128]{1,0:T(8,128)S(1)}, f32[264,128]{1,0:T(8,128)}, u32[]{:S(2)}, u32[]{:S(2)}) collective-permute-start(f32[264,128]{1,0:T(8,128)S(1)} %slice_add_fusion.2.refs_0_), channel_id=1, source_target_pairs={{0,24},{4,28},{8,16},{12,20},{16,8},{20,12},{24,0},{28,4},{1,25},{... | collective-permute-start | bytes 405512 | tf_op jit(solution)/shard_map/ppermute | solution.py:339
  20.4 8.4 %collective-permute-start.4 = (f32[256,128]{1,0:T(8,128)S(1)}, f32[256,128]{1,0:T(8,128)S(1)}, u32[]{:S(2)}, u32[]{:S(2)}) collective-permute-start(f32[256,128]{1,0:T(8,128)S(1)} %get-tuple-element.25.own_ref), channel_id=1, source_target_pairs={{0,28},{4,8},{8,4},{12,16},{16,12},{20,24},{24,20},{28,0},{1,29},{... | collective-permute-start | bytes 393224 | tf_op jit(solution)/shard_map/ppermute | solution.py:371
  22.3 15.1 %copy-start.1 = (bf16[1024,1024]{1,0:T(8,128)(2,1)S(1)}, bf16[1024,1024]{1,0:T(8,128)(2,1)}, u32[]{:S(2)}) copy-start(bf16[1024,1024]{1,0:T(8,128)(2,1)} %copy-done) | copy-start | bytes 6291460
  22.3 15.1 %copy-start.3 = (bf16[1024,1024]{1,0:T(8,128)(2,1)S(1)}, bf16[1024,1024]{1,0:T(8,128)(2,1)}, u32[]{:S(2)}) copy-start(bf16[1024,1024]{1,0:T(8,128)(2,1)} %copy-done.2) | copy-start | bytes 6291460
  28.8 0.7 copy-start.9
  29.5 0.7 copy-start.10
  37.4 1.6 %copy-start.5 = (bf16[1024,1024]{1,0:T(8,128)(2,1)S(1)}, bf16[1024,1024]{1,0:T(8,128)(2,1)}, u32[]{:S(2)}) copy-start(bf16[1024,1024]{1,0:T(8,128)(2,1)} %copy-done.4) | copy-start | bytes 6291460
  43.0 4.6 %collective-permute-start.5 = (f32[24,1024]{1,0:T(8,128)S(1)}, f32[24,1024]{1,0:T(8,128)S(1)}, u32[]{:S(2)}, u32[]{:S(2)}) collective-permute-start(f32[24,1024]{1,0:T(8,128)S(1)} %get-tuple-element.33.refs_0_), channel_id=1, source_target_pairs={{0,1},{1,0},{2,3},{3,2},{4,5},{5,4},{6,7},{7,6},{8,9},{9,8},{10,11... | collective-permute-start | bytes 294920 | tf_op jit(solution)/shard_map/ppermute | solution.py:339
  44.6 10.7 %collective-permute-start.6 = (f32[24,1024]{1,0:T(8,128)S(1)}, f32[24,1024]{1,0:T(8,128)S(1)}, u32[]{:S(2)}, u32[]{:S(2)}) collective-permute-start(f32[24,1024]{1,0:T(8,128)S(1)} %get-tuple-element.33.refs_0_), channel_id=1, source_target_pairs={{0,2},{1,3},{2,0},{3,1},{4,6},{5,7},{6,4},{7,5},{8,10},{9,11},{10,... | collective-permute-start | bytes 294920 | tf_op jit(solution)/shard_map/ppermute | solution.py:339
  47.2 8.1 %collective-permute-start.7 = (f32[24,1024]{1,0:T(8,128)S(1)}, f32[24,1024]{1,0:T(8,128)S(1)}, u32[]{:S(2)}, u32[]{:S(2)}) collective-permute-start(f32[24,1024]{1,0:T(8,128)S(1)} %get-tuple-element.33.refs_0_), channel_id=1, source_target_pairs={{0,3},{1,2},{2,1},{3,0},{4,7},{5,6},{6,5},{7,4},{8,11},{9,10},{10,... | collective-permute-start | bytes 294920 | tf_op jit(solution)/shard_map/ppermute | solution.py:339
  56.8 1.6 %collective-permute-start.8 = (f32[456,128]{1,0:T(8,128)S(1)}, f32[456,128]{1,0:T(8,128)S(1)}, u32[]{:S(2)}, u32[]{:S(2)}) collective-permute-start(f32[456,128]{1,0:T(8,128)S(1)} %get-tuple-element.35.own_ref), channel_id=1, source_target_pairs={{0,4},{4,0},{8,12},{12,8},{16,20},{20,16},{24,28},{28,24},{1,5},{5... | collective-permute-start | bytes 700424 | tf_op jit(solution)/shard_map/ppermute | solution.py:375
  58.4 12.1 %copy-start.6 = (bf16[1024,1024]{1,0:T(8,128)(2,1)S(1)}, bf16[1024,1024]{1,0:T(8,128)(2,1)}, u32[]{:S(2)}) copy-start(bf16[1024,1024]{1,0:T(8,128)(2,1)} %copy-done.4) | copy-start | bytes 6291460
  58.4 12.0 %collective-permute-start.10 = (f32[264,128]{1,0:T(8,128)S(1)}, f32[264,128]{1,0:T(8,128)S(1)}, u32[]{:S(2)}, u32[]{:S(2)}) collective-permute-start(f32[264,128]{1,0:T(8,128)S(1)} %slice_add_fusion.1.refs_0_), channel_id=1, source_target_pairs={{0,16},{4,20},{8,24},{12,28},{16,0},{20,4},{24,8},{28,12},{1,17},{... | collective-permute-start | bytes 405512 | tf_op jit(solution)/shard_map/ppermute | solution.py:339
  59.0 11.5 %collective-permute-start.11 = (f32[264,128]{1,0:T(8,128)S(1)}, f32[264,128]{1,0:T(8,128)S(1)}, u32[]{:S(2)}, u32[]{:S(2)}) collective-permute-start(f32[264,128]{1,0:T(8,128)S(1)} %slice_add_fusion.1.refs_0_), channel_id=1, source_target_pairs={{0,24},{4,28},{8,16},{12,20},{16,8},{20,12},{24,0},{28,4},{1,25},{... | collective-permute-start | bytes 405512 | tf_op jit(solution)/shard_map/ppermute | solution.py:339
  60.5 10.0 %collective-permute-start.9 = (f32[264,128]{1,0:T(8,128)S(1)}, f32[264,128]{1,0:T(8,128)S(1)}, u32[]{:S(2)}, u32[]{:S(2)}) collective-permute-start(f32[264,128]{1,0:T(8,128)S(1)} %slice_add_fusion.1.refs_0_), channel_id=1, source_target_pairs={{0,8},{4,12},{8,0},{12,4},{16,24},{20,28},{24,16},{28,20},{1,9},{5... | collective-permute-start | bytes 405512 | tf_op jit(solution)/shard_map/ppermute | solution.py:339
  62.0 7.2 %collective-permute-start.12 = (f32[192,128]{1,0:T(8,128)S(1)}, f32[192,128]{1,0:T(8,128)S(1)}, u32[]{:S(2)}, u32[]{:S(2)}) collective-permute-start(f32[192,128]{1,0:T(8,128)S(1)} %slice.30), channel_id=1, source_target_pairs={{0,28},{4,8},{8,4},{12,16},{16,12},{20,24},{24,20},{28,0},{1,29},{... | collective-permute-start | bytes 294920 | tf_op jit(solution)/shard_map/ppermute | solution.py:411
  73.1 5.7 %collective-permute-start.13 = (f32[24,1024]{1,0:T(8,128)S(1)}, f32[24,1024]{1,0:T(8,128)S(1)}, u32[]{:S(2)}, u32[]{:S(2)}) collective-permute-start(f32[24,1024]{1,0:T(8,128)S(1)} %get-tuple-element.36.refs_0_), channel_id=1, source_target_pairs={{0,1},{1,0},{2,3},{3,2},{4,5},{5,4},{6,7},{7,6},{8,9},{9,8},{10,11... | collective-permute-start | bytes 294920 | tf_op jit(solution)/shard_map/ppermute | solution.py:339
  75.6 10.7 %collective-permute-start.14 = (f32[24,1024]{1,0:T(8,128)S(1)}, f32[24,1024]{1,0:T(8,128)S(1)}, u32[]{:S(2)}, u32[]{:S(2)}) collective-permute-start(f32[24,1024]{1,0:T(8,128)S(1)} %get-tuple-element.36.refs_0_), channel_id=1, source_target_pairs={{0,2},{1,3},{2,0},{3,1},{4,6},{5,7},{6,4},{7,5},{8,10},{9,11},{10,... | collective-permute-start | bytes 294920 | tf_op jit(solution)/shard_map/ppermute | solution.py:339
  76.7 9.5 %collective-permute-start.15 = (f32[24,1024]{1,0:T(8,128)S(1)}, f32[24,1024]{1,0:T(8,128)S(1)}, u32[]{:S(2)}, u32[]{:S(2)}) collective-permute-start(f32[24,1024]{1,0:T(8,128)S(1)} %get-tuple-element.36.refs_0_), channel_id=1, source_target_pairs={{0,3},{1,2},{2,1},{3,0},{4,7},{5,6},{6,5},{7,4},{8,11},{9,10},{10,... | collective-permute-start | bytes 294920 | tf_op jit(solution)/shard_map/ppermute | solution.py:339
  87.9 1.6 %collective-permute-start.16 = (f32[456,128]{1,0:T(8,128)S(1)}, f32[456,128]{1,0:T(8,128)S(1)}, u32[]{:S(2)}, u32[]{:S(2)}) collective-permute-start(f32[456,128]{1,0:T(8,128)S(1)} %get-tuple-element.38.own_ref), channel_id=1, source_target_pairs={{0,4},{4,0},{8,12},{12,8},{16,20},{20,16},{24,28},{28,24},{1,5},{5... | collective-permute-start | bytes 700424 | tf_op jit(solution)/shard_map/ppermute | solution.py:375
  89.4 11.5 %collective-permute-start.17 = (f32[264,128]{1,0:T(8,128)S(1)}, f32[264,128]{1,0:T(8,128)S(1)}, u32[]{:S(2)}, u32[]{:S(2)}) collective-permute-start(f32[264,128]{1,0:T(8,128)S(1)} %slice_add_fusion.refs_0_), channel_id=1, source_target_pairs={{0,8},{4,12},{8,0},{12,4},{16,24},{20,28},{24,16},{28,20},{1,9},{5... | collective-permute-start | bytes 405512 | tf_op jit(solution)/shard_map/ppermute | solution.py:339
  90.2 10.7 %collective-permute-start.18 = (f32[264,128]{1,0:T(8,128)S(1)}, f32[264,128]{1,0:T(8,128)S(1)}, u32[]{:S(2)}, u32[]{:S(2)}) collective-permute-start(f32[264,128]{1,0:T(8,128)S(1)} %slice_add_fusion.refs_0_), channel_id=1, source_target_pairs={{0,16},{4,20},{8,24},{12,28},{16,0},{20,4},{24,8},{28,12},{1,17},{... | collective-permute-start | bytes 405512 | tf_op jit(solution)/shard_map/ppermute | solution.py:339
  91.6 9.4 %collective-permute-start.19 = (f32[264,128]{1,0:T(8,128)S(1)}, f32[264,128]{1,0:T(8,128)S(1)}, u32[]{:S(2)}, u32[]{:S(2)}) collective-permute-start(f32[264,128]{1,0:T(8,128)S(1)} %slice_add_fusion.refs_0_), channel_id=1, source_target_pairs={{0,24},{4,28},{8,16},{12,20},{16,8},{20,12},{24,0},{28,4},{1,25},{... | collective-permute-start | bytes 405512 | tf_op jit(solution)/shard_map/ppermute | solution.py:339
  93.0 6.7 %collective-permute-start.20 = (f32[192,128]{1,0:T(8,128)S(1)}, f32[192,128]{1,0:T(8,128)S(1)}, u32[]{:S(2)}, u32[]{:S(2)}) collective-permute-start(f32[192,128]{1,0:T(8,128)S(1)} %slice.33), channel_id=1, source_target_pairs={{0,28},{4,8},{8,4},{12,16},{16,12},{20,24},{24,20},{28,0},{1,29},{... | collective-permute-start | bytes 294920 | tf_op jit(solution)/shard_map/ppermute | solution.py:411
  103.6 5.4 %collective-permute-start.21 = (f32[24,1024]{1,0:T(8,128)S(1)}, f32[24,1024]{1,0:T(8,128)S(1)}, u32[]{:S(2)}, u32[]{:S(2)}) collective-permute-start(f32[24,1024]{1,0:T(8,128)S(1)} %get-tuple-element.39.refs_0_), channel_id=1, source_target_pairs={{0,1},{1,0},{2,3},{3,2},{4,5},{5,4},{6,7},{7,6},{8,9},{9,8},{10,11... | collective-permute-start | bytes 294920 | tf_op jit(solution)/shard_map/ppermute | solution.py:339
  105.5 10.7 %collective-permute-start.22 = (f32[24,1024]{1,0:T(8,128)S(1)}, f32[24,1024]{1,0:T(8,128)S(1)}, u32[]{:S(2)}, u32[]{:S(2)}) collective-permute-start(f32[24,1024]{1,0:T(8,128)S(1)} %get-tuple-element.39.refs_0_), channel_id=1, source_target_pairs={{0,2},{1,3},{2,0},{3,1},{4,6},{5,7},{6,4},{7,5},{8,10},{9,11},{10,... | collective-permute-start | bytes 294920 | tf_op jit(solution)/shard_map/ppermute | solution.py:339
  106.7 9.5 %collective-permute-start.23 = (f32[24,1024]{1,0:T(8,128)S(1)}, f32[24,1024]{1,0:T(8,128)S(1)}, u32[]{:S(2)}, u32[]{:S(2)}) collective-permute-start(f32[24,1024]{1,0:T(8,128)S(1)} %get-tuple-element.39.refs_0_), channel_id=1, source_target_pairs={{0,3},{1,2},{2,1},{3,0},{4,7},{5,6},{6,5},{7,4},{8,11},{9,10},{10,... | collective-permute-start | bytes 294920 | tf_op jit(solution)/shard_map/ppermute | solution.py:339

commit v2 on v1

v2 whole, which is shorter than its diff:
```python
import functools
import math

import jax
import jax.numpy as jnp
from jax import lax
from jax.experimental import pallas as pl
from jax.experimental.pallas import tpu as pltpu
from jax.sharding import PartitionSpec as P

TILE = 128
KW = 4096
NB_MOST = 8
DEGREE = 3
PAIR_MOST = 32
GROUP = 4

SIDE_CROSS = 8.0
NEAR_SQUARE = 0.36
NEAR_AMP = 0.15
FAR_AMP = 8.0
SPLIT_SQUARE = 64.0
SCREEN = 4.0
SAFETY = 1.25
SPREAD = 100.0
EPSILON = 1e-06

F32 = jnp.float32
BF16 = jnp.bfloat16
VMEM_LIMIT = 8 << 20

SINE = (4.44287968, -7.30781651, 3.59777427, -0.791199386)
ROUNDER = 12582912.0
COSINE = (1.4142040014266968, -6.97763729095459, 5.715188026428223, -1.728213906288147)


def split(x):
    high = x.astype(BF16)
    return high, (x - high.astype(F32)).astype(BF16)


def poly(coeffs, x):
    acc = coeffs[-1]
    for c in coeffs[-2::-1]:
        acc = acc * x + c
    return acc


def emit(kinds, terms, at, msg_ref):
    width = kinds[0].shape[1]
    t = terms[:, at : at + width]
    pieces = []
    for full in kinds:
        fx, fy, fz = full[0:8], full[8:16], full[16:24]
        pieces.append(t[1:2] * fx + t[2:3] * fy)
        pieces.append(t[3:4] * fx + t[4:5] * fy + t[5:6] * fz)
    stacked = jnp.concatenate(pieces, axis=0)
    for k in range(width // TILE):
        row = (at // TILE + k) * 32
        msg_ref[row : row + 32, :] = stacked[:, k * TILE : (k + 1) * TILE]


def product(both, high_table, low_table):
    first = jnp.dot(both, high_table, preferred_element_type=F32)
    second = jnp.dot(both[:24], low_table, preferred_element_type=F32)
    return first[:24] + (first[24:] + second)


def forward(rows, table_ref, terms, msg_ref):
    waves = table_ref.shape[2]
    both = jnp.concatenate(split(rows), axis=0)
    step = min(512, waves)
    for at in range(0, waves, step):
        cols = slice(at, at + step)
        kinds = [product(both, table_ref[k, :, cols], table_ref[2 + k, :, cols]) for k in range(2)]
        emit(kinds, terms, at, msg_ref)


def own_tiles(rows, share, rank, ranks):
    picked = []
    for k in range(share):
        tiles = [rows[:, t * TILE : (t + 1) * TILE] for t in range(k * ranks, (k + 1) * ranks)]
        mine = tiles[0]
        for r in range(1, ranks):
            mine = jnp.where(jnp.abs(rank - r) < 0.5, tiles[r], mine)
        picked.append(mine)
    return jnp.concatenate(picked, axis=0)


def start_kernel(
    length_x, share, stack_ref, table_ref, flip_ref, terms_ref, msg_ref, mask_ref, turn_ref, left_ref, sum_ref
):
    particles = table_ref.shape[1]
    waves = table_ref.shape[2]
    tiles = particles // TILE
    ranks = tiles // share
    sides = (length_x, SIDE_CROSS, SIDE_CROSS)
    counts = [stack_ref[27 + a : 28 + a, :waves] for a in range(3)]
    k1, k2, k3 = [2.0 * math.pi * counts[a] / sides[a] for a in range(3)]
    square = k1 * k1 + k2 * k2 + k3 * k3
    scaled = square / SPLIT_SQUARE
    weight = FAR_AMP * (1.0 + scaled) * jnp.exp(-scaled) / (KW * (square + SCREEN))
    flat_square = k1 * k1 + k2 * k2
    flat = 1.0 / jnp.sqrt(flat_square)
    both = 1.0 / jnp.sqrt(square * flat_square)
    terms_ref[...] = jnp.concatenate(
        [
            weight,
            -k2 * flat,
            k1 * flat,
            -k1 * k3 * both,
            -k2 * k3 * both,
            flat_square * both,
            stack_ref[30:32, :waves],
        ],
        axis=0,
    )
    mask_ref[...] = jnp.broadcast_to(stack_ref[30:31, :TILE], mask_ref.shape)
    noise = stack_ref[0:24, :particles]
    places = jnp.concatenate([stack_ref[24:27, :particles], jnp.zeros((5, particles), F32)], axis=0)
    base = waves // TILE * 32
    rank = stack_ref[31:32, :TILE]
    row = base + 8 + 24 * share
    msg_ref[base : base + 8, :] = jnp.zeros((8, TILE), F32)
    msg_ref[base + 8 : row, :] = own_tiles(noise, share, rank, ranks)
    msg_ref[row : row + 8 * share, :] = own_tiles(places, share, rank, ranks)
    left_ref[...] = jnp.concatenate(split(noise), axis=0)
    parts = []
    rest = jnp.concatenate([places[a : a + 1] / sides[a] for a in range(3)], axis=0)
    for _ in range(3):
        parts.append(rest.astype(BF16).astype(F32))
        rest = rest - parts[-1]
    turn_ref[...] = jnp.concatenate(parts + [jnp.zeros((7, particles), F32)], axis=0).T.astype(BF16)
    numbers = jnp.concatenate(counts * 3 + [jnp.zeros((7, waves), F32)], axis=0).astype(BF16)
    block = min(512, particles)
    wide = 256

    def make(rows):
        for at in range(0, waves, wide):
            turns = jnp.dot(turn_ref[rows, :], numbers[:, at : at + wide], preferred_element_type=F32)
            for j in range(0, wide, TILE):
                cols = slice(at + j, at + j + TILE)
                t = turns[:, j : j + TILE]
                r = t - ((t + ROUNDER) - ROUNDER)
                x = r * r
                s = r * poly(SINE, x)
                c = poly(COSINE, x)
                table_ref[0, rows, cols], table_ref[2, rows, cols] = split(1.0 - s * s)
                table_ref[1, rows, cols], table_ref[3, rows, cols] = split(s * c)

    def use(rows, first):
        for kind in range(2):
            for at in range(0, waves, wide):
                cols = slice(at, at + wide)
                piece = product(left_ref[:, rows], table_ref[kind, rows, cols], table_ref[2 + kind, rows, cols])
                sum_ref[kind, :, cols] = piece if first else sum_ref[kind, :, cols] + piece
        for kind in range(4):
            flip_ref[kind, :, rows] = table_ref[kind, rows, :].T

    blocks = [slice(at, at + block) for at in range(0, particles, block)]
    make(blocks[0])
    for k in range(1, len(blocks)):
        use(blocks[k - 1], k == 1)
        make(blocks[k])
    use(blocks[-1], len(blocks) == 1)
    emit([sum_ref[0], sum_ref[1]], terms_ref[...], 0, msg_ref)


def pair_kernel(length_x, base, share, meta_ref, lists_ref, counts_ref, pos_ref, own_ref, near_ref, away_ref, out_ref, plan_ref, place_ref, column_ref):
    tiles = lists_ref.shape[0]
    ranks = tiles // share
    odd = meta_ref[0] == 1
    rank = meta_ref[1]
    seen = jnp.int32(0)
    for target in range(tiles):
        for k in range(NB_MOST):
            window = lists_ref[target, k]
            side, tile = lax.div(window, tiles), lax.rem(window, tiles)
            which = jnp.where(side == 1, 0, jnp.where((side == 0) == odd, 1, 2))
            mine = (k < counts_ref[target]) & (lax.rem(tile, ranks) == rank)
            plan_ref[0, seen] = target
            plan_ref[1, seen] = which * share + lax.div(tile, ranks)
            plan_ref[2, seen] = jnp.where(window == tiles + target, 1, 0)
            seen = jnp.minimum(seen + jnp.where(mine, 1, 0), PAIR_MOST)
    plan_ref[3, 0] = seen
    for k in range(GROUP):
        plan_ref[0, seen + k] = tiles
        plan_ref[1, seen + k] = 0
    sides = (length_x, SIDE_CROSS, SIDE_CROSS)
    reach = math.sqrt(NEAR_SQUARE)
    filler = jnp.zeros((5, TILE), F32)
    for i in range(tiles):
        lanes = slice(i * TILE, (i + 1) * TILE)
        place_ref[i] = jnp.concatenate([pos_ref[a : a + 1, lanes] / sides[a] for a in range(3)] + [filler], axis=0)
    for slab, ref in enumerate((own_ref, near_ref, away_ref)):
        for i in range(share):
            row = (base if slab < 2 else 24 * share) + 8 * i
            place = ref[row : row + 8, :]
            place = jnp.concatenate([place[a : a + 1] / sides[a] for a in range(3)] + [filler], axis=0)
            column_ref[slab * share + i] = place.T
    count = 32

    def pair(p, carry):
        target = place_ref[plan_ref[0, p]]
        source = column_ref[plan_ref[1, p]]
        own = plan_ref[2, p].astype(F32)
        lines = [target[a : a + 1] for a in range(3)]
        for at in range(0, TILE, count):
            rows = slice(at, at + count)
            q = []
            for a in range(3):
                offset = lines[a] - jnp.broadcast_to(source[rows, a : a + 1], (count, TILE))
                offset = offset - jnp.floor(offset + 0.5)
                q.append(offset * (sides[a] / reach))
            square = q[0] * q[0] + q[1] * q[1] + q[2] * q[2]
            same = (
                lax.broadcasted_iota(jnp.int32, (count, TILE), 0) + at
                == lax.broadcasted_iota(jnp.int32, (count, TILE), 1)
            )
            envelope = jnp.exp(-square) * jnp.where(same, NEAR_AMP * (1.0 - own), NEAR_AMP)
            slot = 0
            for a in range(3):
                scaled = envelope * q[a]
                for b in range(a, 3):
                    value = scaled * q[b]
                    if a == b:
                        value = value + envelope
                    cols = slice(slot * TILE, (slot + 1) * TILE)
                    out_ref[p, rows, cols], out_ref[p, TILE + at : TILE + at + count, cols] = split(value)
                    slot += 1
        return carry

    lax.fori_loop(0, seen, pair, 0)


def near_kernel(base, share, plan_ref, own_ref, near_ref, away_ref, matrix_ref, out_ref, window_ref, sum_ref):
    tiles = sum_ref.shape[0] - 1
    for slab, ref in enumerate((own_ref, near_ref, away_ref)):
        for i in range(share):
            row = (base if slab < 2 else 0) + 24 * i
            window_ref[slab * share + i] = ref[row : row + 24, :]
    sum_ref[...] = jnp.zeros_like(sum_ref)

    def part(rows, at):
        return rows[:, at * TILE : (at + 1) * TILE]

    def several(at, carry):
        for k in range(GROUP):
            p = at * GROUP + k
            high, low = split(window_ref[plan_ref[1, p]])
            left = jnp.concatenate(
                [
                    jnp.concatenate([high, high], axis=1),
                    jnp.concatenate([low, jnp.zeros_like(low)], axis=1),
                ],
                axis=0,
            )
            both = jnp.dot(left, matrix_ref[p], preferred_element_type=F32)
            full = both[:24] + both[24:]
            x, y, z = full[0:8], full[8:16], full[16:24]
            sum_ref[plan_ref[0, p]] += jnp.concatenate(
                [
                    part(x, 0) + part(y, 1) + part(z, 2),
                    part(x, 1) + part(y, 3) + part(z, 4),
                    part(x, 2) + part(y, 4) + part(z, 5),
                ],
                axis=0,
            )
        return carry

    lax.fori_loop(0, lax.div(plan_ref[3, 0] + (GROUP - 1), GROUP), several, 0)
    for i in range(tiles):
        out_ref[:, i * TILE : (i + 1) * TILE] = sum_ref[i]


def back_kernel(parts, *refs):
    ins, (near_ref, terms_ref, flip_ref, out_ref, norm_ref, left_ref) = (
        refs[:parts],
        refs[parts:],
    )
    waves = terms_ref.shape[1]
    particles = out_ref.shape[1]
    tiles = waves // TILE
    norm = ins[0][32 * tiles : 32 * tiles + 8, :]
    for ref in ins[1:]:
        norm = norm + ref[32 * tiles : 32 * tiles + 8, :]
    norm_ref[...] = norm
    for i in range(tiles):
        block = ins[0][32 * i : 32 * i + 32, :]
        for ref in ins[1:]:
            block = block + ref[32 * i : 32 * i + 32, :]
        t = terms_ref[:, i * TILE : (i + 1) * TILE]
        block = block * t[0:1]
        for kind in range(2):
            one, two = block[16 * kind : 16 * kind + 8], block[16 * kind + 8 : 16 * kind + 16]
            rows = jnp.concatenate(
                [t[1:2] * one + t[3:4] * two, t[2:3] * one + t[4:5] * two, t[5:6] * two], axis=0
            )
            left_ref[kind, :, i * TILE : (i + 1) * TILE] = jnp.concatenate(split(rows), axis=0)
    step = min(512, particles)
    for at in range(0, particles, step):
        cols = slice(at, at + step)
        total = near_ref[:, cols]
        for k in range(2):
            total = total + product(left_ref[k], flip_ref[k, :, cols], flip_ref[2 + k, :, cols])
        out_ref[:, cols] = total


def step_kernel(parts, share, *refs):
    ins, (force_ref, terms_ref, table_ref, rows_ref, msg_ref) = refs[:parts], refs[parts:]
    particles = force_ref.shape[1]
    waves = terms_ref.shape[1]
    total = ins[0][...]
    for ref in ins[1:]:
        total = total + ref[...]
    rows = force_ref[...] + total
    rows_ref[...] = rows
    squares = rows * rows
    squares = squares[0:8] + squares[8:16] + squares[16:24]
    tiles = particles // TILE
    norm = squares[:, 0:TILE]
    for i in range(1, tiles):
        norm = norm + squares[:, i * TILE : (i + 1) * TILE]
    base = waves // TILE * 32
    msg_ref[base : base + 8, :] = norm
    msg_ref[base + 8 : base + 8 + 24 * share, :] = own_tiles(rows, share, terms_ref[7:8, :TILE], tiles // share)
    forward(rows, table_ref, terms_ref[...], msg_ref)


def final_kernel(parts, *refs):
    ins, (noise_ref, one_ref, two_ref, first_ref, second_ref, out_ref) = refs[:parts], refs[parts:]
    total = ins[0][...]
    for ref in ins[1:]:
        total = total + ref[...]
    u0, u1, u2 = noise_ref[...], one_ref[...], two_ref[...]
    u3 = u2 + total
    first = jnp.sum(first_ref[...], axis=1, keepdims=True)
    second = jnp.sum(second_ref[...], axis=1, keepdims=True)
    ratio = jnp.max(second / (first + EPSILON), axis=0, keepdims=True)
    high = SAFETY * jnp.sqrt(ratio)
    low = high / SPREAD
    nodes = DEGREE + 1
    angles = [math.pi * (j + 0.5) / nodes for j in range(nodes)]
    samples = [jnp.sqrt(0.5 * (high - low) * math.cos(t) + 0.5 * (high + low)) for t in angles]
    coeffs = []
    for k in range(nodes):
        acc = samples[0] * math.cos(k * angles[0])
        for j in range(1, nodes):
            acc = acc + samples[j] * math.cos(k * angles[j])
        coeffs.append(acc * (2.0 / nodes) * (0.5 if k == 0 else 1.0))
    p = 2.0 / (high - low)
    q = (high + low) / (high - low)
    v0, v1, v2 = p * u1 - q * u0, p * u2 - q * u1, p * u3 - q * u2
    t2 = 2.0 * (p * v1 - q * v0) - u0
    m2 = 2.0 * (p * v2 - q * v1) - u1
    t3 = 2.0 * (p * m2 - q * t2) - v0
    out_ref[...] = coeffs[0] * u0 + coeffs[1] * v0 + coeffs[2] * t2 + coeffs[3] * t3


def call(kernel, outs, args, scratch=(), smem_in=0, smem_out=(), flops=0, space=pltpu.VMEM):
    vmem = pl.BlockSpec(memory_space=pltpu.VMEM)
    smem = pl.BlockSpec(memory_space=pltpu.SMEM)
    return pl.pallas_call(
        kernel,
        out_shape=[jax.ShapeDtypeStruct(*o) for o in outs],
        in_specs=[smem] * smem_in + [pl.BlockSpec(memory_space=space)] * (len(args) - smem_in),
        out_specs=[smem if i in smem_out else vmem for i in range(len(outs))],
        scratch_shapes=list(scratch),
        cost_estimate=pl.CostEstimate(flops=flops, bytes_accessed=0, transcendentals=0),
        compiler_params=pltpu.CompilerParams(vmem_limit_bytes=VMEM_LIMIT),
    )(*args)


def exchange(x, axis, lowest):
    size = lax.axis_size(axis)
    bit = lowest
    parts = [x]
    while bit < size:
        if len(parts) > 1:
            x = functools.reduce(jnp.add, parts)
        radix = min(4, size // bit)
        parts = [x] + [
            lax.ppermute(x, axis, [(i, i ^ (d * bit)) for i in range(size)]) for d in range(1, radix)
        ]
        bit *= radix
    return parts


def chip_sums(chip, mask, away, work):
    size = lax.axis_size("space")
    done = None if work is None else work(away)
    if size != 8:
        return exchange(chip, "space", 2), away, done
    half = chip.shape[0] // 2
    low = mask < 0.5
    one = lax.ppermute(chip, "space", [(i, i ^ (4 if i % 2 else 2)) for i in range(size)])
    mine = jnp.where(low, chip[:half], chip[half:])
    across = lax.ppermute(mine, "space", [(i, i ^ 6) for i in range(size)])
    across, away, done = lax.optimization_barrier((across, away, done))
    both = jnp.concatenate([jnp.where(low, across, 0.0), jnp.where(low, 0.0, across)], axis=0)
    fetched = one + both
    return [chip, fetched, lax.ppermute(fetched, "space", [(i, i ^ 1) for i in range(size)])], away, done


def body(noise, positions, wave_index, tile_lists, tile_counts):
    slabs = lax.axis_size("space")
    length_x = float(slabs)
    vectors = noise.shape[0]
    particles = positions.shape[1]
    waves = wave_index.shape[1]
    tiles = particles // TILE
    ranks = lax.axis_size("wave")
    share = tiles // ranks
    place = jnp.stack([lax.axis_index("space") & 1, lax.axis_index("wave")]).astype(jnp.int32)
    core = [(i, i ^ 1) for i in range(slabs)]
    third = [(i, (i + 1 if i % 2 else i - 1) % slabs) for i in range(slabs)]
    table = ((4, particles, waves), BF16)
    rows_shape = ((3 * vectors, particles), F32)
    base = waves // TILE * 32 + 8
    far_flops = 2 * 96 * particles * waves * 2

    rows = jnp.transpose(noise, (1, 0, 2)).reshape(3 * vectors, particles)
    width = max(particles, waves)
    stack = jnp.concatenate(
        [
            jnp.pad(x.astype(F32), ((0, 0), (0, width - x.shape[1])))
            for x in (rows, positions, wave_index, jnp.broadcast_to(place[:, None], (2, width)))
        ],
        axis=0,
    )
    phases, flipped, terms, msg, mask = call(
        functools.partial(start_kernel, length_x, share),
        [
            table,
            ((4, waves, particles), BF16),
            ((8, waves), F32),
            ((base + 32 * share, TILE), F32),
            ((base // 2, TILE), F32),
        ],
        (stack,),
        [
            pltpu.VMEM((particles, 16), BF16),
            pltpu.VMEM((6 * vectors, particles), BF16),
            pltpu.VMEM((2, 3 * vectors, waves), F32),
        ],
        flops=4 * far_flops,
    )
    noise_rows = rows
    images, norms = [], []

    matrices = plan = None
    for step in range(DEGREE):
        other = lax.ppermute(msg, "space", core)
        away = lax.ppermute(msg[base:], "space", third)

        def pair_work(away):
            return call(
                functools.partial(pair_kernel, length_x, base + 24 * share, share),
                [((PAIR_MOST + GROUP, 2 * TILE, 6 * TILE), BF16), ((4, PAIR_MOST + GROUP), jnp.int32)],
                (place, tile_lists, tile_counts, positions, msg, other, away),
                [pltpu.VMEM((tiles, 8, TILE), F32), pltpu.VMEM((3 * share, TILE, 8), F32)],
                smem_in=3,
                smem_out=(1,),
                flops=far_flops,
            )

        def near_work():
            return call(
                functools.partial(near_kernel, base, share),
                [rows_shape],
                (plan, msg, other, away, matrices),
                [pltpu.VMEM((3 * share, 24, TILE), F32), pltpu.VMEM((tiles + 1, 24, TILE), F32)],
                smem_in=1,
                flops=far_flops // 2,
            )[0]

        factors, away, made = chip_sums(msg[:base] + other[:base], mask, away, pair_work if step == 0 else None)
        if step == 0:
            matrices, plan = made
        near_part = near_work()
        part, norm = call(
            functools.partial(back_kernel, len(factors)),
            [rows_shape, ((8, TILE), F32)],
            (*factors, near_part, terms, flipped),
            [pltpu.VMEM((2, 48, waves), BF16)],
            flops=far_flops,
        )
        norms.append(norm)
        sums = exchange(part, "wave", 1)
        if step < DEGREE - 1:
            rows, msg = call(
                functools.partial(step_kernel, len(sums), share),
                [rows_shape, ((base + 24 * share, TILE), F32)],
                (*sums, rows, terms, phases),
                flops=far_flops,
            )
            images.append(rows)
    out = call(
        functools.partial(final_kernel, len(sums)),
        [rows_shape],
        (*sums, noise_rows, *images, norms[1], norms[2]),
    )[0]
    return jnp.transpose(out.reshape(3, vectors, particles), (1, 0, 2))


def solution(mesh):
    in_specs = (
        P(None, None, "space"),
        P(None, "space"),
        P(None, "wave"),
        P("space", None),
        P("space"),
    )
    out_specs = P(None, None, "space")
    return jax.shard_map(body, mesh=mesh, in_specs=in_specs, out_specs=out_specs, check_vma=False)
```

time: 118 us -> 91.9 us (0.78)
  waiting for transfers between devices: 47.6 us -> 34.9 us
  local copies, waits for them, and re-layouts: 10.1 us -> 2.15 us
  Pallas kernels: 30 us -> 25.7 us
  starting transfers between devices: 28.9 us -> 26.9 us
  other arithmetic: 0.26 us -> 2 us
    ppermute x18 -> x9, starting transfers between devices: 25.4 us -> 13.4 us  [exchange(): lax.ppermute(x, axis, [(i, i ^ d * bit) for i in range(size)])]
    ppermute x3 -> x12, waiting for transfers between devices: 19.3 us -> 8.14 us  [the longest x3 4.55 us: body(): away = lax.ppermute(msg[base:], 'space', third)]
    ppermute x3 -> x12, starting transfers between devices: 2.84 us -> 12.8 us  [the longest x3 5.7 us: body(): away = lax.ppermute(msg[base:], 'space', third)]
    unnamed x23 -> x8, local copies, waits for them, and re-layouts: 9.39 us -> 2.07 us
    pallas_call x11, Pallas kernels: 30 us -> 25.7 us  [call(): pl.pallas_call(kernel, out_shape=[jax.ShapeDtypeStruct(*o) for o in outs]...]
    ppermute x3, waiting for transfers between devices: 4.13 us -> 2.75 us  [body(): other = lax.ppermute(msg, 'space', core)]
    ppermute x18 -> x9, waiting for transfers between devices: 24.2 us -> 24 us  [exchange(): lax.ppermute(x, axis, [(i, i ^ d * bit) for i in range(size)])]
  transfers between devices with their start and end apart: 24 -> 24, of which waited for: 12 -> 13; matrix products, arithmetic and copies ran while one was open for 0% -> 0% of each run, Pallas kernels for 8% -> 11%
where the time goes in v2:
time: 91.9 us
  waiting for transfers between devices  34.9 us (38%)
  starting transfers between devices  26.9 us (29%)
  Pallas kernels  25.7 us (28%)
  local copies, waits for them, and re-layouts  2.15 us (2%)
  other arithmetic  2 us (2%)
    pallas_call x11, Pallas kernels, call(): pl.pallas_call(kernel, out_shape=[jax.ShapeDtypeStruct(*o) for o in outs]...  25.7 us
    ppermute x9, waiting for transfers between devices, exchange(): lax.ppermute(x, axis, [(i, i ^ d * bit) for i in range(size)])  24 us
    ppermute x9, starting transfers between devices, exchange(): lax.ppermute(x, axis, [(i, i ^ d * bit) for i in range(size)])  13.4 us
    ppermute x3, starting transfers between devices, body(): away = lax.ppermute(msg[base:], 'space', third)  5.7 us
    ppermute x3, waiting for transfers between devices, body(): away = lax.ppermute(msg[base:], 'space', third)  4.55 us
    ppermute x3, starting transfers between devices, chip_sums(): across = lax.ppermute(mine, 'space', [(i, i ^ 6) for i in range(size)])  4.11 us
    ppermute x3, waiting for transfers between devices, chip_sums(): lax.ppermute(chip, 'space', [(i, i ^ (4 if i % 2 else 2)) for i in range(...  3.1 us
    ppermute x3, waiting for transfers between devices, body(): other = lax.ppermute(msg, 'space', core)  2.75 us
  transfers between devices with their start and end apart: 24, of which 13 were waited for; matrix products, arithmetic and copies ran while one was open for 0% of the time, Pallas kernels for 11%

profile of v2, /device:TPU:0, one launch (start us, length us, event | category | flops | bytes accessed | tf_op | source)
XLA Modules:
  0.0 91.9 jit_solution(897054840291134572)
XLA Ops:
  0.0 0.7 convert_element_type.7
  0.9 1.0 %maximum_maximum_fusion.stack_ref = f32[32,1024]{1,0:T(8,128)S(1)} fusion(f32[3,1024]{1,0:T(4,128)S(1)} %convert_element_type.7, f32[3,1024]{1,0:T(4,128)} %pos_ref.1, f32[24,1024]{1,0:T(8,128)} %bitcast.8, f32[32]{0:T(128)S(1)} %pad.9.clone), kind=kLoop, calls=%fused_computation.6 | loop fusion | flops 98304 | bytes 254080 | tf_op jit(solution)/shard_map/concatenate | solution.py:424
  1.9 6.6 %shard_map.55 = (bf16[4,1024,1024]{2,1,0:T(8,128)(2,1)S(1)}, bf16[4,1024,1024]{2,1,0:T(8,128)(2,1)S(1)}, f32[8,1024]{1,0:T(8,128)S(1)}, f32[328,128]{1,0:T(8,128)S(1)}, f32[132,128]{1,0:T(8,128)S(1)}) custom-call(f32[32,1024]{1,0:T(8,128)S(1)} %maximum_maximum_fusion.stack_ref), custom_call_target="tpu_custom_call" | custom-call | flops 1610612736 | tf_op jit(solution)/shard_map/pallas_call | solution.py:363
  8.5 0.5 collective-permute-start
  9.0 3.6 %collective-permute-start.3 = (f32[64,128]{1,0:T(8,128)S(1)}, f32[64,128]{1,0:T(8,128)S(1)}, u32[]{:S(2)}, u32[]{:S(2)}) collective-permute-start(f32[64,128]{1,0:T(8,128)S(1)} %slice.49), channel_id=1, source_target_pairs={{0,28},{4,8},{8,4},{12,16},{16,12},{20,24},{24,20},{28,0},{1,29},{... | collective-permute-start | bytes 98312 | tf_op jit(solution)/shard_map/ppermute | solution.py:454
  12.6 1.3 %collective-permute-start.2 = (f32[132,128]{1,0:T(8,128)S(1)}, f32[132,128]{1,0:T(8,128)S(1)}, u32[]{:S(2)}, u32[]{:S(2)}) collective-permute-start(f32[132,128]{1,0:T(8,128)S(1)} %get-tuple-element.53), channel_id=1, source_target_pairs={{0,24},{4,28},{8,16},{12,20},{16,8},{20,12},{24,0},{28,4},{1,25},{... | collective-permute-start | bytes 202760 | tf_op jit(solution)/shard_map/ppermute | solution.py:398
  14.0 0.7 collective-permute-start.1
  14.7 0.7 copy-done.1
  15.4 0.7 copy-done.2
  16.1 0.7 copy-done.3
  16.7 4.4 %shard_map.56 = (bf16[36,256,768]{2,1,0:T(8,128)(2,1)S(1)}, s32[4,36]{1,0:T(4,128)S(1)}) custom-call(s32[2]{0:T(128)S(1)} %get-tuple-element.56.meta_ref, s32[8,8]{1,0:T(8,128)S(1)} %copy-done.2, s32[8]{0:T(128)S(1)} %copy-done.3, f32[3,1024]{1,0:T(4,128)S(1)} %copy-done.1, f32[328,128]{1,0:T(8,128)S(1)} %get-tuple-element.29.own_ref, ...), custom_call_target="tpu_custom_call" | custom-call | flops 402653184 | tf_op jit(solution)/shard_map/pallas_call | solution.py:363
  21.3 1.8 %shard_map.57.refs_3_ = f32[24,1024]{1,0:T(8,128)S(1)} custom-call(s32[4,36]{1,0:T(4,128)S(1)} %get-tuple-element.34.plan_ref, f32[328,128]{1,0:T(8,128)S(1)} %get-tuple-element.29.own_ref, f32[328,128]{1,0:T(8,128)S(1)} %collective-permute-done.near_ref, f32[64,128]{1,0:T(8,128)S(1)} %collective-permute-done.3.away_ref, ...), custom_call_target="tpu_custom_call" | custom-call | flops 201326592 | tf_op jit(solution)/shard_map/pallas_call | solution.py:363
  23.1 2.1 %shard_map.58 = (f32[24,1024]{1,0:T(8,128)S(1)}, f32[8,128]{1,0:T(8,128)}) custom-call(f32[264,128]{1,0:T(8,128)S(1)} %slice_add_fusion.2.refs_0_, f32[264,128]{1,0:T(8,128)S(1)} %maximum_add_fusion.refs_1_, f32[264,128]{1,0:T(8,128)S(1)} %collective-permute-done.4.refs_2_, f32[24,1024]{1,0:T(8,128)S(1)} %shard_map.57.refs_3_, ...), custom_call_target="tpu_custom_call" | custom-call | flops 402653184 | tf_op jit(solution)/shard_map/pallas_call | solution.py:363
  25.1 1.8 %collective-permute-start.5 = (f32[24,1024]{1,0:T(8,128)S(1)}, f32[24,1024]{1,0:T(8,128)S(1)}, u32[]{:S(2)}, u32[]{:S(2)}) collective-permute-start(f32[24,1024]{1,0:T(8,128)S(1)} %get-tuple-element.39.refs_0_), channel_id=1, source_target_pairs={{0,1},{1,0},{2,3},{3,2},{4,5},{5,4},{6,7},{7,6},{8,9},{9,8},{10,11... | collective-permute-start | bytes 294920 | tf_op jit(solution)/shard_map/ppermute | solution.py:383
  26.9 1.3 %collective-permute-start.6 = (f32[24,1024]{1,0:T(8,128)S(1)}, f32[24,1024]{1,0:T(8,128)S(1)}, u32[]{:S(2)}, u32[]{:S(2)}) collective-permute-start(f32[24,1024]{1,0:T(8,128)S(1)} %get-tuple-element.39.refs_0_), channel_id=1, source_target_pairs={{0,2},{1,3},{2,0},{3,1},{4,6},{5,7},{6,4},{7,5},{8,10},{9,11},{10,... | collective-permute-start | bytes 294920 | tf_op jit(solution)/shard_map/ppermute | solution.py:383
  28.2 1.3 %collective-permute-start.7 = (f32[24,1024]{1,0:T(8,128)S(1)}, f32[24,1024]{1,0:T(8,128)S(1)}, u32[]{:S(2)}, u32[]{:S(2)}) collective-permute-start(f32[24,1024]{1,0:T(8,128)S(1)} %get-tuple-element.39.refs_0_), channel_id=1, source_target_pairs={{0,3},{1,2},{2,1},{3,0},{4,7},{5,6},{6,5},{7,4},{8,11},{9,10},{10,... | collective-permute-start | bytes 294920 | tf_op jit(solution)/shard_map/ppermute | solution.py:383
  29.5 0.9 collective-permute-done.5.refs_1_
  30.4 7.1 %collective-permute-done.6.refs_2_ = f32[24,1024]{1,0:T(8,128)S(1)} collective-permute-done((f32[24,1024]{1,0:T(8,128)S(1)}, f32[24,1024]{1,0:T(8,128)S(1)}, u32[]{:S(2)}, u32[]{:S(2)}) %collective-permute-start.6) | collective-permute-done | bytes 98336 | tf_op jit(solution)/shard_map/ppermute | solution.py:383
  37.5 1.6 %shard_map.59 = (f32[24,1024]{1,0:T(8,128)S(1)}, f32[312,128]{1,0:T(8,128)S(1)}) custom-call(f32[24,1024]{1,0:T(8,128)S(1)} %get-tuple-element.39.refs_0_, f32[24,1024]{1,0:T(8,128)S(1)} %collective-permute-done.5.refs_1_, f32[24,1024]{1,0:T(8,128)S(1)} %collective-permute-done.6.refs_2_, f32[24,1024]{1,0:T(8,128)S(1)} %collective-permute-done.7.refs_3_, ...), custom_call_target="tpu_custom_call" | custom-call | flops 402653184 | tf_op jit(solution)/shard_map/pallas_call | solution.py:363
  39.2 1.4 %collective-permute-done.8.near_ref = f32[312,128]{1,0:T(8,128)S(1)} collective-permute-done((f32[312,128]{1,0:T(8,128)S(1)}, f32[312,128]{1,0:T(8,128)S(1)}, u32[]{:S(2)}, u32[]{:S(2)}) %collective-permute-start.8) | collective-permute-done | bytes 159776 | tf_op jit(solution)/shard_map/ppermute | solution.py:453
  40.6 2.1 %collective-permute-start.10 = (f32[132,128]{1,0:T(8,128)S(1)}, f32[132,128]{1,0:T(8,128)S(1)}, u32[]{:S(2)}, u32[]{:S(2)}) collective-permute-start(f32[132,128]{1,0:T(8,128)S(1)} %slice_select_fusion.1), channel_id=1, source_target_pairs={{0,24},{4,28},{8,16},{12,20},{16,8},{20,12},{24,0},{28,4},{1,25},{... | collective-permute-start | bytes 202760 | tf_op jit(solution)/shard_map/ppermute | solution.py:398
  42.7 0.3 collective-permute-start.11
  43.0 1.2 %collective-permute-start.9 = (f32[264,128]{1,0:T(8,128)S(1)}, f32[264,128]{1,0:T(8,128)S(1)}, u32[]{:S(2)}, u32[]{:S(2)}) collective-permute-start(f32[264,128]{1,0:T(8,128)S(1)} %slice_add_fusion.1.refs_0_), channel_id=1, source_target_pairs={{0,8},{4,20},{8,0},{12,28},{16,24},{20,4},{24,16},{28,12},{1,9},{5... | collective-permute-start | bytes 405512 | tf_op jit(solution)/shard_map/ppermute | solution.py:396
  44.2 2.8 %collective-permute-done.11.away_ref = f32[48,128]{1,0:T(8,128)S(1)} collective-permute-done((f32[48,128]{1,0:T(8,128)S(1)}, f32[48,128]{1,0:T(8,128)S(1)}, u32[]{:S(2)}, u32[]{:S(2)}) %collective-permute-start.11) | collective-permute-done | bytes 24608 | tf_op jit(solution)/shard_map/ppermute | solution.py:454
  47.0 1.2 %collective-permute-done.9 = f32[264,128]{1,0:T(8,128)S(1)} collective-permute-done((f32[264,128]{1,0:T(8,128)S(1)}, f32[264,128]{1,0:T(8,128)S(1)}, u32[]{:S(2)}, u32[]{:S(2)}) %collective-permute-start.9) | collective-permute-done | bytes 135200 | tf_op jit(solution)/shard_map/ppermute | solution.py:396
  48.2 0.2 collective-permute-start.12
  48.4 1.9 %shard_map.60.refs_3_ = f32[24,1024]{1,0:T(8,128)S(1)} custom-call(s32[4,36]{1,0:T(4,128)S(1)} %get-tuple-element.34.plan_ref, f32[312,128]{1,0:T(8,128)S(1)} %get-tuple-element.41.own_ref, f32[312,128]{1,0:T(8,128)S(1)} %collective-permute-done.8.near_ref, f32[48,128]{1,0:T(8,128)S(1)} %collective-permute-done.11.away_ref, ...), custom_call_target="tpu_custom_call" | custom-call | flops 201326592 | tf_op jit(solution)/shard_map/pallas_call | solution.py:363
  50.3 1.6 %shard_map.61 = (f32[24,1024]{1,0:T(8,128)S(1)}, f32[8,128]{1,0:T(8,128)S(1)}) custom-call(f32[264,128]{1,0:T(8,128)S(1)} %slice_add_fusion.1.refs_0_, f32[264,128]{1,0:T(8,128)S(1)} %maximum_add_fusion.1.refs_1_, f32[264,128]{1,0:T(8,128)S(1)} %collective-permute-done.12.refs_2_, f32[24,1024]{1,0:T(8,128)S(1)} %shard_map.60.refs_3_, ...), custom_call_target="tpu_custom_call" | custom-call | flops 402653184 | tf_op jit(solution)/shard_map/pallas_call | solution.py:363
  51.9 2.0 %collective-permute-start.13 = (f32[24,1024]{1,0:T(8,128)S(1)}, f32[24,1024]{1,0:T(8,128)S(1)}, u32[]{:S(2)}, u32[]{:S(2)}) collective-permute-start(f32[24,1024]{1,0:T(8,128)S(1)} %get-tuple-element.44.refs_0_), channel_id=1, source_target_pairs={{0,1},{1,0},{2,3},{3,2},{4,5},{5,4},{6,7},{7,6},{8,9},{9,8},{10,11... | collective-permute-start | bytes 294920 | tf_op jit(solution)/shard_map/ppermute | solution.py:383
  53.9 2.4 %collective-permute-start.15 = (f32[24,1024]{1,0:T(8,128)S(1)}, f32[24,1024]{1,0:T(8,128)S(1)}, u32[]{:S(2)}, u32[]{:S(2)}) collective-permute-start(f32[24,1024]{1,0:T(8,128)S(1)} %get-tuple-element.44.refs_0_), channel_id=1, source_target_pairs={{0,3},{1,2},{2,1},{3,0},{4,7},{5,6},{6,5},{7,4},{8,11},{9,10},{10,... | collective-permute-start | bytes 294920 | tf_op jit(solution)/shard_map/ppermute | solution.py:383
  56.3 1.0 %collective-permute-done.13.refs_1_ = f32[24,1024]{1,0:T(8,128)S(1)} collective-permute-done((f32[24,1024]{1,0:T(8,128)S(1)}, f32[24,1024]{1,0:T(8,128)S(1)}, u32[]{:S(2)}, u32[]{:S(2)}) %collective-permute-start.13) | collective-permute-done | bytes 98336 | tf_op jit(solution)/shard_map/ppermute | solution.py:383
  57.3 7.1 %collective-permute-done.14.refs_2_ = f32[24,1024]{1,0:T(8,128)S(1)} collective-permute-done((f32[24,1024]{1,0:T(8,128)S(1)}, f32[24,1024]{1,0:T(8,128)S(1)}, u32[]{:S(2)}, u32[]{:S(2)}) %collective-permute-start.14) | collective-permute-done | bytes 98336 | tf_op jit(solution)/shard_map/ppermute | solution.py:383
  64.4 1.6 %shard_map.62 = (f32[24,1024]{1,0:T(8,128)S(1)}, f32[312,128]{1,0:T(8,128)S(1)}) custom-call(f32[24,1024]{1,0:T(8,128)S(1)} %get-tuple-element.44.refs_0_, f32[24,1024]{1,0:T(8,128)S(1)} %collective-permute-done.13.refs_1_, f32[24,1024]{1,0:T(8,128)S(1)} %collective-permute-done.14.refs_2_, f32[24,1024]{1,0:T(8,128)S(1)} %collective-permute-done.15.refs_3_, ...), custom_call_target="tpu_custom_call" | custom-call | flops 402653184 | tf_op jit(solution)/shard_map/pallas_call | solution.py:363
  66.1 1.4 %collective-permute-done.16.near_ref = f32[312,128]{1,0:T(8,128)S(1)} collective-permute-done((f32[312,128]{1,0:T(8,128)S(1)}, f32[312,128]{1,0:T(8,128)S(1)}, u32[]{:S(2)}, u32[]{:S(2)}) %collective-permute-start.16) | collective-permute-done | bytes 159776 | tf_op jit(solution)/shard_map/ppermute | solution.py:453
  67.5 0.6 collective-permute-start.18
  68.2 1.8 %collective-permute-start.19 = (f32[48,128]{1,0:T(8,128)S(1)}, f32[48,128]{1,0:T(8,128)S(1)}, u32[]{:S(2)}, u32[]{:S(2)}) collective-permute-start(f32[48,128]{1,0:T(8,128)S(1)} %slice.59), channel_id=1, source_target_pairs={{0,28},{4,8},{8,4},{12,16},{16,12},{20,24},{24,20},{28,0},{1,29},{... | collective-permute-start | bytes 73736 | tf_op jit(solution)/shard_map/ppermute | solution.py:454
  70.0 0.8 collective-permute-start.17
  70.8 1.8 %collective-permute-done.19.away_ref = f32[48,128]{1,0:T(8,128)S(1)} collective-permute-done((f32[48,128]{1,0:T(8,128)S(1)}, f32[48,128]{1,0:T(8,128)S(1)}, u32[]{:S(2)}, u32[]{:S(2)}) %collective-permute-start.19) | collective-permute-done | bytes 24608 | tf_op jit(solution)/shard_map/ppermute | solution.py:454
  72.6 0.5 collective-permute-done.18
  73.1 1.9 %collective-permute-done.17 = f32[264,128]{1,0:T(8,128)S(1)} collective-permute-done((f32[264,128]{1,0:T(8,128)S(1)}, f32[264,128]{1,0:T(8,128)S(1)}, u32[]{:S(2)}, u32[]{:S(2)}) %collective-permute-start.17) | collective-permute-done | bytes 135200 | tf_op jit(solution)/shard_map/ppermute | solution.py:396
  75.0 0.1 collective-permute-start.20
  75.1 1.8 %shard_map.63.refs_3_ = f32[24,1024]{1,0:T(8,128)S(1)} custom-call(s32[4,36]{1,0:T(4,128)S(1)} %get-tuple-element.34.plan_ref, f32[312,128]{1,0:T(8,128)S(1)} %get-tuple-element.46.own_ref, f32[312,128]{1,0:T(8,128)S(1)} %collective-permute-done.16.near_ref, f32[48,128]{1,0:T(8,128)S(1)} %collective-permute-done.19.away_ref, ...), custom_call_target="tpu_custom_call" | custom-call | flops 201326592 | tf_op jit(solution)/shard_map/pallas_call | solution.py:363
  76.9 1.6 %shard_map.64 = (f32[24,1024]{1,0:T(8,128)S(1)}, f32[8,128]{1,0:T(8,128)S(1)}) custom-call(f32[264,128]{1,0:T(8,128)S(1)} %slice_add_fusion.refs_0_, f32[264,128]{1,0:T(8,128)S(1)} %maximum_add_fusion.2.refs_1_, f32[264,128]{1,0:T(8,128)S(1)} %collective-permute-done.20.refs_2_, f32[24,1024]{1,0:T(8,128)S(1)} %shard_map.63.refs_3_, ...), custom_call_target="tpu_custom_call" | custom-call | flops 402653184 | tf_op jit(solution)/shard_map/pallas_call | solution.py:363
  78.5 2.1 %collective-permute-start.21 = (f32[24,1024]{1,0:T(8,128)S(1)}, f32[24,1024]{1,0:T(8,128)S(1)}, u32[]{:S(2)}, u32[]{:S(2)}) collective-permute-start(f32[24,1024]{1,0:T(8,128)S(1)} %get-tuple-element.49.refs_0_), channel_id=1, source_target_pairs={{0,1},{1,0},{2,3},{3,2},{4,5},{5,4},{6,7},{7,6},{8,9},{9,8},{10,11... | collective-permute-start | bytes 294920 | tf_op jit(solution)/shard_map/ppermute | solution.py:383
  80.6 2.4 %collective-permute-start.23 = (f32[24,1024]{1,0:T(8,128)S(1)}, f32[24,1024]{1,0:T(8,128)S(1)}, u32[]{:S(2)}, u32[]{:S(2)}) collective-permute-start(f32[24,1024]{1,0:T(8,128)S(1)} %get-tuple-element.49.refs_0_), channel_id=1, source_target_pairs={{0,3},{1,2},{2,1},{3,0},{4,7},{5,6},{6,5},{7,4},{8,11},{9,10},{10,... | collective-permute-start | bytes 294920 | tf_op jit(solution)/shard_map/ppermute | solution.py:383
  83.1 1.0 %collective-permute-done.21.refs_1_ = f32[24,1024]{1,0:T(8,128)S(1)} collective-permute-done((f32[24,1024]{1,0:T(8,128)S(1)}, f32[24,1024]{1,0:T(8,128)S(1)}, u32[]{:S(2)}, u32[]{:S(2)}) %collective-permute-start.21) | collective-permute-done | bytes 98336 | tf_op jit(solution)/shard_map/ppermute | solution.py:383
  84.1 6.9 %collective-permute-done.22.refs_2_ = f32[24,1024]{1,0:T(8,128)S(1)} collective-permute-done((f32[24,1024]{1,0:T(8,128)S(1)}, f32[24,1024]{1,0:T(8,128)S(1)}, u32[]{:S(2)}, u32[]{:S(2)}) %collective-permute-start.22) | collective-permute-done | bytes 98336 | tf_op jit(solution)/shard_map/ppermute | solution.py:383
  91.0 0.9 shard_map.65
  (38 shorter events, 0.7 us)
Async XLA Ops:
  8.5 4.1 %collective-permute-start = (f32[328,128]{1,0:T(8,128)S(1)}, f32[328,128]{1,0:T(8,128)S(1)}, u32[]{:S(2)}, u32[]{:S(2)}) collective-permute-start(f32[328,128]{1,0:T(8,128)S(1)} %get-tuple-element.29.own_ref), channel_id=1, source_target_pairs={{0,4},{4,0},{8,12},{12,8},{16,20},{20,16},{24,28},{28,24},{1,5},{5... | collective-permute-start | bytes 503816 | tf_op jit(solution)/shard_map/ppermute | solution.py:453
  9.0 5.6 %collective-permute-start.3 = (f32[64,128]{1,0:T(8,128)S(1)}, f32[64,128]{1,0:T(8,128)S(1)}, u32[]{:S(2)}, u32[]{:S(2)}) collective-permute-start(f32[64,128]{1,0:T(8,128)S(1)} %slice.49), channel_id=1, source_target_pairs={{0,28},{4,8},{8,4},{12,16},{16,12},{20,24},{24,20},{28,0},{1,29},{... | collective-permute-start | bytes 98312 | tf_op jit(solution)/shard_map/ppermute | solution.py:454
  12.6 8.5 %collective-permute-start.2 = (f32[132,128]{1,0:T(8,128)S(1)}, f32[132,128]{1,0:T(8,128)S(1)}, u32[]{:S(2)}, u32[]{:S(2)}) collective-permute-start(f32[132,128]{1,0:T(8,128)S(1)} %get-tuple-element.53), channel_id=1, source_target_pairs={{0,24},{4,28},{8,16},{12,20},{16,8},{20,12},{24,0},{28,4},{1,25},{... | collective-permute-start | bytes 202760 | tf_op jit(solution)/shard_map/ppermute | solution.py:398
  14.0 7.2 %collective-permute-start.1 = (f32[264,128]{1,0:T(8,128)S(1)}, f32[264,128]{1,0:T(8,128)S(1)}, u32[]{:S(2)}, u32[]{:S(2)}) collective-permute-start(f32[264,128]{1,0:T(8,128)S(1)} %slice_add_fusion.2.refs_0_), channel_id=1, source_target_pairs={{0,8},{4,20},{8,0},{12,28},{16,24},{20,4},{24,16},{28,12},{1,9},{5... | collective-permute-start | bytes 405512 | tf_op jit(solution)/shard_map/ppermute | solution.py:396
  14.7 0.7 copy-start.1
  15.4 0.7 copy-start.2
  16.1 0.7 copy-start.3
  21.2 16.3 %copy-start = (f32[8,3,1024]{2,0,1:T(8,128)S(1)}, f32[8,3,1024]{2,0,1:T(8,128)}, u32[]{:S(2)}) copy-start(f32[8,3,1024]{2,0,1:T(8,128)} %param.5) | copy-start | bytes 294916
  21.2 1.8 %collective-permute-start.4 = (f32[264,128]{1,0:T(8,128)S(1)}, f32[264,128]{1,0:T(8,128)S(1)}, u32[]{:S(2)}, u32[]{:S(2)}) collective-permute-start(f32[264,128]{1,0:T(8,128)S(1)} %maximum_add_fusion.refs_1_), channel_id=1, source_target_pairs={{0,4},{4,0},{8,12},{12,8},{16,20},{20,16},{24,28},{28,24},{1,5},{5... | collective-permute-start | bytes 405512 | tf_op jit(solution)/shard_map/ppermute | solution.py:402
  25.1 5.2 %collective-permute-start.5 = (f32[24,1024]{1,0:T(8,128)S(1)}, f32[24,1024]{1,0:T(8,128)S(1)}, u32[]{:S(2)}, u32[]{:S(2)}) collective-permute-start(f32[24,1024]{1,0:T(8,128)S(1)} %get-tuple-element.39.refs_0_), channel_id=1, source_target_pairs={{0,1},{1,0},{2,3},{3,2},{4,5},{5,4},{6,7},{7,6},{8,9},{9,8},{10,11... | collective-permute-start | bytes 294920 | tf_op jit(solution)/shard_map/ppermute | solution.py:383
  26.9 10.5 %collective-permute-start.6 = (f32[24,1024]{1,0:T(8,128)S(1)}, f32[24,1024]{1,0:T(8,128)S(1)}, u32[]{:S(2)}, u32[]{:S(2)}) collective-permute-start(f32[24,1024]{1,0:T(8,128)S(1)} %get-tuple-element.39.refs_0_), channel_id=1, source_target_pairs={{0,2},{1,3},{2,0},{3,1},{4,6},{5,7},{6,4},{7,5},{8,10},{9,11},{10,... | collective-permute-start | bytes 294920 | tf_op jit(solution)/shard_map/ppermute | solution.py:383
  28.2 9.2 %collective-permute-start.7 = (f32[24,1024]{1,0:T(8,128)S(1)}, f32[24,1024]{1,0:T(8,128)S(1)}, u32[]{:S(2)}, u32[]{:S(2)}) collective-permute-start(f32[24,1024]{1,0:T(8,128)S(1)} %get-tuple-element.39.refs_0_), channel_id=1, source_target_pairs={{0,3},{1,2},{2,1},{3,0},{4,7},{5,6},{6,5},{7,4},{8,11},{9,10},{10,... | collective-permute-start | bytes 294920 | tf_op jit(solution)/shard_map/ppermute | solution.py:383
  39.1 1.5 %collective-permute-start.8 = (f32[312,128]{1,0:T(8,128)S(1)}, f32[312,128]{1,0:T(8,128)S(1)}, u32[]{:S(2)}, u32[]{:S(2)}) collective-permute-start(f32[312,128]{1,0:T(8,128)S(1)} %get-tuple-element.41.own_ref), channel_id=1, source_target_pairs={{0,4},{4,0},{8,12},{12,8},{16,20},{20,16},{24,28},{28,24},{1,5},{5... | collective-permute-start | bytes 479240 | tf_op jit(solution)/shard_map/ppermute | solution.py:453
  40.6 6.4 %collective-permute-start.10 = (f32[132,128]{1,0:T(8,128)S(1)}, f32[132,128]{1,0:T(8,128)S(1)}, u32[]{:S(2)}, u32[]{:S(2)}) collective-permute-start(f32[132,128]{1,0:T(8,128)S(1)} %slice_select_fusion.1), channel_id=1, source_target_pairs={{0,24},{4,28},{8,16},{12,20},{16,8},{20,12},{24,0},{28,4},{1,25},{... | collective-permute-start | bytes 202760 | tf_op jit(solution)/shard_map/ppermute | solution.py:398
  42.7 4.3 %collective-permute-start.11 = (f32[48,128]{1,0:T(8,128)S(1)}, f32[48,128]{1,0:T(8,128)S(1)}, u32[]{:S(2)}, u32[]{:S(2)}) collective-permute-start(f32[48,128]{1,0:T(8,128)S(1)} %slice.54), channel_id=1, source_target_pairs={{0,28},{4,8},{8,4},{12,16},{16,12},{20,24},{24,20},{28,0},{1,29},{... | collective-permute-start | bytes 73736 | tf_op jit(solution)/shard_map/ppermute | solution.py:454
  43.0 5.1 %collective-permute-start.9 = (f32[264,128]{1,0:T(8,128)S(1)}, f32[264,128]{1,0:T(8,128)S(1)}, u32[]{:S(2)}, u32[]{:S(2)}) collective-permute-start(f32[264,128]{1,0:T(8,128)S(1)} %slice_add_fusion.1.refs_0_), channel_id=1, source_target_pairs={{0,8},{4,20},{8,0},{12,28},{16,24},{20,4},{24,16},{28,12},{1,9},{5... | collective-permute-start | bytes 405512 | tf_op jit(solution)/shard_map/ppermute | solution.py:396
  48.2 2.1 %collective-permute-start.12 = (f32[264,128]{1,0:T(8,128)S(1)}, f32[264,128]{1,0:T(8,128)S(1)}, u32[]{:S(2)}, u32[]{:S(2)}) collective-permute-start(f32[264,128]{1,0:T(8,128)S(1)} %maximum_add_fusion.1.refs_1_), channel_id=1, source_target_pairs={{0,4},{4,0},{8,12},{12,8},{16,20},{20,16},{24,28},{28,24},{1,5},{5... | collective-permute-start | bytes 405512 | tf_op jit(solution)/shard_map/ppermute | solution.py:402
  51.9 5.4 %collective-permute-start.13 = (f32[24,1024]{1,0:T(8,128)S(1)}, f32[24,1024]{1,0:T(8,128)S(1)}, u32[]{:S(2)}, u32[]{:S(2)}) collective-permute-start(f32[24,1024]{1,0:T(8,128)S(1)} %get-tuple-element.44.refs_0_), channel_id=1, source_target_pairs={{0,1},{1,0},{2,3},{3,2},{4,5},{5,4},{6,7},{7,6},{8,9},{9,8},{10,11... | collective-permute-start | bytes 294920 | tf_op jit(solution)/shard_map/ppermute | solution.py:383
  53.9 10.6 %collective-permute-start.14 = (f32[24,1024]{1,0:T(8,128)S(1)}, f32[24,1024]{1,0:T(8,128)S(1)}, u32[]{:S(2)}, u32[]{:S(2)}) collective-permute-start(f32[24,1024]{1,0:T(8,128)S(1)} %get-tuple-element.44.refs_0_), channel_id=1, source_target_pairs={{0,2},{1,3},{2,0},{3,1},{4,6},{5,7},{6,4},{7,5},{8,10},{9,11},{10,... | collective-permute-start | bytes 294920 | tf_op jit(solution)/shard_map/ppermute | solution.py:383
  53.9 10.5 %collective-permute-start.15 = (f32[24,1024]{1,0:T(8,128)S(1)}, f32[24,1024]{1,0:T(8,128)S(1)}, u32[]{:S(2)}, u32[]{:S(2)}) collective-permute-start(f32[24,1024]{1,0:T(8,128)S(1)} %get-tuple-element.44.refs_0_), channel_id=1, source_target_pairs={{0,3},{1,2},{2,1},{3,0},{4,7},{5,6},{6,5},{7,4},{8,11},{9,10},{10,... | collective-permute-start | bytes 294920 | tf_op jit(solution)/shard_map/ppermute | solution.py:383
  66.0 1.5 %collective-permute-start.16 = (f32[312,128]{1,0:T(8,128)S(1)}, f32[312,128]{1,0:T(8,128)S(1)}, u32[]{:S(2)}, u32[]{:S(2)}) collective-permute-start(f32[312,128]{1,0:T(8,128)S(1)} %get-tuple-element.46.own_ref), channel_id=1, source_target_pairs={{0,4},{4,0},{8,12},{12,8},{16,20},{20,16},{24,28},{28,24},{1,5},{5... | collective-permute-start | bytes 479240 | tf_op jit(solution)/shard_map/ppermute | solution.py:453
  67.5 5.5 %collective-permute-start.18 = (f32[132,128]{1,0:T(8,128)S(1)}, f32[132,128]{1,0:T(8,128)S(1)}, u32[]{:S(2)}, u32[]{:S(2)}) collective-permute-start(f32[132,128]{1,0:T(8,128)S(1)} %slice_select_fusion), channel_id=1, source_target_pairs={{0,24},{4,28},{8,16},{12,20},{16,8},{20,12},{24,0},{28,4},{1,25},{... | collective-permute-start | bytes 202760 | tf_op jit(solution)/shard_map/ppermute | solution.py:398
  68.2 4.4 %collective-permute-start.19 = (f32[48,128]{1,0:T(8,128)S(1)}, f32[48,128]{1,0:T(8,128)S(1)}, u32[]{:S(2)}, u32[]{:S(2)}) collective-permute-start(f32[48,128]{1,0:T(8,128)S(1)} %slice.59), channel_id=1, source_target_pairs={{0,28},{4,8},{8,4},{12,16},{16,12},{20,24},{24,20},{28,0},{1,29},{... | collective-permute-start | bytes 73736 | tf_op jit(solution)/shard_map/ppermute | solution.py:454
  70.0 5.0 %collective-permute-start.17 = (f32[264,128]{1,0:T(8,128)S(1)}, f32[264,128]{1,0:T(8,128)S(1)}, u32[]{:S(2)}, u32[]{:S(2)}) collective-permute-start(f32[264,128]{1,0:T(8,128)S(1)} %slice_add_fusion.refs_0_), channel_id=1, source_target_pairs={{0,8},{4,20},{8,0},{12,28},{16,24},{20,4},{24,16},{28,12},{1,9},{5... | collective-permute-start | bytes 405512 | tf_op jit(solution)/shard_map/ppermute | solution.py:396
  75.0 1.9 %collective-permute-start.20 = (f32[264,128]{1,0:T(8,128)S(1)}, f32[264,128]{1,0:T(8,128)S(1)}, u32[]{:S(2)}, u32[]{:S(2)}) collective-permute-start(f32[264,128]{1,0:T(8,128)S(1)} %maximum_add_fusion.2.refs_1_), channel_id=1, source_target_pairs={{0,4},{4,0},{8,12},{12,8},{16,20},{20,16},{24,28},{28,24},{1,5},{5... | collective-permute-start | bytes 405512 | tf_op jit(solution)/shard_map/ppermute | solution.py:402
  78.5 5.6 %collective-permute-start.21 = (f32[24,1024]{1,0:T(8,128)S(1)}, f32[24,1024]{1,0:T(8,128)S(1)}, u32[]{:S(2)}, u32[]{:S(2)}) collective-permute-start(f32[24,1024]{1,0:T(8,128)S(1)} %get-tuple-element.49.refs_0_), channel_id=1, source_target_pairs={{0,1},{1,0},{2,3},{3,2},{4,5},{5,4},{6,7},{7,6},{8,9},{9,8},{10,11... | collective-permute-start | bytes 294920 | tf_op jit(solution)/shard_map/ppermute | solution.py:383
  80.6 10.4 %collective-permute-start.22 = (f32[24,1024]{1,0:T(8,128)S(1)}, f32[24,1024]{1,0:T(8,128)S(1)}, u32[]{:S(2)}, u32[]{:S(2)}) collective-permute-start(f32[24,1024]{1,0:T(8,128)S(1)} %get-tuple-element.49.refs_0_), channel_id=1, source_target_pairs={{0,2},{1,3},{2,0},{3,1},{4,6},{5,7},{6,4},{7,5},{8,10},{9,11},{10,... | collective-permute-start | bytes 294920 | tf_op jit(solution)/shard_map/ppermute | solution.py:383
  80.6 10.4 %collective-permute-start.23 = (f32[24,1024]{1,0:T(8,128)S(1)}, f32[24,1024]{1,0:T(8,128)S(1)}, u32[]{:S(2)}, u32[]{:S(2)}) collective-permute-start(f32[24,1024]{1,0:T(8,128)S(1)} %get-tuple-element.49.refs_0_), channel_id=1, source_target_pairs={{0,3},{1,2},{2,1},{3,0},{4,7},{5,6},{6,5},{7,4},{8,11},{9,10},{10,... | collective-permute-start | bytes 294920 | tf_op jit(solution)/shard_map/ppermute | solution.py:383

commit v3 on v2

--- a/solution.py
+++ b/solution.py
@@ -14,6 +14,7 @@
 DEGREE = 3
 PAIR_MOST = 32
 GROUP = 4
+SLOTS = PAIR_MOST + 2 * GROUP
 
 SIDE_CROSS = 8.0
 NEAR_SQUARE = 0.36
@@ -88,14 +89,16 @@
 
 
 def start_kernel(
-    length_x, share, stack_ref, table_ref, flip_ref, terms_ref, msg_ref, mask_ref, turn_ref, left_ref, sum_ref
+    length_x, share, index_ref, place_ref, stack_ref, table_ref, flip_ref, terms_ref, msg_ref, mask_ref, turn_ref, left_ref, sum_ref
 ):
     particles = table_ref.shape[1]
     waves = table_ref.shape[2]
     tiles = particles // TILE
     ranks = tiles // share
     sides = (length_x, SIDE_CROSS, SIDE_CROSS)
-    counts = [stack_ref[27 + a : 28 + a, :waves] for a in range(3)]
+    counts = [index_ref[a : a + 1, :].astype(F32) for a in range(3)]
+    core = place_ref[0:1]
+    rank = place_ref[1:2]
     k1, k2, k3 = [2.0 * math.pi * counts[a] / sides[a] for a in range(3)]
     square = k1 * k1 + k2 * k2 + k3 * k3
     scaled = square / SPLIT_SQUARE
@@ -111,15 +114,14 @@
             -k1 * k3 * both,
             -k2 * k3 * both,
             flat_square * both,
-            stack_ref[30:32, :waves],
+            jnp.concatenate([place_ref[...]] * (waves // TILE), axis=1),
         ],
         axis=0,
     )
-    mask_ref[...] = jnp.broadcast_to(stack_ref[30:31, :TILE], mask_ref.shape)
+    mask_ref[...] = jnp.broadcast_to(core, mask_ref.shape)
     noise = stack_ref[0:24, :particles]
     places = jnp.concatenate([stack_ref[24:27, :particles], jnp.zeros((5, particles), F32)], axis=0)
     base = waves // TILE * 32
-    rank = stack_ref[31:32, :TILE]
     row = base + 8 + 24 * share
     msg_ref[base : base + 8, :] = jnp.zeros((8, TILE), F32)
     msg_ref[base + 8 : row, :] = own_tiles(noise, share, rank, ranks)
@@ -132,7 +134,6 @@
         rest = rest - parts[-1]
     turn_ref[...] = jnp.concatenate(parts + [jnp.zeros((7, particles), F32)], axis=0).T.astype(BF16)
     numbers = jnp.concatenate(counts * 3 + [jnp.zeros((7, waves), F32)], axis=0).astype(BF16)
-    block = min(512, particles)
     wide = 256
 
     def make(rows):
@@ -157,7 +158,8 @@
         for kind in range(4):
             flip_ref[kind, :, rows] = table_ref[kind, rows, :].T
 
-    blocks = [slice(at, at + block) for at in range(0, particles, block)]
+    ends = [0] + [particles * k // 8 for k in (4, 6, 8)]
+    blocks = [slice(low, high) for low, high in zip(ends, ends[1:])]
     make(blocks[0])
     for k in range(1, len(blocks)):
         use(blocks[k - 1], k == 1)
@@ -166,32 +168,37 @@
     emit([sum_ref[0], sum_ref[1]], terms_ref[...], 0, msg_ref)
 
 
-def pair_kernel(length_x, base, share, meta_ref, lists_ref, counts_ref, pos_ref, own_ref, near_ref, away_ref, out_ref, plan_ref, place_ref, column_ref):
-    tiles = lists_ref.shape[0]
+def pair_kernel(length_x, base, share, core_ref, live_ref, pos_ref, own_ref, near_ref, away_ref, out_ref, plan_ref, place_ref, column_ref):
+    tiles = pos_ref.shape[1] // TILE
     ranks = tiles // share
-    odd = meta_ref[0] == 1
-    rank = meta_ref[1]
-    seen = jnp.int32(0)
+    odd = core_ref[0] == 1
+    rank = core_ref[1]
+    inner = outer = jnp.int32(0)
     for target in range(tiles):
         for k in range(NB_MOST):
-            window = lists_ref[target, k]
+            window = live_ref[target, k]
             side, tile = lax.div(window, tiles), lax.rem(window, tiles)
             which = jnp.where(side == 1, 0, jnp.where((side == 0) == odd, 1, 2))
-            mine = (k < counts_ref[target]) & (lax.rem(tile, ranks) == rank)
-            plan_ref[0, seen] = target
-            plan_ref[1, seen] = which * share + lax.div(tile, ranks)
-            plan_ref[2, seen] = jnp.where(window == tiles + target, 1, 0)
-            seen = jnp.minimum(seen + jnp.where(mine, 1, 0), PAIR_MOST)
-    plan_ref[3, 0] = seen
+            mine = jnp.where((window >= 0) & (lax.rem(tile, ranks) == rank), 1, 0)
+            third = jnp.where(which == 2, 1, 0)
+            at = jnp.where(which == 2, SLOTS - 1 - outer, inner)
+            plan_ref[0, at] = target
+            plan_ref[1, at] = which * share + lax.div(tile, ranks)
+            plan_ref[2, at] = jnp.where(window == tiles + target, 1, 0)
+            inner = jnp.minimum(inner + mine * (1 - third), PAIR_MOST)
+            outer = jnp.minimum(outer + mine * third, PAIR_MOST)
+    plan_ref[3, 0] = inner
+    plan_ref[3, 1] = outer
     for k in range(GROUP):
-        plan_ref[0, seen + k] = tiles
-        plan_ref[1, seen + k] = 0
+        for at in (inner + k, SLOTS - 1 - outer - k):
+            plan_ref[0, at] = tiles
+            plan_ref[1, at] = 0
     sides = (length_x, SIDE_CROSS, SIDE_CROSS)
     reach = math.sqrt(NEAR_SQUARE)
     filler = jnp.zeros((5, TILE), F32)
     for i in range(tiles):
         lanes = slice(i * TILE, (i + 1) * TILE)
-        place_ref[i] = jnp.concatenate([pos_ref[a : a + 1, lanes] / sides[a] for a in range(3)] + [filler], axis=0)
+        place_ref[i] = jnp.concatenate([pos_ref[24 + a : 25 + a, lanes] / sides[a] for a in range(3)] + [filler], axis=0)
     for slab, ref in enumerate((own_ref, near_ref, away_ref)):
         for i in range(share):
             row = (base if slab < 2 else 24 * share) + 8 * i
@@ -200,13 +207,14 @@
             column_ref[slab * share + i] = place.T
     count = 32
 
-    def pair(p, carry):
+    def pair(at, carry):
+        p = jnp.where(at < inner, at, SLOTS - 1 + inner - at)
         target = place_ref[plan_ref[0, p]]
         source = column_ref[plan_ref[1, p]]
         own = plan_ref[2, p].astype(F32)
         lines = [target[a : a + 1] for a in range(3)]
-        for at in range(0, TILE, count):
-            rows = slice(at, at + count)
+        for low in range(0, TILE, count):
+            rows = slice(low, low + count)
             q = []
             for a in range(3):
                 offset = lines[a] - jnp.broadcast_to(source[rows, a : a + 1], (count, TILE))
@@ -214,7 +222,7 @@
                 q.append(offset * (sides[a] / reach))
             square = q[0] * q[0] + q[1] * q[1] + q[2] * q[2]
             same = (
-                lax.broadcasted_iota(jnp.int32, (count, TILE), 0) + at
+                lax.broadcasted_iota(jnp.int32, (count, TILE), 0) + low
                 == lax.broadcasted_iota(jnp.int32, (count, TILE), 1)
             )
             envelope = jnp.exp(-square) * jnp.where(same, NEAR_AMP * (1.0 - own), NEAR_AMP)
@@ -226,65 +234,79 @@
                     if a == b:
                         value = value + envelope
                     cols = slice(slot * TILE, (slot + 1) * TILE)
-                    out_ref[p, rows, cols], out_ref[p, TILE + at : TILE + at + count, cols] = split(value)
+                    out_ref[p, rows, cols], out_ref[p, TILE + low : TILE + low + count, cols] = split(value)
                     slot += 1
         return carry
 
-    lax.fori_loop(0, seen, pair, 0)
-
-
-def near_kernel(base, share, plan_ref, own_ref, near_ref, away_ref, matrix_ref, out_ref, window_ref, sum_ref):
+    lax.fori_loop(0, inner + outer, pair, 0)
+
+
+def near_kernel(base, share, within, beyond, plan_ref, *refs):
+    matrix_ref, out_ref, window_ref, sum_ref = refs[-4:]
+    sources = list(refs[:-4])
+    before_ref = None if within else sources.pop()
+    slabs = [(0, base), (1, base)] * within + [(2, 0)] * beyond
+    slabs = [(slab, ref, start) for (slab, start), ref in zip(slabs, sources)]
     tiles = sum_ref.shape[0] - 1
-    for slab, ref in enumerate((own_ref, near_ref, away_ref)):
+    for slab, ref, start in slabs:
         for i in range(share):
-            row = (base if slab < 2 else 0) + 24 * i
+            row = start + 24 * i
             window_ref[slab * share + i] = ref[row : row + 24, :]
-    sum_ref[...] = jnp.zeros_like(sum_ref)
+    if before_ref is None:
+        sum_ref[...] = jnp.zeros_like(sum_ref)
+    else:
+        for i in range(tiles):
+            sum_ref[i] = before_ref[:, i * TILE : (i + 1) * TILE]
+        sum_ref[tiles] = jnp.zeros_like(sum_ref[tiles])
 
     def part(rows, at):
         return rows[:, at * TILE : (at + 1) * TILE]
 
-    def several(at, carry):
-        for k in range(GROUP):
-            p = at * GROUP + k
-            high, low = split(window_ref[plan_ref[1, p]])
-            left = jnp.concatenate(
-                [
-                    jnp.concatenate([high, high], axis=1),
-                    jnp.concatenate([low, jnp.zeros_like(low)], axis=1),
-                ],
-                axis=0,
-            )
-            both = jnp.dot(left, matrix_ref[p], preferred_element_type=F32)
-            full = both[:24] + both[24:]
-            x, y, z = full[0:8], full[8:16], full[16:24]
-            sum_ref[plan_ref[0, p]] += jnp.concatenate(
-                [
-                    part(x, 0) + part(y, 1) + part(z, 2),
-                    part(x, 1) + part(y, 3) + part(z, 4),
-                    part(x, 2) + part(y, 4) + part(z, 5),
-                ],
-                axis=0,
-            )
-        return carry
-
-    lax.fori_loop(0, lax.div(plan_ref[3, 0] + (GROUP - 1), GROUP), several, 0)
+    def add(p):
+        high, low = split(window_ref[plan_ref[1, p]])
+        left = jnp.concatenate(
+            [
+                jnp.concatenate([high, high], axis=1),
+                jnp.concatenate([low, jnp.zeros_like(low)], axis=1),
+            ],
+            axis=0,
+        )
+        both = jnp.dot(left, matrix_ref[p], preferred_element_type=F32)
+        full = both[:24] + both[24:]
+        x, y, z = full[0:8], full[8:16], full[16:24]
+        sum_ref[plan_ref[0, p]] += jnp.concatenate(
+            [
+                part(x, 0) + part(y, 1) + part(z, 2),
+                part(x, 1) + part(y, 3) + part(z, 4),
+                part(x, 2) + part(y, 4) + part(z, 5),
+            ],
+            axis=0,
+        )
+
+    for wanted, row, start, step in ((within, 0, 0, 1), (beyond, 1, SLOTS - 1, -1)):
+        if wanted:
+
+            def several(at, carry):
+                for k in range(GROUP):
+                    add(start + step * (at * GROUP + k))
+                return carry
+
+            lax.fori_loop(0, lax.div(plan_ref[3, row] + (GROUP - 1), GROUP), several, 0)
     for i in range(tiles):
         out_ref[:, i * TILE : (i + 1) * TILE] = sum_ref[i]
 
 
 def back_kernel(parts, *refs):
-    ins, (near_ref, terms_ref, flip_ref, out_ref, norm_ref, left_ref) = (
-        refs[:parts],
-        refs[parts:],
-    )
+    ins, (near_ref, terms_ref, flip_ref, out_ref) = refs[:parts], refs[parts : parts + 4]
+    norm_refs, left_ref = refs[parts + 4 : -1], refs[-1]
     waves = terms_ref.shape[1]
     particles = out_ref.shape[1]
     tiles = waves // TILE
-    norm = ins[0][32 * tiles : 32 * tiles + 8, :]
-    for ref in ins[1:]:
-        norm = norm + ref[32 * tiles : 32 * tiles + 8, :]
-    norm_ref[...] = norm
+    for norm_ref in norm_refs:
+        norm = ins[0][32 * tiles : 32 * tiles + 8, :]
+        for ref in ins[1:]:
+            norm = norm + ref[32 * tiles : 32 * tiles + 8, :]
+        norm_ref[...] = norm
     for i in range(tiles):
         block = ins[0][32 * i : 32 * i + 32, :]
         for ref in ins[1:]:
@@ -306,25 +328,28 @@
         out_ref[:, cols] = total
 
 
-def step_kernel(parts, share, *refs):
-    ins, (force_ref, terms_ref, table_ref, rows_ref, msg_ref) = refs[:parts], refs[parts:]
+def next_kernel(parts, share, *refs):
+    ins, (force_ref, terms_ref, rows_ref, tiles_ref, norm_ref) = refs[:parts], refs[parts:]
     particles = force_ref.shape[1]
-    waves = terms_ref.shape[1]
     total = ins[0][...]
     for ref in ins[1:]:
         total = total + ref[...]
     rows = force_ref[...] + total
     rows_ref[...] = rows
+    tiles_ref[...] = own_tiles(rows, share, terms_ref[7:8, :TILE], particles // TILE // share)
     squares = rows * rows
     squares = squares[0:8] + squares[8:16] + squares[16:24]
-    tiles = particles // TILE
     norm = squares[:, 0:TILE]
-    for i in range(1, tiles):
+    for i in range(1, particles // TILE):
         norm = norm + squares[:, i * TILE : (i + 1) * TILE]
-    base = waves // TILE * 32
-    msg_ref[base : base + 8, :] = norm
-    msg_ref[base + 8 : base + 8 + 24 * share, :] = own_tiles(rows, share, terms_ref[7:8, :TILE], tiles // share)
-    forward(rows, table_ref, terms_ref[...], msg_ref)
+    norm_ref[...] = norm
+
+
+def factor_kernel(rows_ref, tiles_ref, norm_ref, terms_ref, table_ref, msg_ref):
+    base = terms_ref.shape[1] // TILE * 32
+    msg_ref[base : base + 8, :] = norm_ref[...]
+    msg_ref[base + 8 :, :] = tiles_ref[...]
+    forward(rows_ref[...], table_ref, terms_ref[...], msg_ref)
 
 
 def final_kernel(parts, *refs):
@@ -380,23 +405,26 @@
             x = functools.reduce(jnp.add, parts)
         radix = min(4, size // bit)
         parts = [x] + [
-            lax.ppermute(x, axis, [(i, i ^ (d * bit)) for i in range(size)]) for d in range(1, radix)
+            lax.ppermute(x, axis, [(i, i ^ (d * bit)) for i in range(size)]) for d in ((2, 1, 3) if radix == 4 else range(1, radix))
         ]
         bit *= radix
     return parts
 
 
-def chip_sums(chip, mask, away, work):
+def chip_sums(chip, mask, send_away, work):
     size = lax.axis_size("space")
-    done = None if work is None else work(away)
     if size != 8:
-        return exchange(chip, "space", 2), away, done
+        away = send_away()
+        return exchange(chip, "space", 2), away, work(away)
     half = chip.shape[0] // 2
     low = mask < 0.5
+    mine = jnp.where(low, chip[:half], chip[half:])
+    away = send_away()
     one = lax.ppermute(chip, "space", [(i, i ^ (4 if i % 2 else 2)) for i in range(size)])
-    mine = jnp.where(low, chip[:half], chip[half:])
     across = lax.ppermute(mine, "space", [(i, i ^ 6) for i in range(size)])
-    across, away, done = lax.optimization_barrier((across, away, done))
+    done = work(away)
+    one, done = lax.optimization_barrier((one, done))
+    across, away = lax.optimization_barrier((across, away))
     both = jnp.concatenate([jnp.where(low, across, 0.0), jnp.where(low, 0.0, across)], axis=0)
     fetched = one + both
     return [chip, fetched, lax.ppermute(fetched, "space", [(i, i ^ 1) for i in range(size)])], away, done
@@ -412,6 +440,7 @@
     ranks = lax.axis_size("wave")
     share = tiles // ranks
     place = jnp.stack([lax.axis_index("space") & 1, lax.axis_index("wave")]).astype(jnp.int32)
+    live = jnp.where(jnp.arange(NB_MOST)[None] < tile_counts[:, None], tile_lists, -1)
     core = [(i, i ^ 1) for i in range(slabs)]
     third = [(i, (i + 1 if i % 2 else i - 1) % slabs) for i in range(slabs)]
     table = ((4, particles, waves), BF16)
@@ -420,14 +449,8 @@
     far_flops = 2 * 96 * particles * waves * 2
 
     rows = jnp.transpose(noise, (1, 0, 2)).reshape(3 * vectors, particles)
-    width = max(particles, waves)
-    stack = jnp.concatenate(
-        [
-            jnp.pad(x.astype(F32), ((0, 0), (0, width - x.shape[1])))
-            for x in (rows, positions, wave_index, jnp.broadcast_to(place[:, None], (2, width)))
-        ],
-        axis=0,
-    )
+    lines = jnp.broadcast_to(place.astype(F32)[:, None], (2, TILE))
+    stack = jnp.concatenate([rows, positions], axis=0)
     phases, flipped, terms, msg, mask = call(
         functools.partial(start_kernel, length_x, share),
         [
@@ -437,7 +460,7 @@
             ((base + 32 * share, TILE), F32),
             ((base // 2, TILE), F32),
         ],
-        (stack,),
+        (wave_index, lines, stack),
         [
             pltpu.VMEM((particles, 16), BF16),
             pltpu.VMEM((6 * vectors, particles), BF16),
@@ -451,54 +474,69 @@
     matrices = plan = None
     for step in range(DEGREE):
         other = lax.ppermute(msg, "space", core)
-        away = lax.ppermute(msg[base:], "space", third)
+        def send_away():
+            return lax.ppermute(msg[base:] if step == 0 else own, "space", third)
+
 
         def pair_work(away):
             return call(
                 functools.partial(pair_kernel, length_x, base + 24 * share, share),
-                [((PAIR_MOST + GROUP, 2 * TILE, 6 * TILE), BF16), ((4, PAIR_MOST + GROUP), jnp.int32)],
-                (place, tile_lists, tile_counts, positions, msg, other, away),
+                [((SLOTS, 2 * TILE, 6 * TILE), BF16), ((4, SLOTS), jnp.int32)],
+                (place, live, stack, msg, other, away),
                 [pltpu.VMEM((tiles, 8, TILE), F32), pltpu.VMEM((3 * share, TILE, 8), F32)],
-                smem_in=3,
+                smem_in=2,
                 smem_out=(1,),
                 flops=far_flops,
             )
 
-        def near_work():
+        def near_work(within, beyond, *sources):
             return call(
-                functools.partial(near_kernel, base, share),
+                functools.partial(near_kernel, base, share, within, beyond),
                 [rows_shape],
-                (plan, msg, other, away, matrices),
+                (plan, *sources, matrices),
                 [pltpu.VMEM((3 * share, 24, TILE), F32), pltpu.VMEM((tiles + 1, 24, TILE), F32)],
                 smem_in=1,
                 flops=far_flops // 2,
             )[0]
 
-        factors, away, made = chip_sums(msg[:base] + other[:base], mask, away, pair_work if step == 0 else None)
         if step == 0:
-            matrices, plan = made
-        near_part = near_work()
-        part, norm = call(
+            other, live = lax.optimization_barrier((other, live))
+        chip = msg[:base] + other[:base]
+        if step == 0:
+            factors, away, (matrices, plan) = chip_sums(chip, mask, send_away, pair_work)
+            near_part = near_work(True, True, msg, other, away)
+        else:
+            factors, away, near_part = chip_sums(
+                chip, mask, send_away, lambda away: near_work(True, False, msg, other)
+            )
+            near_part = near_work(False, True, away, near_part)
+        part, *norm = call(
             functools.partial(back_kernel, len(factors)),
-            [rows_shape, ((8, TILE), F32)],
+            [rows_shape] + [((8, TILE), F32)] * (step > 0),
             (*factors, near_part, terms, flipped),
             [pltpu.VMEM((2, 48, waves), BF16)],
             flops=far_flops,
         )
-        norms.append(norm)
+        norms += norm
         sums = exchange(part, "wave", 1)
         if step < DEGREE - 1:
-            rows, msg = call(
-                functools.partial(step_kernel, len(sums), share),
-                [rows_shape, ((base + 24 * share, TILE), F32)],
-                (*sums, rows, terms, phases),
+            rows, own, norm = call(
+                functools.partial(next_kernel, len(sums), share),
+                [rows_shape, ((24 * share, TILE), F32), ((8, TILE), F32)],
+                (*sums, rows, terms),
+                flops=1,
+            )
+            msg = call(
+                factor_kernel,
+                [((base + 24 * share, TILE), F32)],
+                (rows, own, norm, terms, phases),
                 flops=far_flops,
-            )
+            )[0]
             images.append(rows)
     out = call(
         functools.partial(final_kernel, len(sums)),
         [rows_shape],
-        (*sums, noise_rows, *images, norms[1], norms[2]),
+        (*sums, noise_rows, *images, *norms),
     )[0]
     return jnp.transpose(out.reshape(3, vectors, particles), (1, 0, 2))
 

time: 91.9 us -> 86.2 us (0.938)
  waiting for transfers between devices: 34.9 us -> 29.4 us
  local copies, waits for them, and re-layouts: 2.15 us -> 0.8 us
    ppermute x9, waiting for transfers between devices: 24 us -> 20.5 us  [exchange(): lax.ppermute(x, axis, [(i, i ^ d * bit) for i in range(size)])]
    ppermute x3, waiting for transfers between devices: 4.55 us -> 1.93 us  [send_away(): return lax.ppermute(msg[base:] if step == 0 else own, 'space', third)]
    unnamed x8 -> x4, local copies, waits for them, and re-layouts: 2.07 us -> 0.72 us
    pallas_call x11 -> x15, Pallas kernels: 25.7 us -> 26.4 us  [call(): pl.pallas_call(kernel, out_shape=[jax.ShapeDtypeStruct(*o) for o in outs]...]
  transfers between devices with their start and end apart: 24 -> 24, of which waited for: 13 -> 14; matrix products, arithmetic and copies ran while one was open for 0% -> 1% of each run, Pallas kernels for 11% -> 13%
where the time goes in v3:
time: 86.2 us; the launch traced here: 86.1 us
  waiting for transfers between devices  29.4 us (34%)
  starting transfers between devices  27.3 us (32%)
  Pallas kernels  26.4 us (31%)
  other arithmetic  1.96 us (2%)
    pallas_call x15, Pallas kernels, call(): pl.pallas_call(kernel, out_shape=[jax.ShapeDtypeStruct(*o) for o in outs]...  26.4 us
    ppermute x9, waiting for transfers between devices, exchange(): lax.ppermute(x, axis, [(i, i ^ d * bit) for i in range(size)])  20.5 us
    ppermute x9, starting transfers between devices, exchange(): lax.ppermute(x, axis, [(i, i ^ d * bit) for i in range(size)])  13.8 us
    ppermute x3, starting transfers between devices, send_away(): return lax.ppermute(msg[base:] if step == 0 else own, 'space', third)  4.89 us
    ppermute x3, starting transfers between devices, chip_sums(): across = lax.ppermute(mine, 'space', [(i, i ^ 6) for i in range(size)])  4.18 us
    ppermute x3, starting transfers between devices, chip_sums(): lax.ppermute(chip, 'space', [(i, i ^ (4 if i % 2 else 2)) for i in range(...  3.55 us
    ppermute x3, waiting for transfers between devices, chip_sums(): lax.ppermute(chip, 'space', [(i, i ^ (4 if i % 2 else 2)) for i in range(...  3.53 us
    ppermute x3, waiting for transfers between devices, body(): other = lax.ppermute(msg, 'space', core)  2.75 us
  transfers between devices with their start and end apart: 24, of which 14 were waited for; matrix products, arithmetic and copies ran while one was open for 1% of the time, Pallas kernels for 13%

profile of v3, /device:TPU:0, one launch (start us, length us, event | category | flops | bytes accessed | tf_op | source)
XLA Modules:
  0.0 86.1 jit_solution(1353857564183400212)
XLA Ops:
  0.0 0.9 %pad_maximum_fusion.stack_ref.pos_ref = f32[27,1024]{1,0:T(8,128)S(1)} fusion(f32[3,1024]{1,0:T(4,128)} %param.6, f32[24,1024]{1,0:T(8,128)} %bitcast.8), kind=kLoop, calls=%fused_computation.6 | loop fusion | flops 27648 | bytes 221184 | tf_op jit(solution)/shard_map/concatenate | solution.py:453
  1.1 0.7 copy-done.1
  1.8 6.6 %shard_map.55 = (bf16[4,1024,1024]{2,1,0:T(8,128)(2,1)S(1)}, bf16[4,1024,1024]{2,1,0:T(8,128)(2,1)S(1)}, f32[8,1024]{1,0:T(8,128)S(1)}, f32[328,128]{1,0:T(8,128)S(1)}, f32[132,128]{1,0:T(8,128)S(1)}) custom-call(s32[3,1024]{1,0:T(4,128)S(1)} %copy-done.1, f32[2,128]{1,0:T(2,128)S(1)} %broadcast_in_dim.22.place_ref, ...), custom_call_target="tpu_custom_call" | custom-call | flops 1610612736 | tf_op jit(solution)/shard_map/pallas_call | solution.py:388
  8.4 0.5 collective-permute-start
  8.9 3.6 %collective-permute-start.2 = (f32[64,128]{1,0:T(8,128)S(1)}, f32[64,128]{1,0:T(8,128)S(1)}, u32[]{:S(2)}, u32[]{:S(2)}) collective-permute-start(f32[64,128]{1,0:T(8,128)S(1)} %slice.41), channel_id=1, source_target_pairs={{0,28},{4,8},{8,4},{12,16},{16,12},{20,24},{24,20},{28,0},{1,29},{... | collective-permute-start | bytes 98312 | tf_op jit(solution)/shard_map/ppermute | solution.py:478
  12.5 0.8 fusion.live_ref
  13.3 0.6 collective-permute-start.3
  13.9 1.4 %collective-permute-start.1 = (f32[264,128]{1,0:T(8,128)S(1)}, f32[264,128]{1,0:T(8,128)S(1)}, u32[]{:S(2)}, u32[]{:S(2)}) collective-permute-start(f32[264,128]{1,0:T(8,128)S(1)} %slice_add_fusion.2.refs_0_), channel_id=1, source_target_pairs={{0,8},{4,20},{8,0},{12,28},{16,24},{20,4},{24,16},{28,12},{1,9},{5... | collective-permute-start | bytes 405512 | tf_op jit(solution)/shard_map/ppermute | solution.py:423
  15.3 4.4 %shard_map.56 = (bf16[40,256,768]{2,1,0:T(8,128)(2,1)S(1)}, s32[4,40]{1,0:T(4,128)S(1)}) custom-call(s32[2]{0:T(128)S(1)} %get-tuple-element.72.core_ref, s32[8,8]{1,0:T(8,128)S(1)} %fusion.live_ref, f32[27,1024]{1,0:T(8,128)S(1)} %pad_maximum_fusion.stack_ref.pos_ref, f32[328,128]{1,0:T(8,128)S(1)} %get-tuple-element.37.own_ref.refs_0_, ...), custom_call_target="tpu_custom_call" | custom-call | flops 402653184 | tf_op jit(solution)/shard_map/pallas_call | solution.py:388
  19.9 1.8 %shard_map.57.refs_3_ = f32[24,1024]{1,0:T(8,128)S(1)} custom-call(s32[4,40]{1,0:T(4,128)S(1)} %get-tuple-element.45.plan_ref, f32[328,128]{1,0:T(8,128)S(1)} %get-tuple-element.37.own_ref.refs_0_, f32[328,128]{1,0:T(8,128)S(1)} %collective-permute-done.near_ref.refs_1_, f32[64,128]{1,0:T(8,128)S(1)} %collective-permute-done.2.away_ref.refs_2_, ...), custom_call_target="tpu_custom_call" | custom-call | flops 201326592 | tf_op jit(solution)/shard_map/pallas_call | solution.py:388
  21.7 1.6 %shard_map.58.refs_0_ = f32[24,1024]{1,0:T(8,128)S(1)} custom-call(f32[264,128]{1,0:T(8,128)S(1)} %slice_add_fusion.2.refs_0_, f32[264,128]{1,0:T(8,128)S(1)} %maximum_add_fusion.refs_1_, f32[264,128]{1,0:T(8,128)S(1)} %collective-permute-done.4.refs_2_, f32[24,1024]{1,0:T(8,128)S(1)} %shard_map.57.refs_3_, ...), custom_call_target="tpu_custom_call" | custom-call | flops 402653184 | tf_op jit(solution)/shard_map/pallas_call | solution.py:388
  23.2 1.8 %collective-permute-start.5 = (f32[24,1024]{1,0:T(8,128)S(1)}, f32[24,1024]{1,0:T(8,128)S(1)}, u32[]{:S(2)}, u32[]{:S(2)}) collective-permute-start(f32[24,1024]{1,0:T(8,128)S(1)} %shard_map.58.refs_0_), channel_id=1, source_target_pairs={{0,2},{1,3},{2,0},{3,1},{4,6},{5,7},{6,4},{7,5},{8,10},{9,11},{10,... | collective-permute-start | bytes 294920 | tf_op jit(solution)/shard_map/ppermute | solution.py:408
  25.0 2.9 %collective-permute-start.6 = (f32[24,1024]{1,0:T(8,128)S(1)}, f32[24,1024]{1,0:T(8,128)S(1)}, u32[]{:S(2)}, u32[]{:S(2)}) collective-permute-start(f32[24,1024]{1,0:T(8,128)S(1)} %shard_map.58.refs_0_), channel_id=1, source_target_pairs={{0,1},{1,0},{2,3},{3,2},{4,5},{5,4},{6,7},{7,6},{8,9},{9,8},{10,11... | collective-permute-start | bytes 294920 | tf_op jit(solution)/shard_map/ppermute | solution.py:408
  27.9 3.3 %collective-permute-done.5.refs_1_ = f32[24,1024]{1,0:T(8,128)S(1)} collective-permute-done((f32[24,1024]{1,0:T(8,128)S(1)}, f32[24,1024]{1,0:T(8,128)S(1)}, u32[]{:S(2)}, u32[]{:S(2)}) %collective-permute-start.5) | collective-permute-done | bytes 98336 | tf_op jit(solution)/shard_map/ppermute | solution.py:408
  31.3 3.9 %collective-permute-done.7.refs_3_ = f32[24,1024]{1,0:T(8,128)S(1)} collective-permute-done((f32[24,1024]{1,0:T(8,128)S(1)}, f32[24,1024]{1,0:T(8,128)S(1)}, u32[]{:S(2)}, u32[]{:S(2)}) %collective-permute-start.7) | collective-permute-done | bytes 98336 | tf_op jit(solution)/shard_map/ppermute | solution.py:408
  35.2 1.6 %shard_map.60.refs_0_ = f32[312,128]{1,0:T(8,128)S(1)} custom-call(f32[24,1024]{1,0:T(8,128)S(1)} %get-tuple-element.50.rows_ref.refs_4_.refs_5_, f32[48,128]{1,0:T(8,128)S(1)} %get-tuple-element.51.tiles_ref, f32[8,128]{1,0:T(8,128)S(1)} %get-tuple-element.52.norm_ref, f32[8,1024]{1,0:T(8,128)S(1)} %get-tuple-element.48.refs_4_.refs_5_.terms_ref, ...), custom_call_target="tpu_custom_call" | custom-call | flops 402653184 | tf_op jit(solution)/shard_map/pallas_call | solution.py:388
  36.9 1.4 %collective-permute-done.8.refs_1_ = f32[312,128]{1,0:T(8,128)S(1)} collective-permute-done((f32[312,128]{1,0:T(8,128)S(1)}, f32[312,128]{1,0:T(8,128)S(1)}, u32[]{:S(2)}, u32[]{:S(2)}) %collective-permute-start.8) | collective-permute-done | bytes 159776 | tf_op jit(solution)/shard_map/ppermute | solution.py:476
  38.3 1.8 %collective-permute-start.10 = (f32[132,128]{1,0:T(8,128)S(1)}, f32[132,128]{1,0:T(8,128)S(1)}, u32[]{:S(2)}, u32[]{:S(2)}) collective-permute-start(f32[132,128]{1,0:T(8,128)S(1)} %slice_select_fusion.1), channel_id=1, source_target_pairs={{0,24},{4,28},{8,16},{12,20},{16,8},{20,12},{24,0},{28,4},{1,25},{... | collective-permute-start | bytes 202760 | tf_op jit(solution)/shard_map/ppermute | solution.py:424
  40.1 0.7 collective-permute-start.11
  40.8 1.3 %collective-permute-start.9 = (f32[264,128]{1,0:T(8,128)S(1)}, f32[264,128]{1,0:T(8,128)S(1)}, u32[]{:S(2)}, u32[]{:S(2)}) collective-permute-start(f32[264,128]{1,0:T(8,128)S(1)} %slice_add_fusion.1.refs_0_), channel_id=1, source_target_pairs={{0,8},{4,20},{8,0},{12,28},{16,24},{20,4},{24,16},{28,12},{1,9},{5... | collective-permute-start | bytes 405512 | tf_op jit(solution)/shard_map/ppermute | solution.py:423
  42.0 1.5 %shard_map.61.refs_1_ = f32[24,1024]{1,0:T(8,128)S(1)} custom-call(s32[4,40]{1,0:T(4,128)S(1)} %get-tuple-element.45.plan_ref, f32[312,128]{1,0:T(8,128)S(1)} %shard_map.60.refs_0_, f32[312,128]{1,0:T(8,128)S(1)} %collective-permute-done.8.refs_1_, bf16[40,256,768]{2,1,0:T(8,128)(2,1)S(1)} %get-tuple-element.47.refs_3_.refs_2_), custom_call_target="tpu_custom_call" | custom-call | flops 201326592 | tf_op jit(solution)/shard_map/pallas_call | solution.py:388
  43.6 0.7 collective-permute-done.11.refs_0_
  44.3 1.9 %collective-permute-done.9 = f32[264,128]{1,0:T(8,128)S(1)} collective-permute-done((f32[264,128]{1,0:T(8,128)S(1)}, f32[264,128]{1,0:T(8,128)S(1)}, u32[]{:S(2)}, u32[]{:S(2)}) %collective-permute-start.9) | collective-permute-done | bytes 135200 | tf_op jit(solution)/shard_map/ppermute | solution.py:423
  46.2 0.2 collective-permute-start.12
  46.4 1.0 %shard_map.62.refs_3_ = f32[24,1024]{1,0:T(8,128)S(1)} custom-call(s32[4,40]{1,0:T(4,128)S(1)} %get-tuple-element.45.plan_ref, f32[48,128]{1,0:T(8,128)S(1)} %collective-permute-done.11.refs_0_, f32[24,1024]{1,0:T(8,128)S(1)} %shard_map.61.refs_1_, bf16[40,256,768]{2,1,0:T(8,128)(2,1)S(1)} %get-tuple-element.47.refs_3_.refs_2_), custom_call_target="tpu_custom_call" | custom-call | flops 201326592 | tf_op jit(solution)/shard_map/pallas_call | solution.py:388
  47.3 0.3 collective-permute-done.12.refs_2_
  47.6 1.6 %shard_map.63 = (f32[24,1024]{1,0:T(8,128)S(1)}, f32[8,128]{1,0:T(8,128)S(1)}) custom-call(f32[264,128]{1,0:T(8,128)S(1)} %slice_add_fusion.1.refs_0_, f32[264,128]{1,0:T(8,128)S(1)} %maximum_add_fusion.1.refs_1_, f32[264,128]{1,0:T(8,128)S(1)} %collective-permute-done.12.refs_2_, f32[24,1024]{1,0:T(8,128)S(1)} %shard_map.62.refs_3_, ...), custom_call_target="tpu_custom_call" | custom-call | flops 402653184 | tf_op jit(solution)/shard_map/pallas_call | solution.py:388
  49.2 2.1 %collective-permute-start.13 = (f32[24,1024]{1,0:T(8,128)S(1)}, f32[24,1024]{1,0:T(8,128)S(1)}, u32[]{:S(2)}, u32[]{:S(2)}) collective-permute-start(f32[24,1024]{1,0:T(8,128)S(1)} %get-tuple-element.58.refs_0_), channel_id=1, source_target_pairs={{0,2},{1,3},{2,0},{3,1},{4,6},{5,7},{6,4},{7,5},{8,10},{9,11},{10,... | collective-permute-start | bytes 294920 | tf_op jit(solution)/shard_map/ppermute | solution.py:408
  51.3 0.8 collective-permute-start.14
  52.1 1.5 %collective-permute-start.15 = (f32[24,1024]{1,0:T(8,128)S(1)}, f32[24,1024]{1,0:T(8,128)S(1)}, u32[]{:S(2)}, u32[]{:S(2)}) collective-permute-start(f32[24,1024]{1,0:T(8,128)S(1)} %get-tuple-element.58.refs_0_), channel_id=1, source_target_pairs={{0,3},{1,2},{2,1},{3,0},{4,7},{5,6},{6,5},{7,4},{8,11},{9,10},{10,... | collective-permute-start | bytes 294920 | tf_op jit(solution)/shard_map/ppermute | solution.py:408
  53.6 4.7 %collective-permute-done.13.refs_1_ = f32[24,1024]{1,0:T(8,128)S(1)} collective-permute-done((f32[24,1024]{1,0:T(8,128)S(1)}, f32[24,1024]{1,0:T(8,128)S(1)}, u32[]{:S(2)}, u32[]{:S(2)}) %collective-permute-start.13) | collective-permute-done | bytes 98336 | tf_op jit(solution)/shard_map/ppermute | solution.py:408
  58.3 1.4 %collective-permute-done.15.refs_3_ = f32[24,1024]{1,0:T(8,128)S(1)} collective-permute-done((f32[24,1024]{1,0:T(8,128)S(1)}, f32[24,1024]{1,0:T(8,128)S(1)}, u32[]{:S(2)}, u32[]{:S(2)}) %collective-permute-start.15) | collective-permute-done | bytes 98336 | tf_op jit(solution)/shard_map/ppermute | solution.py:408
  59.7 1.6 %shard_map.65.refs_0_ = f32[312,128]{1,0:T(8,128)S(1)} custom-call(f32[24,1024]{1,0:T(8,128)S(1)} %get-tuple-element.59.rows_ref.refs_6_, f32[48,128]{1,0:T(8,128)S(1)} %get-tuple-element.60.tiles_ref, f32[8,128]{1,0:T(8,128)S(1)} %get-tuple-element.61.norm_ref, f32[8,1024]{1,0:T(8,128)S(1)} %get-tuple-element.48.refs_4_.refs_5_.terms_ref, ...), custom_call_target="tpu_custom_call" | custom-call | flops 402653184 | tf_op jit(solution)/shard_map/pallas_call | solution.py:388
  61.4 1.4 %collective-permute-done.16.refs_1_ = f32[312,128]{1,0:T(8,128)S(1)} collective-permute-done((f32[312,128]{1,0:T(8,128)S(1)}, f32[312,128]{1,0:T(8,128)S(1)}, u32[]{:S(2)}, u32[]{:S(2)}) %collective-permute-start.16) | collective-permute-done | bytes 159776 | tf_op jit(solution)/shard_map/ppermute | solution.py:476
  62.8 1.8 %collective-permute-start.18 = (f32[132,128]{1,0:T(8,128)S(1)}, f32[132,128]{1,0:T(8,128)S(1)}, u32[]{:S(2)}, u32[]{:S(2)}) collective-permute-start(f32[132,128]{1,0:T(8,128)S(1)} %slice_select_fusion), channel_id=1, source_target_pairs={{0,24},{4,28},{8,16},{12,20},{16,8},{20,12},{24,0},{28,4},{1,25},{... | collective-permute-start | bytes 202760 | tf_op jit(solution)/shard_map/ppermute | solution.py:424
  64.6 0.7 collective-permute-start.19
  65.3 0.8 collective-permute-start.17
  66.1 1.4 %shard_map.66.refs_1_ = f32[24,1024]{1,0:T(8,128)S(1)} custom-call(s32[4,40]{1,0:T(4,128)S(1)} %get-tuple-element.45.plan_ref, f32[312,128]{1,0:T(8,128)S(1)} %shard_map.65.refs_0_, f32[312,128]{1,0:T(8,128)S(1)} %collective-permute-done.16.refs_1_, bf16[40,256,768]{2,1,0:T(8,128)(2,1)S(1)} %get-tuple-element.47.refs_3_.refs_2_), custom_call_target="tpu_custom_call" | custom-call | flops 201326592 | tf_op jit(solution)/shard_map/pallas_call | solution.py:388
  67.5 1.3 %collective-permute-done.19.refs_0_ = f32[48,128]{1,0:T(8,128)S(1)} collective-permute-done((f32[48,128]{1,0:T(8,128)S(1)}, f32[48,128]{1,0:T(8,128)S(1)}, u32[]{:S(2)}, u32[]{:S(2)}) %collective-permute-start.19) | collective-permute-done | bytes 24608 | tf_op jit(solution)/shard_map/ppermute | solution.py:478
  68.8 1.6 %collective-permute-done.17 = f32[264,128]{1,0:T(8,128)S(1)} collective-permute-done((f32[264,128]{1,0:T(8,128)S(1)}, f32[264,128]{1,0:T(8,128)S(1)}, u32[]{:S(2)}, u32[]{:S(2)}) %collective-permute-start.17) | collective-permute-done | bytes 135200 | tf_op jit(solution)/shard_map/ppermute | solution.py:423
  70.5 1.0 %shard_map.67.refs_3_ = f32[24,1024]{1,0:T(8,128)S(1)} custom-call(s32[4,40]{1,0:T(4,128)S(1)} %get-tuple-element.45.plan_ref, f32[48,128]{1,0:T(8,128)S(1)} %collective-permute-done.19.refs_0_, f32[24,1024]{1,0:T(8,128)S(1)} %shard_map.66.refs_1_, bf16[40,256,768]{2,1,0:T(8,128)(2,1)S(1)} %get-tuple-element.47.refs_3_.refs_2_), custom_call_target="tpu_custom_call" | custom-call | flops 201326592 | tf_op jit(solution)/shard_map/pallas_call | solution.py:388
  71.5 0.4 collective-permute-done.20.refs_2_
  71.8 1.6 %shard_map.68 = (f32[24,1024]{1,0:T(8,128)S(1)}, f32[8,128]{1,0:T(8,128)S(1)}) custom-call(f32[264,128]{1,0:T(8,128)S(1)} %slice_add_fusion.refs_0_, f32[264,128]{1,0:T(8,128)S(1)} %maximum_add_fusion.2.refs_1_, f32[264,128]{1,0:T(8,128)S(1)} %collective-permute-done.20.refs_2_, f32[24,1024]{1,0:T(8,128)S(1)} %shard_map.67.refs_3_, ...), custom_call_target="tpu_custom_call" | custom-call | flops 402653184 | tf_op jit(solution)/shard_map/pallas_call | solution.py:388
  73.4 3.0 %collective-permute-start.21 = (f32[24,1024]{1,0:T(8,128)S(1)}, f32[24,1024]{1,0:T(8,128)S(1)}, u32[]{:S(2)}, u32[]{:S(2)}) collective-permute-start(f32[24,1024]{1,0:T(8,128)S(1)} %get-tuple-element.66.refs_0_), channel_id=1, source_target_pairs={{0,2},{1,3},{2,0},{3,1},{4,6},{5,7},{6,4},{7,5},{8,10},{9,11},{10,... | collective-permute-start | bytes 294920 | tf_op jit(solution)/shard_map/ppermute | solution.py:408
  76.5 1.5 %collective-permute-start.23 = (f32[24,1024]{1,0:T(8,128)S(1)}, f32[24,1024]{1,0:T(8,128)S(1)}, u32[]{:S(2)}, u32[]{:S(2)}) collective-permute-start(f32[24,1024]{1,0:T(8,128)S(1)} %get-tuple-element.66.refs_0_), channel_id=1, source_target_pairs={{0,3},{1,2},{2,1},{3,0},{4,7},{5,6},{6,5},{7,4},{8,11},{9,10},{10,... | collective-permute-start | bytes 294920 | tf_op jit(solution)/shard_map/ppermute | solution.py:408
  78.0 4.0 %collective-permute-done.21.refs_1_ = f32[24,1024]{1,0:T(8,128)S(1)} collective-permute-done((f32[24,1024]{1,0:T(8,128)S(1)}, f32[24,1024]{1,0:T(8,128)S(1)}, u32[]{:S(2)}, u32[]{:S(2)}) %collective-permute-start.21) | collective-permute-done | bytes 98336 | tf_op jit(solution)/shard_map/ppermute | solution.py:408
  82.1 3.1 %collective-permute-done.23.refs_3_ = f32[24,1024]{1,0:T(8,128)S(1)} collective-permute-done((f32[24,1024]{1,0:T(8,128)S(1)}, f32[24,1024]{1,0:T(8,128)S(1)}, u32[]{:S(2)}, u32[]{:S(2)}) %collective-permute-start.23) | collective-permute-done | bytes 98336 | tf_op jit(solution)/shard_map/ppermute | solution.py:408
  85.2 0.9 %shard_map.69 = f32[24,1024]{1,0:T(8,128)} custom-call(f32[24,1024]{1,0:T(8,128)S(1)} %get-tuple-element.66.refs_0_, f32[24,1024]{1,0:T(8,128)S(1)} %collective-permute-done.21.refs_1_, f32[24,1024]{1,0:T(8,128)S(1)} %collective-permute-done.22.refs_2_, f32[24,1024]{1,0:T(8,128)S(1)} %collective-permute-done.23.refs_3_, f32[24,1024]{1,0:T(8,128)S(1)} %bitcast.10, ...), custom_call_target="tpu_custom_call" | custom-call | tf_op jit(solution)/shard_map/pallas_call | solution.py:388
  (36 shorter events, 0.9 us)
Async XLA Ops:
  1.1 0.7 copy-start.1
  8.4 4.8 %collective-permute-start = (f32[328,128]{1,0:T(8,128)S(1)}, f32[328,128]{1,0:T(8,128)S(1)}, u32[]{:S(2)}, u32[]{:S(2)}) collective-permute-start(f32[328,128]{1,0:T(8,128)S(1)} %get-tuple-element.37.own_ref.refs_0_), channel_id=1, source_target_pairs={{0,4},{4,0},{8,12},{12,8},{16,20},{20,16},{24,28},{28,24},{1,5},{5... | collective-permute-start | bytes 503816 | tf_op jit(solution)/shard_map/ppermute | solution.py:476
  8.9 6.4 %collective-permute-start.2 = (f32[64,128]{1,0:T(8,128)S(1)}, f32[64,128]{1,0:T(8,128)S(1)}, u32[]{:S(2)}, u32[]{:S(2)}) collective-permute-start(f32[64,128]{1,0:T(8,128)S(1)} %slice.41), channel_id=1, source_target_pairs={{0,28},{4,8},{8,4},{12,16},{16,12},{20,24},{24,20},{28,0},{1,29},{... | collective-permute-start | bytes 98312 | tf_op jit(solution)/shard_map/ppermute | solution.py:478
  13.3 6.4 %collective-permute-start.3 = (f32[132,128]{1,0:T(8,128)S(1)}, f32[132,128]{1,0:T(8,128)S(1)}, u32[]{:S(2)}, u32[]{:S(2)}) collective-permute-start(f32[132,128]{1,0:T(8,128)S(1)} %get-tuple-element.69), channel_id=1, source_target_pairs={{0,24},{4,28},{8,16},{12,20},{16,8},{20,12},{24,0},{28,4},{1,25},{... | collective-permute-start | bytes 202760 | tf_op jit(solution)/shard_map/ppermute | solution.py:424
  13.9 5.9 %collective-permute-start.1 = (f32[264,128]{1,0:T(8,128)S(1)}, f32[264,128]{1,0:T(8,128)S(1)}, u32[]{:S(2)}, u32[]{:S(2)}) collective-permute-start(f32[264,128]{1,0:T(8,128)S(1)} %slice_add_fusion.2.refs_0_), channel_id=1, source_target_pairs={{0,8},{4,20},{8,0},{12,28},{16,24},{20,4},{24,16},{28,12},{1,9},{5... | collective-permute-start | bytes 405512 | tf_op jit(solution)/shard_map/ppermute | solution.py:423
  19.8 1.9 %collective-permute-start.4 = (f32[264,128]{1,0:T(8,128)S(1)}, f32[264,128]{1,0:T(8,128)S(1)}, u32[]{:S(2)}, u32[]{:S(2)}) collective-permute-start(f32[264,128]{1,0:T(8,128)S(1)} %maximum_add_fusion.refs_1_), channel_id=1, source_target_pairs={{0,4},{4,0},{8,12},{12,8},{16,20},{20,16},{24,28},{28,24},{1,5},{5... | collective-permute-start | bytes 405512 | tf_op jit(solution)/shard_map/ppermute | solution.py:430
  21.6 13.5 %copy-start = (f32[8,3,1024]{2,0,1:T(8,128)S(1)}, f32[8,3,1024]{2,0,1:T(8,128)}, u32[]{:S(2)}) copy-start(f32[8,3,1024]{2,0,1:T(8,128)} %param.5) | copy-start | bytes 294916
  23.2 8.0 %collective-permute-start.5 = (f32[24,1024]{1,0:T(8,128)S(1)}, f32[24,1024]{1,0:T(8,128)S(1)}, u32[]{:S(2)}, u32[]{:S(2)}) collective-permute-start(f32[24,1024]{1,0:T(8,128)S(1)} %shard_map.58.refs_0_), channel_id=1, source_target_pairs={{0,2},{1,3},{2,0},{3,1},{4,6},{5,7},{6,4},{7,5},{8,10},{9,11},{10,... | collective-permute-start | bytes 294920 | tf_op jit(solution)/shard_map/ppermute | solution.py:408
  25.0 6.2 %collective-permute-start.6 = (f32[24,1024]{1,0:T(8,128)S(1)}, f32[24,1024]{1,0:T(8,128)S(1)}, u32[]{:S(2)}, u32[]{:S(2)}) collective-permute-start(f32[24,1024]{1,0:T(8,128)S(1)} %shard_map.58.refs_0_), channel_id=1, source_target_pairs={{0,1},{1,0},{2,3},{3,2},{4,5},{5,4},{6,7},{7,6},{8,9},{9,8},{10,11... | collective-permute-start | bytes 294920 | tf_op jit(solution)/shard_map/ppermute | solution.py:408
  27.9 7.3 %collective-permute-start.7 = (f32[24,1024]{1,0:T(8,128)S(1)}, f32[24,1024]{1,0:T(8,128)S(1)}, u32[]{:S(2)}, u32[]{:S(2)}) collective-permute-start(f32[24,1024]{1,0:T(8,128)S(1)} %shard_map.58.refs_0_), channel_id=1, source_target_pairs={{0,3},{1,2},{2,1},{3,0},{4,7},{5,6},{6,5},{7,4},{8,11},{9,10},{10,... | collective-permute-start | bytes 294920 | tf_op jit(solution)/shard_map/ppermute | solution.py:408
  36.8 1.5 %collective-permute-start.8 = (f32[312,128]{1,0:T(8,128)S(1)}, f32[312,128]{1,0:T(8,128)S(1)}, u32[]{:S(2)}, u32[]{:S(2)}) collective-permute-start(f32[312,128]{1,0:T(8,128)S(1)} %shard_map.60.refs_0_), channel_id=1, source_target_pairs={{0,4},{4,0},{8,12},{12,8},{16,20},{20,16},{24,28},{28,24},{1,5},{5... | collective-permute-start | bytes 479240 | tf_op jit(solution)/shard_map/ppermute | solution.py:476
  38.3 5.9 %collective-permute-start.10 = (f32[132,128]{1,0:T(8,128)S(1)}, f32[132,128]{1,0:T(8,128)S(1)}, u32[]{:S(2)}, u32[]{:S(2)}) collective-permute-start(f32[132,128]{1,0:T(8,128)S(1)} %slice_select_fusion.1), channel_id=1, source_target_pairs={{0,24},{4,28},{8,16},{12,20},{16,8},{20,12},{24,0},{28,4},{1,25},{... | collective-permute-start | bytes 202760 | tf_op jit(solution)/shard_map/ppermute | solution.py:424
  40.1 4.2 %collective-permute-start.11 = (f32[48,128]{1,0:T(8,128)S(1)}, f32[48,128]{1,0:T(8,128)S(1)}, u32[]{:S(2)}, u32[]{:S(2)}) collective-permute-start(f32[48,128]{1,0:T(8,128)S(1)} %get-tuple-element.51.tiles_ref), channel_id=1, source_target_pairs={{0,28},{4,8},{8,4},{12,16},{16,12},{20,24},{24,20},{28,0},{1,29},{... | collective-permute-start | bytes 73736 | tf_op jit(solution)/shard_map/ppermute | solution.py:478
  40.8 5.4 %collective-permute-start.9 = (f32[264,128]{1,0:T(8,128)S(1)}, f32[264,128]{1,0:T(8,128)S(1)}, u32[]{:S(2)}, u32[]{:S(2)}) collective-permute-start(f32[264,128]{1,0:T(8,128)S(1)} %slice_add_fusion.1.refs_0_), channel_id=1, source_target_pairs={{0,8},{4,20},{8,0},{12,28},{16,24},{20,4},{24,16},{28,12},{1,9},{5... | collective-permute-start | bytes 405512 | tf_op jit(solution)/shard_map/ppermute | solution.py:423
  46.2 1.4 %collective-permute-start.12 = (f32[264,128]{1,0:T(8,128)S(1)}, f32[264,128]{1,0:T(8,128)S(1)}, u32[]{:S(2)}, u32[]{:S(2)}) collective-permute-start(f32[264,128]{1,0:T(8,128)S(1)} %maximum_add_fusion.1.refs_1_), channel_id=1, source_target_pairs={{0,4},{4,0},{8,12},{12,8},{16,20},{20,16},{24,28},{28,24},{1,5},{5... | collective-permute-start | bytes 405512 | tf_op jit(solution)/shard_map/ppermute | solution.py:430
  49.2 9.1 %collective-permute-start.13 = (f32[24,1024]{1,0:T(8,128)S(1)}, f32[24,1024]{1,0:T(8,128)S(1)}, u32[]{:S(2)}, u32[]{:S(2)}) collective-permute-start(f32[24,1024]{1,0:T(8,128)S(1)} %get-tuple-element.58.refs_0_), channel_id=1, source_target_pairs={{0,2},{1,3},{2,0},{3,1},{4,6},{5,7},{6,4},{7,5},{8,10},{9,11},{10,... | collective-permute-start | bytes 294920 | tf_op jit(solution)/shard_map/ppermute | solution.py:408
  51.3 7.0 %collective-permute-start.14 = (f32[24,1024]{1,0:T(8,128)S(1)}, f32[24,1024]{1,0:T(8,128)S(1)}, u32[]{:S(2)}, u32[]{:S(2)}) collective-permute-start(f32[24,1024]{1,0:T(8,128)S(1)} %get-tuple-element.58.refs_0_), channel_id=1, source_target_pairs={{0,1},{1,0},{2,3},{3,2},{4,5},{5,4},{6,7},{7,6},{8,9},{9,8},{10,11... | collective-permute-start | bytes 294920 | tf_op jit(solution)/shard_map/ppermute | solution.py:408
  52.1 7.6 %collective-permute-start.15 = (f32[24,1024]{1,0:T(8,128)S(1)}, f32[24,1024]{1,0:T(8,128)S(1)}, u32[]{:S(2)}, u32[]{:S(2)}) collective-permute-start(f32[24,1024]{1,0:T(8,128)S(1)} %get-tuple-element.58.refs_0_), channel_id=1, source_target_pairs={{0,3},{1,2},{2,1},{3,0},{4,7},{5,6},{6,5},{7,4},{8,11},{9,10},{10,... | collective-permute-start | bytes 294920 | tf_op jit(solution)/shard_map/ppermute | solution.py:408
  61.3 1.5 %collective-permute-start.16 = (f32[312,128]{1,0:T(8,128)S(1)}, f32[312,128]{1,0:T(8,128)S(1)}, u32[]{:S(2)}, u32[]{:S(2)}) collective-permute-start(f32[312,128]{1,0:T(8,128)S(1)} %shard_map.65.refs_0_), channel_id=1, source_target_pairs={{0,4},{4,0},{8,12},{12,8},{16,20},{20,16},{24,28},{28,24},{1,5},{5... | collective-permute-start | bytes 479240 | tf_op jit(solution)/shard_map/ppermute | solution.py:476
  62.8 5.9 %collective-permute-start.18 = (f32[132,128]{1,0:T(8,128)S(1)}, f32[132,128]{1,0:T(8,128)S(1)}, u32[]{:S(2)}, u32[]{:S(2)}) collective-permute-start(f32[132,128]{1,0:T(8,128)S(1)} %slice_select_fusion), channel_id=1, source_target_pairs={{0,24},{4,28},{8,16},{12,20},{16,8},{20,12},{24,0},{28,4},{1,25},{... | collective-permute-start | bytes 202760 | tf_op jit(solution)/shard_map/ppermute | solution.py:424
  64.6 4.2 %collective-permute-start.19 = (f32[48,128]{1,0:T(8,128)S(1)}, f32[48,128]{1,0:T(8,128)S(1)}, u32[]{:S(2)}, u32[]{:S(2)}) collective-permute-start(f32[48,128]{1,0:T(8,128)S(1)} %get-tuple-element.60.tiles_ref), channel_id=1, source_target_pairs={{0,28},{4,8},{8,4},{12,16},{16,12},{20,24},{24,20},{28,0},{1,29},{... | collective-permute-start | bytes 73736 | tf_op jit(solution)/shard_map/ppermute | solution.py:478
  65.3 5.1 %collective-permute-start.17 = (f32[264,128]{1,0:T(8,128)S(1)}, f32[264,128]{1,0:T(8,128)S(1)}, u32[]{:S(2)}, u32[]{:S(2)}) collective-permute-start(f32[264,128]{1,0:T(8,128)S(1)} %slice_add_fusion.refs_0_), channel_id=1, source_target_pairs={{0,8},{4,20},{8,0},{12,28},{16,24},{20,4},{24,16},{28,12},{1,9},{5... | collective-permute-start | bytes 405512 | tf_op jit(solution)/shard_map/ppermute | solution.py:423
  70.4 1.4 %collective-permute-start.20 = (f32[264,128]{1,0:T(8,128)S(1)}, f32[264,128]{1,0:T(8,128)S(1)}, u32[]{:S(2)}, u32[]{:S(2)}) collective-permute-start(f32[264,128]{1,0:T(8,128)S(1)} %maximum_add_fusion.2.refs_1_), channel_id=1, source_target_pairs={{0,4},{4,0},{8,12},{12,8},{16,20},{20,16},{24,28},{28,24},{1,5},{5... | collective-permute-start | bytes 405512 | tf_op jit(solution)/shard_map/ppermute | solution.py:430
  73.4 8.7 %collective-permute-start.21 = (f32[24,1024]{1,0:T(8,128)S(1)}, f32[24,1024]{1,0:T(8,128)S(1)}, u32[]{:S(2)}, u32[]{:S(2)}) collective-permute-start(f32[24,1024]{1,0:T(8,128)S(1)} %get-tuple-element.66.refs_0_), channel_id=1, source_target_pairs={{0,2},{1,3},{2,0},{3,1},{4,6},{5,7},{6,4},{7,5},{8,10},{9,11},{10,... | collective-permute-start | bytes 294920 | tf_op jit(solution)/shard_map/ppermute | solution.py:408
  76.4 5.7 %collective-permute-start.22 = (f32[24,1024]{1,0:T(8,128)S(1)}, f32[24,1024]{1,0:T(8,128)S(1)}, u32[]{:S(2)}, u32[]{:S(2)}) collective-permute-start(f32[24,1024]{1,0:T(8,128)S(1)} %get-tuple-element.66.refs_0_), channel_id=1, source_target_pairs={{0,1},{1,0},{2,3},{3,2},{4,5},{5,4},{6,7},{7,6},{8,9},{9,8},{10,11... | collective-permute-start | bytes 294920 | tf_op jit(solution)/shard_map/ppermute | solution.py:408
  76.5 8.7 %collective-permute-start.23 = (f32[24,1024]{1,0:T(8,128)S(1)}, f32[24,1024]{1,0:T(8,128)S(1)}, u32[]{:S(2)}, u32[]{:S(2)}) collective-permute-start(f32[24,1024]{1,0:T(8,128)S(1)} %get-tuple-element.66.refs_0_), channel_id=1, source_target_pairs={{0,3},{1,2},{2,1},{3,0},{4,7},{5,6},{6,5},{7,4},{8,11},{9,10},{10,... | collective-permute-start | bytes 294920 | tf_op jit(solution)/shard_map/ppermute | solution.py:408

commit v4 on v3

--- a/solution.py
+++ b/solution.py
@@ -47,7 +47,7 @@
     return acc
 
 
-def emit(kinds, terms, at, msg_ref):
+def emit(kinds, terms, at, mine_ref, rest_ref):
     width = kinds[0].shape[1]
     t = terms[:, at : at + width]
     pieces = []
@@ -56,9 +56,11 @@
         pieces.append(t[1:2] * fx + t[2:3] * fy)
         pieces.append(t[3:4] * fx + t[4:5] * fy + t[5:6] * fz)
     stacked = jnp.concatenate(pieces, axis=0)
+    half = mine_ref.shape[0]
     for k in range(width // TILE):
         row = (at // TILE + k) * 32
-        msg_ref[row : row + 32, :] = stacked[:, k * TILE : (k + 1) * TILE]
+        ref, row = (mine_ref, row) if row < half else (rest_ref, row - half)
+        ref[row : row + 32, :] = stacked[:, k * TILE : (k + 1) * TILE]
 
 
 def product(both, high_table, low_table):
@@ -67,14 +69,14 @@
     return first[:24] + (first[24:] + second)
 
 
-def forward(rows, table_ref, terms, msg_ref):
+def forward(rows, table_ref, terms, mine_ref, rest_ref):
     waves = table_ref.shape[2]
     both = jnp.concatenate(split(rows), axis=0)
     step = min(512, waves)
     for at in range(0, waves, step):
         cols = slice(at, at + step)
         kinds = [product(both, table_ref[k, :, cols], table_ref[2 + k, :, cols]) for k in range(2)]
-        emit(kinds, terms, at, msg_ref)
+        emit(kinds, terms, at, mine_ref, rest_ref)
 
 
 def own_tiles(rows, share, rank, ranks):
@@ -89,16 +91,21 @@
 
 
 def start_kernel(
-    length_x, share, index_ref, place_ref, stack_ref, table_ref, flip_ref, terms_ref, msg_ref, mask_ref, turn_ref, left_ref, sum_ref
+    length_x, share, index_ref, place_ref, stack_ref, table_ref, flip_ref, terms_ref, mine_ref, rest_ref,
+    turn_ref, left_ref, sum_ref
 ):
     particles = table_ref.shape[1]
     waves = table_ref.shape[2]
     tiles = particles // TILE
     ranks = tiles // share
     sides = (length_x, SIDE_CROSS, SIDE_CROSS)
-    counts = [index_ref[a : a + 1, :].astype(F32) for a in range(3)]
     core = place_ref[0:1]
     rank = place_ref[1:2]
+    whole = index_ref[...].astype(F32)
+    turned = jnp.concatenate([whole[:, waves // 2 :], whole[:, : waves // 2]], axis=1)
+    first = jnp.broadcast_to(jnp.concatenate([core] * (waves // TILE), axis=1), whole.shape) < 0.5
+    whole = jnp.where(first, whole, turned)
+    counts = [whole[a : a + 1] for a in range(3)]
     k1, k2, k3 = [2.0 * math.pi * counts[a] / sides[a] for a in range(3)]
     square = k1 * k1 + k2 * k2 + k3 * k3
     scaled = square / SPLIT_SQUARE
@@ -118,14 +125,13 @@
         ],
         axis=0,
     )
-    mask_ref[...] = jnp.broadcast_to(core, mask_ref.shape)
     noise = stack_ref[0:24, :particles]
     places = jnp.concatenate([stack_ref[24:27, :particles], jnp.zeros((5, particles), F32)], axis=0)
-    base = waves // TILE * 32
+    base = waves // TILE * 16
     row = base + 8 + 24 * share
-    msg_ref[base : base + 8, :] = jnp.zeros((8, TILE), F32)
-    msg_ref[base + 8 : row, :] = own_tiles(noise, share, rank, ranks)
-    msg_ref[row : row + 8 * share, :] = own_tiles(places, share, rank, ranks)
+    rest_ref[base : base + 8, :] = jnp.zeros((8, TILE), F32)
+    rest_ref[base + 8 : row, :] = own_tiles(noise, share, rank, ranks)
+    rest_ref[row : row + 8 * share, :] = own_tiles(places, share, rank, ranks)
     left_ref[...] = jnp.concatenate(split(noise), axis=0)
     parts = []
     rest = jnp.concatenate([places[a : a + 1] / sides[a] for a in range(3)], axis=0)
@@ -165,7 +171,7 @@
         use(blocks[k - 1], k == 1)
         make(blocks[k])
     use(blocks[-1], len(blocks) == 1)
-    emit([sum_ref[0], sum_ref[1]], terms_ref[...], 0, msg_ref)
+    emit([sum_ref[0], sum_ref[1]], terms_ref[...], 0, mine_ref, rest_ref)
 
 
 def pair_kernel(length_x, base, share, core_ref, live_ref, pos_ref, own_ref, near_ref, away_ref, out_ref, plan_ref, place_ref, column_ref):
@@ -296,22 +302,12 @@
         out_ref[:, i * TILE : (i + 1) * TILE] = sum_ref[i]
 
 
-def back_kernel(parts, *refs):
-    ins, (near_ref, terms_ref, flip_ref, out_ref) = refs[:parts], refs[parts : parts + 4]
-    norm_refs, left_ref = refs[parts + 4 : -1], refs[-1]
-    waves = terms_ref.shape[1]
+def back_kernel(begin, factor_ref, before_ref, terms_ref, flip_ref, out_ref, left_ref):
+    waves = left_ref.shape[2]
     particles = out_ref.shape[1]
-    tiles = waves // TILE
-    for norm_ref in norm_refs:
-        norm = ins[0][32 * tiles : 32 * tiles + 8, :]
-        for ref in ins[1:]:
-            norm = norm + ref[32 * tiles : 32 * tiles + 8, :]
-        norm_ref[...] = norm
-    for i in range(tiles):
-        block = ins[0][32 * i : 32 * i + 32, :]
-        for ref in ins[1:]:
-            block = block + ref[32 * i : 32 * i + 32, :]
-        t = terms_ref[:, i * TILE : (i + 1) * TILE]
+    for i in range(waves // TILE):
+        block = factor_ref[32 * i : 32 * i + 32, :]
+        t = terms_ref[:, begin + i * TILE : begin + (i + 1) * TILE]
         block = block * t[0:1]
         for kind in range(2):
             one, two = block[16 * kind : 16 * kind + 8], block[16 * kind + 8 : 16 * kind + 16]
@@ -320,11 +316,12 @@
             )
             left_ref[kind, :, i * TILE : (i + 1) * TILE] = jnp.concatenate(split(rows), axis=0)
     step = min(512, particles)
+    rows = slice(begin, begin + waves)
     for at in range(0, particles, step):
         cols = slice(at, at + step)
-        total = near_ref[:, cols]
+        total = before_ref[:, cols]
         for k in range(2):
-            total = total + product(left_ref[k], flip_ref[k, :, cols], flip_ref[2 + k, :, cols])
+            total = total + product(left_ref[k], flip_ref[k, rows, cols], flip_ref[2 + k, rows, cols])
         out_ref[:, cols] = total
 
 
@@ -345,11 +342,11 @@
     norm_ref[...] = norm
 
 
-def factor_kernel(rows_ref, tiles_ref, norm_ref, terms_ref, table_ref, msg_ref):
-    base = terms_ref.shape[1] // TILE * 32
-    msg_ref[base : base + 8, :] = norm_ref[...]
-    msg_ref[base + 8 :, :] = tiles_ref[...]
-    forward(rows_ref[...], table_ref, terms_ref[...], msg_ref)
+def factor_kernel(rows_ref, tiles_ref, norm_ref, terms_ref, table_ref, mine_ref, rest_ref):
+    base = mine_ref.shape[0]
+    rest_ref[base : base + 8, :] = norm_ref[...]
+    rest_ref[base + 8 :, :] = tiles_ref[...]
+    forward(rows_ref[...], table_ref, terms_ref[...], mine_ref, rest_ref)
 
 
 def final_kernel(parts, *refs):
@@ -359,8 +356,8 @@
         total = total + ref[...]
     u0, u1, u2 = noise_ref[...], one_ref[...], two_ref[...]
     u3 = u2 + total
-    first = jnp.sum(first_ref[...], axis=1, keepdims=True)
-    second = jnp.sum(second_ref[...], axis=1, keepdims=True)
+    first = jnp.sum(first_ref[-8:, :], axis=1, keepdims=True)
+    second = jnp.sum(second_ref[-8:, :], axis=1, keepdims=True)
     ratio = jnp.max(second / (first + EPSILON), axis=0, keepdims=True)
     high = SAFETY * jnp.sqrt(ratio)
     low = high / SPREAD
@@ -411,25 +408,6 @@
     return parts
 
 
-def chip_sums(chip, mask, send_away, work):
-    size = lax.axis_size("space")
-    if size != 8:
-        away = send_away()
-        return exchange(chip, "space", 2), away, work(away)
-    half = chip.shape[0] // 2
-    low = mask < 0.5
-    mine = jnp.where(low, chip[:half], chip[half:])
-    away = send_away()
-    one = lax.ppermute(chip, "space", [(i, i ^ (4 if i % 2 else 2)) for i in range(size)])
-    across = lax.ppermute(mine, "space", [(i, i ^ 6) for i in range(size)])
-    done = work(away)
-    one, done = lax.optimization_barrier((one, done))
-    across, away = lax.optimization_barrier((across, away))
-    both = jnp.concatenate([jnp.where(low, across, 0.0), jnp.where(low, 0.0, across)], axis=0)
-    fetched = one + both
-    return [chip, fetched, lax.ppermute(fetched, "space", [(i, i ^ 1) for i in range(size)])], away, done
-
-
 def body(noise, positions, wave_index, tile_lists, tile_counts):
     slabs = lax.axis_size("space")
     length_x = float(slabs)
@@ -445,20 +423,21 @@
     third = [(i, (i + 1 if i % 2 else i - 1) % slabs) for i in range(slabs)]
     table = ((4, particles, waves), BF16)
     rows_shape = ((3 * vectors, particles), F32)
-    base = waves // TILE * 32 + 8
+    half = waves // TILE * 16
+    base = half + 8
     far_flops = 2 * 96 * particles * waves * 2
 
     rows = jnp.transpose(noise, (1, 0, 2)).reshape(3 * vectors, particles)
     lines = jnp.broadcast_to(place.astype(F32)[:, None], (2, TILE))
     stack = jnp.concatenate([rows, positions], axis=0)
-    phases, flipped, terms, msg, mask = call(
+    phases, flipped, terms, mine, rest = call(
         functools.partial(start_kernel, length_x, share),
         [
             table,
             ((4, waves, particles), BF16),
             ((8, waves), F32),
+            ((half, TILE), F32),
             ((base + 32 * share, TILE), F32),
-            ((base // 2, TILE), F32),
         ],
         (wave_index, lines, stack),
         [
@@ -473,51 +452,46 @@
 
     matrices = plan = None
     for step in range(DEGREE):
-        other = lax.ppermute(msg, "space", core)
-        def send_away():
-            return lax.ppermute(msg[base:] if step == 0 else own, "space", third)
-
-
-        def pair_work(away):
-            return call(
+        other = lax.ppermute(rest, "space", core)
+        away = lax.ppermute(rest[base:] if step == 0 else own, "space", third)
+        if step == 0:
+            other, live = lax.optimization_barrier((other, live))
+        chip = jnp.concatenate([mine, rest[half:base]], axis=0) + other[:base]
+        parts = exchange(chip, "space", 2)
+        if step == 0:
+            matrices, plan = call(
                 functools.partial(pair_kernel, length_x, base + 24 * share, share),
                 [((SLOTS, 2 * TILE, 6 * TILE), BF16), ((4, SLOTS), jnp.int32)],
-                (place, live, stack, msg, other, away),
+                (place, live, stack, rest, other, away),
                 [pltpu.VMEM((tiles, 8, TILE), F32), pltpu.VMEM((3 * share, TILE, 8), F32)],
                 smem_in=2,
                 smem_out=(1,),
                 flops=far_flops,
             )
-
-        def near_work(within, beyond, *sources):
-            return call(
-                functools.partial(near_kernel, base, share, within, beyond),
+        near_part = call(
+            functools.partial(near_kernel, base, share, True, True),
+            [rows_shape],
+            (plan, rest, other, away, matrices),
+            [pltpu.VMEM((3 * share, 24, TILE), F32), pltpu.VMEM((tiles + 1, 24, TILE), F32)],
+            smem_in=1,
+            flops=20 * far_flops,
+        )[0]
+        if step == 0:
+            parts[-1], matrices = lax.optimization_barrier((parts[-1], matrices))
+        else:
+            parts[-1], near_part = lax.optimization_barrier((parts[-1], near_part))
+        total = functools.reduce(jnp.add, parts)
+        swapped = lax.ppermute(total[:half], "space", core)
+        part = near_part
+        for begin, factors in ((0, total), (waves // 2, swapped)):
+            part = call(
+                functools.partial(back_kernel, begin),
                 [rows_shape],
-                (plan, *sources, matrices),
-                [pltpu.VMEM((3 * share, 24, TILE), F32), pltpu.VMEM((tiles + 1, 24, TILE), F32)],
-                smem_in=1,
+                (factors, part, terms, flipped),
+                [pltpu.VMEM((2, 6 * vectors, waves // 2), BF16)],
                 flops=far_flops // 2,
             )[0]
-
-        if step == 0:
-            other, live = lax.optimization_barrier((other, live))
-        chip = msg[:base] + other[:base]
-        if step == 0:
-            factors, away, (matrices, plan) = chip_sums(chip, mask, send_away, pair_work)
-            near_part = near_work(True, True, msg, other, away)
-        else:
-            factors, away, near_part = chip_sums(
-                chip, mask, send_away, lambda away: near_work(True, False, msg, other)
-            )
-            near_part = near_work(False, True, away, near_part)
-        part, *norm = call(
-            functools.partial(back_kernel, len(factors)),
-            [rows_shape] + [((8, TILE), F32)] * (step > 0),
-            (*factors, near_part, terms, flipped),
-            [pltpu.VMEM((2, 48, waves), BF16)],
-            flops=far_flops,
-        )
-        norms += norm
+        norms.append(total)
         sums = exchange(part, "wave", 1)
         if step < DEGREE - 1:
             rows, own, norm = call(
@@ -526,17 +500,17 @@
                 (*sums, rows, terms),
                 flops=1,
             )
-            msg = call(
+            mine, rest = call(
                 factor_kernel,
-                [((base + 24 * share, TILE), F32)],
+                [((half, TILE), F32), ((base + 24 * share, TILE), F32)],
                 (rows, own, norm, terms, phases),
                 flops=far_flops,
-            )[0]
+            )
             images.append(rows)
     out = call(
         functools.partial(final_kernel, len(sums)),
         [rows_shape],
-        (*sums, noise_rows, *images, *norms),
+        (*sums, noise_rows, *images, *norms[1:]),
     )[0]
     return jnp.transpose(out.reshape(3, vectors, particles), (1, 0, 2))
 

time: 86.2 us -> 85.3 us (0.990)
  starting transfers between devices: 27.3 us -> 31.1 us
  Pallas kernels: 26.4 us -> 23.5 us
  waiting for transfers between devices: 29.4 us -> 27.8 us
    ppermute x9 -> x18, starting transfers between devices: 13.8 us -> 24.7 us  [exchange(): lax.ppermute(x, axis, [(i, i ^ d * bit) for i in range(size)])]
    ppermute x15 -> x9, waiting for transfers between devices: 8.88 us -> 1.6 us  [the longest x3 0.83 us: body(): swapped = lax.ppermute(total[:half], 'space', core)]
    ppermute x15 -> x9, starting transfers between devices: 13.6 us -> 6.45 us  [the longest x3 5.48 us: body(): away = lax.ppermute(rest[base:] if step == 0 else own, 'space', third)]
    ppermute x9 -> x18, waiting for transfers between devices: 20.5 us -> 26.2 us  [exchange(): lax.ppermute(x, axis, [(i, i ^ d * bit) for i in range(size)])]
    pallas_call x15 -> x16, Pallas kernels: 26.4 us -> 23.5 us  [call(): pl.pallas_call(kernel, out_shape=[jax.ShapeDtypeStruct(*o) for o in outs]...]
  transfers between devices with their start and end apart: 24 -> 27, of which waited for: 14 -> 16; matrix products, arithmetic and copies ran while one was open for 1% -> 1% of each run, Pallas kernels for 13% -> 12%
where the time goes in v4:
time: 85.3 us
  starting transfers between devices  31.1 us (36%)
  waiting for transfers between devices  27.8 us (33%)
  Pallas kernels  23.5 us (28%)
  other arithmetic  1.85 us (2%)
    ppermute x18, waiting for transfers between devices, exchange(): lax.ppermute(x, axis, [(i, i ^ d * bit) for i in range(size)])  26.2 us
    ppermute x18, starting transfers between devices, exchange(): lax.ppermute(x, axis, [(i, i ^ d * bit) for i in range(size)])  24.7 us
    pallas_call x16, Pallas kernels, call(): pl.pallas_call(kernel, out_shape=[jax.ShapeDtypeStruct(*o) for o in outs]...  23.5 us
    ppermute x3, starting transfers between devices, body(): away = lax.ppermute(rest[base:] if step == 0 else own, 'space', third)  5.48 us
  transfers between devices with their start and end apart: 27, of which 16 were waited for; matrix products, arithmetic and copies ran while one was open for 1% of the time, Pallas kernels for 12%

profile of v4, /device:TPU:0, one launch (start us, length us, event | category | flops | bytes accessed | tf_op | source)
XLA Modules:
  0.0 85.3 jit_solution(4065176812636176244)
XLA Ops:
  0.1 0.9 %pad_maximum_fusion.stack_ref.pos_ref = f32[27,1024]{1,0:T(8,128)S(1)} fusion(f32[3,1024]{1,0:T(4,128)} %param.6, f32[24,1024]{1,0:T(8,128)} %bitcast.8), kind=kLoop, calls=%fused_computation | loop fusion | flops 27648 | bytes 221184 | tf_op jit(solution)/shard_map/concatenate | solution.py:432
  1.1 0.7 copy-done.1
  1.8 6.6 %shard_map.55 = (bf16[4,1024,1024]{2,1,0:T(8,128)(2,1)S(1)}, bf16[4,1024,1024]{2,1,0:T(8,128)(2,1)S(1)}, f32[8,1024]{1,0:T(8,128)S(1)}, f32[128,128]{1,0:T(8,128)S(1)}, f32[200,128]{1,0:T(8,128)S(1)}) custom-call(s32[3,1024]{1,0:T(4,128)S(1)} %copy-done.1, f32[2,128]{1,0:T(2,128)S(1)} %broadcast_in_dim.6.place_ref, ...), custom_call_target="tpu_custom_call" | custom-call | flops 1610612736 | tf_op jit(solution)/shard_map/pallas_call | solution.py:385
  8.4 0.5 collective-permute-start
  8.9 3.6 %collective-permute-start.4 = (f32[64,128]{1,0:T(8,128)S(1)}, f32[64,128]{1,0:T(8,128)S(1)}, u32[]{:S(2)}, u32[]{:S(2)}) collective-permute-start(f32[64,128]{1,0:T(8,128)S(1)} %slice.32), channel_id=1, source_target_pairs={{0,28},{4,8},{8,4},{12,16},{16,12},{20,24},{24,20},{28,0},{1,29},{... | collective-permute-start | bytes 98312 | tf_op jit(solution)/shard_map/ppermute | solution.py:456
  12.5 0.8 fusion.live_ref
  13.3 0.6 collective-permute-start.3
  13.9 1.4 %collective-permute-start.2 = (f32[136,128]{1,0:T(8,128)S(1)}, f32[136,128]{1,0:T(8,128)S(1)}, u32[]{:S(2)}, u32[]{:S(2)}) collective-permute-start(f32[136,128]{1,0:T(8,128)S(1)} %maximum_add_fusion), channel_id=1, source_target_pairs={{0,8},{4,12},{8,0},{12,4},{16,24},{20,28},{24,16},{28,20},{1,9},{5... | collective-permute-start | bytes 208904 | tf_op jit(solution)/shard_map/ppermute | solution.py:405
  15.3 1.5 %collective-permute-start.1 = (f32[136,128]{1,0:T(8,128)S(1)}, f32[136,128]{1,0:T(8,128)S(1)}, u32[]{:S(2)}, u32[]{:S(2)}) collective-permute-start(f32[136,128]{1,0:T(8,128)S(1)} %maximum_add_fusion), channel_id=1, source_target_pairs={{0,16},{4,20},{8,24},{12,28},{16,0},{20,4},{24,8},{28,12},{1,17},{... | collective-permute-start | bytes 208904 | tf_op jit(solution)/shard_map/ppermute | solution.py:405
  16.8 3.5 %shard_map.56 = (bf16[40,256,768]{2,1,0:T(8,128)(2,1)S(1)}, s32[4,40]{1,0:T(4,128)S(1)}) custom-call(s32[2]{0:T(128)S(1)} %get-tuple-element.56.core_ref, s32[8,8]{1,0:T(8,128)S(1)} %fusion.live_ref, f32[27,1024]{1,0:T(8,128)S(1)} %pad_maximum_fusion.stack_ref.pos_ref, f32[200,128]{1,0:T(8,128)S(1)} %get-tuple-element.31.own_ref.refs_0_, ...), custom_call_target="tpu_custom_call" | custom-call | flops 402653184 | tf_op jit(solution)/shard_map/pallas_call | solution.py:385
  20.5 1.4 %shard_map.57.before_ref = f32[24,1024]{1,0:T(8,128)S(1)} custom-call(s32[4,40]{1,0:T(4,128)S(1)} %get-tuple-element.36.plan_ref, f32[200,128]{1,0:T(8,128)S(1)} %get-tuple-element.31.own_ref.refs_0_, f32[200,128]{1,0:T(8,128)S(1)} %collective-permute-done.near_ref.refs_1_, f32[64,128]{1,0:T(8,128)S(1)} %collective-permute-done.4.away_ref.refs_2_, ...), custom_call_target="tpu_custom_call" | custom-call | flops 8053063680 | tf_op jit(solution)/shard_map/pallas_call | solution.py:385
  21.9 0.8 shard_map.58.before_ref
  22.7 0.8 shard_map.59.refs_0_
  23.6 4.5 %collective-permute-start.8 = (f32[24,1024]{1,0:T(8,128)S(1)}, f32[24,1024]{1,0:T(8,128)S(1)}, u32[]{:S(2)}, u32[]{:S(2)}) collective-permute-start(f32[24,1024]{1,0:T(8,128)S(1)} %shard_map.59.refs_0_), channel_id=1, source_target_pairs={{0,3},{1,2},{2,1},{3,0},{4,7},{5,6},{6,5},{7,4},{8,11},{9,10},{10,... | collective-permute-start | bytes 294920 | tf_op jit(solution)/shard_map/ppermute | solution.py:405
  28.1 0.6 collective-permute-start.6
  28.7 3.0 %collective-permute-done.8.refs_3_ = f32[24,1024]{1,0:T(8,128)S(1)} collective-permute-done((f32[24,1024]{1,0:T(8,128)S(1)}, f32[24,1024]{1,0:T(8,128)S(1)}, u32[]{:S(2)}, u32[]{:S(2)}) %collective-permute-start.8) | collective-permute-done | bytes 98336 | tf_op jit(solution)/shard_map/ppermute | solution.py:405
  31.7 2.0 %collective-permute-done.7.refs_2_ = f32[24,1024]{1,0:T(8,128)S(1)} collective-permute-done((f32[24,1024]{1,0:T(8,128)S(1)}, f32[24,1024]{1,0:T(8,128)S(1)}, u32[]{:S(2)}, u32[]{:S(2)}) %collective-permute-start.7) | collective-permute-done | bytes 98336 | tf_op jit(solution)/shard_map/ppermute | solution.py:405
  33.7 4.1 %collective-permute-done.6.refs_1_ = f32[24,1024]{1,0:T(8,128)S(1)} collective-permute-done((f32[24,1024]{1,0:T(8,128)S(1)}, f32[24,1024]{1,0:T(8,128)S(1)}, u32[]{:S(2)}, u32[]{:S(2)}) %collective-permute-start.6) | collective-permute-done | bytes 98336 | tf_op jit(solution)/shard_map/ppermute | solution.py:405
  37.9 1.6 %shard_map.61 = (f32[128,128]{1,0:T(8,128)S(1)}, f32[184,128]{1,0:T(8,128)S(1)}) custom-call(f32[24,1024]{1,0:T(8,128)S(1)} %get-tuple-element.39.rows_ref.refs_4_.refs_5_, f32[48,128]{1,0:T(8,128)S(1)} %get-tuple-element.40.tiles_ref, f32[8,128]{1,0:T(8,128)S(1)} %get-tuple-element.41.norm_ref, f32[8,1024]{1,0:T(8,128)S(1)} %get-tuple-element.37.terms_ref.refs_5_, ...), custom_call_target="tpu_custom_call" | custom-call | flops 402653184 | tf_op jit(solution)/shard_map/pallas_call | solution.py:385
  40.1 0.8 collective-permute-done.9.refs_1_
  40.8 0.5 collective-permute-start.12
  41.3 1.2 %collective-permute-start.11 = (f32[136,128]{1,0:T(8,128)S(1)}, f32[136,128]{1,0:T(8,128)S(1)}, u32[]{:S(2)}, u32[]{:S(2)}) collective-permute-start(f32[136,128]{1,0:T(8,128)S(1)} %slice_add_fusion.1), channel_id=1, source_target_pairs={{0,8},{4,12},{8,0},{12,4},{16,24},{20,28},{24,16},{28,20},{1,9},{5... | collective-permute-start | bytes 208904 | tf_op jit(solution)/shard_map/ppermute | solution.py:405
  42.5 1.8 %collective-permute-start.10 = (f32[136,128]{1,0:T(8,128)S(1)}, f32[136,128]{1,0:T(8,128)S(1)}, u32[]{:S(2)}, u32[]{:S(2)}) collective-permute-start(f32[136,128]{1,0:T(8,128)S(1)} %slice_add_fusion.1), channel_id=1, source_target_pairs={{0,16},{4,20},{8,24},{12,28},{16,0},{20,4},{24,8},{28,12},{1,17},{... | collective-permute-start | bytes 208904 | tf_op jit(solution)/shard_map/ppermute | solution.py:405
  44.4 1.5 %shard_map.62.before_ref = f32[24,1024]{1,0:T(8,128)S(1)} custom-call(s32[4,40]{1,0:T(4,128)S(1)} %get-tuple-element.36.plan_ref, f32[184,128]{1,0:T(8,128)S(1)} %get-tuple-element.44.refs_0_, f32[184,128]{1,0:T(8,128)S(1)} %collective-permute-done.9.refs_1_, f32[48,128]{1,0:T(8,128)S(1)} %collective-permute-done.13.refs_2_, ...), custom_call_target="tpu_custom_call" | custom-call | flops 8053063680 | tf_op jit(solution)/shard_map/pallas_call | solution.py:385
  45.9 0.8 collective-permute-done.12
  46.8 0.7 collective-permute-done.10
  47.6 0.8 shard_map.63.before_ref
  48.9 0.8 shard_map.64.refs_0_
  49.7 2.0 %collective-permute-start.17 = (f32[24,1024]{1,0:T(8,128)S(1)}, f32[24,1024]{1,0:T(8,128)S(1)}, u32[]{:S(2)}, u32[]{:S(2)}) collective-permute-start(f32[24,1024]{1,0:T(8,128)S(1)} %shard_map.64.refs_0_), channel_id=1, source_target_pairs={{0,3},{1,2},{2,1},{3,0},{4,7},{5,6},{6,5},{7,4},{8,11},{9,10},{10,... | collective-permute-start | bytes 294920 | tf_op jit(solution)/shard_map/ppermute | solution.py:405
  51.7 2.4 %collective-permute-start.15 = (f32[24,1024]{1,0:T(8,128)S(1)}, f32[24,1024]{1,0:T(8,128)S(1)}, u32[]{:S(2)}, u32[]{:S(2)}) collective-permute-start(f32[24,1024]{1,0:T(8,128)S(1)} %shard_map.64.refs_0_), channel_id=1, source_target_pairs={{0,2},{1,3},{2,0},{3,1},{4,6},{5,7},{6,4},{7,5},{8,10},{9,11},{10,... | collective-permute-start | bytes 294920 | tf_op jit(solution)/shard_map/ppermute | solution.py:405
  54.2 3.1 %collective-permute-done.17.refs_3_ = f32[24,1024]{1,0:T(8,128)S(1)} collective-permute-done((f32[24,1024]{1,0:T(8,128)S(1)}, f32[24,1024]{1,0:T(8,128)S(1)}, u32[]{:S(2)}, u32[]{:S(2)}) %collective-permute-start.17) | collective-permute-done | bytes 98336 | tf_op jit(solution)/shard_map/ppermute | solution.py:405
  57.3 3.3 %collective-permute-done.16.refs_2_ = f32[24,1024]{1,0:T(8,128)S(1)} collective-permute-done((f32[24,1024]{1,0:T(8,128)S(1)}, f32[24,1024]{1,0:T(8,128)S(1)}, u32[]{:S(2)}, u32[]{:S(2)}) %collective-permute-start.16) | collective-permute-done | bytes 98336 | tf_op jit(solution)/shard_map/ppermute | solution.py:405
  60.6 1.6 %shard_map.66 = (f32[128,128]{1,0:T(8,128)S(1)}, f32[184,128]{1,0:T(8,128)S(1)}) custom-call(f32[24,1024]{1,0:T(8,128)S(1)} %get-tuple-element.48.rows_ref.refs_6_, f32[48,128]{1,0:T(8,128)S(1)} %get-tuple-element.49.tiles_ref, f32[8,128]{1,0:T(8,128)S(1)} %get-tuple-element.50.norm_ref, f32[8,1024]{1,0:T(8,128)S(1)} %get-tuple-element.37.terms_ref.refs_5_, ...), custom_call_target="tpu_custom_call" | custom-call | flops 402653184 | tf_op jit(solution)/shard_map/pallas_call | solution.py:385
  62.2 1.5 %collective-permute-start.22 = (f32[48,128]{1,0:T(8,128)S(1)}, f32[48,128]{1,0:T(8,128)S(1)}, u32[]{:S(2)}, u32[]{:S(2)}) collective-permute-start(f32[48,128]{1,0:T(8,128)S(1)} %get-tuple-element.49.tiles_ref), channel_id=1, source_target_pairs={{0,28},{4,8},{8,4},{12,16},{16,12},{20,24},{24,20},{28,0},{1,29},{... | collective-permute-start | bytes 73736 | tf_op jit(solution)/shard_map/ppermute | solution.py:456
  63.7 1.2 %collective-permute-start.21 = (f32[136,128]{1,0:T(8,128)S(1)}, f32[136,128]{1,0:T(8,128)S(1)}, u32[]{:S(2)}, u32[]{:S(2)}) collective-permute-start(f32[136,128]{1,0:T(8,128)S(1)} %slice_add_fusion), channel_id=1, source_target_pairs={{0,24},{4,28},{8,16},{12,20},{16,8},{20,12},{24,0},{28,4},{1,25},{... | collective-permute-start | bytes 208904 | tf_op jit(solution)/shard_map/ppermute | solution.py:405
  65.0 1.2 %collective-permute-start.20 = (f32[136,128]{1,0:T(8,128)S(1)}, f32[136,128]{1,0:T(8,128)S(1)}, u32[]{:S(2)}, u32[]{:S(2)}) collective-permute-start(f32[136,128]{1,0:T(8,128)S(1)} %slice_add_fusion), channel_id=1, source_target_pairs={{0,8},{4,12},{8,0},{12,4},{16,24},{20,28},{24,16},{28,20},{1,9},{5... | collective-permute-start | bytes 208904 | tf_op jit(solution)/shard_map/ppermute | solution.py:405
  66.2 1.1 %collective-permute-start.19 = (f32[136,128]{1,0:T(8,128)S(1)}, f32[136,128]{1,0:T(8,128)S(1)}, u32[]{:S(2)}, u32[]{:S(2)}) collective-permute-start(f32[136,128]{1,0:T(8,128)S(1)} %slice_add_fusion), channel_id=1, source_target_pairs={{0,16},{4,20},{8,24},{12,28},{16,0},{20,4},{24,8},{28,12},{1,17},{... | collective-permute-start | bytes 208904 | tf_op jit(solution)/shard_map/ppermute | solution.py:405
  67.3 1.4 %shard_map.67.before_ref = f32[24,1024]{1,0:T(8,128)S(1)} custom-call(s32[4,40]{1,0:T(4,128)S(1)} %get-tuple-element.36.plan_ref, f32[184,128]{1,0:T(8,128)S(1)} %get-tuple-element.52.refs_0_, f32[184,128]{1,0:T(8,128)S(1)} %collective-permute-done.18.refs_1_, f32[48,128]{1,0:T(8,128)S(1)} %collective-permute-done.22.refs_2_, ...), custom_call_target="tpu_custom_call" | custom-call | flops 8053063680 | tf_op jit(solution)/shard_map/pallas_call | solution.py:385
  68.7 1.1 %collective-permute-done.21 = f32[136,128]{1,0:T(8,128)S(1)} collective-permute-done((f32[136,128]{1,0:T(8,128)S(1)}, f32[136,128]{1,0:T(8,128)S(1)}, u32[]{:S(2)}, u32[]{:S(2)}) %collective-permute-start.21) | collective-permute-done | bytes 69664 | tf_op jit(solution)/shard_map/ppermute | solution.py:405
  70.0 0.6 collective-permute-done.19
  70.7 0.8 shard_map.68.before_ref
  71.9 0.8 shard_map.69.refs_0_
  72.7 2.4 %collective-permute-start.26 = (f32[24,1024]{1,0:T(8,128)S(1)}, f32[24,1024]{1,0:T(8,128)S(1)}, u32[]{:S(2)}, u32[]{:S(2)}) collective-permute-start(f32[24,1024]{1,0:T(8,128)S(1)} %shard_map.69.refs_0_), channel_id=1, source_target_pairs={{0,3},{1,2},{2,1},{3,0},{4,7},{5,6},{6,5},{7,4},{8,11},{9,10},{10,... | collective-permute-start | bytes 294920 | tf_op jit(solution)/shard_map/ppermute | solution.py:405
  75.1 2.1 %collective-permute-start.24 = (f32[24,1024]{1,0:T(8,128)S(1)}, f32[24,1024]{1,0:T(8,128)S(1)}, u32[]{:S(2)}, u32[]{:S(2)}) collective-permute-start(f32[24,1024]{1,0:T(8,128)S(1)} %shard_map.69.refs_0_), channel_id=1, source_target_pairs={{0,2},{1,3},{2,0},{3,1},{4,6},{5,7},{6,4},{7,5},{8,10},{9,11},{10,... | collective-permute-start | bytes 294920 | tf_op jit(solution)/shard_map/ppermute | solution.py:405
  77.2 3.1 %collective-permute-done.26.refs_3_ = f32[24,1024]{1,0:T(8,128)S(1)} collective-permute-done((f32[24,1024]{1,0:T(8,128)S(1)}, f32[24,1024]{1,0:T(8,128)S(1)}, u32[]{:S(2)}, u32[]{:S(2)}) %collective-permute-start.26) | collective-permute-done | bytes 98336 | tf_op jit(solution)/shard_map/ppermute | solution.py:405
  80.3 2.9 %collective-permute-done.25.refs_2_ = f32[24,1024]{1,0:T(8,128)S(1)} collective-permute-done((f32[24,1024]{1,0:T(8,128)S(1)}, f32[24,1024]{1,0:T(8,128)S(1)}, u32[]{:S(2)}, u32[]{:S(2)}) %collective-permute-start.25) | collective-permute-done | bytes 98336 | tf_op jit(solution)/shard_map/ppermute | solution.py:405
  83.1 1.3 %collective-permute-done.24.refs_1_ = f32[24,1024]{1,0:T(8,128)S(1)} collective-permute-done((f32[24,1024]{1,0:T(8,128)S(1)}, f32[24,1024]{1,0:T(8,128)S(1)}, u32[]{:S(2)}, u32[]{:S(2)}) %collective-permute-start.24) | collective-permute-done | bytes 98336 | tf_op jit(solution)/shard_map/ppermute | solution.py:405
  84.4 0.9 %shard_map.70 = f32[24,1024]{1,0:T(8,128)} custom-call(f32[24,1024]{1,0:T(8,128)S(1)} %shard_map.69.refs_0_, f32[24,1024]{1,0:T(8,128)S(1)} %collective-permute-done.24.refs_1_, f32[24,1024]{1,0:T(8,128)S(1)} %collective-permute-done.25.refs_2_, f32[24,1024]{1,0:T(8,128)S(1)} %collective-permute-done.26.refs_3_, f32[24,1024]{1,0:T(8,128)S(1)} %bitcast.10, ...), custom_call_target="tpu_custom_call" | custom-call | tf_op jit(solution)/shard_map/pallas_call | solution.py:385
  (43 shorter events, 2.3 us)
Async XLA Ops:
  1.1 0.7 copy-start.1
  8.4 4.8 %collective-permute-start = (f32[200,128]{1,0:T(8,128)S(1)}, f32[200,128]{1,0:T(8,128)S(1)}, u32[]{:S(2)}, u32[]{:S(2)}) collective-permute-start(f32[200,128]{1,0:T(8,128)S(1)} %get-tuple-element.31.own_ref.refs_0_), channel_id=1, source_target_pairs={{0,4},{4,0},{8,12},{12,8},{16,20},{20,16},{24,28},{28,24},{1,5},{5... | collective-permute-start | bytes 307208 | tf_op jit(solution)/shard_map/ppermute | solution.py:455
  8.9 7.9 %collective-permute-start.4 = (f32[64,128]{1,0:T(8,128)S(1)}, f32[64,128]{1,0:T(8,128)S(1)}, u32[]{:S(2)}, u32[]{:S(2)}) collective-permute-start(f32[64,128]{1,0:T(8,128)S(1)} %slice.32), channel_id=1, source_target_pairs={{0,28},{4,8},{8,4},{12,16},{16,12},{20,24},{24,20},{28,0},{1,29},{... | collective-permute-start | bytes 98312 | tf_op jit(solution)/shard_map/ppermute | solution.py:456
  13.3 7.1 %collective-permute-start.3 = (f32[136,128]{1,0:T(8,128)S(1)}, f32[136,128]{1,0:T(8,128)S(1)}, u32[]{:S(2)}, u32[]{:S(2)}) collective-permute-start(f32[136,128]{1,0:T(8,128)S(1)} %maximum_add_fusion), channel_id=1, source_target_pairs={{0,24},{4,28},{8,16},{12,20},{16,8},{20,12},{24,0},{28,4},{1,25},{... | collective-permute-start | bytes 208904 | tf_op jit(solution)/shard_map/ppermute | solution.py:405
  13.9 6.5 %collective-permute-start.2 = (f32[136,128]{1,0:T(8,128)S(1)}, f32[136,128]{1,0:T(8,128)S(1)}, u32[]{:S(2)}, u32[]{:S(2)}) collective-permute-start(f32[136,128]{1,0:T(8,128)S(1)} %maximum_add_fusion), channel_id=1, source_target_pairs={{0,8},{4,12},{8,0},{12,4},{16,24},{20,28},{24,16},{28,20},{1,9},{5... | collective-permute-start | bytes 208904 | tf_op jit(solution)/shard_map/ppermute | solution.py:405
  15.3 5.0 %collective-permute-start.1 = (f32[136,128]{1,0:T(8,128)S(1)}, f32[136,128]{1,0:T(8,128)S(1)}, u32[]{:S(2)}, u32[]{:S(2)}) collective-permute-start(f32[136,128]{1,0:T(8,128)S(1)} %maximum_add_fusion), channel_id=1, source_target_pairs={{0,16},{4,20},{8,24},{12,28},{16,0},{20,4},{24,8},{28,12},{1,17},{... | collective-permute-start | bytes 208904 | tf_op jit(solution)/shard_map/ppermute | solution.py:405
  20.4 2.3 %collective-permute-start.5 = (f32[128,128]{1,0:T(8,128)S(1)}, f32[128,128]{1,0:T(8,128)S(1)}, u32[]{:S(2)}, u32[]{:S(2)}) collective-permute-start(f32[128,128]{1,0:T(8,128)S(1)} %slice.40), channel_id=1, source_target_pairs={{0,4},{4,0},{8,12},{12,8},{16,20},{20,16},{24,28},{28,24},{1,5},{5... | collective-permute-start | bytes 196616 | tf_op jit(solution)/shard_map/ppermute | solution.py:484
  21.9 16.0 %copy-start = (f32[8,3,1024]{2,0,1:T(8,128)S(1)}, f32[8,3,1024]{2,0,1:T(8,128)}, u32[]{:S(2)}) copy-start(f32[8,3,1024]{2,0,1:T(8,128)} %param.5) | copy-start | bytes 294916
  23.6 8.1 %collective-permute-start.8 = (f32[24,1024]{1,0:T(8,128)S(1)}, f32[24,1024]{1,0:T(8,128)S(1)}, u32[]{:S(2)}, u32[]{:S(2)}) collective-permute-start(f32[24,1024]{1,0:T(8,128)S(1)} %shard_map.59.refs_0_), channel_id=1, source_target_pairs={{0,3},{1,2},{2,1},{3,0},{4,7},{5,6},{6,5},{7,4},{8,11},{9,10},{10,... | collective-permute-start | bytes 294920 | tf_op jit(solution)/shard_map/ppermute | solution.py:405
  28.1 5.7 %collective-permute-start.7 = (f32[24,1024]{1,0:T(8,128)S(1)}, f32[24,1024]{1,0:T(8,128)S(1)}, u32[]{:S(2)}, u32[]{:S(2)}) collective-permute-start(f32[24,1024]{1,0:T(8,128)S(1)} %shard_map.59.refs_0_), channel_id=1, source_target_pairs={{0,1},{1,0},{2,3},{3,2},{4,5},{5,4},{6,7},{7,6},{8,9},{9,8},{10,11... | collective-permute-start | bytes 294920 | tf_op jit(solution)/shard_map/ppermute | solution.py:405
  28.1 9.8 %collective-permute-start.6 = (f32[24,1024]{1,0:T(8,128)S(1)}, f32[24,1024]{1,0:T(8,128)S(1)}, u32[]{:S(2)}, u32[]{:S(2)}) collective-permute-start(f32[24,1024]{1,0:T(8,128)S(1)} %shard_map.59.refs_0_), channel_id=1, source_target_pairs={{0,2},{1,3},{2,0},{3,1},{4,6},{5,7},{6,4},{7,5},{8,10},{9,11},{10,... | collective-permute-start | bytes 294920 | tf_op jit(solution)/shard_map/ppermute | solution.py:405
  39.5 1.4 %collective-permute-start.9 = (f32[184,128]{1,0:T(8,128)S(1)}, f32[184,128]{1,0:T(8,128)S(1)}, u32[]{:S(2)}, u32[]{:S(2)}) collective-permute-start(f32[184,128]{1,0:T(8,128)S(1)} %get-tuple-element.44.refs_0_), channel_id=1, source_target_pairs={{0,4},{4,0},{8,12},{12,8},{16,20},{20,16},{24,28},{28,24},{1,5},{5... | collective-permute-start | bytes 282632 | tf_op jit(solution)/shard_map/ppermute | solution.py:455
  39.6 4.8 %collective-permute-start.13 = (f32[48,128]{1,0:T(8,128)S(1)}, f32[48,128]{1,0:T(8,128)S(1)}, u32[]{:S(2)}, u32[]{:S(2)}) collective-permute-start(f32[48,128]{1,0:T(8,128)S(1)} %get-tuple-element.40.tiles_ref), channel_id=1, source_target_pairs={{0,28},{4,8},{8,4},{12,16},{16,12},{20,24},{24,20},{28,0},{1,29},{... | collective-permute-start | bytes 73736 | tf_op jit(solution)/shard_map/ppermute | solution.py:456
  40.8 5.9 %collective-permute-start.12 = (f32[136,128]{1,0:T(8,128)S(1)}, f32[136,128]{1,0:T(8,128)S(1)}, u32[]{:S(2)}, u32[]{:S(2)}) collective-permute-start(f32[136,128]{1,0:T(8,128)S(1)} %slice_add_fusion.1), channel_id=1, source_target_pairs={{0,24},{4,28},{8,16},{12,20},{16,8},{20,12},{24,0},{28,4},{1,25},{... | collective-permute-start | bytes 208904 | tf_op jit(solution)/shard_map/ppermute | solution.py:405
  41.3 5.5 %collective-permute-start.11 = (f32[136,128]{1,0:T(8,128)S(1)}, f32[136,128]{1,0:T(8,128)S(1)}, u32[]{:S(2)}, u32[]{:S(2)}) collective-permute-start(f32[136,128]{1,0:T(8,128)S(1)} %slice_add_fusion.1), channel_id=1, source_target_pairs={{0,8},{4,12},{8,0},{12,4},{16,24},{20,28},{24,16},{28,20},{1,9},{5... | collective-permute-start | bytes 208904 | tf_op jit(solution)/shard_map/ppermute | solution.py:405
  42.5 5.0 %collective-permute-start.10 = (f32[136,128]{1,0:T(8,128)S(1)}, f32[136,128]{1,0:T(8,128)S(1)}, u32[]{:S(2)}, u32[]{:S(2)}) collective-permute-start(f32[136,128]{1,0:T(8,128)S(1)} %slice_add_fusion.1), channel_id=1, source_target_pairs={{0,16},{4,20},{8,24},{12,28},{16,0},{20,4},{24,8},{28,12},{1,17},{... | collective-permute-start | bytes 208904 | tf_op jit(solution)/shard_map/ppermute | solution.py:405
  47.6 1.3 %collective-permute-start.14 = (f32[128,128]{1,0:T(8,128)S(1)}, f32[128,128]{1,0:T(8,128)S(1)}, u32[]{:S(2)}, u32[]{:S(2)}) collective-permute-start(f32[128,128]{1,0:T(8,128)S(1)} %slice.42), channel_id=1, source_target_pairs={{0,4},{4,0},{8,12},{12,8},{16,20},{20,16},{24,28},{28,24},{1,5},{5... | collective-permute-start | bytes 196616 | tf_op jit(solution)/shard_map/ppermute | solution.py:484
  49.7 7.6 %collective-permute-start.17 = (f32[24,1024]{1,0:T(8,128)S(1)}, f32[24,1024]{1,0:T(8,128)S(1)}, u32[]{:S(2)}, u32[]{:S(2)}) collective-permute-start(f32[24,1024]{1,0:T(8,128)S(1)} %shard_map.64.refs_0_), channel_id=1, source_target_pairs={{0,3},{1,2},{2,1},{3,0},{4,7},{5,6},{6,5},{7,4},{8,11},{9,10},{10,... | collective-permute-start | bytes 294920 | tf_op jit(solution)/shard_map/ppermute | solution.py:405
  51.7 8.8 %collective-permute-start.16 = (f32[24,1024]{1,0:T(8,128)S(1)}, f32[24,1024]{1,0:T(8,128)S(1)}, u32[]{:S(2)}, u32[]{:S(2)}) collective-permute-start(f32[24,1024]{1,0:T(8,128)S(1)} %shard_map.64.refs_0_), channel_id=1, source_target_pairs={{0,1},{1,0},{2,3},{3,2},{4,5},{5,4},{6,7},{7,6},{8,9},{9,8},{10,11... | collective-permute-start | bytes 294920 | tf_op jit(solution)/shard_map/ppermute | solution.py:405
  51.7 8.8 %collective-permute-start.15 = (f32[24,1024]{1,0:T(8,128)S(1)}, f32[24,1024]{1,0:T(8,128)S(1)}, u32[]{:S(2)}, u32[]{:S(2)}) collective-permute-start(f32[24,1024]{1,0:T(8,128)S(1)} %shard_map.64.refs_0_), channel_id=1, source_target_pairs={{0,2},{1,3},{2,0},{3,1},{4,6},{5,7},{6,4},{7,5},{8,10},{9,11},{10,... | collective-permute-start | bytes 294920 | tf_op jit(solution)/shard_map/ppermute | solution.py:405
  62.1 1.6 %collective-permute-start.18 = (f32[184,128]{1,0:T(8,128)S(1)}, f32[184,128]{1,0:T(8,128)S(1)}, u32[]{:S(2)}, u32[]{:S(2)}) collective-permute-start(f32[184,128]{1,0:T(8,128)S(1)} %get-tuple-element.52.refs_0_), channel_id=1, source_target_pairs={{0,4},{4,0},{8,12},{12,8},{16,20},{20,16},{24,28},{28,24},{1,5},{5... | collective-permute-start | bytes 282632 | tf_op jit(solution)/shard_map/ppermute | solution.py:455
  62.2 5.1 %collective-permute-start.22 = (f32[48,128]{1,0:T(8,128)S(1)}, f32[48,128]{1,0:T(8,128)S(1)}, u32[]{:S(2)}, u32[]{:S(2)}) collective-permute-start(f32[48,128]{1,0:T(8,128)S(1)} %get-tuple-element.49.tiles_ref), channel_id=1, source_target_pairs={{0,28},{4,8},{8,4},{12,16},{16,12},{20,24},{24,20},{28,0},{1,29},{... | collective-permute-start | bytes 73736 | tf_op jit(solution)/shard_map/ppermute | solution.py:456
  63.7 6.0 %collective-permute-start.21 = (f32[136,128]{1,0:T(8,128)S(1)}, f32[136,128]{1,0:T(8,128)S(1)}, u32[]{:S(2)}, u32[]{:S(2)}) collective-permute-start(f32[136,128]{1,0:T(8,128)S(1)} %slice_add_fusion), channel_id=1, source_target_pairs={{0,24},{4,28},{8,16},{12,20},{16,8},{20,12},{24,0},{28,4},{1,25},{... | collective-permute-start | bytes 208904 | tf_op jit(solution)/shard_map/ppermute | solution.py:405
  65.0 5.0 %collective-permute-start.20 = (f32[136,128]{1,0:T(8,128)S(1)}, f32[136,128]{1,0:T(8,128)S(1)}, u32[]{:S(2)}, u32[]{:S(2)}) collective-permute-start(f32[136,128]{1,0:T(8,128)S(1)} %slice_add_fusion), channel_id=1, source_target_pairs={{0,8},{4,12},{8,0},{12,4},{16,24},{20,28},{24,16},{28,20},{1,9},{5... | collective-permute-start | bytes 208904 | tf_op jit(solution)/shard_map/ppermute | solution.py:405
  66.2 4.3 %collective-permute-start.19 = (f32[136,128]{1,0:T(8,128)S(1)}, f32[136,128]{1,0:T(8,128)S(1)}, u32[]{:S(2)}, u32[]{:S(2)}) collective-permute-start(f32[136,128]{1,0:T(8,128)S(1)} %slice_add_fusion), channel_id=1, source_target_pairs={{0,16},{4,20},{8,24},{12,28},{16,0},{20,4},{24,8},{28,12},{1,17},{... | collective-permute-start | bytes 208904 | tf_op jit(solution)/shard_map/ppermute | solution.py:405
  70.6 1.3 %collective-permute-start.23 = (f32[128,128]{1,0:T(8,128)S(1)}, f32[128,128]{1,0:T(8,128)S(1)}, u32[]{:S(2)}, u32[]{:S(2)}) collective-permute-start(f32[128,128]{1,0:T(8,128)S(1)} %slice.44), channel_id=1, source_target_pairs={{0,4},{4,0},{8,12},{12,8},{16,20},{20,16},{24,28},{28,24},{1,5},{5... | collective-permute-start | bytes 196616 | tf_op jit(solution)/shard_map/ppermute | solution.py:484
  72.7 7.5 %collective-permute-start.26 = (f32[24,1024]{1,0:T(8,128)S(1)}, f32[24,1024]{1,0:T(8,128)S(1)}, u32[]{:S(2)}, u32[]{:S(2)}) collective-permute-start(f32[24,1024]{1,0:T(8,128)S(1)} %shard_map.69.refs_0_), channel_id=1, source_target_pairs={{0,3},{1,2},{2,1},{3,0},{4,7},{5,6},{6,5},{7,4},{8,11},{9,10},{10,... | collective-permute-start | bytes 294920 | tf_op jit(solution)/shard_map/ppermute | solution.py:405
  75.1 8.1 %collective-permute-start.25 = (f32[24,1024]{1,0:T(8,128)S(1)}, f32[24,1024]{1,0:T(8,128)S(1)}, u32[]{:S(2)}, u32[]{:S(2)}) collective-permute-start(f32[24,1024]{1,0:T(8,128)S(1)} %shard_map.69.refs_0_), channel_id=1, source_target_pairs={{0,1},{1,0},{2,3},{3,2},{4,5},{5,4},{6,7},{7,6},{8,9},{9,8},{10,11... | collective-permute-start | bytes 294920 | tf_op jit(solution)/shard_map/ppermute | solution.py:405
  75.1 9.3 %collective-permute-start.24 = (f32[24,1024]{1,0:T(8,128)S(1)}, f32[24,1024]{1,0:T(8,128)S(1)}, u32[]{:S(2)}, u32[]{:S(2)}) collective-permute-start(f32[24,1024]{1,0:T(8,128)S(1)} %shard_map.69.refs_0_), channel_id=1, source_target_pairs={{0,2},{1,3},{2,0},{3,1},{4,6},{5,7},{6,4},{7,5},{8,10},{9,11},{10,... | collective-permute-start | bytes 294920 | tf_op jit(solution)/shard_map/ppermute | solution.py:405

commit v5 on v4

--- a/solution.py
+++ b/solution.py
@@ -14,7 +14,7 @@
 DEGREE = 3
 PAIR_MOST = 32
 GROUP = 4
-SLOTS = PAIR_MOST + 2 * GROUP
+SLOTS = PAIR_MOST + GROUP
 
 SIDE_CROSS = 8.0
 NEAR_SQUARE = 0.36
@@ -174,31 +174,58 @@
     emit([sum_ref[0], sum_ref[1]], terms_ref[...], 0, mine_ref, rest_ref)
 
 
-def pair_kernel(length_x, base, share, core_ref, live_ref, pos_ref, own_ref, near_ref, away_ref, out_ref, plan_ref, place_ref, column_ref):
+def fill_window(sources, share, window_ref):
+    for slab, (ref, start) in enumerate(sources):
+        for i in range(share):
+            row = start + 24 * i
+            window_ref[slab * share + i] = ref[row : row + 24, :]
+
+
+def add_pair(target, source, matrix, sum_ref):
+    high, low = split(source)
+    left = jnp.concatenate(
+        [
+            jnp.concatenate([high, high], axis=1),
+            jnp.concatenate([low, jnp.zeros_like(low)], axis=1),
+        ],
+        axis=0,
+    )
+    both = jnp.dot(left, matrix, preferred_element_type=F32)
+    full = both[:24] + both[24:]
+    x, y, z = full[0:8], full[8:16], full[16:24]
+
+    def part(rows, at):
+        return rows[:, at * TILE : (at + 1) * TILE]
+
+    sum_ref[target] += jnp.concatenate(
+        [
+            part(x, 0) + part(y, 1) + part(z, 2),
+            part(x, 1) + part(y, 3) + part(z, 4),
+            part(x, 2) + part(y, 4) + part(z, 5),
+        ],
+        axis=0,
+    )
+
+
+def pair_kernel(
+    length_x, base, share, live_ref, pos_ref, own_ref, near_ref, away_ref, out_ref, plan_ref, near_out_ref,
+    place_ref, column_ref, window_ref, sum_ref
+):
     tiles = pos_ref.shape[1] // TILE
-    ranks = tiles // share
-    odd = core_ref[0] == 1
-    rank = core_ref[1]
-    inner = outer = jnp.int32(0)
+    seen = jnp.int32(0)
     for target in range(tiles):
         for k in range(NB_MOST):
-            window = live_ref[target, k]
-            side, tile = lax.div(window, tiles), lax.rem(window, tiles)
-            which = jnp.where(side == 1, 0, jnp.where((side == 0) == odd, 1, 2))
-            mine = jnp.where((window >= 0) & (lax.rem(tile, ranks) == rank), 1, 0)
-            third = jnp.where(which == 2, 1, 0)
-            at = jnp.where(which == 2, SLOTS - 1 - outer, inner)
-            plan_ref[0, at] = target
-            plan_ref[1, at] = which * share + lax.div(tile, ranks)
-            plan_ref[2, at] = jnp.where(window == tiles + target, 1, 0)
-            inner = jnp.minimum(inner + mine * (1 - third), PAIR_MOST)
-            outer = jnp.minimum(outer + mine * third, PAIR_MOST)
-    plan_ref[3, 0] = inner
-    plan_ref[3, 1] = outer
+            code = live_ref[target, k]
+            plan_ref[0, seen] = target
+            plan_ref[1, seen] = code
+            seen = seen + jnp.where(code >= 0, 1, 0)
+    plan_ref[2, 0] = seen
     for k in range(GROUP):
-        for at in (inner + k, SLOTS - 1 - outer - k):
-            plan_ref[0, at] = tiles
-            plan_ref[1, at] = 0
+        plan_ref[0, seen + k] = tiles
+        plan_ref[1, seen + k] = 0
+    fill_window(((own_ref, base), (near_ref, base), (away_ref, 0)), share, window_ref)
+    sum_ref[...] = jnp.zeros_like(sum_ref)
+    base = base + 24 * share
     sides = (length_x, SIDE_CROSS, SIDE_CROSS)
     reach = math.sqrt(NEAR_SQUARE)
     filler = jnp.zeros((5, TILE), F32)
@@ -213,11 +240,14 @@
             column_ref[slab * share + i] = place.T
     count = 32
 
-    def pair(at, carry):
-        p = jnp.where(at < inner, at, SLOTS - 1 + inner - at)
+    def pair(p, carry):
+        q = jnp.maximum(p - 1, 0)
+        add_pair(
+            jnp.where(p == 0, tiles, plan_ref[0, q]), window_ref[plan_ref[1, q] >> 1], out_ref[q], sum_ref
+        )
         target = place_ref[plan_ref[0, p]]
-        source = column_ref[plan_ref[1, p]]
-        own = plan_ref[2, p].astype(F32)
+        source = column_ref[plan_ref[1, p] >> 1]
+        own = (plan_ref[1, p] & 1).astype(F32)
         lines = [target[a : a + 1] for a in range(3)]
         for low in range(0, TILE, count):
             rows = slice(low, low + count)
@@ -244,61 +274,23 @@
                     slot += 1
         return carry
 
-    lax.fori_loop(0, inner + outer, pair, 0)
-
-
-def near_kernel(base, share, within, beyond, plan_ref, *refs):
-    matrix_ref, out_ref, window_ref, sum_ref = refs[-4:]
-    sources = list(refs[:-4])
-    before_ref = None if within else sources.pop()
-    slabs = [(0, base), (1, base)] * within + [(2, 0)] * beyond
-    slabs = [(slab, ref, start) for (slab, start), ref in zip(slabs, sources)]
-    tiles = sum_ref.shape[0] - 1
-    for slab, ref, start in slabs:
-        for i in range(share):
-            row = start + 24 * i
-            window_ref[slab * share + i] = ref[row : row + 24, :]
-    if before_ref is None:
-        sum_ref[...] = jnp.zeros_like(sum_ref)
-    else:
-        for i in range(tiles):
-            sum_ref[i] = before_ref[:, i * TILE : (i + 1) * TILE]
-        sum_ref[tiles] = jnp.zeros_like(sum_ref[tiles])
-
-    def part(rows, at):
-        return rows[:, at * TILE : (at + 1) * TILE]
-
-    def add(p):
-        high, low = split(window_ref[plan_ref[1, p]])
-        left = jnp.concatenate(
-            [
-                jnp.concatenate([high, high], axis=1),
-                jnp.concatenate([low, jnp.zeros_like(low)], axis=1),
-            ],
-            axis=0,
-        )
-        both = jnp.dot(left, matrix_ref[p], preferred_element_type=F32)
-        full = both[:24] + both[24:]
-        x, y, z = full[0:8], full[8:16], full[16:24]
-        sum_ref[plan_ref[0, p]] += jnp.concatenate(
-            [
-                part(x, 0) + part(y, 1) + part(z, 2),
-                part(x, 1) + part(y, 3) + part(z, 4),
-                part(x, 2) + part(y, 4) + part(z, 5),
-            ],
-            axis=0,
-        )
-
-    for wanted, row, start, step in ((within, 0, 0, 1), (beyond, 1, SLOTS - 1, -1)):
-        if wanted:
-
-            def several(at, carry):
-                for k in range(GROUP):
-                    add(start + step * (at * GROUP + k))
-                return carry
-
-            lax.fori_loop(0, lax.div(plan_ref[3, row] + (GROUP - 1), GROUP), several, 0)
+    lax.fori_loop(0, seen + 1, pair, 0)
     for i in range(tiles):
+        near_out_ref[:, i * TILE : (i + 1) * TILE] = sum_ref[i]
+
+
+def near_kernel(base, share, plan_ref, own_ref, near_ref, away_ref, matrix_ref, out_ref, window_ref, sum_ref):
+    fill_window(((own_ref, base), (near_ref, base), (away_ref, 0)), share, window_ref)
+    sum_ref[...] = jnp.zeros_like(sum_ref)
+
+    def several(at, carry):
+        for k in range(GROUP):
+            p = at * GROUP + k
+            add_pair(plan_ref[0, p], window_ref[plan_ref[1, p] >> 1], matrix_ref[p], sum_ref)
+        return carry
+
+    lax.fori_loop(0, lax.div(plan_ref[2, 0] + (GROUP - 1), GROUP), several, 0)
+    for i in range(sum_ref.shape[0] - 1):
         out_ref[:, i * TILE : (i + 1) * TILE] = sum_ref[i]
 
 
@@ -418,7 +410,6 @@
     ranks = lax.axis_size("wave")
     share = tiles // ranks
     place = jnp.stack([lax.axis_index("space") & 1, lax.axis_index("wave")]).astype(jnp.int32)
-    live = jnp.where(jnp.arange(NB_MOST)[None] < tile_counts[:, None], tile_lists, -1)
     core = [(i, i ^ 1) for i in range(slabs)]
     third = [(i, (i + 1 if i % 2 else i - 1) % slabs) for i in range(slabs)]
     table = ((4, particles, waves), BF16)
@@ -447,6 +438,16 @@
         ],
         flops=4 * far_flops,
     )
+    core_line = jnp.broadcast_to(terms[6:7, :NB_MOST], tile_lists.shape)
+    rank_line = jnp.broadcast_to(terms[7:8, :NB_MOST], tile_lists.shape)
+    side, tile = tile_lists // tiles, tile_lists % tiles
+    which = jnp.where(side == 1, 0, jnp.where((side == 0) == (core_line > 0.5), 1, 2))
+    targets = lax.broadcasted_iota(jnp.int32, tile_lists.shape, 0)
+    slots = lax.broadcasted_iota(jnp.int32, tile_lists.shape, 1)
+    itself = tile_lists - targets == tiles
+    code = 2 * (which * share + tile // ranks) + itself.astype(jnp.int32)
+    wanted = (slots < tile_counts[:, None]) & (tile % ranks == rank_line.astype(jnp.int32))
+    live = jnp.where(wanted, code, -1)
     noise_rows = rows
     images, norms = [], []
 
@@ -458,28 +459,27 @@
             other, live = lax.optimization_barrier((other, live))
         chip = jnp.concatenate([mine, rest[half:base]], axis=0) + other[:base]
         parts = exchange(chip, "space", 2)
+        window = [pltpu.VMEM((3 * share, 24, TILE), F32), pltpu.VMEM((tiles + 1, 24, TILE), F32)]
         if step == 0:
-            matrices, plan = call(
-                functools.partial(pair_kernel, length_x, base + 24 * share, share),
-                [((SLOTS, 2 * TILE, 6 * TILE), BF16), ((4, SLOTS), jnp.int32)],
-                (place, live, stack, rest, other, away),
-                [pltpu.VMEM((tiles, 8, TILE), F32), pltpu.VMEM((3 * share, TILE, 8), F32)],
-                smem_in=2,
+            matrices, plan, near_part = call(
+                functools.partial(pair_kernel, length_x, base, share),
+                [((SLOTS, 2 * TILE, 6 * TILE), BF16), ((3, SLOTS), jnp.int32), rows_shape],
+                (live, stack, rest, other, away),
+                [pltpu.VMEM((tiles + 1, 8, TILE), F32), pltpu.VMEM((3 * share, TILE, 8), F32), *window],
+                smem_in=1,
                 smem_out=(1,),
-                flops=far_flops,
+                flops=20 * far_flops,
             )
-        near_part = call(
-            functools.partial(near_kernel, base, share, True, True),
-            [rows_shape],
-            (plan, rest, other, away, matrices),
-            [pltpu.VMEM((3 * share, 24, TILE), F32), pltpu.VMEM((tiles + 1, 24, TILE), F32)],
-            smem_in=1,
-            flops=20 * far_flops,
-        )[0]
-        if step == 0:
-            parts[-1], matrices = lax.optimization_barrier((parts[-1], matrices))
         else:
-            parts[-1], near_part = lax.optimization_barrier((parts[-1], near_part))
+            near_part = call(
+                functools.partial(near_kernel, base, share),
+                [rows_shape],
+                (plan, rest, other, away, matrices),
+                window,
+                smem_in=1,
+                flops=20 * far_flops,
+            )[0]
+        parts[-1], near_part = lax.optimization_barrier((parts[-1], near_part))
         total = functools.reduce(jnp.add, parts)
         swapped = lax.ppermute(total[:half], "space", core)
         part = near_part

time: 85.3 us -> 82.6 us (0.968)
  waiting for transfers between devices: 27.8 us -> 25.6 us
  Pallas kernels: 23.5 us -> 21.4 us
  starting transfers between devices: 31.1 us -> 32.8 us
    ppermute x18, waiting for transfers between devices: 26.2 us -> 23.3 us  [exchange(): lax.ppermute(x, axis, [(i, i ^ d * bit) for i in range(size)])]
    pallas_call x16 -> x15, Pallas kernels: 23.5 us -> 21.4 us  [call(): pl.pallas_call(kernel, out_shape=[jax.ShapeDtypeStruct(*o) for o in outs]...]
    ppermute x18, starting transfers between devices: 24.7 us -> 26.5 us  [exchange(): lax.ppermute(x, axis, [(i, i ^ d * bit) for i in range(size)])]
  transfers between devices with their start and end apart: 27 -> 27, of which waited for: 16 -> 16; matrix products, arithmetic and copies ran while one was open for 1% -> 1% of each run, Pallas kernels for 12% -> 10%
where the time goes in v5:
time: 82.6 us
  starting transfers between devices  32.8 us (40%)
  waiting for transfers between devices  25.6 us (31%)
  Pallas kernels  21.4 us (26%)
  other arithmetic  1.87 us (2%)
    ppermute x18, starting transfers between devices, exchange(): lax.ppermute(x, axis, [(i, i ^ d * bit) for i in range(size)])  26.5 us
    ppermute x18, waiting for transfers between devices, exchange(): lax.ppermute(x, axis, [(i, i ^ d * bit) for i in range(size)])  23.3 us
    pallas_call x15, Pallas kernels, call(): pl.pallas_call(kernel, out_shape=[jax.ShapeDtypeStruct(*o) for o in outs]...  21.4 us
    ppermute x3, starting transfers between devices, body(): away = lax.ppermute(rest[base:] if step == 0 else own, 'space', third)  5.28 us
  transfers between devices with their start and end apart: 27, of which 16 were waited for; matrix products, arithmetic and copies ran while one was open for 1% of the time, Pallas kernels for 10%

profile of v5, /device:TPU:0, one launch (start us, length us, event | category | flops | bytes accessed | tf_op | source)
XLA Modules:
  0.0 82.6 jit_solution(16543907689302447522)
XLA Ops:
  0.0 0.9 %pad_maximum_fusion.stack_ref.pos_ref = f32[27,1024]{1,0:T(8,128)S(1)} fusion(f32[3,1024]{1,0:T(4,128)} %param.6, f32[24,1024]{1,0:T(8,128)} %bitcast.12), kind=kLoop, calls=%fused_computation | loop fusion | flops 27648 | bytes 221184 | tf_op jit(solution)/shard_map/concatenate | solution.py:423
  1.1 0.7 copy-done.1
  1.8 6.6 %shard_map.55 = (bf16[4,1024,1024]{2,1,0:T(8,128)(2,1)S(1)}, bf16[4,1024,1024]{2,1,0:T(8,128)(2,1)S(1)}, f32[8,1024]{1,0:T(8,128)S(1)}, f32[128,128]{1,0:T(8,128)S(1)}, f32[200,128]{1,0:T(8,128)S(1)}) custom-call(s32[3,1024]{1,0:T(4,128)S(1)} %copy-done.1, f32[2,128]{1,0:T(2,128)S(1)} %broadcast_in_dim.14.place_ref, ...), custom_call_target="tpu_custom_call" | custom-call | flops 1610612736 | tf_op jit(solution)/shard_map/pallas_call | solution.py:377
  8.4 0.5 collective-permute-start
  9.0 3.6 %collective-permute-start.4 = (f32[64,128]{1,0:T(8,128)S(1)}, f32[64,128]{1,0:T(8,128)S(1)}, u32[]{:S(2)}, u32[]{:S(2)}) collective-permute-start(f32[64,128]{1,0:T(8,128)S(1)} %slice.40), channel_id=1, source_target_pairs={{0,28},{4,8},{8,4},{12,16},{16,12},{20,24},{24,20},{28,0},{1,29},{... | collective-permute-start | bytes 98312 | tf_op jit(solution)/shard_map/ppermute | solution.py:457
  12.5 0.8 fusion.4.live_ref
  13.3 0.6 collective-permute-start.3
  13.9 0.4 collective-permute-start.1
  14.3 2.6 %collective-permute-start.2 = (f32[136,128]{1,0:T(8,128)S(1)}, f32[136,128]{1,0:T(8,128)S(1)}, u32[]{:S(2)}, u32[]{:S(2)}) collective-permute-start(f32[136,128]{1,0:T(8,128)S(1)} %maximum_add_fusion), channel_id=1, source_target_pairs={{0,8},{4,12},{8,0},{12,4},{16,24},{20,28},{24,16},{28,20},{1,9},{5... | collective-permute-start | bytes 208904 | tf_op jit(solution)/shard_map/ppermute | solution.py:397
  16.9 2.8 %shard_map.56 = (bf16[36,256,768]{2,1,0:T(8,128)(2,1)S(1)}, s32[3,36]{1,0:T(4,128)S(1)}, f32[24,1024]{1,0:T(8,128)S(1)}) custom-call(s32[8,8]{1,0:T(8,128)S(1)} %fusion.4.live_ref, f32[27,1024]{1,0:T(8,128)S(1)} %pad_maximum_fusion.stack_ref.pos_ref, f32[200,128]{1,0:T(8,128)S(1)} %get-tuple-element.32.own_ref, ...), custom_call_target="tpu_custom_call" | custom-call | flops 8053063680 | tf_op jit(solution)/shard_map/pallas_call | solution.py:377
  19.8 0.8 %shard_map.57.before_ref = f32[24,1024]{1,0:T(8,128)S(1)} custom-call(f32[136,128]{1,0:T(8,128)S(1)} %add_add_fusion.2.factor_ref, f32[24,1024]{1,0:T(8,128)S(1)} %get-tuple-element.38.before_ref, f32[8,1024]{1,0:T(8,128)S(1)} %get-tuple-element.33.terms_ref.refs_5_, bf16[4,1024,1024]{2,1,0:T(8,128)(2,1)S(1)} %get-tuple-element.39.flip_ref), custom_call_target="tpu_custom_call" | custom-call | flops 201326592 | tf_op jit(solution)/shard_map/pallas_call | solution.py:377
  20.6 0.4 collective-permute-done.5.factor_ref
  21.0 0.8 %shard_map.58.refs_0_ = f32[24,1024]{1,0:T(8,128)S(1)} custom-call(f32[128,128]{1,0:T(8,128)S(1)} %collective-permute-done.5.factor_ref, f32[24,1024]{1,0:T(8,128)S(1)} %shard_map.57.before_ref, f32[8,1024]{1,0:T(8,128)S(1)} %get-tuple-element.33.terms_ref.refs_5_, bf16[4,1024,1024]{2,1,0:T(8,128)(2,1)S(1)} %get-tuple-element.39.flip_ref), custom_call_target="tpu_custom_call" | custom-call | flops 201326592 | tf_op jit(solution)/shard_map/pallas_call | solution.py:377
  21.9 2.9 %collective-permute-start.6 = (f32[24,1024]{1,0:T(8,128)S(1)}, f32[24,1024]{1,0:T(8,128)S(1)}, u32[]{:S(2)}, u32[]{:S(2)}) collective-permute-start(f32[24,1024]{1,0:T(8,128)S(1)} %shard_map.58.refs_0_), channel_id=1, source_target_pairs={{0,2},{1,3},{2,0},{3,1},{4,6},{5,7},{6,4},{7,5},{8,10},{9,11},{10,... | collective-permute-start | bytes 294920 | tf_op jit(solution)/shard_map/ppermute | solution.py:397
  24.7 3.8 %collective-permute-start.7 = (f32[24,1024]{1,0:T(8,128)S(1)}, f32[24,1024]{1,0:T(8,128)S(1)}, u32[]{:S(2)}, u32[]{:S(2)}) collective-permute-start(f32[24,1024]{1,0:T(8,128)S(1)} %shard_map.58.refs_0_), channel_id=1, source_target_pairs={{0,1},{1,0},{2,3},{3,2},{4,5},{5,4},{6,7},{7,6},{8,9},{9,8},{10,11... | collective-permute-start | bytes 294920 | tf_op jit(solution)/shard_map/ppermute | solution.py:397
  28.5 3.2 %collective-permute-done.7.refs_2_ = f32[24,1024]{1,0:T(8,128)S(1)} collective-permute-done((f32[24,1024]{1,0:T(8,128)S(1)}, f32[24,1024]{1,0:T(8,128)S(1)}, u32[]{:S(2)}, u32[]{:S(2)}) %collective-permute-start.7) | collective-permute-done | bytes 98336 | tf_op jit(solution)/shard_map/ppermute | solution.py:397
  31.7 3.6 %collective-permute-done.8.refs_3_ = f32[24,1024]{1,0:T(8,128)S(1)} collective-permute-done((f32[24,1024]{1,0:T(8,128)S(1)}, f32[24,1024]{1,0:T(8,128)S(1)}, u32[]{:S(2)}, u32[]{:S(2)}) %collective-permute-start.8) | collective-permute-done | bytes 98336 | tf_op jit(solution)/shard_map/ppermute | solution.py:397
  35.3 1.6 %shard_map.60 = (f32[128,128]{1,0:T(8,128)S(1)}, f32[184,128]{1,0:T(8,128)S(1)}) custom-call(f32[24,1024]{1,0:T(8,128)S(1)} %get-tuple-element.40.rows_ref.refs_4_.refs_5_, f32[48,128]{1,0:T(8,128)S(1)} %get-tuple-element.41.tiles_ref, f32[8,128]{1,0:T(8,128)S(1)} %get-tuple-element.42.norm_ref, f32[8,1024]{1,0:T(8,128)S(1)} %get-tuple-element.33.terms_ref.refs_5_, ...), custom_call_target="tpu_custom_call" | custom-call | flops 402653184 | tf_op jit(solution)/shard_map/pallas_call | solution.py:377
  37.1 1.2 %collective-permute-done.9.near_ref = f32[184,128]{1,0:T(8,128)S(1)} collective-permute-done((f32[184,128]{1,0:T(8,128)S(1)}, f32[184,128]{1,0:T(8,128)S(1)}, u32[]{:S(2)}, u32[]{:S(2)}) %collective-permute-start.9) | collective-permute-done | bytes 94240 | tf_op jit(solution)/shard_map/ppermute | solution.py:456
  38.5 2.2 %collective-permute-start.10 = (f32[136,128]{1,0:T(8,128)S(1)}, f32[136,128]{1,0:T(8,128)S(1)}, u32[]{:S(2)}, u32[]{:S(2)}) collective-permute-start(f32[136,128]{1,0:T(8,128)S(1)} %slice_add_fusion.1), channel_id=1, source_target_pairs={{0,16},{4,20},{8,24},{12,28},{16,0},{20,4},{24,8},{28,12},{1,17},{... | collective-permute-start | bytes 208904 | tf_op jit(solution)/shard_map/ppermute | solution.py:397
  40.7 1.2 %collective-permute-start.11 = (f32[136,128]{1,0:T(8,128)S(1)}, f32[136,128]{1,0:T(8,128)S(1)}, u32[]{:S(2)}, u32[]{:S(2)}) collective-permute-start(f32[136,128]{1,0:T(8,128)S(1)} %slice_add_fusion.1), channel_id=1, source_target_pairs={{0,8},{4,12},{8,0},{12,4},{16,24},{20,28},{24,16},{28,20},{1,9},{5... | collective-permute-start | bytes 208904 | tf_op jit(solution)/shard_map/ppermute | solution.py:397
  41.9 1.5 %shard_map.61.before_ref = f32[24,1024]{1,0:T(8,128)S(1)} custom-call(s32[3,36]{1,0:T(4,128)S(1)} %get-tuple-element.46.plan_ref, f32[184,128]{1,0:T(8,128)S(1)} %get-tuple-element.45.own_ref, f32[184,128]{1,0:T(8,128)S(1)} %collective-permute-done.9.near_ref, f32[48,128]{1,0:T(8,128)S(1)} %collective-permute-done.13.away_ref, ...), custom_call_target="tpu_custom_call" | custom-call | flops 8053063680 | tf_op jit(solution)/shard_map/pallas_call | solution.py:377
  43.6 1.3 %collective-permute-done.10 = f32[136,128]{1,0:T(8,128)S(1)} collective-permute-done((f32[136,128]{1,0:T(8,128)S(1)}, f32[136,128]{1,0:T(8,128)S(1)}, u32[]{:S(2)}, u32[]{:S(2)}) %collective-permute-start.10) | collective-permute-done | bytes 69664 | tf_op jit(solution)/shard_map/ppermute | solution.py:397
  45.2 0.8 %shard_map.62.before_ref = f32[24,1024]{1,0:T(8,128)S(1)} custom-call(f32[136,128]{1,0:T(8,128)S(1)} %add_add_fusion.1.factor_ref.refs_7_, f32[24,1024]{1,0:T(8,128)S(1)} %shard_map.61.before_ref, f32[8,1024]{1,0:T(8,128)S(1)} %get-tuple-element.33.terms_ref.refs_5_, bf16[4,1024,1024]{2,1,0:T(8,128)(2,1)S(1)} %get-tuple-element.39.flip_ref), custom_call_target="tpu_custom_call" | custom-call | flops 201326592 | tf_op jit(solution)/shard_map/pallas_call | solution.py:377
  46.0 0.3 collective-permute-done.14.factor_ref
  46.3 0.8 %shard_map.63.refs_0_ = f32[24,1024]{1,0:T(8,128)S(1)} custom-call(f32[128,128]{1,0:T(8,128)S(1)} %collective-permute-done.14.factor_ref, f32[24,1024]{1,0:T(8,128)S(1)} %shard_map.62.before_ref, f32[8,1024]{1,0:T(8,128)S(1)} %get-tuple-element.33.terms_ref.refs_5_, bf16[4,1024,1024]{2,1,0:T(8,128)(2,1)S(1)} %get-tuple-element.39.flip_ref), custom_call_target="tpu_custom_call" | custom-call | flops 201326592 | tf_op jit(solution)/shard_map/pallas_call | solution.py:377
  47.2 2.0 %collective-permute-start.15 = (f32[24,1024]{1,0:T(8,128)S(1)}, f32[24,1024]{1,0:T(8,128)S(1)}, u32[]{:S(2)}, u32[]{:S(2)}) collective-permute-start(f32[24,1024]{1,0:T(8,128)S(1)} %shard_map.63.refs_0_), channel_id=1, source_target_pairs={{0,2},{1,3},{2,0},{3,1},{4,6},{5,7},{6,4},{7,5},{8,10},{9,11},{10,... | collective-permute-start | bytes 294920 | tf_op jit(solution)/shard_map/ppermute | solution.py:397
  49.1 0.5 collective-permute-start.16
  49.6 2.0 %collective-permute-start.17 = (f32[24,1024]{1,0:T(8,128)S(1)}, f32[24,1024]{1,0:T(8,128)S(1)}, u32[]{:S(2)}, u32[]{:S(2)}) collective-permute-start(f32[24,1024]{1,0:T(8,128)S(1)} %shard_map.63.refs_0_), channel_id=1, source_target_pairs={{0,3},{1,2},{2,1},{3,0},{4,7},{5,6},{6,5},{7,4},{8,11},{9,10},{10,... | collective-permute-start | bytes 294920 | tf_op jit(solution)/shard_map/ppermute | solution.py:397
  51.6 5.2 %collective-permute-done.15.refs_1_ = f32[24,1024]{1,0:T(8,128)S(1)} collective-permute-done((f32[24,1024]{1,0:T(8,128)S(1)}, f32[24,1024]{1,0:T(8,128)S(1)}, u32[]{:S(2)}, u32[]{:S(2)}) %collective-permute-start.15) | collective-permute-done | bytes 98336 | tf_op jit(solution)/shard_map/ppermute | solution.py:397
  56.8 1.1 %collective-permute-done.16.refs_2_ = f32[24,1024]{1,0:T(8,128)S(1)} collective-permute-done((f32[24,1024]{1,0:T(8,128)S(1)}, f32[24,1024]{1,0:T(8,128)S(1)}, u32[]{:S(2)}, u32[]{:S(2)}) %collective-permute-start.16) | collective-permute-done | bytes 98336 | tf_op jit(solution)/shard_map/ppermute | solution.py:397
  57.9 1.6 %shard_map.65 = (f32[128,128]{1,0:T(8,128)S(1)}, f32[184,128]{1,0:T(8,128)S(1)}) custom-call(f32[24,1024]{1,0:T(8,128)S(1)} %get-tuple-element.50.rows_ref.refs_6_, f32[48,128]{1,0:T(8,128)S(1)} %get-tuple-element.51.tiles_ref, f32[8,128]{1,0:T(8,128)S(1)} %get-tuple-element.52.norm_ref, f32[8,1024]{1,0:T(8,128)S(1)} %get-tuple-element.33.terms_ref.refs_5_, ...), custom_call_target="tpu_custom_call" | custom-call | flops 402653184 | tf_op jit(solution)/shard_map/pallas_call | solution.py:377
  59.6 1.6 %collective-permute-start.22 = (f32[48,128]{1,0:T(8,128)S(1)}, f32[48,128]{1,0:T(8,128)S(1)}, u32[]{:S(2)}, u32[]{:S(2)}) collective-permute-start(f32[48,128]{1,0:T(8,128)S(1)} %get-tuple-element.51.tiles_ref), channel_id=1, source_target_pairs={{0,28},{4,8},{8,4},{12,16},{16,12},{20,24},{24,20},{28,0},{1,29},{... | collective-permute-start | bytes 73736 | tf_op jit(solution)/shard_map/ppermute | solution.py:457
  61.2 1.2 %collective-permute-start.21 = (f32[136,128]{1,0:T(8,128)S(1)}, f32[136,128]{1,0:T(8,128)S(1)}, u32[]{:S(2)}, u32[]{:S(2)}) collective-permute-start(f32[136,128]{1,0:T(8,128)S(1)} %slice_add_fusion), channel_id=1, source_target_pairs={{0,24},{4,28},{8,16},{12,20},{16,8},{20,12},{24,0},{28,4},{1,25},{... | collective-permute-start | bytes 208904 | tf_op jit(solution)/shard_map/ppermute | solution.py:397
  62.5 0.8 %collective-permute-start.19 = (f32[136,128]{1,0:T(8,128)S(1)}, f32[136,128]{1,0:T(8,128)S(1)}, u32[]{:S(2)}, u32[]{:S(2)}) collective-permute-start(f32[136,128]{1,0:T(8,128)S(1)} %slice_add_fusion), channel_id=1, source_target_pairs={{0,16},{4,20},{8,24},{12,28},{16,0},{20,4},{24,8},{28,12},{1,17},{... | collective-permute-start | bytes 208904 | tf_op jit(solution)/shard_map/ppermute | solution.py:397
  63.3 1.5 %collective-permute-start.20 = (f32[136,128]{1,0:T(8,128)S(1)}, f32[136,128]{1,0:T(8,128)S(1)}, u32[]{:S(2)}, u32[]{:S(2)}) collective-permute-start(f32[136,128]{1,0:T(8,128)S(1)} %slice_add_fusion), channel_id=1, source_target_pairs={{0,8},{4,12},{8,0},{12,4},{16,24},{20,28},{24,16},{28,20},{1,9},{5... | collective-permute-start | bytes 208904 | tf_op jit(solution)/shard_map/ppermute | solution.py:397
  64.8 1.4 %shard_map.66.before_ref = f32[24,1024]{1,0:T(8,128)S(1)} custom-call(s32[3,36]{1,0:T(4,128)S(1)} %get-tuple-element.46.plan_ref, f32[184,128]{1,0:T(8,128)S(1)} %get-tuple-element.54.own_ref, f32[184,128]{1,0:T(8,128)S(1)} %collective-permute-done.18.near_ref, f32[48,128]{1,0:T(8,128)S(1)} %collective-permute-done.22.away_ref, ...), custom_call_target="tpu_custom_call" | custom-call | flops 8053063680 | tf_op jit(solution)/shard_map/pallas_call | solution.py:377
  66.2 0.7 collective-permute-done.21
  66.8 0.7 collective-permute-done.19
  67.7 0.8 %shard_map.67.before_ref = f32[24,1024]{1,0:T(8,128)S(1)} custom-call(f32[136,128]{1,0:T(8,128)S(1)} %add_add_fusion.factor_ref.refs_8_, f32[24,1024]{1,0:T(8,128)S(1)} %shard_map.66.before_ref, f32[8,1024]{1,0:T(8,128)S(1)} %get-tuple-element.33.terms_ref.refs_5_, bf16[4,1024,1024]{2,1,0:T(8,128)(2,1)S(1)} %get-tuple-element.39.flip_ref), custom_call_target="tpu_custom_call" | custom-call | flops 201326592 | tf_op jit(solution)/shard_map/pallas_call | solution.py:377
  68.6 0.4 collective-permute-done.23.factor_ref
  69.0 0.8 %shard_map.68.refs_0_ = f32[24,1024]{1,0:T(8,128)S(1)} custom-call(f32[128,128]{1,0:T(8,128)S(1)} %collective-permute-done.23.factor_ref, f32[24,1024]{1,0:T(8,128)S(1)} %shard_map.67.before_ref, f32[8,1024]{1,0:T(8,128)S(1)} %get-tuple-element.33.terms_ref.refs_5_, bf16[4,1024,1024]{2,1,0:T(8,128)(2,1)S(1)} %get-tuple-element.39.flip_ref), custom_call_target="tpu_custom_call" | custom-call | flops 201326592 | tf_op jit(solution)/shard_map/pallas_call | solution.py:377
  69.8 2.7 %collective-permute-start.24 = (f32[24,1024]{1,0:T(8,128)S(1)}, f32[24,1024]{1,0:T(8,128)S(1)}, u32[]{:S(2)}, u32[]{:S(2)}) collective-permute-start(f32[24,1024]{1,0:T(8,128)S(1)} %shard_map.68.refs_0_), channel_id=1, source_target_pairs={{0,2},{1,3},{2,0},{3,1},{4,6},{5,7},{6,4},{7,5},{8,10},{9,11},{10,... | collective-permute-start | bytes 294920 | tf_op jit(solution)/shard_map/ppermute | solution.py:397
  72.5 0.4 collective-permute-start.25
  72.8 1.7 %collective-permute-start.26 = (f32[24,1024]{1,0:T(8,128)S(1)}, f32[24,1024]{1,0:T(8,128)S(1)}, u32[]{:S(2)}, u32[]{:S(2)}) collective-permute-start(f32[24,1024]{1,0:T(8,128)S(1)} %shard_map.68.refs_0_), channel_id=1, source_target_pairs={{0,3},{1,2},{2,1},{3,0},{4,7},{5,6},{6,5},{7,4},{8,11},{9,10},{10,... | collective-permute-start | bytes 294920 | tf_op jit(solution)/shard_map/ppermute | solution.py:397
  74.5 3.2 %collective-permute-done.24.refs_1_ = f32[24,1024]{1,0:T(8,128)S(1)} collective-permute-done((f32[24,1024]{1,0:T(8,128)S(1)}, f32[24,1024]{1,0:T(8,128)S(1)}, u32[]{:S(2)}, u32[]{:S(2)}) %collective-permute-start.24) | collective-permute-done | bytes 98336 | tf_op jit(solution)/shard_map/ppermute | solution.py:397
  77.8 3.9 %collective-permute-done.26.refs_3_ = f32[24,1024]{1,0:T(8,128)S(1)} collective-permute-done((f32[24,1024]{1,0:T(8,128)S(1)}, f32[24,1024]{1,0:T(8,128)S(1)}, u32[]{:S(2)}, u32[]{:S(2)}) %collective-permute-start.26) | collective-permute-done | bytes 98336 | tf_op jit(solution)/shard_map/ppermute | solution.py:397
  81.7 0.9 %shard_map.69 = f32[24,1024]{1,0:T(8,128)} custom-call(f32[24,1024]{1,0:T(8,128)S(1)} %shard_map.68.refs_0_, f32[24,1024]{1,0:T(8,128)S(1)} %collective-permute-done.24.refs_1_, f32[24,1024]{1,0:T(8,128)S(1)} %collective-permute-done.25.refs_2_, f32[24,1024]{1,0:T(8,128)S(1)} %collective-permute-done.26.refs_3_, f32[24,1024]{1,0:T(8,128)S(1)} %bitcast.14, ...), custom_call_target="tpu_custom_call" | custom-call | tf_op jit(solution)/shard_map/pallas_call | solution.py:377
  (44 shorter events, 1.6 us)
Async XLA Ops:
  1.1 0.7 copy-start.1
  8.4 4.9 %collective-permute-start = (f32[200,128]{1,0:T(8,128)S(1)}, f32[200,128]{1,0:T(8,128)S(1)}, u32[]{:S(2)}, u32[]{:S(2)}) collective-permute-start(f32[200,128]{1,0:T(8,128)S(1)} %get-tuple-element.32.own_ref), channel_id=1, source_target_pairs={{0,4},{4,0},{8,12},{12,8},{16,20},{20,16},{24,28},{28,24},{1,5},{5... | collective-permute-start | bytes 307208 | tf_op jit(solution)/shard_map/ppermute | solution.py:456
  9.0 7.9 %collective-permute-start.4 = (f32[64,128]{1,0:T(8,128)S(1)}, f32[64,128]{1,0:T(8,128)S(1)}, u32[]{:S(2)}, u32[]{:S(2)}) collective-permute-start(f32[64,128]{1,0:T(8,128)S(1)} %slice.40), channel_id=1, source_target_pairs={{0,28},{4,8},{8,4},{12,16},{16,12},{20,24},{24,20},{28,0},{1,29},{... | collective-permute-start | bytes 98312 | tf_op jit(solution)/shard_map/ppermute | solution.py:457
  13.3 6.3 %collective-permute-start.3 = (f32[136,128]{1,0:T(8,128)S(1)}, f32[136,128]{1,0:T(8,128)S(1)}, u32[]{:S(2)}, u32[]{:S(2)}) collective-permute-start(f32[136,128]{1,0:T(8,128)S(1)} %maximum_add_fusion), channel_id=1, source_target_pairs={{0,24},{4,28},{8,16},{12,20},{16,8},{20,12},{24,0},{28,4},{1,25},{... | collective-permute-start | bytes 208904 | tf_op jit(solution)/shard_map/ppermute | solution.py:397
  13.9 5.7 %collective-permute-start.1 = (f32[136,128]{1,0:T(8,128)S(1)}, f32[136,128]{1,0:T(8,128)S(1)}, u32[]{:S(2)}, u32[]{:S(2)}) collective-permute-start(f32[136,128]{1,0:T(8,128)S(1)} %maximum_add_fusion), channel_id=1, source_target_pairs={{0,16},{4,20},{8,24},{12,28},{16,0},{20,4},{24,8},{28,12},{1,17},{... | collective-permute-start | bytes 208904 | tf_op jit(solution)/shard_map/ppermute | solution.py:397
  14.3 5.4 %collective-permute-start.2 = (f32[136,128]{1,0:T(8,128)S(1)}, f32[136,128]{1,0:T(8,128)S(1)}, u32[]{:S(2)}, u32[]{:S(2)}) collective-permute-start(f32[136,128]{1,0:T(8,128)S(1)} %maximum_add_fusion), channel_id=1, source_target_pairs={{0,8},{4,12},{8,0},{12,4},{16,24},{20,28},{24,16},{28,20},{1,9},{5... | collective-permute-start | bytes 208904 | tf_op jit(solution)/shard_map/ppermute | solution.py:397
  19.7 1.3 %collective-permute-start.5 = (f32[128,128]{1,0:T(8,128)S(1)}, f32[128,128]{1,0:T(8,128)S(1)}, u32[]{:S(2)}, u32[]{:S(2)}) collective-permute-start(f32[128,128]{1,0:T(8,128)S(1)} %slice.48), channel_id=1, source_target_pairs={{0,4},{4,0},{8,12},{12,8},{16,20},{20,16},{24,28},{28,24},{1,5},{5... | collective-permute-start | bytes 196616 | tf_op jit(solution)/shard_map/ppermute | solution.py:484
  19.8 15.5 %copy-start = (f32[8,3,1024]{2,0,1:T(8,128)S(1)}, f32[8,3,1024]{2,0,1:T(8,128)}, u32[]{:S(2)}) copy-start(f32[8,3,1024]{2,0,1:T(8,128)} %param.5) | copy-start | bytes 294916
  21.9 6.7 %collective-permute-start.6 = (f32[24,1024]{1,0:T(8,128)S(1)}, f32[24,1024]{1,0:T(8,128)S(1)}, u32[]{:S(2)}, u32[]{:S(2)}) collective-permute-start(f32[24,1024]{1,0:T(8,128)S(1)} %shard_map.58.refs_0_), channel_id=1, source_target_pairs={{0,2},{1,3},{2,0},{3,1},{4,6},{5,7},{6,4},{7,5},{8,10},{9,11},{10,... | collective-permute-start | bytes 294920 | tf_op jit(solution)/shard_map/ppermute | solution.py:397
  24.7 7.0 %collective-permute-start.7 = (f32[24,1024]{1,0:T(8,128)S(1)}, f32[24,1024]{1,0:T(8,128)S(1)}, u32[]{:S(2)}, u32[]{:S(2)}) collective-permute-start(f32[24,1024]{1,0:T(8,128)S(1)} %shard_map.58.refs_0_), channel_id=1, source_target_pairs={{0,1},{1,0},{2,3},{3,2},{4,5},{5,4},{6,7},{7,6},{8,9},{9,8},{10,11... | collective-permute-start | bytes 294920 | tf_op jit(solution)/shard_map/ppermute | solution.py:397
  28.5 6.8 %collective-permute-start.8 = (f32[24,1024]{1,0:T(8,128)S(1)}, f32[24,1024]{1,0:T(8,128)S(1)}, u32[]{:S(2)}, u32[]{:S(2)}) collective-permute-start(f32[24,1024]{1,0:T(8,128)S(1)} %shard_map.58.refs_0_), channel_id=1, source_target_pairs={{0,3},{1,2},{2,1},{3,0},{4,7},{5,6},{6,5},{7,4},{8,11},{9,10},{10,... | collective-permute-start | bytes 294920 | tf_op jit(solution)/shard_map/ppermute | solution.py:397
  36.9 1.4 %collective-permute-start.9 = (f32[184,128]{1,0:T(8,128)S(1)}, f32[184,128]{1,0:T(8,128)S(1)}, u32[]{:S(2)}, u32[]{:S(2)}) collective-permute-start(f32[184,128]{1,0:T(8,128)S(1)} %get-tuple-element.45.own_ref), channel_id=1, source_target_pairs={{0,4},{4,0},{8,12},{12,8},{16,20},{20,16},{24,28},{28,24},{1,5},{5... | collective-permute-start | bytes 282632 | tf_op jit(solution)/shard_map/ppermute | solution.py:456
  37.0 4.9 %collective-permute-start.13 = (f32[48,128]{1,0:T(8,128)S(1)}, f32[48,128]{1,0:T(8,128)S(1)}, u32[]{:S(2)}, u32[]{:S(2)}) collective-permute-start(f32[48,128]{1,0:T(8,128)S(1)} %get-tuple-element.41.tiles_ref), channel_id=1, source_target_pairs={{0,28},{4,8},{8,4},{12,16},{16,12},{20,24},{24,20},{28,0},{1,29},{... | collective-permute-start | bytes 73736 | tf_op jit(solution)/shard_map/ppermute | solution.py:457
  38.3 5.3 %collective-permute-start.12 = (f32[136,128]{1,0:T(8,128)S(1)}, f32[136,128]{1,0:T(8,128)S(1)}, u32[]{:S(2)}, u32[]{:S(2)}) collective-permute-start(f32[136,128]{1,0:T(8,128)S(1)} %slice_add_fusion.1), channel_id=1, source_target_pairs={{0,24},{4,28},{8,16},{12,20},{16,8},{20,12},{24,0},{28,4},{1,25},{... | collective-permute-start | bytes 208904 | tf_op jit(solution)/shard_map/ppermute | solution.py:397
  38.5 6.4 %collective-permute-start.10 = (f32[136,128]{1,0:T(8,128)S(1)}, f32[136,128]{1,0:T(8,128)S(1)}, u32[]{:S(2)}, u32[]{:S(2)}) collective-permute-start(f32[136,128]{1,0:T(8,128)S(1)} %slice_add_fusion.1), channel_id=1, source_target_pairs={{0,16},{4,20},{8,24},{12,28},{16,0},{20,4},{24,8},{28,12},{1,17},{... | collective-permute-start | bytes 208904 | tf_op jit(solution)/shard_map/ppermute | solution.py:397
  40.7 4.3 %collective-permute-start.11 = (f32[136,128]{1,0:T(8,128)S(1)}, f32[136,128]{1,0:T(8,128)S(1)}, u32[]{:S(2)}, u32[]{:S(2)}) collective-permute-start(f32[136,128]{1,0:T(8,128)S(1)} %slice_add_fusion.1), channel_id=1, source_target_pairs={{0,8},{4,12},{8,0},{12,4},{16,24},{20,28},{24,16},{28,20},{1,9},{5... | collective-permute-start | bytes 208904 | tf_op jit(solution)/shard_map/ppermute | solution.py:397
  45.0 1.3 %collective-permute-start.14 = (f32[128,128]{1,0:T(8,128)S(1)}, f32[128,128]{1,0:T(8,128)S(1)}, u32[]{:S(2)}, u32[]{:S(2)}) collective-permute-start(f32[128,128]{1,0:T(8,128)S(1)} %slice.50), channel_id=1, source_target_pairs={{0,4},{4,0},{8,12},{12,8},{16,20},{20,16},{24,28},{28,24},{1,5},{5... | collective-permute-start | bytes 196616 | tf_op jit(solution)/shard_map/ppermute | solution.py:484
  47.2 9.6 %collective-permute-start.15 = (f32[24,1024]{1,0:T(8,128)S(1)}, f32[24,1024]{1,0:T(8,128)S(1)}, u32[]{:S(2)}, u32[]{:S(2)}) collective-permute-start(f32[24,1024]{1,0:T(8,128)S(1)} %shard_map.63.refs_0_), channel_id=1, source_target_pairs={{0,2},{1,3},{2,0},{3,1},{4,6},{5,7},{6,4},{7,5},{8,10},{9,11},{10,... | collective-permute-start | bytes 294920 | tf_op jit(solution)/shard_map/ppermute | solution.py:397
  49.1 8.7 %collective-permute-start.16 = (f32[24,1024]{1,0:T(8,128)S(1)}, f32[24,1024]{1,0:T(8,128)S(1)}, u32[]{:S(2)}, u32[]{:S(2)}) collective-permute-start(f32[24,1024]{1,0:T(8,128)S(1)} %shard_map.63.refs_0_), channel_id=1, source_target_pairs={{0,1},{1,0},{2,3},{3,2},{4,5},{5,4},{6,7},{7,6},{8,9},{9,8},{10,11... | collective-permute-start | bytes 294920 | tf_op jit(solution)/shard_map/ppermute | solution.py:397
  49.6 8.2 %collective-permute-start.17 = (f32[24,1024]{1,0:T(8,128)S(1)}, f32[24,1024]{1,0:T(8,128)S(1)}, u32[]{:S(2)}, u32[]{:S(2)}) collective-permute-start(f32[24,1024]{1,0:T(8,128)S(1)} %shard_map.63.refs_0_), channel_id=1, source_target_pairs={{0,3},{1,2},{2,1},{3,0},{4,7},{5,6},{6,5},{7,4},{8,11},{9,10},{10,... | collective-permute-start | bytes 294920 | tf_op jit(solution)/shard_map/ppermute | solution.py:397
  59.5 1.7 %collective-permute-start.18 = (f32[184,128]{1,0:T(8,128)S(1)}, f32[184,128]{1,0:T(8,128)S(1)}, u32[]{:S(2)}, u32[]{:S(2)}) collective-permute-start(f32[184,128]{1,0:T(8,128)S(1)} %get-tuple-element.54.own_ref), channel_id=1, source_target_pairs={{0,4},{4,0},{8,12},{12,8},{16,20},{20,16},{24,28},{28,24},{1,5},{5... | collective-permute-start | bytes 282632 | tf_op jit(solution)/shard_map/ppermute | solution.py:456
  59.6 5.2 %collective-permute-start.22 = (f32[48,128]{1,0:T(8,128)S(1)}, f32[48,128]{1,0:T(8,128)S(1)}, u32[]{:S(2)}, u32[]{:S(2)}) collective-permute-start(f32[48,128]{1,0:T(8,128)S(1)} %get-tuple-element.51.tiles_ref), channel_id=1, source_target_pairs={{0,28},{4,8},{8,4},{12,16},{16,12},{20,24},{24,20},{28,0},{1,29},{... | collective-permute-start | bytes 73736 | tf_op jit(solution)/shard_map/ppermute | solution.py:457
  61.2 5.6 %collective-permute-start.21 = (f32[136,128]{1,0:T(8,128)S(1)}, f32[136,128]{1,0:T(8,128)S(1)}, u32[]{:S(2)}, u32[]{:S(2)}) collective-permute-start(f32[136,128]{1,0:T(8,128)S(1)} %slice_add_fusion), channel_id=1, source_target_pairs={{0,24},{4,28},{8,16},{12,20},{16,8},{20,12},{24,0},{28,4},{1,25},{... | collective-permute-start | bytes 208904 | tf_op jit(solution)/shard_map/ppermute | solution.py:397
  62.5 5.1 %collective-permute-start.19 = (f32[136,128]{1,0:T(8,128)S(1)}, f32[136,128]{1,0:T(8,128)S(1)}, u32[]{:S(2)}, u32[]{:S(2)}) collective-permute-start(f32[136,128]{1,0:T(8,128)S(1)} %slice_add_fusion), channel_id=1, source_target_pairs={{0,16},{4,20},{8,24},{12,28},{16,0},{20,4},{24,8},{28,12},{1,17},{... | collective-permute-start | bytes 208904 | tf_op jit(solution)/shard_map/ppermute | solution.py:397
  63.3 4.3 %collective-permute-start.20 = (f32[136,128]{1,0:T(8,128)S(1)}, f32[136,128]{1,0:T(8,128)S(1)}, u32[]{:S(2)}, u32[]{:S(2)}) collective-permute-start(f32[136,128]{1,0:T(8,128)S(1)} %slice_add_fusion), channel_id=1, source_target_pairs={{0,8},{4,12},{8,0},{12,4},{16,24},{20,28},{24,16},{28,20},{1,9},{5... | collective-permute-start | bytes 208904 | tf_op jit(solution)/shard_map/ppermute | solution.py:397
  67.7 1.3 %collective-permute-start.23 = (f32[128,128]{1,0:T(8,128)S(1)}, f32[128,128]{1,0:T(8,128)S(1)}, u32[]{:S(2)}, u32[]{:S(2)}) collective-permute-start(f32[128,128]{1,0:T(8,128)S(1)} %slice.52), channel_id=1, source_target_pairs={{0,4},{4,0},{8,12},{12,8},{16,20},{20,16},{24,28},{28,24},{1,5},{5... | collective-permute-start | bytes 196616 | tf_op jit(solution)/shard_map/ppermute | solution.py:484
  69.8 7.9 %collective-permute-start.24 = (f32[24,1024]{1,0:T(8,128)S(1)}, f32[24,1024]{1,0:T(8,128)S(1)}, u32[]{:S(2)}, u32[]{:S(2)}) collective-permute-start(f32[24,1024]{1,0:T(8,128)S(1)} %shard_map.68.refs_0_), channel_id=1, source_target_pairs={{0,2},{1,3},{2,0},{3,1},{4,6},{5,7},{6,4},{7,5},{8,10},{9,11},{10,... | collective-permute-start | bytes 294920 | tf_op jit(solution)/shard_map/ppermute | solution.py:397
  72.5 5.3 %collective-permute-start.25 = (f32[24,1024]{1,0:T(8,128)S(1)}, f32[24,1024]{1,0:T(8,128)S(1)}, u32[]{:S(2)}, u32[]{:S(2)}) collective-permute-start(f32[24,1024]{1,0:T(8,128)S(1)} %shard_map.68.refs_0_), channel_id=1, source_target_pairs={{0,1},{1,0},{2,3},{3,2},{4,5},{5,4},{6,7},{7,6},{8,9},{9,8},{10,11... | collective-permute-start | bytes 294920 | tf_op jit(solution)/shard_map/ppermute | solution.py:397
  72.8 8.9 %collective-permute-start.26 = (f32[24,1024]{1,0:T(8,128)S(1)}, f32[24,1024]{1,0:T(8,128)S(1)}, u32[]{:S(2)}, u32[]{:S(2)}) collective-permute-start(f32[24,1024]{1,0:T(8,128)S(1)} %shard_map.68.refs_0_), channel_id=1, source_target_pairs={{0,3},{1,2},{2,1},{3,0},{4,7},{5,6},{6,5},{7,4},{8,11},{9,10},{10,... | collective-permute-start | bytes 294920 | tf_op jit(solution)/shard_map/ppermute | solution.py:397

commit v6 on v5

--- a/solution.py
+++ b/solution.py
@@ -341,13 +341,8 @@
     forward(rows_ref[...], table_ref, terms_ref[...], mine_ref, rest_ref)
 
 
-def final_kernel(parts, *refs):
-    ins, (noise_ref, one_ref, two_ref, first_ref, second_ref, out_ref) = refs[:parts], refs[parts:]
-    total = ins[0][...]
-    for ref in ins[1:]:
-        total = total + ref[...]
+def series_kernel(noise_ref, one_ref, two_ref, first_ref, second_ref, base_ref, scale_ref):
     u0, u1, u2 = noise_ref[...], one_ref[...], two_ref[...]
-    u3 = u2 + total
     first = jnp.sum(first_ref[-8:, :], axis=1, keepdims=True)
     second = jnp.sum(second_ref[-8:, :], axis=1, keepdims=True)
     ratio = jnp.max(second / (first + EPSILON), axis=0, keepdims=True)
@@ -364,11 +359,22 @@
         coeffs.append(acc * (2.0 / nodes) * (0.5 if k == 0 else 1.0))
     p = 2.0 / (high - low)
     q = (high + low) / (high - low)
-    v0, v1, v2 = p * u1 - q * u0, p * u2 - q * u1, p * u3 - q * u2
+    v0, v1, v2 = p * u1 - q * u0, p * u2 - q * u1, p * u2 - q * u2
     t2 = 2.0 * (p * v1 - q * v0) - u0
     m2 = 2.0 * (p * v2 - q * v1) - u1
     t3 = 2.0 * (p * m2 - q * t2) - v0
-    out_ref[...] = coeffs[0] * u0 + coeffs[1] * v0 + coeffs[2] * t2 + coeffs[3] * t3
+    base_ref[...] = coeffs[0] * u0 + coeffs[1] * v0 + coeffs[2] * t2 + coeffs[3] * t3
+    scale_ref[0:8, :] = jnp.broadcast_to(p, (8, TILE))
+    scale_ref[8:16, :] = jnp.broadcast_to(coeffs[3], (8, TILE))
+
+
+def final_kernel(parts, *refs):
+    ins, (base_ref, scale_ref, out_ref) = refs[:parts], refs[parts:]
+    total = ins[0][...]
+    for ref in ins[1:]:
+        total = total + ref[...]
+    p, last = scale_ref[0:1, 0:1], scale_ref[8:9, 0:1]
+    out_ref[...] = base_ref[...] + last * (2.0 * p * (2.0 * p * (p * total)))
 
 
 def call(kernel, outs, args, scratch=(), smem_in=0, smem_out=(), flops=0, space=pltpu.VMEM):
@@ -507,10 +513,17 @@
                 flops=far_flops,
             )
             images.append(rows)
+    series, scale = call(
+        series_kernel,
+        [rows_shape, ((16, TILE), F32)],
+        (noise_rows, *images, *norms[1:]),
+        flops=5 * far_flops,
+    )
     out = call(
         functools.partial(final_kernel, len(sums)),
         [rows_shape],
-        (*sums, noise_rows, *images, *norms[1:]),
+        (*sums, series, scale),
+        flops=1,
     )[0]
     return jnp.transpose(out.reshape(3, vectors, particles), (1, 0, 2))
 

time: 82.6 us -> 82.7 us (level)
    pallas_call x15 -> x16, Pallas kernels: 21.4 us -> 21.7 us  [call(): pl.pallas_call(kernel, out_shape=[jax.ShapeDtypeStruct(*o) for o in outs]...]
  transfers between devices with their start and end apart: 27 -> 27, of which waited for: 16 -> 15; matrix products, arithmetic and copies ran while one was open for 1% -> 1% of each run, Pallas kernels for 10% -> 10%
where the time goes in v6:
time: 82.7 us; the launch traced here: 82.5 us
  starting transfers between devices  32.1 us (39%)
  waiting for transfers between devices  25.8 us (31%)
  Pallas kernels  21.7 us (26%)
  other arithmetic  1.88 us (2%)
    ppermute x18, starting transfers between devices, exchange(): lax.ppermute(x, axis, [(i, i ^ d * bit) for i in range(size)])  25.9 us
    ppermute x18, waiting for transfers between devices, exchange(): lax.ppermute(x, axis, [(i, i ^ d * bit) for i in range(size)])  23.5 us
    pallas_call x16, Pallas kernels, call(): pl.pallas_call(kernel, out_shape=[jax.ShapeDtypeStruct(*o) for o in outs]...  21.7 us
    ppermute x3, starting transfers between devices, body(): away = lax.ppermute(rest[base:] if step == 0 else own, 'space', third)  5.19 us
  transfers between devices with their start and end apart: 27, of which 15 were waited for; matrix products, arithmetic and copies ran while one was open for 1% of the time, Pallas kernels for 10%

profile of v6, /device:TPU:0, one launch (start us, length us, event | category | flops | bytes accessed | tf_op | source)
XLA Modules:
  0.0 82.5 jit_solution(8522142905782364437)
XLA Ops:
  0.0 0.9 %pad_maximum_fusion.stack_ref.pos_ref = f32[27,1024]{1,0:T(8,128)S(1)} fusion(f32[3,1024]{1,0:T(4,128)} %param.6, f32[24,1024]{1,0:T(8,128)} %bitcast.12), kind=kLoop, calls=%fused_computation | loop fusion | flops 27648 | bytes 221184 | tf_op jit(solution)/shard_map/concatenate | solution.py:429
  1.1 0.7 copy-done.1
  1.8 6.6 %shard_map.55 = (bf16[4,1024,1024]{2,1,0:T(8,128)(2,1)S(1)}, bf16[4,1024,1024]{2,1,0:T(8,128)(2,1)S(1)}, f32[8,1024]{1,0:T(8,128)S(1)}, f32[128,128]{1,0:T(8,128)S(1)}, f32[200,128]{1,0:T(8,128)S(1)}) custom-call(s32[3,1024]{1,0:T(4,128)S(1)} %copy-done.1, f32[2,128]{1,0:T(2,128)S(1)} %broadcast_in_dim.14.place_ref, ...), custom_call_target="tpu_custom_call" | custom-call | flops 1610612736 | tf_op jit(solution)/shard_map/pallas_call | solution.py:383
  8.4 0.5 collective-permute-start
  9.0 3.6 %collective-permute-start.4 = (f32[64,128]{1,0:T(8,128)S(1)}, f32[64,128]{1,0:T(8,128)S(1)}, u32[]{:S(2)}, u32[]{:S(2)}) collective-permute-start(f32[64,128]{1,0:T(8,128)S(1)} %slice.40), channel_id=1, source_target_pairs={{0,28},{4,8},{8,4},{12,16},{16,12},{20,24},{24,20},{28,0},{1,29},{... | collective-permute-start | bytes 98312 | tf_op jit(solution)/shard_map/ppermute | solution.py:463
  12.5 0.8 fusion.4.live_ref
  13.3 0.6 collective-permute-start.3
  13.9 0.4 collective-permute-start.1
  14.3 2.6 %collective-permute-start.2 = (f32[136,128]{1,0:T(8,128)S(1)}, f32[136,128]{1,0:T(8,128)S(1)}, u32[]{:S(2)}, u32[]{:S(2)}) collective-permute-start(f32[136,128]{1,0:T(8,128)S(1)} %maximum_add_fusion), channel_id=1, source_target_pairs={{0,8},{4,12},{8,0},{12,4},{16,24},{20,28},{24,16},{28,20},{1,9},{5... | collective-permute-start | bytes 208904 | tf_op jit(solution)/shard_map/ppermute | solution.py:403
  16.9 3.0 %shard_map.56 = (bf16[36,256,768]{2,1,0:T(8,128)(2,1)S(1)}, s32[3,36]{1,0:T(4,128)S(1)}, f32[24,1024]{1,0:T(8,128)S(1)}) custom-call(s32[8,8]{1,0:T(8,128)S(1)} %fusion.4.live_ref, f32[27,1024]{1,0:T(8,128)S(1)} %pad_maximum_fusion.stack_ref.pos_ref, f32[200,128]{1,0:T(8,128)S(1)} %get-tuple-element.34.own_ref, ...), custom_call_target="tpu_custom_call" | custom-call | flops 8053063680 | tf_op jit(solution)/shard_map/pallas_call | solution.py:383
  20.0 0.8 %shard_map.57.before_ref = f32[24,1024]{1,0:T(8,128)S(1)} custom-call(f32[136,128]{1,0:T(8,128)S(1)} %add_add_fusion.2.factor_ref, f32[24,1024]{1,0:T(8,128)S(1)} %get-tuple-element.40.before_ref, f32[8,1024]{1,0:T(8,128)S(1)} %get-tuple-element.35.terms_ref.refs_5_, bf16[4,1024,1024]{2,1,0:T(8,128)(2,1)S(1)} %get-tuple-element.41.flip_ref), custom_call_target="tpu_custom_call" | custom-call | flops 201326592 | tf_op jit(solution)/shard_map/pallas_call | solution.py:383
  20.9 0.4 collective-permute-done.5.factor_ref
  21.3 0.8 %shard_map.58.refs_0_ = f32[24,1024]{1,0:T(8,128)S(1)} custom-call(f32[128,128]{1,0:T(8,128)S(1)} %collective-permute-done.5.factor_ref, f32[24,1024]{1,0:T(8,128)S(1)} %shard_map.57.before_ref, f32[8,1024]{1,0:T(8,128)S(1)} %get-tuple-element.35.terms_ref.refs_5_, bf16[4,1024,1024]{2,1,0:T(8,128)(2,1)S(1)} %get-tuple-element.41.flip_ref), custom_call_target="tpu_custom_call" | custom-call | flops 201326592 | tf_op jit(solution)/shard_map/pallas_call | solution.py:383
  22.1 4.6 %collective-permute-start.6 = (f32[24,1024]{1,0:T(8,128)S(1)}, f32[24,1024]{1,0:T(8,128)S(1)}, u32[]{:S(2)}, u32[]{:S(2)}) collective-permute-start(f32[24,1024]{1,0:T(8,128)S(1)} %shard_map.58.refs_0_), channel_id=1, source_target_pairs={{0,2},{1,3},{2,0},{3,1},{4,6},{5,7},{6,4},{7,5},{8,10},{9,11},{10,... | collective-permute-start | bytes 294920 | tf_op jit(solution)/shard_map/ppermute | solution.py:403
  26.7 1.5 %collective-permute-start.8 = (f32[24,1024]{1,0:T(8,128)S(1)}, f32[24,1024]{1,0:T(8,128)S(1)}, u32[]{:S(2)}, u32[]{:S(2)}) collective-permute-start(f32[24,1024]{1,0:T(8,128)S(1)} %shard_map.58.refs_0_), channel_id=1, source_target_pairs={{0,3},{1,2},{2,1},{3,0},{4,7},{5,6},{6,5},{7,4},{8,11},{9,10},{10,... | collective-permute-start | bytes 294920 | tf_op jit(solution)/shard_map/ppermute | solution.py:403
  28.3 3.3 %collective-permute-done.6.refs_1_ = f32[24,1024]{1,0:T(8,128)S(1)} collective-permute-done((f32[24,1024]{1,0:T(8,128)S(1)}, f32[24,1024]{1,0:T(8,128)S(1)}, u32[]{:S(2)}, u32[]{:S(2)}) %collective-permute-start.6) | collective-permute-done | bytes 98336 | tf_op jit(solution)/shard_map/ppermute | solution.py:403
  31.6 3.9 %collective-permute-done.7.refs_2_ = f32[24,1024]{1,0:T(8,128)S(1)} collective-permute-done((f32[24,1024]{1,0:T(8,128)S(1)}, f32[24,1024]{1,0:T(8,128)S(1)}, u32[]{:S(2)}, u32[]{:S(2)}) %collective-permute-start.7) | collective-permute-done | bytes 98336 | tf_op jit(solution)/shard_map/ppermute | solution.py:403
  35.5 1.6 %shard_map.60 = (f32[128,128]{1,0:T(8,128)S(1)}, f32[184,128]{1,0:T(8,128)S(1)}) custom-call(f32[24,1024]{1,0:T(8,128)S(1)} %get-tuple-element.42.rows_ref.refs_4_.one_ref, f32[48,128]{1,0:T(8,128)S(1)} %get-tuple-element.43.tiles_ref, f32[8,128]{1,0:T(8,128)S(1)} %get-tuple-element.44.norm_ref, f32[8,1024]{1,0:T(8,128)S(1)} %get-tuple-element.35.terms_ref.refs_5_, ...), custom_call_target="tpu_custom_call" | custom-call | flops 402653184 | tf_op jit(solution)/shard_map/pallas_call | solution.py:383
  37.2 1.2 %collective-permute-done.9.near_ref = f32[184,128]{1,0:T(8,128)S(1)} collective-permute-done((f32[184,128]{1,0:T(8,128)S(1)}, f32[184,128]{1,0:T(8,128)S(1)}, u32[]{:S(2)}, u32[]{:S(2)}) %collective-permute-start.9) | collective-permute-done | bytes 94240 | tf_op jit(solution)/shard_map/ppermute | solution.py:462
  38.5 2.3 %collective-permute-start.10 = (f32[136,128]{1,0:T(8,128)S(1)}, f32[136,128]{1,0:T(8,128)S(1)}, u32[]{:S(2)}, u32[]{:S(2)}) collective-permute-start(f32[136,128]{1,0:T(8,128)S(1)} %slice_add_fusion.1), channel_id=1, source_target_pairs={{0,16},{4,20},{8,24},{12,28},{16,0},{20,4},{24,8},{28,12},{1,17},{... | collective-permute-start | bytes 208904 | tf_op jit(solution)/shard_map/ppermute | solution.py:403
  40.8 1.2 %collective-permute-start.11 = (f32[136,128]{1,0:T(8,128)S(1)}, f32[136,128]{1,0:T(8,128)S(1)}, u32[]{:S(2)}, u32[]{:S(2)}) collective-permute-start(f32[136,128]{1,0:T(8,128)S(1)} %slice_add_fusion.1), channel_id=1, source_target_pairs={{0,8},{4,12},{8,0},{12,4},{16,24},{20,28},{24,16},{28,20},{1,9},{5... | collective-permute-start | bytes 208904 | tf_op jit(solution)/shard_map/ppermute | solution.py:403
  42.0 1.5 %shard_map.61.before_ref = f32[24,1024]{1,0:T(8,128)S(1)} custom-call(s32[3,36]{1,0:T(4,128)S(1)} %get-tuple-element.48.plan_ref, f32[184,128]{1,0:T(8,128)S(1)} %get-tuple-element.47.own_ref, f32[184,128]{1,0:T(8,128)S(1)} %collective-permute-done.9.near_ref, f32[48,128]{1,0:T(8,128)S(1)} %collective-permute-done.13.away_ref, ...), custom_call_target="tpu_custom_call" | custom-call | flops 8053063680 | tf_op jit(solution)/shard_map/pallas_call | solution.py:383
  43.7 1.3 %collective-permute-done.10 = f32[136,128]{1,0:T(8,128)S(1)} collective-permute-done((f32[136,128]{1,0:T(8,128)S(1)}, f32[136,128]{1,0:T(8,128)S(1)}, u32[]{:S(2)}, u32[]{:S(2)}) %collective-permute-start.10) | collective-permute-done | bytes 69664 | tf_op jit(solution)/shard_map/ppermute | solution.py:403
  45.3 0.8 %shard_map.62.before_ref = f32[24,1024]{1,0:T(8,128)S(1)} custom-call(f32[136,128]{1,0:T(8,128)S(1)} %add_add_fusion.1.factor_ref.first_ref, f32[24,1024]{1,0:T(8,128)S(1)} %shard_map.61.before_ref, f32[8,1024]{1,0:T(8,128)S(1)} %get-tuple-element.35.terms_ref.refs_5_, bf16[4,1024,1024]{2,1,0:T(8,128)(2,1)S(1)} %get-tuple-element.41.flip_ref), custom_call_target="tpu_custom_call" | custom-call | flops 201326592 | tf_op jit(solution)/shard_map/pallas_call | solution.py:383
  46.2 0.3 collective-permute-done.14.factor_ref
  46.5 0.8 %shard_map.63.refs_0_ = f32[24,1024]{1,0:T(8,128)S(1)} custom-call(f32[128,128]{1,0:T(8,128)S(1)} %collective-permute-done.14.factor_ref, f32[24,1024]{1,0:T(8,128)S(1)} %shard_map.62.before_ref, f32[8,1024]{1,0:T(8,128)S(1)} %get-tuple-element.35.terms_ref.refs_5_, bf16[4,1024,1024]{2,1,0:T(8,128)(2,1)S(1)} %get-tuple-element.41.flip_ref), custom_call_target="tpu_custom_call" | custom-call | flops 201326592 | tf_op jit(solution)/shard_map/pallas_call | solution.py:383
  47.3 1.9 %collective-permute-start.15 = (f32[24,1024]{1,0:T(8,128)S(1)}, f32[24,1024]{1,0:T(8,128)S(1)}, u32[]{:S(2)}, u32[]{:S(2)}) collective-permute-start(f32[24,1024]{1,0:T(8,128)S(1)} %shard_map.63.refs_0_), channel_id=1, source_target_pairs={{0,2},{1,3},{2,0},{3,1},{4,6},{5,7},{6,4},{7,5},{8,10},{9,11},{10,... | collective-permute-start | bytes 294920 | tf_op jit(solution)/shard_map/ppermute | solution.py:403
  49.2 1.1 %collective-permute-start.16 = (f32[24,1024]{1,0:T(8,128)S(1)}, f32[24,1024]{1,0:T(8,128)S(1)}, u32[]{:S(2)}, u32[]{:S(2)}) collective-permute-start(f32[24,1024]{1,0:T(8,128)S(1)} %shard_map.63.refs_0_), channel_id=1, source_target_pairs={{0,1},{1,0},{2,3},{3,2},{4,5},{5,4},{6,7},{7,6},{8,9},{9,8},{10,11... | collective-permute-start | bytes 294920 | tf_op jit(solution)/shard_map/ppermute | solution.py:403
  50.2 1.5 %collective-permute-start.17 = (f32[24,1024]{1,0:T(8,128)S(1)}, f32[24,1024]{1,0:T(8,128)S(1)}, u32[]{:S(2)}, u32[]{:S(2)}) collective-permute-start(f32[24,1024]{1,0:T(8,128)S(1)} %shard_map.63.refs_0_), channel_id=1, source_target_pairs={{0,3},{1,2},{2,1},{3,0},{4,7},{5,6},{6,5},{7,4},{8,11},{9,10},{10,... | collective-permute-start | bytes 294920 | tf_op jit(solution)/shard_map/ppermute | solution.py:403
  51.7 5.8 %collective-permute-done.15.refs_1_ = f32[24,1024]{1,0:T(8,128)S(1)} collective-permute-done((f32[24,1024]{1,0:T(8,128)S(1)}, f32[24,1024]{1,0:T(8,128)S(1)}, u32[]{:S(2)}, u32[]{:S(2)}) %collective-permute-start.15) | collective-permute-done | bytes 98336 | tf_op jit(solution)/shard_map/ppermute | solution.py:403
  57.8 1.6 %shard_map.65 = (f32[128,128]{1,0:T(8,128)S(1)}, f32[184,128]{1,0:T(8,128)S(1)}) custom-call(f32[24,1024]{1,0:T(8,128)S(1)} %get-tuple-element.52.rows_ref.two_ref, f32[48,128]{1,0:T(8,128)S(1)} %get-tuple-element.53.tiles_ref, f32[8,128]{1,0:T(8,128)S(1)} %get-tuple-element.54.norm_ref, f32[8,1024]{1,0:T(8,128)S(1)} %get-tuple-element.35.terms_ref.refs_5_, ...), custom_call_target="tpu_custom_call" | custom-call | flops 402653184 | tf_op jit(solution)/shard_map/pallas_call | solution.py:383
  59.5 1.6 %collective-permute-start.22 = (f32[48,128]{1,0:T(8,128)S(1)}, f32[48,128]{1,0:T(8,128)S(1)}, u32[]{:S(2)}, u32[]{:S(2)}) collective-permute-start(f32[48,128]{1,0:T(8,128)S(1)} %get-tuple-element.53.tiles_ref), channel_id=1, source_target_pairs={{0,28},{4,8},{8,4},{12,16},{16,12},{20,24},{24,20},{28,0},{1,29},{... | collective-permute-start | bytes 73736 | tf_op jit(solution)/shard_map/ppermute | solution.py:463
  61.0 1.3 %collective-permute-start.21 = (f32[136,128]{1,0:T(8,128)S(1)}, f32[136,128]{1,0:T(8,128)S(1)}, u32[]{:S(2)}, u32[]{:S(2)}) collective-permute-start(f32[136,128]{1,0:T(8,128)S(1)} %slice_add_fusion), channel_id=1, source_target_pairs={{0,24},{4,28},{8,16},{12,20},{16,8},{20,12},{24,0},{28,4},{1,25},{... | collective-permute-start | bytes 208904 | tf_op jit(solution)/shard_map/ppermute | solution.py:403
  62.3 1.2 %collective-permute-start.19 = (f32[136,128]{1,0:T(8,128)S(1)}, f32[136,128]{1,0:T(8,128)S(1)}, u32[]{:S(2)}, u32[]{:S(2)}) collective-permute-start(f32[136,128]{1,0:T(8,128)S(1)} %slice_add_fusion), channel_id=1, source_target_pairs={{0,16},{4,20},{8,24},{12,28},{16,0},{20,4},{24,8},{28,12},{1,17},{... | collective-permute-start | bytes 208904 | tf_op jit(solution)/shard_map/ppermute | solution.py:403
  63.5 1.1 %collective-permute-start.20 = (f32[136,128]{1,0:T(8,128)S(1)}, f32[136,128]{1,0:T(8,128)S(1)}, u32[]{:S(2)}, u32[]{:S(2)}) collective-permute-start(f32[136,128]{1,0:T(8,128)S(1)} %slice_add_fusion), channel_id=1, source_target_pairs={{0,8},{4,12},{8,0},{12,4},{16,24},{20,28},{24,16},{28,20},{1,9},{5... | collective-permute-start | bytes 208904 | tf_op jit(solution)/shard_map/ppermute | solution.py:403
  64.6 1.4 %shard_map.66.before_ref = f32[24,1024]{1,0:T(8,128)S(1)} custom-call(s32[3,36]{1,0:T(4,128)S(1)} %get-tuple-element.48.plan_ref, f32[184,128]{1,0:T(8,128)S(1)} %get-tuple-element.56.own_ref, f32[184,128]{1,0:T(8,128)S(1)} %collective-permute-done.18.near_ref, f32[48,128]{1,0:T(8,128)S(1)} %collective-permute-done.22.away_ref, ...), custom_call_target="tpu_custom_call" | custom-call | flops 8053063680 | tf_op jit(solution)/shard_map/pallas_call | solution.py:383
  66.0 0.6 collective-permute-done.21
  66.5 0.9 %collective-permute-done.19 = f32[136,128]{1,0:T(8,128)S(1)} collective-permute-done((f32[136,128]{1,0:T(8,128)S(1)}, f32[136,128]{1,0:T(8,128)S(1)}, u32[]{:S(2)}, u32[]{:S(2)}) %collective-permute-start.19) | collective-permute-done | bytes 69664 | tf_op jit(solution)/shard_map/ppermute | solution.py:403
  67.5 0.3 collective-permute-done.20
  67.9 0.8 %shard_map.67.before_ref = f32[24,1024]{1,0:T(8,128)S(1)} custom-call(f32[136,128]{1,0:T(8,128)S(1)} %add_add_fusion.factor_ref.second_ref, f32[24,1024]{1,0:T(8,128)S(1)} %shard_map.66.before_ref, f32[8,1024]{1,0:T(8,128)S(1)} %get-tuple-element.35.terms_ref.refs_5_, bf16[4,1024,1024]{2,1,0:T(8,128)(2,1)S(1)} %get-tuple-element.41.flip_ref), custom_call_target="tpu_custom_call" | custom-call | flops 201326592 | tf_op jit(solution)/shard_map/pallas_call | solution.py:383
  68.7 0.4 collective-permute-done.23.factor_ref
  69.1 0.8 %shard_map.68.refs_0_ = f32[24,1024]{1,0:T(8,128)S(1)} custom-call(f32[128,128]{1,0:T(8,128)S(1)} %collective-permute-done.23.factor_ref, f32[24,1024]{1,0:T(8,128)S(1)} %shard_map.67.before_ref, f32[8,1024]{1,0:T(8,128)S(1)} %get-tuple-element.35.terms_ref.refs_5_, bf16[4,1024,1024]{2,1,0:T(8,128)(2,1)S(1)} %get-tuple-element.41.flip_ref), custom_call_target="tpu_custom_call" | custom-call | flops 201326592 | tf_op jit(solution)/shard_map/pallas_call | solution.py:383
  70.0 3.1 %collective-permute-start.24 = (f32[24,1024]{1,0:T(8,128)S(1)}, f32[24,1024]{1,0:T(8,128)S(1)}, u32[]{:S(2)}, u32[]{:S(2)}) collective-permute-start(f32[24,1024]{1,0:T(8,128)S(1)} %shard_map.68.refs_0_), channel_id=1, source_target_pairs={{0,2},{1,3},{2,0},{3,1},{4,6},{5,7},{6,4},{7,5},{8,10},{9,11},{10,... | collective-permute-start | bytes 294920 | tf_op jit(solution)/shard_map/ppermute | solution.py:403
  73.1 1.5 %collective-permute-start.26 = (f32[24,1024]{1,0:T(8,128)S(1)}, f32[24,1024]{1,0:T(8,128)S(1)}, u32[]{:S(2)}, u32[]{:S(2)}) collective-permute-start(f32[24,1024]{1,0:T(8,128)S(1)} %shard_map.68.refs_0_), channel_id=1, source_target_pairs={{0,3},{1,2},{2,1},{3,0},{4,7},{5,6},{6,5},{7,4},{8,11},{9,10},{10,... | collective-permute-start | bytes 294920 | tf_op jit(solution)/shard_map/ppermute | solution.py:403
  74.6 0.2 shard_map.69
  74.9 3.9 %collective-permute-done.24.refs_1_ = f32[24,1024]{1,0:T(8,128)S(1)} collective-permute-done((f32[24,1024]{1,0:T(8,128)S(1)}, f32[24,1024]{1,0:T(8,128)S(1)}, u32[]{:S(2)}, u32[]{:S(2)}) %collective-permute-start.24) | collective-permute-done | bytes 98336 | tf_op jit(solution)/shard_map/ppermute | solution.py:403
  78.8 3.1 %collective-permute-done.26.refs_3_ = f32[24,1024]{1,0:T(8,128)S(1)} collective-permute-done((f32[24,1024]{1,0:T(8,128)S(1)}, f32[24,1024]{1,0:T(8,128)S(1)}, u32[]{:S(2)}, u32[]{:S(2)}) %collective-permute-start.26) | collective-permute-done | bytes 98336 | tf_op jit(solution)/shard_map/ppermute | solution.py:403
  81.8 0.7 shard_map.70
  (45 shorter events, 1.5 us)
Async XLA Ops:
  1.1 0.7 copy-start.1
  8.4 4.9 %collective-permute-start = (f32[200,128]{1,0:T(8,128)S(1)}, f32[200,128]{1,0:T(8,128)S(1)}, u32[]{:S(2)}, u32[]{:S(2)}) collective-permute-start(f32[200,128]{1,0:T(8,128)S(1)} %get-tuple-element.34.own_ref), channel_id=1, source_target_pairs={{0,4},{4,0},{8,12},{12,8},{16,20},{20,16},{24,28},{28,24},{1,5},{5... | collective-permute-start | bytes 307208 | tf_op jit(solution)/shard_map/ppermute | solution.py:462
  9.0 7.9 %collective-permute-start.4 = (f32[64,128]{1,0:T(8,128)S(1)}, f32[64,128]{1,0:T(8,128)S(1)}, u32[]{:S(2)}, u32[]{:S(2)}) collective-permute-start(f32[64,128]{1,0:T(8,128)S(1)} %slice.40), channel_id=1, source_target_pairs={{0,28},{4,8},{8,4},{12,16},{16,12},{20,24},{24,20},{28,0},{1,29},{... | collective-permute-start | bytes 98312 | tf_op jit(solution)/shard_map/ppermute | solution.py:463
  13.3 6.6 %collective-permute-start.3 = (f32[136,128]{1,0:T(8,128)S(1)}, f32[136,128]{1,0:T(8,128)S(1)}, u32[]{:S(2)}, u32[]{:S(2)}) collective-permute-start(f32[136,128]{1,0:T(8,128)S(1)} %maximum_add_fusion), channel_id=1, source_target_pairs={{0,24},{4,28},{8,16},{12,20},{16,8},{20,12},{24,0},{28,4},{1,25},{... | collective-permute-start | bytes 208904 | tf_op jit(solution)/shard_map/ppermute | solution.py:403
  13.9 6.0 %collective-permute-start.1 = (f32[136,128]{1,0:T(8,128)S(1)}, f32[136,128]{1,0:T(8,128)S(1)}, u32[]{:S(2)}, u32[]{:S(2)}) collective-permute-start(f32[136,128]{1,0:T(8,128)S(1)} %maximum_add_fusion), channel_id=1, source_target_pairs={{0,16},{4,20},{8,24},{12,28},{16,0},{20,4},{24,8},{28,12},{1,17},{... | collective-permute-start | bytes 208904 | tf_op jit(solution)/shard_map/ppermute | solution.py:403
  14.3 5.6 %collective-permute-start.2 = (f32[136,128]{1,0:T(8,128)S(1)}, f32[136,128]{1,0:T(8,128)S(1)}, u32[]{:S(2)}, u32[]{:S(2)}) collective-permute-start(f32[136,128]{1,0:T(8,128)S(1)} %maximum_add_fusion), channel_id=1, source_target_pairs={{0,8},{4,12},{8,0},{12,4},{16,24},{20,28},{24,16},{28,20},{1,9},{5... | collective-permute-start | bytes 208904 | tf_op jit(solution)/shard_map/ppermute | solution.py:403
  19.9 1.3 %collective-permute-start.5 = (f32[128,128]{1,0:T(8,128)S(1)}, f32[128,128]{1,0:T(8,128)S(1)}, u32[]{:S(2)}, u32[]{:S(2)}) collective-permute-start(f32[128,128]{1,0:T(8,128)S(1)} %slice.48), channel_id=1, source_target_pairs={{0,4},{4,0},{8,12},{12,8},{16,20},{20,16},{24,28},{28,24},{1,5},{5... | collective-permute-start | bytes 196616 | tf_op jit(solution)/shard_map/ppermute | solution.py:490
  20.0 15.4 %copy-start = (f32[8,3,1024]{2,0,1:T(8,128)S(1)}, f32[8,3,1024]{2,0,1:T(8,128)}, u32[]{:S(2)}) copy-start(f32[8,3,1024]{2,0,1:T(8,128)} %param.5) | copy-start | bytes 294916
  22.1 9.5 %collective-permute-start.6 = (f32[24,1024]{1,0:T(8,128)S(1)}, f32[24,1024]{1,0:T(8,128)S(1)}, u32[]{:S(2)}, u32[]{:S(2)}) collective-permute-start(f32[24,1024]{1,0:T(8,128)S(1)} %shard_map.58.refs_0_), channel_id=1, source_target_pairs={{0,2},{1,3},{2,0},{3,1},{4,6},{5,7},{6,4},{7,5},{8,10},{9,11},{10,... | collective-permute-start | bytes 294920 | tf_op jit(solution)/shard_map/ppermute | solution.py:403
  26.7 8.7 %collective-permute-start.7 = (f32[24,1024]{1,0:T(8,128)S(1)}, f32[24,1024]{1,0:T(8,128)S(1)}, u32[]{:S(2)}, u32[]{:S(2)}) collective-permute-start(f32[24,1024]{1,0:T(8,128)S(1)} %shard_map.58.refs_0_), channel_id=1, source_target_pairs={{0,1},{1,0},{2,3},{3,2},{4,5},{5,4},{6,7},{7,6},{8,9},{9,8},{10,11... | collective-permute-start | bytes 294920 | tf_op jit(solution)/shard_map/ppermute | solution.py:403
  26.7 8.7 %collective-permute-start.8 = (f32[24,1024]{1,0:T(8,128)S(1)}, f32[24,1024]{1,0:T(8,128)S(1)}, u32[]{:S(2)}, u32[]{:S(2)}) collective-permute-start(f32[24,1024]{1,0:T(8,128)S(1)} %shard_map.58.refs_0_), channel_id=1, source_target_pairs={{0,3},{1,2},{2,1},{3,0},{4,7},{5,6},{6,5},{7,4},{8,11},{9,10},{10,... | collective-permute-start | bytes 294920 | tf_op jit(solution)/shard_map/ppermute | solution.py:403
  37.0 1.4 %collective-permute-start.9 = (f32[184,128]{1,0:T(8,128)S(1)}, f32[184,128]{1,0:T(8,128)S(1)}, u32[]{:S(2)}, u32[]{:S(2)}) collective-permute-start(f32[184,128]{1,0:T(8,128)S(1)} %get-tuple-element.47.own_ref), channel_id=1, source_target_pairs={{0,4},{4,0},{8,12},{12,8},{16,20},{20,16},{24,28},{28,24},{1,5},{5... | collective-permute-start | bytes 282632 | tf_op jit(solution)/shard_map/ppermute | solution.py:462
  37.1 4.9 %collective-permute-start.13 = (f32[48,128]{1,0:T(8,128)S(1)}, f32[48,128]{1,0:T(8,128)S(1)}, u32[]{:S(2)}, u32[]{:S(2)}) collective-permute-start(f32[48,128]{1,0:T(8,128)S(1)} %get-tuple-element.43.tiles_ref), channel_id=1, source_target_pairs={{0,28},{4,8},{8,4},{12,16},{16,12},{20,24},{24,20},{28,0},{1,29},{... | collective-permute-start | bytes 73736 | tf_op jit(solution)/shard_map/ppermute | solution.py:463
  38.4 5.3 %collective-permute-start.12 = (f32[136,128]{1,0:T(8,128)S(1)}, f32[136,128]{1,0:T(8,128)S(1)}, u32[]{:S(2)}, u32[]{:S(2)}) collective-permute-start(f32[136,128]{1,0:T(8,128)S(1)} %slice_add_fusion.1), channel_id=1, source_target_pairs={{0,24},{4,28},{8,16},{12,20},{16,8},{20,12},{24,0},{28,4},{1,25},{... | collective-permute-start | bytes 208904 | tf_op jit(solution)/shard_map/ppermute | solution.py:403
  38.5 6.6 %collective-permute-start.10 = (f32[136,128]{1,0:T(8,128)S(1)}, f32[136,128]{1,0:T(8,128)S(1)}, u32[]{:S(2)}, u32[]{:S(2)}) collective-permute-start(f32[136,128]{1,0:T(8,128)S(1)} %slice_add_fusion.1), channel_id=1, source_target_pairs={{0,16},{4,20},{8,24},{12,28},{16,0},{20,4},{24,8},{28,12},{1,17},{... | collective-permute-start | bytes 208904 | tf_op jit(solution)/shard_map/ppermute | solution.py:403
  40.8 4.3 %collective-permute-start.11 = (f32[136,128]{1,0:T(8,128)S(1)}, f32[136,128]{1,0:T(8,128)S(1)}, u32[]{:S(2)}, u32[]{:S(2)}) collective-permute-start(f32[136,128]{1,0:T(8,128)S(1)} %slice_add_fusion.1), channel_id=1, source_target_pairs={{0,8},{4,12},{8,0},{12,4},{16,24},{20,28},{24,16},{28,20},{1,9},{5... | collective-permute-start | bytes 208904 | tf_op jit(solution)/shard_map/ppermute | solution.py:403
  45.1 1.3 %collective-permute-start.14 = (f32[128,128]{1,0:T(8,128)S(1)}, f32[128,128]{1,0:T(8,128)S(1)}, u32[]{:S(2)}, u32[]{:S(2)}) collective-permute-start(f32[128,128]{1,0:T(8,128)S(1)} %slice.50), channel_id=1, source_target_pairs={{0,4},{4,0},{8,12},{12,8},{16,20},{20,16},{24,28},{28,24},{1,5},{5... | collective-permute-start | bytes 196616 | tf_op jit(solution)/shard_map/ppermute | solution.py:490
  47.3 10.3 %collective-permute-start.15 = (f32[24,1024]{1,0:T(8,128)S(1)}, f32[24,1024]{1,0:T(8,128)S(1)}, u32[]{:S(2)}, u32[]{:S(2)}) collective-permute-start(f32[24,1024]{1,0:T(8,128)S(1)} %shard_map.63.refs_0_), channel_id=1, source_target_pairs={{0,2},{1,3},{2,0},{3,1},{4,6},{5,7},{6,4},{7,5},{8,10},{9,11},{10,... | collective-permute-start | bytes 294920 | tf_op jit(solution)/shard_map/ppermute | solution.py:403
  49.2 8.6 %collective-permute-start.16 = (f32[24,1024]{1,0:T(8,128)S(1)}, f32[24,1024]{1,0:T(8,128)S(1)}, u32[]{:S(2)}, u32[]{:S(2)}) collective-permute-start(f32[24,1024]{1,0:T(8,128)S(1)} %shard_map.63.refs_0_), channel_id=1, source_target_pairs={{0,1},{1,0},{2,3},{3,2},{4,5},{5,4},{6,7},{7,6},{8,9},{9,8},{10,11... | collective-permute-start | bytes 294920 | tf_op jit(solution)/shard_map/ppermute | solution.py:403
  50.2 7.5 %collective-permute-start.17 = (f32[24,1024]{1,0:T(8,128)S(1)}, f32[24,1024]{1,0:T(8,128)S(1)}, u32[]{:S(2)}, u32[]{:S(2)}) collective-permute-start(f32[24,1024]{1,0:T(8,128)S(1)} %shard_map.63.refs_0_), channel_id=1, source_target_pairs={{0,3},{1,2},{2,1},{3,0},{4,7},{5,6},{6,5},{7,4},{8,11},{9,10},{10,... | collective-permute-start | bytes 294920 | tf_op jit(solution)/shard_map/ppermute | solution.py:403
  59.4 1.6 %collective-permute-start.18 = (f32[184,128]{1,0:T(8,128)S(1)}, f32[184,128]{1,0:T(8,128)S(1)}, u32[]{:S(2)}, u32[]{:S(2)}) collective-permute-start(f32[184,128]{1,0:T(8,128)S(1)} %get-tuple-element.56.own_ref), channel_id=1, source_target_pairs={{0,4},{4,0},{8,12},{12,8},{16,20},{20,16},{24,28},{28,24},{1,5},{5... | collective-permute-start | bytes 282632 | tf_op jit(solution)/shard_map/ppermute | solution.py:462
  59.5 5.1 %collective-permute-start.22 = (f32[48,128]{1,0:T(8,128)S(1)}, f32[48,128]{1,0:T(8,128)S(1)}, u32[]{:S(2)}, u32[]{:S(2)}) collective-permute-start(f32[48,128]{1,0:T(8,128)S(1)} %get-tuple-element.53.tiles_ref), channel_id=1, source_target_pairs={{0,28},{4,8},{8,4},{12,16},{16,12},{20,24},{24,20},{28,0},{1,29},{... | collective-permute-start | bytes 73736 | tf_op jit(solution)/shard_map/ppermute | solution.py:463
  61.0 5.5 %collective-permute-start.21 = (f32[136,128]{1,0:T(8,128)S(1)}, f32[136,128]{1,0:T(8,128)S(1)}, u32[]{:S(2)}, u32[]{:S(2)}) collective-permute-start(f32[136,128]{1,0:T(8,128)S(1)} %slice_add_fusion), channel_id=1, source_target_pairs={{0,24},{4,28},{8,16},{12,20},{16,8},{20,12},{24,0},{28,4},{1,25},{... | collective-permute-start | bytes 208904 | tf_op jit(solution)/shard_map/ppermute | solution.py:403
  62.3 5.2 %collective-permute-start.19 = (f32[136,128]{1,0:T(8,128)S(1)}, f32[136,128]{1,0:T(8,128)S(1)}, u32[]{:S(2)}, u32[]{:S(2)}) collective-permute-start(f32[136,128]{1,0:T(8,128)S(1)} %slice_add_fusion), channel_id=1, source_target_pairs={{0,16},{4,20},{8,24},{12,28},{16,0},{20,4},{24,8},{28,12},{1,17},{... | collective-permute-start | bytes 208904 | tf_op jit(solution)/shard_map/ppermute | solution.py:403
  63.5 4.3 %collective-permute-start.20 = (f32[136,128]{1,0:T(8,128)S(1)}, f32[136,128]{1,0:T(8,128)S(1)}, u32[]{:S(2)}, u32[]{:S(2)}) collective-permute-start(f32[136,128]{1,0:T(8,128)S(1)} %slice_add_fusion), channel_id=1, source_target_pairs={{0,8},{4,12},{8,0},{12,4},{16,24},{20,28},{24,16},{28,20},{1,9},{5... | collective-permute-start | bytes 208904 | tf_op jit(solution)/shard_map/ppermute | solution.py:403
  67.8 1.3 %collective-permute-start.23 = (f32[128,128]{1,0:T(8,128)S(1)}, f32[128,128]{1,0:T(8,128)S(1)}, u32[]{:S(2)}, u32[]{:S(2)}) collective-permute-start(f32[128,128]{1,0:T(8,128)S(1)} %slice.52), channel_id=1, source_target_pairs={{0,4},{4,0},{8,12},{12,8},{16,20},{20,16},{24,28},{28,24},{1,5},{5... | collective-permute-start | bytes 196616 | tf_op jit(solution)/shard_map/ppermute | solution.py:490
  70.0 8.8 %collective-permute-start.24 = (f32[24,1024]{1,0:T(8,128)S(1)}, f32[24,1024]{1,0:T(8,128)S(1)}, u32[]{:S(2)}, u32[]{:S(2)}) collective-permute-start(f32[24,1024]{1,0:T(8,128)S(1)} %shard_map.68.refs_0_), channel_id=1, source_target_pairs={{0,2},{1,3},{2,0},{3,1},{4,6},{5,7},{6,4},{7,5},{8,10},{9,11},{10,... | collective-permute-start | bytes 294920 | tf_op jit(solution)/shard_map/ppermute | solution.py:403
  73.1 5.7 %collective-permute-start.25 = (f32[24,1024]{1,0:T(8,128)S(1)}, f32[24,1024]{1,0:T(8,128)S(1)}, u32[]{:S(2)}, u32[]{:S(2)}) collective-permute-start(f32[24,1024]{1,0:T(8,128)S(1)} %shard_map.68.refs_0_), channel_id=1, source_target_pairs={{0,1},{1,0},{2,3},{3,2},{4,5},{5,4},{6,7},{7,6},{8,9},{9,8},{10,11... | collective-permute-start | bytes 294920 | tf_op jit(solution)/shard_map/ppermute | solution.py:403
  73.1 8.7 %collective-permute-start.26 = (f32[24,1024]{1,0:T(8,128)S(1)}, f32[24,1024]{1,0:T(8,128)S(1)}, u32[]{:S(2)}, u32[]{:S(2)}) collective-permute-start(f32[24,1024]{1,0:T(8,128)S(1)} %shard_map.68.refs_0_), channel_id=1, source_target_pairs={{0,3},{1,2},{2,1},{3,0},{4,7},{5,6},{6,5},{7,4},{8,11},{9,10},{10,... | collective-permute-start | bytes 294920 | tf_op jit(solution)/shard_map/ppermute | solution.py:403

commit v7 on v6

--- a/solution.py
+++ b/solution.py
@@ -164,7 +164,7 @@
         for kind in range(4):
             flip_ref[kind, :, rows] = table_ref[kind, rows, :].T
 
-    ends = [0] + [particles * k // 8 for k in (4, 6, 8)]
+    ends = [0] + [particles * k // 8 for k in (4, 7, 8)]
     blocks = [slice(low, high) for low, high in zip(ends, ends[1:])]
     make(blocks[0])
     for k in range(1, len(blocks)):

time: 82.7 us -> 81.9 us (level)
  waiting for transfers between devices: 25.8 us -> 24.4 us
    ppermute x3, starting transfers between devices: 5.19 us -> 6.5 us  [body(): away = lax.ppermute(rest[base:] if step == 0 else own, 'space', third)]
    ppermute x3, waiting for transfers between devices: 1.2 us -> 0.22 us  [body(): other = lax.ppermute(rest, 'space', core)]
  transfers between devices with their start and end apart: 27 -> 27, of which waited for: 15 -> 15; matrix products, arithmetic and copies ran while one was open for 1% -> 1% of each run, Pallas kernels for 10% -> 11%
where the time goes in v7:
time: 81.9 us; the launch traced here: 81.8 us
  starting transfers between devices  32.8 us (40%)
  waiting for transfers between devices  24.4 us (30%)
  Pallas kernels  21.7 us (26%)
  other arithmetic  1.88 us (2%)
  local copies, waits for them, and re-layouts  0.82 us (1%)
    ppermute x18, starting transfers between devices, exchange(): lax.ppermute(x, axis, [(i, i ^ d * bit) for i in range(size)])  25.4 us
    ppermute x18, waiting for transfers between devices, exchange(): lax.ppermute(x, axis, [(i, i ^ d * bit) for i in range(size)])  23 us
    pallas_call x16, Pallas kernels, call(): pl.pallas_call(kernel, out_shape=[jax.ShapeDtypeStruct(*o) for o in outs]...  21.7 us
    ppermute x3, starting transfers between devices, body(): away = lax.ppermute(rest[base:] if step == 0 else own, 'space', third)  6.5 us
  transfers between devices with their start and end apart: 27, of which 15 were waited for; matrix products, arithmetic and copies ran while one was open for 1% of the time, Pallas kernels for 11%

profile of v7, /device:TPU:0, one launch (start us, length us, event | category | flops | bytes accessed | tf_op | source)
XLA Modules:
  0.0 81.8 jit_solution(1767998340047028533)
XLA Ops:
  0.0 0.9 %pad_maximum_fusion.stack_ref.pos_ref = f32[27,1024]{1,0:T(8,128)S(1)} fusion(f32[3,1024]{1,0:T(4,128)} %param.6, f32[24,1024]{1,0:T(8,128)} %bitcast.12), kind=kLoop, calls=%fused_computation | loop fusion | flops 27648 | bytes 221184 | tf_op jit(solution)/shard_map/concatenate | solution.py:429
  1.1 0.7 copy-done.1
  1.8 6.6 %shard_map.55 = (bf16[4,1024,1024]{2,1,0:T(8,128)(2,1)S(1)}, bf16[4,1024,1024]{2,1,0:T(8,128)(2,1)S(1)}, f32[8,1024]{1,0:T(8,128)S(1)}, f32[128,128]{1,0:T(8,128)S(1)}, f32[200,128]{1,0:T(8,128)S(1)}) custom-call(s32[3,1024]{1,0:T(4,128)S(1)} %copy-done.1, f32[2,128]{1,0:T(2,128)S(1)} %broadcast_in_dim.14.place_ref, ...), custom_call_target="tpu_custom_call" | custom-call | flops 1610612736 | tf_op jit(solution)/shard_map/pallas_call | solution.py:383
  8.4 0.5 collective-permute-start
  8.9 3.6 %collective-permute-start.4 = (f32[64,128]{1,0:T(8,128)S(1)}, f32[64,128]{1,0:T(8,128)S(1)}, u32[]{:S(2)}, u32[]{:S(2)}) collective-permute-start(f32[64,128]{1,0:T(8,128)S(1)} %slice.40), channel_id=1, source_target_pairs={{0,28},{4,8},{8,4},{12,16},{16,12},{20,24},{24,20},{28,0},{1,29},{... | collective-permute-start | bytes 98312 | tf_op jit(solution)/shard_map/ppermute | solution.py:463
  12.5 0.8 fusion.4.live_ref
  13.3 0.6 collective-permute-start.3
  13.9 0.4 collective-permute-start.1
  14.3 2.6 %collective-permute-start.2 = (f32[136,128]{1,0:T(8,128)S(1)}, f32[136,128]{1,0:T(8,128)S(1)}, u32[]{:S(2)}, u32[]{:S(2)}) collective-permute-start(f32[136,128]{1,0:T(8,128)S(1)} %maximum_add_fusion), channel_id=1, source_target_pairs={{0,8},{4,12},{8,0},{12,4},{16,24},{20,28},{24,16},{28,20},{1,9},{5... | collective-permute-start | bytes 208904 | tf_op jit(solution)/shard_map/ppermute | solution.py:403
  16.8 3.0 %shard_map.56 = (bf16[36,256,768]{2,1,0:T(8,128)(2,1)S(1)}, s32[3,36]{1,0:T(4,128)S(1)}, f32[24,1024]{1,0:T(8,128)S(1)}) custom-call(s32[8,8]{1,0:T(8,128)S(1)} %fusion.4.live_ref, f32[27,1024]{1,0:T(8,128)S(1)} %pad_maximum_fusion.stack_ref.pos_ref, f32[200,128]{1,0:T(8,128)S(1)} %get-tuple-element.34.own_ref, ...), custom_call_target="tpu_custom_call" | custom-call | flops 8053063680 | tf_op jit(solution)/shard_map/pallas_call | solution.py:383
  20.0 0.8 %shard_map.57.before_ref = f32[24,1024]{1,0:T(8,128)S(1)} custom-call(f32[136,128]{1,0:T(8,128)S(1)} %add_add_fusion.2.factor_ref, f32[24,1024]{1,0:T(8,128)S(1)} %get-tuple-element.40.before_ref, f32[8,1024]{1,0:T(8,128)S(1)} %get-tuple-element.35.terms_ref.refs_5_, bf16[4,1024,1024]{2,1,0:T(8,128)(2,1)S(1)} %get-tuple-element.41.flip_ref), custom_call_target="tpu_custom_call" | custom-call | flops 201326592 | tf_op jit(solution)/shard_map/pallas_call | solution.py:383
  20.8 0.4 collective-permute-done.5.factor_ref
  21.2 0.8 %shard_map.58.refs_0_ = f32[24,1024]{1,0:T(8,128)S(1)} custom-call(f32[128,128]{1,0:T(8,128)S(1)} %collective-permute-done.5.factor_ref, f32[24,1024]{1,0:T(8,128)S(1)} %shard_map.57.before_ref, f32[8,1024]{1,0:T(8,128)S(1)} %get-tuple-element.35.terms_ref.refs_5_, bf16[4,1024,1024]{2,1,0:T(8,128)(2,1)S(1)} %get-tuple-element.41.flip_ref), custom_call_target="tpu_custom_call" | custom-call | flops 201326592 | tf_op jit(solution)/shard_map/pallas_call | solution.py:383
  22.1 3.6 %collective-permute-start.6 = (f32[24,1024]{1,0:T(8,128)S(1)}, f32[24,1024]{1,0:T(8,128)S(1)}, u32[]{:S(2)}, u32[]{:S(2)}) collective-permute-start(f32[24,1024]{1,0:T(8,128)S(1)} %shard_map.58.refs_0_), channel_id=1, source_target_pairs={{0,2},{1,3},{2,0},{3,1},{4,6},{5,7},{6,4},{7,5},{8,10},{9,11},{10,... | collective-permute-start | bytes 294920 | tf_op jit(solution)/shard_map/ppermute | solution.py:403
  25.7 1.1 %collective-permute-start.7 = (f32[24,1024]{1,0:T(8,128)S(1)}, f32[24,1024]{1,0:T(8,128)S(1)}, u32[]{:S(2)}, u32[]{:S(2)}) collective-permute-start(f32[24,1024]{1,0:T(8,128)S(1)} %shard_map.58.refs_0_), channel_id=1, source_target_pairs={{0,1},{1,0},{2,3},{3,2},{4,5},{5,4},{6,7},{7,6},{8,9},{9,8},{10,11... | collective-permute-start | bytes 294920 | tf_op jit(solution)/shard_map/ppermute | solution.py:403
  26.8 0.5 collective-permute-start.8
  27.3 4.7 %collective-permute-done.6.refs_1_ = f32[24,1024]{1,0:T(8,128)S(1)} collective-permute-done((f32[24,1024]{1,0:T(8,128)S(1)}, f32[24,1024]{1,0:T(8,128)S(1)}, u32[]{:S(2)}, u32[]{:S(2)}) %collective-permute-start.6) | collective-permute-done | bytes 98336 | tf_op jit(solution)/shard_map/ppermute | solution.py:403
  31.9 1.9 %collective-permute-done.7.refs_2_ = f32[24,1024]{1,0:T(8,128)S(1)} collective-permute-done((f32[24,1024]{1,0:T(8,128)S(1)}, f32[24,1024]{1,0:T(8,128)S(1)}, u32[]{:S(2)}, u32[]{:S(2)}) %collective-permute-start.7) | collective-permute-done | bytes 98336 | tf_op jit(solution)/shard_map/ppermute | solution.py:403
  33.9 1.6 %shard_map.60 = (f32[128,128]{1,0:T(8,128)S(1)}, f32[184,128]{1,0:T(8,128)S(1)}) custom-call(f32[24,1024]{1,0:T(8,128)S(1)} %get-tuple-element.42.rows_ref.refs_4_.one_ref, f32[48,128]{1,0:T(8,128)S(1)} %get-tuple-element.43.tiles_ref, f32[8,128]{1,0:T(8,128)S(1)} %get-tuple-element.44.norm_ref, f32[8,1024]{1,0:T(8,128)S(1)} %get-tuple-element.35.terms_ref.refs_5_, ...), custom_call_target="tpu_custom_call" | custom-call | flops 402653184 | tf_op jit(solution)/shard_map/pallas_call | solution.py:383
  35.5 1.1 %collective-permute-start.13 = (f32[48,128]{1,0:T(8,128)S(1)}, f32[48,128]{1,0:T(8,128)S(1)}, u32[]{:S(2)}, u32[]{:S(2)}) collective-permute-start(f32[48,128]{1,0:T(8,128)S(1)} %get-tuple-element.43.tiles_ref), channel_id=1, source_target_pairs={{0,28},{4,8},{8,4},{12,16},{16,12},{20,24},{24,20},{28,0},{1,29},{... | collective-permute-start | bytes 73736 | tf_op jit(solution)/shard_map/ppermute | solution.py:463
  36.8 1.0 %collective-permute-start.12 = (f32[136,128]{1,0:T(8,128)S(1)}, f32[136,128]{1,0:T(8,128)S(1)}, u32[]{:S(2)}, u32[]{:S(2)}) collective-permute-start(f32[136,128]{1,0:T(8,128)S(1)} %slice_add_fusion.1), channel_id=1, source_target_pairs={{0,24},{4,28},{8,16},{12,20},{16,8},{20,12},{24,0},{28,4},{1,25},{... | collective-permute-start | bytes 208904 | tf_op jit(solution)/shard_map/ppermute | solution.py:403
  37.9 1.3 %collective-permute-start.10 = (f32[136,128]{1,0:T(8,128)S(1)}, f32[136,128]{1,0:T(8,128)S(1)}, u32[]{:S(2)}, u32[]{:S(2)}) collective-permute-start(f32[136,128]{1,0:T(8,128)S(1)} %slice_add_fusion.1), channel_id=1, source_target_pairs={{0,16},{4,20},{8,24},{12,28},{16,0},{20,4},{24,8},{28,12},{1,17},{... | collective-permute-start | bytes 208904 | tf_op jit(solution)/shard_map/ppermute | solution.py:403
  39.2 1.2 %collective-permute-start.11 = (f32[136,128]{1,0:T(8,128)S(1)}, f32[136,128]{1,0:T(8,128)S(1)}, u32[]{:S(2)}, u32[]{:S(2)}) collective-permute-start(f32[136,128]{1,0:T(8,128)S(1)} %slice_add_fusion.1), channel_id=1, source_target_pairs={{0,8},{4,12},{8,0},{12,4},{16,24},{20,28},{24,16},{28,20},{1,9},{5... | collective-permute-start | bytes 208904 | tf_op jit(solution)/shard_map/ppermute | solution.py:403
  40.4 1.5 %shard_map.61.before_ref = f32[24,1024]{1,0:T(8,128)S(1)} custom-call(s32[3,36]{1,0:T(4,128)S(1)} %get-tuple-element.48.plan_ref, f32[184,128]{1,0:T(8,128)S(1)} %get-tuple-element.47.own_ref, f32[184,128]{1,0:T(8,128)S(1)} %collective-permute-done.9.near_ref, f32[48,128]{1,0:T(8,128)S(1)} %collective-permute-done.13.away_ref, ...), custom_call_target="tpu_custom_call" | custom-call | flops 8053063680 | tf_op jit(solution)/shard_map/pallas_call | solution.py:383
  42.2 1.4 %collective-permute-done.10 = f32[136,128]{1,0:T(8,128)S(1)} collective-permute-done((f32[136,128]{1,0:T(8,128)S(1)}, f32[136,128]{1,0:T(8,128)S(1)}, u32[]{:S(2)}, u32[]{:S(2)}) %collective-permute-start.10) | collective-permute-done | bytes 69664 | tf_op jit(solution)/shard_map/ppermute | solution.py:403
  43.7 0.8 %shard_map.62.before_ref = f32[24,1024]{1,0:T(8,128)S(1)} custom-call(f32[136,128]{1,0:T(8,128)S(1)} %add_add_fusion.1.factor_ref.first_ref, f32[24,1024]{1,0:T(8,128)S(1)} %shard_map.61.before_ref, f32[8,1024]{1,0:T(8,128)S(1)} %get-tuple-element.35.terms_ref.refs_5_, bf16[4,1024,1024]{2,1,0:T(8,128)(2,1)S(1)} %get-tuple-element.41.flip_ref), custom_call_target="tpu_custom_call" | custom-call | flops 201326592 | tf_op jit(solution)/shard_map/pallas_call | solution.py:383
  44.5 0.4 collective-permute-done.14.factor_ref
  44.9 0.8 %shard_map.63.refs_0_ = f32[24,1024]{1,0:T(8,128)S(1)} custom-call(f32[128,128]{1,0:T(8,128)S(1)} %collective-permute-done.14.factor_ref, f32[24,1024]{1,0:T(8,128)S(1)} %shard_map.62.before_ref, f32[8,1024]{1,0:T(8,128)S(1)} %get-tuple-element.35.terms_ref.refs_5_, bf16[4,1024,1024]{2,1,0:T(8,128)(2,1)S(1)} %get-tuple-element.41.flip_ref), custom_call_target="tpu_custom_call" | custom-call | flops 201326592 | tf_op jit(solution)/shard_map/pallas_call | solution.py:383
  45.7 3.6 %collective-permute-start.15 = (f32[24,1024]{1,0:T(8,128)S(1)}, f32[24,1024]{1,0:T(8,128)S(1)}, u32[]{:S(2)}, u32[]{:S(2)}) collective-permute-start(f32[24,1024]{1,0:T(8,128)S(1)} %shard_map.63.refs_0_), channel_id=1, source_target_pairs={{0,2},{1,3},{2,0},{3,1},{4,6},{5,7},{6,4},{7,5},{8,10},{9,11},{10,... | collective-permute-start | bytes 294920 | tf_op jit(solution)/shard_map/ppermute | solution.py:403
  49.3 1.5 %collective-permute-start.17 = (f32[24,1024]{1,0:T(8,128)S(1)}, f32[24,1024]{1,0:T(8,128)S(1)}, u32[]{:S(2)}, u32[]{:S(2)}) collective-permute-start(f32[24,1024]{1,0:T(8,128)S(1)} %shard_map.63.refs_0_), channel_id=1, source_target_pairs={{0,3},{1,2},{2,1},{3,0},{4,7},{5,6},{6,5},{7,4},{8,11},{9,10},{10,... | collective-permute-start | bytes 294920 | tf_op jit(solution)/shard_map/ppermute | solution.py:403
  50.9 4.9 %collective-permute-done.15.refs_1_ = f32[24,1024]{1,0:T(8,128)S(1)} collective-permute-done((f32[24,1024]{1,0:T(8,128)S(1)}, f32[24,1024]{1,0:T(8,128)S(1)}, u32[]{:S(2)}, u32[]{:S(2)}) %collective-permute-start.15) | collective-permute-done | bytes 98336 | tf_op jit(solution)/shard_map/ppermute | solution.py:403
  55.7 1.9 %collective-permute-done.16.refs_2_ = f32[24,1024]{1,0:T(8,128)S(1)} collective-permute-done((f32[24,1024]{1,0:T(8,128)S(1)}, f32[24,1024]{1,0:T(8,128)S(1)}, u32[]{:S(2)}, u32[]{:S(2)}) %collective-permute-start.16) | collective-permute-done | bytes 98336 | tf_op jit(solution)/shard_map/ppermute | solution.py:403
  57.7 1.6 %shard_map.65 = (f32[128,128]{1,0:T(8,128)S(1)}, f32[184,128]{1,0:T(8,128)S(1)}) custom-call(f32[24,1024]{1,0:T(8,128)S(1)} %get-tuple-element.52.rows_ref.two_ref, f32[48,128]{1,0:T(8,128)S(1)} %get-tuple-element.53.tiles_ref, f32[8,128]{1,0:T(8,128)S(1)} %get-tuple-element.54.norm_ref, f32[8,1024]{1,0:T(8,128)S(1)} %get-tuple-element.35.terms_ref.refs_5_, ...), custom_call_target="tpu_custom_call" | custom-call | flops 402653184 | tf_op jit(solution)/shard_map/pallas_call | solution.py:383
  59.4 1.9 %collective-permute-start.22 = (f32[48,128]{1,0:T(8,128)S(1)}, f32[48,128]{1,0:T(8,128)S(1)}, u32[]{:S(2)}, u32[]{:S(2)}) collective-permute-start(f32[48,128]{1,0:T(8,128)S(1)} %get-tuple-element.53.tiles_ref), channel_id=1, source_target_pairs={{0,28},{4,8},{8,4},{12,16},{16,12},{20,24},{24,20},{28,0},{1,29},{... | collective-permute-start | bytes 73736 | tf_op jit(solution)/shard_map/ppermute | solution.py:463
  61.3 1.2 %collective-permute-start.21 = (f32[136,128]{1,0:T(8,128)S(1)}, f32[136,128]{1,0:T(8,128)S(1)}, u32[]{:S(2)}, u32[]{:S(2)}) collective-permute-start(f32[136,128]{1,0:T(8,128)S(1)} %slice_add_fusion), channel_id=1, source_target_pairs={{0,24},{4,28},{8,16},{12,20},{16,8},{20,12},{24,0},{28,4},{1,25},{... | collective-permute-start | bytes 208904 | tf_op jit(solution)/shard_map/ppermute | solution.py:403
  62.5 0.8 %collective-permute-start.19 = (f32[136,128]{1,0:T(8,128)S(1)}, f32[136,128]{1,0:T(8,128)S(1)}, u32[]{:S(2)}, u32[]{:S(2)}) collective-permute-start(f32[136,128]{1,0:T(8,128)S(1)} %slice_add_fusion), channel_id=1, source_target_pairs={{0,16},{4,20},{8,24},{12,28},{16,0},{20,4},{24,8},{28,12},{1,17},{... | collective-permute-start | bytes 208904 | tf_op jit(solution)/shard_map/ppermute | solution.py:403
  63.3 1.5 %collective-permute-start.20 = (f32[136,128]{1,0:T(8,128)S(1)}, f32[136,128]{1,0:T(8,128)S(1)}, u32[]{:S(2)}, u32[]{:S(2)}) collective-permute-start(f32[136,128]{1,0:T(8,128)S(1)} %slice_add_fusion), channel_id=1, source_target_pairs={{0,8},{4,12},{8,0},{12,4},{16,24},{20,28},{24,16},{28,20},{1,9},{5... | collective-permute-start | bytes 208904 | tf_op jit(solution)/shard_map/ppermute | solution.py:403
  64.8 1.4 %shard_map.66.before_ref = f32[24,1024]{1,0:T(8,128)S(1)} custom-call(s32[3,36]{1,0:T(4,128)S(1)} %get-tuple-element.48.plan_ref, f32[184,128]{1,0:T(8,128)S(1)} %get-tuple-element.56.own_ref, f32[184,128]{1,0:T(8,128)S(1)} %collective-permute-done.18.near_ref, f32[48,128]{1,0:T(8,128)S(1)} %collective-permute-done.22.away_ref, ...), custom_call_target="tpu_custom_call" | custom-call | flops 8053063680 | tf_op jit(solution)/shard_map/pallas_call | solution.py:383
  66.2 0.8 %collective-permute-done.21 = f32[136,128]{1,0:T(8,128)S(1)} collective-permute-done((f32[136,128]{1,0:T(8,128)S(1)}, f32[136,128]{1,0:T(8,128)S(1)}, u32[]{:S(2)}, u32[]{:S(2)}) %collective-permute-start.21) | collective-permute-done | bytes 69664 | tf_op jit(solution)/shard_map/ppermute | solution.py:403
  67.8 0.8 %shard_map.67.before_ref = f32[24,1024]{1,0:T(8,128)S(1)} custom-call(f32[136,128]{1,0:T(8,128)S(1)} %add_add_fusion.factor_ref.second_ref, f32[24,1024]{1,0:T(8,128)S(1)} %shard_map.66.before_ref, f32[8,1024]{1,0:T(8,128)S(1)} %get-tuple-element.35.terms_ref.refs_5_, bf16[4,1024,1024]{2,1,0:T(8,128)(2,1)S(1)} %get-tuple-element.41.flip_ref), custom_call_target="tpu_custom_call" | custom-call | flops 201326592 | tf_op jit(solution)/shard_map/pallas_call | solution.py:383
  68.6 0.4 collective-permute-done.23.factor_ref
  69.0 0.8 %shard_map.68.refs_0_ = f32[24,1024]{1,0:T(8,128)S(1)} custom-call(f32[128,128]{1,0:T(8,128)S(1)} %collective-permute-done.23.factor_ref, f32[24,1024]{1,0:T(8,128)S(1)} %shard_map.67.before_ref, f32[8,1024]{1,0:T(8,128)S(1)} %get-tuple-element.35.terms_ref.refs_5_, bf16[4,1024,1024]{2,1,0:T(8,128)(2,1)S(1)} %get-tuple-element.41.flip_ref), custom_call_target="tpu_custom_call" | custom-call | flops 201326592 | tf_op jit(solution)/shard_map/pallas_call | solution.py:383
  69.8 2.2 %collective-permute-start.24 = (f32[24,1024]{1,0:T(8,128)S(1)}, f32[24,1024]{1,0:T(8,128)S(1)}, u32[]{:S(2)}, u32[]{:S(2)}) collective-permute-start(f32[24,1024]{1,0:T(8,128)S(1)} %shard_map.68.refs_0_), channel_id=1, source_target_pairs={{0,2},{1,3},{2,0},{3,1},{4,6},{5,7},{6,4},{7,5},{8,10},{9,11},{10,... | collective-permute-start | bytes 294920 | tf_op jit(solution)/shard_map/ppermute | solution.py:403
  72.1 1.1 %collective-permute-start.25 = (f32[24,1024]{1,0:T(8,128)S(1)}, f32[24,1024]{1,0:T(8,128)S(1)}, u32[]{:S(2)}, u32[]{:S(2)}) collective-permute-start(f32[24,1024]{1,0:T(8,128)S(1)} %shard_map.68.refs_0_), channel_id=1, source_target_pairs={{0,1},{1,0},{2,3},{3,2},{4,5},{5,4},{6,7},{7,6},{8,9},{9,8},{10,11... | collective-permute-start | bytes 294920 | tf_op jit(solution)/shard_map/ppermute | solution.py:403
  73.2 1.1 %collective-permute-start.26 = (f32[24,1024]{1,0:T(8,128)S(1)}, f32[24,1024]{1,0:T(8,128)S(1)}, u32[]{:S(2)}, u32[]{:S(2)}) collective-permute-start(f32[24,1024]{1,0:T(8,128)S(1)} %shard_map.68.refs_0_), channel_id=1, source_target_pairs={{0,3},{1,2},{2,1},{3,0},{4,7},{5,6},{6,5},{7,4},{8,11},{9,10},{10,... | collective-permute-start | bytes 294920 | tf_op jit(solution)/shard_map/ppermute | solution.py:403
  74.5 4.4 %collective-permute-done.24.refs_1_ = f32[24,1024]{1,0:T(8,128)S(1)} collective-permute-done((f32[24,1024]{1,0:T(8,128)S(1)}, f32[24,1024]{1,0:T(8,128)S(1)}, u32[]{:S(2)}, u32[]{:S(2)}) %collective-permute-start.24) | collective-permute-done | bytes 98336 | tf_op jit(solution)/shard_map/ppermute | solution.py:403
  78.9 2.2 %collective-permute-done.26.refs_3_ = f32[24,1024]{1,0:T(8,128)S(1)} collective-permute-done((f32[24,1024]{1,0:T(8,128)S(1)}, f32[24,1024]{1,0:T(8,128)S(1)}, u32[]{:S(2)}, u32[]{:S(2)}) %collective-permute-start.26) | collective-permute-done | bytes 98336 | tf_op jit(solution)/shard_map/ppermute | solution.py:403
  81.1 0.7 shard_map.70
  (45 shorter events, 2.1 us)
Async XLA Ops:
  1.1 0.7 copy-start.1
  8.4 4.9 %collective-permute-start = (f32[200,128]{1,0:T(8,128)S(1)}, f32[200,128]{1,0:T(8,128)S(1)}, u32[]{:S(2)}, u32[]{:S(2)}) collective-permute-start(f32[200,128]{1,0:T(8,128)S(1)} %get-tuple-element.34.own_ref), channel_id=1, source_target_pairs={{0,4},{4,0},{8,12},{12,8},{16,20},{20,16},{24,28},{28,24},{1,5},{5... | collective-permute-start | bytes 307208 | tf_op jit(solution)/shard_map/ppermute | solution.py:462
  8.9 7.9 %collective-permute-start.4 = (f32[64,128]{1,0:T(8,128)S(1)}, f32[64,128]{1,0:T(8,128)S(1)}, u32[]{:S(2)}, u32[]{:S(2)}) collective-permute-start(f32[64,128]{1,0:T(8,128)S(1)} %slice.40), channel_id=1, source_target_pairs={{0,28},{4,8},{8,4},{12,16},{16,12},{20,24},{24,20},{28,0},{1,29},{... | collective-permute-start | bytes 98312 | tf_op jit(solution)/shard_map/ppermute | solution.py:463
  13.3 6.6 %collective-permute-start.3 = (f32[136,128]{1,0:T(8,128)S(1)}, f32[136,128]{1,0:T(8,128)S(1)}, u32[]{:S(2)}, u32[]{:S(2)}) collective-permute-start(f32[136,128]{1,0:T(8,128)S(1)} %maximum_add_fusion), channel_id=1, source_target_pairs={{0,24},{4,28},{8,16},{12,20},{16,8},{20,12},{24,0},{28,4},{1,25},{... | collective-permute-start | bytes 208904 | tf_op jit(solution)/shard_map/ppermute | solution.py:403
  13.9 6.0 %collective-permute-start.1 = (f32[136,128]{1,0:T(8,128)S(1)}, f32[136,128]{1,0:T(8,128)S(1)}, u32[]{:S(2)}, u32[]{:S(2)}) collective-permute-start(f32[136,128]{1,0:T(8,128)S(1)} %maximum_add_fusion), channel_id=1, source_target_pairs={{0,16},{4,20},{8,24},{12,28},{16,0},{20,4},{24,8},{28,12},{1,17},{... | collective-permute-start | bytes 208904 | tf_op jit(solution)/shard_map/ppermute | solution.py:403
  14.3 5.6 %collective-permute-start.2 = (f32[136,128]{1,0:T(8,128)S(1)}, f32[136,128]{1,0:T(8,128)S(1)}, u32[]{:S(2)}, u32[]{:S(2)}) collective-permute-start(f32[136,128]{1,0:T(8,128)S(1)} %maximum_add_fusion), channel_id=1, source_target_pairs={{0,8},{4,12},{8,0},{12,4},{16,24},{20,28},{24,16},{28,20},{1,9},{5... | collective-permute-start | bytes 208904 | tf_op jit(solution)/shard_map/ppermute | solution.py:403
  19.9 1.3 %collective-permute-start.5 = (f32[128,128]{1,0:T(8,128)S(1)}, f32[128,128]{1,0:T(8,128)S(1)}, u32[]{:S(2)}, u32[]{:S(2)}) collective-permute-start(f32[128,128]{1,0:T(8,128)S(1)} %slice.48), channel_id=1, source_target_pairs={{0,4},{4,0},{8,12},{12,8},{16,20},{20,16},{24,28},{28,24},{1,5},{5... | collective-permute-start | bytes 196616 | tf_op jit(solution)/shard_map/ppermute | solution.py:490
  20.0 13.8 %copy-start = (f32[8,3,1024]{2,0,1:T(8,128)S(1)}, f32[8,3,1024]{2,0,1:T(8,128)}, u32[]{:S(2)}) copy-start(f32[8,3,1024]{2,0,1:T(8,128)} %param.5) | copy-start | bytes 294916
  22.1 9.9 %collective-permute-start.6 = (f32[24,1024]{1,0:T(8,128)S(1)}, f32[24,1024]{1,0:T(8,128)S(1)}, u32[]{:S(2)}, u32[]{:S(2)}) collective-permute-start(f32[24,1024]{1,0:T(8,128)S(1)} %shard_map.58.refs_0_), channel_id=1, source_target_pairs={{0,2},{1,3},{2,0},{3,1},{4,6},{5,7},{6,4},{7,5},{8,10},{9,11},{10,... | collective-permute-start | bytes 294920 | tf_op jit(solution)/shard_map/ppermute | solution.py:403
  25.7 8.1 %collective-permute-start.7 = (f32[24,1024]{1,0:T(8,128)S(1)}, f32[24,1024]{1,0:T(8,128)S(1)}, u32[]{:S(2)}, u32[]{:S(2)}) collective-permute-start(f32[24,1024]{1,0:T(8,128)S(1)} %shard_map.58.refs_0_), channel_id=1, source_target_pairs={{0,1},{1,0},{2,3},{3,2},{4,5},{5,4},{6,7},{7,6},{8,9},{9,8},{10,11... | collective-permute-start | bytes 294920 | tf_op jit(solution)/shard_map/ppermute | solution.py:403
  26.8 7.0 %collective-permute-start.8 = (f32[24,1024]{1,0:T(8,128)S(1)}, f32[24,1024]{1,0:T(8,128)S(1)}, u32[]{:S(2)}, u32[]{:S(2)}) collective-permute-start(f32[24,1024]{1,0:T(8,128)S(1)} %shard_map.58.refs_0_), channel_id=1, source_target_pairs={{0,3},{1,2},{2,1},{3,0},{4,7},{5,6},{6,5},{7,4},{8,11},{9,10},{10,... | collective-permute-start | bytes 294920 | tf_op jit(solution)/shard_map/ppermute | solution.py:403
  35.5 1.4 %collective-permute-start.9 = (f32[184,128]{1,0:T(8,128)S(1)}, f32[184,128]{1,0:T(8,128)S(1)}, u32[]{:S(2)}, u32[]{:S(2)}) collective-permute-start(f32[184,128]{1,0:T(8,128)S(1)} %get-tuple-element.47.own_ref), channel_id=1, source_target_pairs={{0,4},{4,0},{8,12},{12,8},{16,20},{20,16},{24,28},{28,24},{1,5},{5... | collective-permute-start | bytes 282632 | tf_op jit(solution)/shard_map/ppermute | solution.py:462
  35.5 4.9 %collective-permute-start.13 = (f32[48,128]{1,0:T(8,128)S(1)}, f32[48,128]{1,0:T(8,128)S(1)}, u32[]{:S(2)}, u32[]{:S(2)}) collective-permute-start(f32[48,128]{1,0:T(8,128)S(1)} %get-tuple-element.43.tiles_ref), channel_id=1, source_target_pairs={{0,28},{4,8},{8,4},{12,16},{16,12},{20,24},{24,20},{28,0},{1,29},{... | collective-permute-start | bytes 73736 | tf_op jit(solution)/shard_map/ppermute | solution.py:463
  36.8 5.3 %collective-permute-start.12 = (f32[136,128]{1,0:T(8,128)S(1)}, f32[136,128]{1,0:T(8,128)S(1)}, u32[]{:S(2)}, u32[]{:S(2)}) collective-permute-start(f32[136,128]{1,0:T(8,128)S(1)} %slice_add_fusion.1), channel_id=1, source_target_pairs={{0,24},{4,28},{8,16},{12,20},{16,8},{20,12},{24,0},{28,4},{1,25},{... | collective-permute-start | bytes 208904 | tf_op jit(solution)/shard_map/ppermute | solution.py:403
  37.9 5.7 %collective-permute-start.10 = (f32[136,128]{1,0:T(8,128)S(1)}, f32[136,128]{1,0:T(8,128)S(1)}, u32[]{:S(2)}, u32[]{:S(2)}) collective-permute-start(f32[136,128]{1,0:T(8,128)S(1)} %slice_add_fusion.1), channel_id=1, source_target_pairs={{0,16},{4,20},{8,24},{12,28},{16,0},{20,4},{24,8},{28,12},{1,17},{... | collective-permute-start | bytes 208904 | tf_op jit(solution)/shard_map/ppermute | solution.py:403
  39.2 4.3 %collective-permute-start.11 = (f32[136,128]{1,0:T(8,128)S(1)}, f32[136,128]{1,0:T(8,128)S(1)}, u32[]{:S(2)}, u32[]{:S(2)}) collective-permute-start(f32[136,128]{1,0:T(8,128)S(1)} %slice_add_fusion.1), channel_id=1, source_target_pairs={{0,8},{4,12},{8,0},{12,4},{16,24},{20,28},{24,16},{28,20},{1,9},{5... | collective-permute-start | bytes 208904 | tf_op jit(solution)/shard_map/ppermute | solution.py:403
  43.6 1.3 %collective-permute-start.14 = (f32[128,128]{1,0:T(8,128)S(1)}, f32[128,128]{1,0:T(8,128)S(1)}, u32[]{:S(2)}, u32[]{:S(2)}) collective-permute-start(f32[128,128]{1,0:T(8,128)S(1)} %slice.50), channel_id=1, source_target_pairs={{0,4},{4,0},{8,12},{12,8},{16,20},{20,16},{24,28},{28,24},{1,5},{5... | collective-permute-start | bytes 196616 | tf_op jit(solution)/shard_map/ppermute | solution.py:490
  45.7 10.0 %collective-permute-start.15 = (f32[24,1024]{1,0:T(8,128)S(1)}, f32[24,1024]{1,0:T(8,128)S(1)}, u32[]{:S(2)}, u32[]{:S(2)}) collective-permute-start(f32[24,1024]{1,0:T(8,128)S(1)} %shard_map.63.refs_0_), channel_id=1, source_target_pairs={{0,2},{1,3},{2,0},{3,1},{4,6},{5,7},{6,4},{7,5},{8,10},{9,11},{10,... | collective-permute-start | bytes 294920 | tf_op jit(solution)/shard_map/ppermute | solution.py:403
  49.3 8.3 %collective-permute-start.16 = (f32[24,1024]{1,0:T(8,128)S(1)}, f32[24,1024]{1,0:T(8,128)S(1)}, u32[]{:S(2)}, u32[]{:S(2)}) collective-permute-start(f32[24,1024]{1,0:T(8,128)S(1)} %shard_map.63.refs_0_), channel_id=1, source_target_pairs={{0,1},{1,0},{2,3},{3,2},{4,5},{5,4},{6,7},{7,6},{8,9},{9,8},{10,11... | collective-permute-start | bytes 294920 | tf_op jit(solution)/shard_map/ppermute | solution.py:403
  49.3 8.3 %collective-permute-start.17 = (f32[24,1024]{1,0:T(8,128)S(1)}, f32[24,1024]{1,0:T(8,128)S(1)}, u32[]{:S(2)}, u32[]{:S(2)}) collective-permute-start(f32[24,1024]{1,0:T(8,128)S(1)} %shard_map.63.refs_0_), channel_id=1, source_target_pairs={{0,3},{1,2},{2,1},{3,0},{4,7},{5,6},{6,5},{7,4},{8,11},{9,10},{10,... | collective-permute-start | bytes 294920 | tf_op jit(solution)/shard_map/ppermute | solution.py:403
  59.3 2.0 %collective-permute-start.18 = (f32[184,128]{1,0:T(8,128)S(1)}, f32[184,128]{1,0:T(8,128)S(1)}, u32[]{:S(2)}, u32[]{:S(2)}) collective-permute-start(f32[184,128]{1,0:T(8,128)S(1)} %get-tuple-element.56.own_ref), channel_id=1, source_target_pairs={{0,4},{4,0},{8,12},{12,8},{16,20},{20,16},{24,28},{28,24},{1,5},{5... | collective-permute-start | bytes 282632 | tf_op jit(solution)/shard_map/ppermute | solution.py:462
  59.4 5.5 %collective-permute-start.22 = (f32[48,128]{1,0:T(8,128)S(1)}, f32[48,128]{1,0:T(8,128)S(1)}, u32[]{:S(2)}, u32[]{:S(2)}) collective-permute-start(f32[48,128]{1,0:T(8,128)S(1)} %get-tuple-element.53.tiles_ref), channel_id=1, source_target_pairs={{0,28},{4,8},{8,4},{12,16},{16,12},{20,24},{24,20},{28,0},{1,29},{... | collective-permute-start | bytes 73736 | tf_op jit(solution)/shard_map/ppermute | solution.py:463
  61.3 5.7 %collective-permute-start.21 = (f32[136,128]{1,0:T(8,128)S(1)}, f32[136,128]{1,0:T(8,128)S(1)}, u32[]{:S(2)}, u32[]{:S(2)}) collective-permute-start(f32[136,128]{1,0:T(8,128)S(1)} %slice_add_fusion), channel_id=1, source_target_pairs={{0,24},{4,28},{8,16},{12,20},{16,8},{20,12},{24,0},{28,4},{1,25},{... | collective-permute-start | bytes 208904 | tf_op jit(solution)/shard_map/ppermute | solution.py:403
  62.5 4.9 %collective-permute-start.19 = (f32[136,128]{1,0:T(8,128)S(1)}, f32[136,128]{1,0:T(8,128)S(1)}, u32[]{:S(2)}, u32[]{:S(2)}) collective-permute-start(f32[136,128]{1,0:T(8,128)S(1)} %slice_add_fusion), channel_id=1, source_target_pairs={{0,16},{4,20},{8,24},{12,28},{16,0},{20,4},{24,8},{28,12},{1,17},{... | collective-permute-start | bytes 208904 | tf_op jit(solution)/shard_map/ppermute | solution.py:403
  63.3 4.3 %collective-permute-start.20 = (f32[136,128]{1,0:T(8,128)S(1)}, f32[136,128]{1,0:T(8,128)S(1)}, u32[]{:S(2)}, u32[]{:S(2)}) collective-permute-start(f32[136,128]{1,0:T(8,128)S(1)} %slice_add_fusion), channel_id=1, source_target_pairs={{0,8},{4,12},{8,0},{12,4},{16,24},{20,28},{24,16},{28,20},{1,9},{5... | collective-permute-start | bytes 208904 | tf_op jit(solution)/shard_map/ppermute | solution.py:403
  67.7 1.3 %collective-permute-start.23 = (f32[128,128]{1,0:T(8,128)S(1)}, f32[128,128]{1,0:T(8,128)S(1)}, u32[]{:S(2)}, u32[]{:S(2)}) collective-permute-start(f32[128,128]{1,0:T(8,128)S(1)} %slice.52), channel_id=1, source_target_pairs={{0,4},{4,0},{8,12},{12,8},{16,20},{20,16},{24,28},{28,24},{1,5},{5... | collective-permute-start | bytes 196616 | tf_op jit(solution)/shard_map/ppermute | solution.py:490
  69.8 9.1 %collective-permute-start.24 = (f32[24,1024]{1,0:T(8,128)S(1)}, f32[24,1024]{1,0:T(8,128)S(1)}, u32[]{:S(2)}, u32[]{:S(2)}) collective-permute-start(f32[24,1024]{1,0:T(8,128)S(1)} %shard_map.68.refs_0_), channel_id=1, source_target_pairs={{0,2},{1,3},{2,0},{3,1},{4,6},{5,7},{6,4},{7,5},{8,10},{9,11},{10,... | collective-permute-start | bytes 294920 | tf_op jit(solution)/shard_map/ppermute | solution.py:403
  72.1 6.9 %collective-permute-start.25 = (f32[24,1024]{1,0:T(8,128)S(1)}, f32[24,1024]{1,0:T(8,128)S(1)}, u32[]{:S(2)}, u32[]{:S(2)}) collective-permute-start(f32[24,1024]{1,0:T(8,128)S(1)} %shard_map.68.refs_0_), channel_id=1, source_target_pairs={{0,1},{1,0},{2,3},{3,2},{4,5},{5,4},{6,7},{7,6},{8,9},{9,8},{10,11... | collective-permute-start | bytes 294920 | tf_op jit(solution)/shard_map/ppermute | solution.py:403
  73.2 8.0 %collective-permute-start.26 = (f32[24,1024]{1,0:T(8,128)S(1)}, f32[24,1024]{1,0:T(8,128)S(1)}, u32[]{:S(2)}, u32[]{:S(2)}) collective-permute-start(f32[24,1024]{1,0:T(8,128)S(1)} %shard_map.68.refs_0_), channel_id=1, source_target_pairs={{0,3},{1,2},{2,1},{3,0},{4,7},{5,6},{6,5},{7,4},{8,11},{9,10},{10,... | collective-permute-start | bytes 294920 | tf_op jit(solution)/shard_map/ppermute | solution.py:403

commit v8 on v7

--- a/solution.py
+++ b/solution.py
@@ -238,7 +238,7 @@
             place = ref[row : row + 8, :]
             place = jnp.concatenate([place[a : a + 1] / sides[a] for a in range(3)] + [filler], axis=0)
             column_ref[slab * share + i] = place.T
-    count = 32
+    count = 64
 
     def pair(p, carry):
         q = jnp.maximum(p - 1, 0)

time: 81.9 us -> 82 us (level)
  Pallas kernels: 21.7 us -> 20.4 us
  waiting for transfers between devices: 24.4 us -> 25.5 us
    pallas_call x16, Pallas kernels: 21.7 us -> 20.4 us  [call(): pl.pallas_call(kernel, out_shape=[jax.ShapeDtypeStruct(*o) for o in outs]...]
  transfers between devices with their start and end apart: 27 -> 27, of which waited for: 15 -> 16; matrix products, arithmetic and copies ran while one was open for 1% -> 1% of each run, Pallas kernels for 11% -> 9%
where the time goes in v8:
time: 82 us; the launch traced here: 81.8 us
  starting transfers between devices  33 us (40%)
  waiting for transfers between devices  25.5 us (31%)
  Pallas kernels  20.4 us (25%)
  other arithmetic  1.88 us (2%)
    ppermute x18, starting transfers between devices, exchange(): lax.ppermute(x, axis, [(i, i ^ d * bit) for i in range(size)])  25.9 us
    ppermute x18, waiting for transfers between devices, exchange(): lax.ppermute(x, axis, [(i, i ^ d * bit) for i in range(size)])  23.5 us
    pallas_call x16, Pallas kernels, call(): pl.pallas_call(kernel, out_shape=[jax.ShapeDtypeStruct(*o) for o in outs]...  20.4 us
    ppermute x3, starting transfers between devices, body(): away = lax.ppermute(rest[base:] if step == 0 else own, 'space', third)  6.23 us
  transfers between devices with their start and end apart: 27, of which 16 were waited for; matrix products, arithmetic and copies ran while one was open for 1% of the time, Pallas kernels for 9%

profile of v8, /device:TPU:0, one launch (start us, length us, event | category | flops | bytes accessed | tf_op | source)
XLA Modules:
  0.0 81.8 jit_solution(5839906442890512522)
XLA Ops:
  0.0 0.9 %pad_maximum_fusion.stack_ref.pos_ref = f32[27,1024]{1,0:T(8,128)S(1)} fusion(f32[3,1024]{1,0:T(4,128)} %param.6, f32[24,1024]{1,0:T(8,128)} %bitcast.12), kind=kLoop, calls=%fused_computation | loop fusion | flops 27648 | bytes 221184 | tf_op jit(solution)/shard_map/concatenate | solution.py:429
  1.1 0.7 copy-done.1
  1.8 6.6 %shard_map.55 = (bf16[4,1024,1024]{2,1,0:T(8,128)(2,1)S(1)}, bf16[4,1024,1024]{2,1,0:T(8,128)(2,1)S(1)}, f32[8,1024]{1,0:T(8,128)S(1)}, f32[128,128]{1,0:T(8,128)S(1)}, f32[200,128]{1,0:T(8,128)S(1)}) custom-call(s32[3,1024]{1,0:T(4,128)S(1)} %copy-done.1, f32[2,128]{1,0:T(2,128)S(1)} %broadcast_in_dim.14.place_ref, ...), custom_call_target="tpu_custom_call" | custom-call | flops 1610612736 | tf_op jit(solution)/shard_map/pallas_call | solution.py:383
  8.4 0.5 collective-permute-start
  8.9 3.6 %collective-permute-start.4 = (f32[64,128]{1,0:T(8,128)S(1)}, f32[64,128]{1,0:T(8,128)S(1)}, u32[]{:S(2)}, u32[]{:S(2)}) collective-permute-start(f32[64,128]{1,0:T(8,128)S(1)} %slice.40), channel_id=1, source_target_pairs={{0,28},{4,8},{8,4},{12,16},{16,12},{20,24},{24,20},{28,0},{1,29},{... | collective-permute-start | bytes 98312 | tf_op jit(solution)/shard_map/ppermute | solution.py:463
  12.5 0.8 fusion.4.live_ref
  13.3 0.6 collective-permute-start.3
  14.3 2.6 %collective-permute-start.2 = (f32[136,128]{1,0:T(8,128)S(1)}, f32[136,128]{1,0:T(8,128)S(1)}, u32[]{:S(2)}, u32[]{:S(2)}) collective-permute-start(f32[136,128]{1,0:T(8,128)S(1)} %maximum_add_fusion), channel_id=1, source_target_pairs={{0,8},{4,12},{8,0},{12,4},{16,24},{20,28},{24,16},{28,20},{1,9},{5... | collective-permute-start | bytes 208904 | tf_op jit(solution)/shard_map/ppermute | solution.py:403
  16.8 2.5 %shard_map.56 = (bf16[36,256,768]{2,1,0:T(8,128)(2,1)S(1)}, s32[3,36]{1,0:T(4,128)S(1)}, f32[24,1024]{1,0:T(8,128)S(1)}) custom-call(s32[8,8]{1,0:T(8,128)S(1)} %fusion.4.live_ref, f32[27,1024]{1,0:T(8,128)S(1)} %pad_maximum_fusion.stack_ref.pos_ref, f32[200,128]{1,0:T(8,128)S(1)} %get-tuple-element.34.own_ref, ...), custom_call_target="tpu_custom_call" | custom-call | flops 8053063680 | tf_op jit(solution)/shard_map/pallas_call | solution.py:383
  19.5 0.8 %shard_map.57.before_ref = f32[24,1024]{1,0:T(8,128)S(1)} custom-call(f32[136,128]{1,0:T(8,128)S(1)} %add_add_fusion.2.factor_ref, f32[24,1024]{1,0:T(8,128)S(1)} %get-tuple-element.40.before_ref, f32[8,1024]{1,0:T(8,128)S(1)} %get-tuple-element.35.terms_ref.refs_5_, bf16[4,1024,1024]{2,1,0:T(8,128)(2,1)S(1)} %get-tuple-element.41.flip_ref), custom_call_target="tpu_custom_call" | custom-call | flops 201326592 | tf_op jit(solution)/shard_map/pallas_call | solution.py:383
  20.7 0.8 %shard_map.58.refs_0_ = f32[24,1024]{1,0:T(8,128)S(1)} custom-call(f32[128,128]{1,0:T(8,128)S(1)} %collective-permute-done.5.factor_ref, f32[24,1024]{1,0:T(8,128)S(1)} %shard_map.57.before_ref, f32[8,1024]{1,0:T(8,128)S(1)} %get-tuple-element.35.terms_ref.refs_5_, bf16[4,1024,1024]{2,1,0:T(8,128)(2,1)S(1)} %get-tuple-element.41.flip_ref), custom_call_target="tpu_custom_call" | custom-call | flops 201326592 | tf_op jit(solution)/shard_map/pallas_call | solution.py:383
  21.6 4.4 %collective-permute-start.6 = (f32[24,1024]{1,0:T(8,128)S(1)}, f32[24,1024]{1,0:T(8,128)S(1)}, u32[]{:S(2)}, u32[]{:S(2)}) collective-permute-start(f32[24,1024]{1,0:T(8,128)S(1)} %shard_map.58.refs_0_), channel_id=1, source_target_pairs={{0,2},{1,3},{2,0},{3,1},{4,6},{5,7},{6,4},{7,5},{8,10},{9,11},{10,... | collective-permute-start | bytes 294920 | tf_op jit(solution)/shard_map/ppermute | solution.py:403
  25.9 0.8 %collective-permute-start.7 = (f32[24,1024]{1,0:T(8,128)S(1)}, f32[24,1024]{1,0:T(8,128)S(1)}, u32[]{:S(2)}, u32[]{:S(2)}) collective-permute-start(f32[24,1024]{1,0:T(8,128)S(1)} %shard_map.58.refs_0_), channel_id=1, source_target_pairs={{0,1},{1,0},{2,3},{3,2},{4,5},{5,4},{6,7},{7,6},{8,9},{9,8},{10,11... | collective-permute-start | bytes 294920 | tf_op jit(solution)/shard_map/ppermute | solution.py:403
  26.8 0.7 collective-permute-start.8
  27.5 4.8 %collective-permute-done.6.refs_1_ = f32[24,1024]{1,0:T(8,128)S(1)} collective-permute-done((f32[24,1024]{1,0:T(8,128)S(1)}, f32[24,1024]{1,0:T(8,128)S(1)}, u32[]{:S(2)}, u32[]{:S(2)}) %collective-permute-start.6) | collective-permute-done | bytes 98336 | tf_op jit(solution)/shard_map/ppermute | solution.py:403
  32.2 1.8 %collective-permute-done.7.refs_2_ = f32[24,1024]{1,0:T(8,128)S(1)} collective-permute-done((f32[24,1024]{1,0:T(8,128)S(1)}, f32[24,1024]{1,0:T(8,128)S(1)}, u32[]{:S(2)}, u32[]{:S(2)}) %collective-permute-start.7) | collective-permute-done | bytes 98336 | tf_op jit(solution)/shard_map/ppermute | solution.py:403
  34.1 1.6 %shard_map.60 = (f32[128,128]{1,0:T(8,128)S(1)}, f32[184,128]{1,0:T(8,128)S(1)}) custom-call(f32[24,1024]{1,0:T(8,128)S(1)} %get-tuple-element.42.rows_ref.refs_4_.one_ref, f32[48,128]{1,0:T(8,128)S(1)} %get-tuple-element.43.tiles_ref, f32[8,128]{1,0:T(8,128)S(1)} %get-tuple-element.44.norm_ref, f32[8,1024]{1,0:T(8,128)S(1)} %get-tuple-element.35.terms_ref.refs_5_, ...), custom_call_target="tpu_custom_call" | custom-call | flops 402653184 | tf_op jit(solution)/shard_map/pallas_call | solution.py:383
  35.7 0.5 collective-permute-start.13
  36.3 0.8 collective-permute-done.9.near_ref
  37.0 1.5 %collective-permute-start.12 = (f32[136,128]{1,0:T(8,128)S(1)}, f32[136,128]{1,0:T(8,128)S(1)}, u32[]{:S(2)}, u32[]{:S(2)}) collective-permute-start(f32[136,128]{1,0:T(8,128)S(1)} %slice_add_fusion.1), channel_id=1, source_target_pairs={{0,24},{4,28},{8,16},{12,20},{16,8},{20,12},{24,0},{28,4},{1,25},{... | collective-permute-start | bytes 208904 | tf_op jit(solution)/shard_map/ppermute | solution.py:403
  38.6 0.8 %collective-permute-start.10 = (f32[136,128]{1,0:T(8,128)S(1)}, f32[136,128]{1,0:T(8,128)S(1)}, u32[]{:S(2)}, u32[]{:S(2)}) collective-permute-start(f32[136,128]{1,0:T(8,128)S(1)} %slice_add_fusion.1), channel_id=1, source_target_pairs={{0,16},{4,20},{8,24},{12,28},{16,0},{20,4},{24,8},{28,12},{1,17},{... | collective-permute-start | bytes 208904 | tf_op jit(solution)/shard_map/ppermute | solution.py:403
  39.4 1.2 %collective-permute-start.11 = (f32[136,128]{1,0:T(8,128)S(1)}, f32[136,128]{1,0:T(8,128)S(1)}, u32[]{:S(2)}, u32[]{:S(2)}) collective-permute-start(f32[136,128]{1,0:T(8,128)S(1)} %slice_add_fusion.1), channel_id=1, source_target_pairs={{0,8},{4,12},{8,0},{12,4},{16,24},{20,28},{24,16},{28,20},{1,9},{5... | collective-permute-start | bytes 208904 | tf_op jit(solution)/shard_map/ppermute | solution.py:403
  40.6 1.2 %shard_map.61.before_ref = f32[24,1024]{1,0:T(8,128)S(1)} custom-call(s32[3,36]{1,0:T(4,128)S(1)} %get-tuple-element.48.plan_ref, f32[184,128]{1,0:T(8,128)S(1)} %get-tuple-element.47.own_ref, f32[184,128]{1,0:T(8,128)S(1)} %collective-permute-done.9.near_ref, f32[48,128]{1,0:T(8,128)S(1)} %collective-permute-done.13.away_ref, ...), custom_call_target="tpu_custom_call" | custom-call | flops 8053063680 | tf_op jit(solution)/shard_map/pallas_call | solution.py:383
  41.8 0.6 collective-permute-done.12
  42.4 1.4 %collective-permute-done.10 = f32[136,128]{1,0:T(8,128)S(1)} collective-permute-done((f32[136,128]{1,0:T(8,128)S(1)}, f32[136,128]{1,0:T(8,128)S(1)}, u32[]{:S(2)}, u32[]{:S(2)}) %collective-permute-start.10) | collective-permute-done | bytes 69664 | tf_op jit(solution)/shard_map/ppermute | solution.py:403
  43.9 0.8 %shard_map.62.before_ref = f32[24,1024]{1,0:T(8,128)S(1)} custom-call(f32[136,128]{1,0:T(8,128)S(1)} %add_add_fusion.1.factor_ref.first_ref, f32[24,1024]{1,0:T(8,128)S(1)} %shard_map.61.before_ref, f32[8,1024]{1,0:T(8,128)S(1)} %get-tuple-element.35.terms_ref.refs_5_, bf16[4,1024,1024]{2,1,0:T(8,128)(2,1)S(1)} %get-tuple-element.41.flip_ref), custom_call_target="tpu_custom_call" | custom-call | flops 201326592 | tf_op jit(solution)/shard_map/pallas_call | solution.py:383
  45.1 0.8 %shard_map.63.refs_0_ = f32[24,1024]{1,0:T(8,128)S(1)} custom-call(f32[128,128]{1,0:T(8,128)S(1)} %collective-permute-done.14.factor_ref, f32[24,1024]{1,0:T(8,128)S(1)} %shard_map.62.before_ref, f32[8,1024]{1,0:T(8,128)S(1)} %get-tuple-element.35.terms_ref.refs_5_, bf16[4,1024,1024]{2,1,0:T(8,128)(2,1)S(1)} %get-tuple-element.41.flip_ref), custom_call_target="tpu_custom_call" | custom-call | flops 201326592 | tf_op jit(solution)/shard_map/pallas_call | solution.py:383
  45.9 3.4 %collective-permute-start.15 = (f32[24,1024]{1,0:T(8,128)S(1)}, f32[24,1024]{1,0:T(8,128)S(1)}, u32[]{:S(2)}, u32[]{:S(2)}) collective-permute-start(f32[24,1024]{1,0:T(8,128)S(1)} %shard_map.63.refs_0_), channel_id=1, source_target_pairs={{0,2},{1,3},{2,0},{3,1},{4,6},{5,7},{6,4},{7,5},{8,10},{9,11},{10,... | collective-permute-start | bytes 294920 | tf_op jit(solution)/shard_map/ppermute | solution.py:403
  49.4 1.4 %collective-permute-start.17 = (f32[24,1024]{1,0:T(8,128)S(1)}, f32[24,1024]{1,0:T(8,128)S(1)}, u32[]{:S(2)}, u32[]{:S(2)}) collective-permute-start(f32[24,1024]{1,0:T(8,128)S(1)} %shard_map.63.refs_0_), channel_id=1, source_target_pairs={{0,3},{1,2},{2,1},{3,0},{4,7},{5,6},{6,5},{7,4},{8,11},{9,10},{10,... | collective-permute-start | bytes 294920 | tf_op jit(solution)/shard_map/ppermute | solution.py:403
  50.9 4.7 %collective-permute-done.15.refs_1_ = f32[24,1024]{1,0:T(8,128)S(1)} collective-permute-done((f32[24,1024]{1,0:T(8,128)S(1)}, f32[24,1024]{1,0:T(8,128)S(1)}, u32[]{:S(2)}, u32[]{:S(2)}) %collective-permute-start.15) | collective-permute-done | bytes 98336 | tf_op jit(solution)/shard_map/ppermute | solution.py:403
  55.6 0.5 collective-permute-done.16.refs_2_
  56.1 1.3 %collective-permute-done.17.refs_3_ = f32[24,1024]{1,0:T(8,128)S(1)} collective-permute-done((f32[24,1024]{1,0:T(8,128)S(1)}, f32[24,1024]{1,0:T(8,128)S(1)}, u32[]{:S(2)}, u32[]{:S(2)}) %collective-permute-start.17) | collective-permute-done | bytes 98336 | tf_op jit(solution)/shard_map/ppermute | solution.py:403
  57.4 1.6 %shard_map.65 = (f32[128,128]{1,0:T(8,128)S(1)}, f32[184,128]{1,0:T(8,128)S(1)}) custom-call(f32[24,1024]{1,0:T(8,128)S(1)} %get-tuple-element.52.rows_ref.two_ref, f32[48,128]{1,0:T(8,128)S(1)} %get-tuple-element.53.tiles_ref, f32[8,128]{1,0:T(8,128)S(1)} %get-tuple-element.54.norm_ref, f32[8,1024]{1,0:T(8,128)S(1)} %get-tuple-element.35.terms_ref.refs_5_, ...), custom_call_target="tpu_custom_call" | custom-call | flops 402653184 | tf_op jit(solution)/shard_map/pallas_call | solution.py:383
  59.1 2.1 %collective-permute-start.22 = (f32[48,128]{1,0:T(8,128)S(1)}, f32[48,128]{1,0:T(8,128)S(1)}, u32[]{:S(2)}, u32[]{:S(2)}) collective-permute-start(f32[48,128]{1,0:T(8,128)S(1)} %get-tuple-element.53.tiles_ref), channel_id=1, source_target_pairs={{0,28},{4,8},{8,4},{12,16},{16,12},{20,24},{24,20},{28,0},{1,29},{... | collective-permute-start | bytes 73736 | tf_op jit(solution)/shard_map/ppermute | solution.py:463
  61.3 1.2 %collective-permute-start.21 = (f32[136,128]{1,0:T(8,128)S(1)}, f32[136,128]{1,0:T(8,128)S(1)}, u32[]{:S(2)}, u32[]{:S(2)}) collective-permute-start(f32[136,128]{1,0:T(8,128)S(1)} %slice_add_fusion), channel_id=1, source_target_pairs={{0,24},{4,28},{8,16},{12,20},{16,8},{20,12},{24,0},{28,4},{1,25},{... | collective-permute-start | bytes 208904 | tf_op jit(solution)/shard_map/ppermute | solution.py:403
  62.5 0.6 collective-permute-start.19
  63.1 1.7 %collective-permute-start.20 = (f32[136,128]{1,0:T(8,128)S(1)}, f32[136,128]{1,0:T(8,128)S(1)}, u32[]{:S(2)}, u32[]{:S(2)}) collective-permute-start(f32[136,128]{1,0:T(8,128)S(1)} %slice_add_fusion), channel_id=1, source_target_pairs={{0,8},{4,12},{8,0},{12,4},{16,24},{20,28},{24,16},{28,20},{1,9},{5... | collective-permute-start | bytes 208904 | tf_op jit(solution)/shard_map/ppermute | solution.py:403
  64.8 1.0 %shard_map.66.before_ref = f32[24,1024]{1,0:T(8,128)S(1)} custom-call(s32[3,36]{1,0:T(4,128)S(1)} %get-tuple-element.48.plan_ref, f32[184,128]{1,0:T(8,128)S(1)} %get-tuple-element.56.own_ref, f32[184,128]{1,0:T(8,128)S(1)} %collective-permute-done.18.near_ref, f32[48,128]{1,0:T(8,128)S(1)} %collective-permute-done.22.away_ref, ...), custom_call_target="tpu_custom_call" | custom-call | flops 8053063680 | tf_op jit(solution)/shard_map/pallas_call | solution.py:383
  65.8 1.2 %collective-permute-done.21 = f32[136,128]{1,0:T(8,128)S(1)} collective-permute-done((f32[136,128]{1,0:T(8,128)S(1)}, f32[136,128]{1,0:T(8,128)S(1)}, u32[]{:S(2)}, u32[]{:S(2)}) %collective-permute-start.21) | collective-permute-done | bytes 69664 | tf_op jit(solution)/shard_map/ppermute | solution.py:403
  67.5 0.8 %shard_map.67.before_ref = f32[24,1024]{1,0:T(8,128)S(1)} custom-call(f32[136,128]{1,0:T(8,128)S(1)} %add_add_fusion.factor_ref.second_ref, f32[24,1024]{1,0:T(8,128)S(1)} %shard_map.66.before_ref, f32[8,1024]{1,0:T(8,128)S(1)} %get-tuple-element.35.terms_ref.refs_5_, bf16[4,1024,1024]{2,1,0:T(8,128)(2,1)S(1)} %get-tuple-element.41.flip_ref), custom_call_target="tpu_custom_call" | custom-call | flops 201326592 | tf_op jit(solution)/shard_map/pallas_call | solution.py:383
  68.4 0.4 collective-permute-done.23.factor_ref
  68.8 0.8 %shard_map.68.refs_0_ = f32[24,1024]{1,0:T(8,128)S(1)} custom-call(f32[128,128]{1,0:T(8,128)S(1)} %collective-permute-done.23.factor_ref, f32[24,1024]{1,0:T(8,128)S(1)} %shard_map.67.before_ref, f32[8,1024]{1,0:T(8,128)S(1)} %get-tuple-element.35.terms_ref.refs_5_, bf16[4,1024,1024]{2,1,0:T(8,128)(2,1)S(1)} %get-tuple-element.41.flip_ref), custom_call_target="tpu_custom_call" | custom-call | flops 201326592 | tf_op jit(solution)/shard_map/pallas_call | solution.py:383
  69.6 2.7 %collective-permute-start.24 = (f32[24,1024]{1,0:T(8,128)S(1)}, f32[24,1024]{1,0:T(8,128)S(1)}, u32[]{:S(2)}, u32[]{:S(2)}) collective-permute-start(f32[24,1024]{1,0:T(8,128)S(1)} %shard_map.68.refs_0_), channel_id=1, source_target_pairs={{0,2},{1,3},{2,0},{3,1},{4,6},{5,7},{6,4},{7,5},{8,10},{9,11},{10,... | collective-permute-start | bytes 294920 | tf_op jit(solution)/shard_map/ppermute | solution.py:403
  72.3 0.8 %collective-permute-start.25 = (f32[24,1024]{1,0:T(8,128)S(1)}, f32[24,1024]{1,0:T(8,128)S(1)}, u32[]{:S(2)}, u32[]{:S(2)}) collective-permute-start(f32[24,1024]{1,0:T(8,128)S(1)} %shard_map.68.refs_0_), channel_id=1, source_target_pairs={{0,1},{1,0},{2,3},{3,2},{4,5},{5,4},{6,7},{7,6},{8,9},{9,8},{10,11... | collective-permute-start | bytes 294920 | tf_op jit(solution)/shard_map/ppermute | solution.py:403
  73.1 0.9 %collective-permute-start.26 = (f32[24,1024]{1,0:T(8,128)S(1)}, f32[24,1024]{1,0:T(8,128)S(1)}, u32[]{:S(2)}, u32[]{:S(2)}) collective-permute-start(f32[24,1024]{1,0:T(8,128)S(1)} %shard_map.68.refs_0_), channel_id=1, source_target_pairs={{0,3},{1,2},{2,1},{3,0},{4,7},{5,6},{6,5},{7,4},{8,11},{9,10},{10,... | collective-permute-start | bytes 294920 | tf_op jit(solution)/shard_map/ppermute | solution.py:403
  74.3 3.9 %collective-permute-done.24.refs_1_ = f32[24,1024]{1,0:T(8,128)S(1)} collective-permute-done((f32[24,1024]{1,0:T(8,128)S(1)}, f32[24,1024]{1,0:T(8,128)S(1)}, u32[]{:S(2)}, u32[]{:S(2)}) %collective-permute-start.24) | collective-permute-done | bytes 98336 | tf_op jit(solution)/shard_map/ppermute | solution.py:403
  78.1 3.0 %collective-permute-done.26.refs_3_ = f32[24,1024]{1,0:T(8,128)S(1)} collective-permute-done((f32[24,1024]{1,0:T(8,128)S(1)}, f32[24,1024]{1,0:T(8,128)S(1)}, u32[]{:S(2)}, u32[]{:S(2)}) %collective-permute-start.26) | collective-permute-done | bytes 98336 | tf_op jit(solution)/shard_map/ppermute | solution.py:403
  81.1 0.7 shard_map.70
  (45 shorter events, 2.7 us)
Async XLA Ops:
  1.1 0.7 copy-start.1
  8.4 4.9 %collective-permute-start = (f32[200,128]{1,0:T(8,128)S(1)}, f32[200,128]{1,0:T(8,128)S(1)}, u32[]{:S(2)}, u32[]{:S(2)}) collective-permute-start(f32[200,128]{1,0:T(8,128)S(1)} %get-tuple-element.34.own_ref), channel_id=1, source_target_pairs={{0,4},{4,0},{8,12},{12,8},{16,20},{20,16},{24,28},{28,24},{1,5},{5... | collective-permute-start | bytes 307208 | tf_op jit(solution)/shard_map/ppermute | solution.py:462
  8.9 7.9 %collective-permute-start.4 = (f32[64,128]{1,0:T(8,128)S(1)}, f32[64,128]{1,0:T(8,128)S(1)}, u32[]{:S(2)}, u32[]{:S(2)}) collective-permute-start(f32[64,128]{1,0:T(8,128)S(1)} %slice.40), channel_id=1, source_target_pairs={{0,28},{4,8},{8,4},{12,16},{16,12},{20,24},{24,20},{28,0},{1,29},{... | collective-permute-start | bytes 98312 | tf_op jit(solution)/shard_map/ppermute | solution.py:463
  13.3 6.1 %collective-permute-start.3 = (f32[136,128]{1,0:T(8,128)S(1)}, f32[136,128]{1,0:T(8,128)S(1)}, u32[]{:S(2)}, u32[]{:S(2)}) collective-permute-start(f32[136,128]{1,0:T(8,128)S(1)} %maximum_add_fusion), channel_id=1, source_target_pairs={{0,24},{4,28},{8,16},{12,20},{16,8},{20,12},{24,0},{28,4},{1,25},{... | collective-permute-start | bytes 208904 | tf_op jit(solution)/shard_map/ppermute | solution.py:403
  13.9 5.5 %collective-permute-start.1 = (f32[136,128]{1,0:T(8,128)S(1)}, f32[136,128]{1,0:T(8,128)S(1)}, u32[]{:S(2)}, u32[]{:S(2)}) collective-permute-start(f32[136,128]{1,0:T(8,128)S(1)} %maximum_add_fusion), channel_id=1, source_target_pairs={{0,16},{4,20},{8,24},{12,28},{16,0},{20,4},{24,8},{28,12},{1,17},{... | collective-permute-start | bytes 208904 | tf_op jit(solution)/shard_map/ppermute | solution.py:403
  14.3 5.1 %collective-permute-start.2 = (f32[136,128]{1,0:T(8,128)S(1)}, f32[136,128]{1,0:T(8,128)S(1)}, u32[]{:S(2)}, u32[]{:S(2)}) collective-permute-start(f32[136,128]{1,0:T(8,128)S(1)} %maximum_add_fusion), channel_id=1, source_target_pairs={{0,8},{4,12},{8,0},{12,4},{16,24},{20,28},{24,16},{28,20},{1,9},{5... | collective-permute-start | bytes 208904 | tf_op jit(solution)/shard_map/ppermute | solution.py:403
  19.4 1.3 %collective-permute-start.5 = (f32[128,128]{1,0:T(8,128)S(1)}, f32[128,128]{1,0:T(8,128)S(1)}, u32[]{:S(2)}, u32[]{:S(2)}) collective-permute-start(f32[128,128]{1,0:T(8,128)S(1)} %slice.48), channel_id=1, source_target_pairs={{0,4},{4,0},{8,12},{12,8},{16,20},{20,16},{24,28},{28,24},{1,5},{5... | collective-permute-start | bytes 196616 | tf_op jit(solution)/shard_map/ppermute | solution.py:490
  19.5 14.6 %copy-start = (f32[8,3,1024]{2,0,1:T(8,128)S(1)}, f32[8,3,1024]{2,0,1:T(8,128)}, u32[]{:S(2)}) copy-start(f32[8,3,1024]{2,0,1:T(8,128)} %param.5) | copy-start | bytes 294916
  21.6 10.7 %collective-permute-start.6 = (f32[24,1024]{1,0:T(8,128)S(1)}, f32[24,1024]{1,0:T(8,128)S(1)}, u32[]{:S(2)}, u32[]{:S(2)}) collective-permute-start(f32[24,1024]{1,0:T(8,128)S(1)} %shard_map.58.refs_0_), channel_id=1, source_target_pairs={{0,2},{1,3},{2,0},{3,1},{4,6},{5,7},{6,4},{7,5},{8,10},{9,11},{10,... | collective-permute-start | bytes 294920 | tf_op jit(solution)/shard_map/ppermute | solution.py:403
  25.9 8.1 %collective-permute-start.7 = (f32[24,1024]{1,0:T(8,128)S(1)}, f32[24,1024]{1,0:T(8,128)S(1)}, u32[]{:S(2)}, u32[]{:S(2)}) collective-permute-start(f32[24,1024]{1,0:T(8,128)S(1)} %shard_map.58.refs_0_), channel_id=1, source_target_pairs={{0,1},{1,0},{2,3},{3,2},{4,5},{5,4},{6,7},{7,6},{8,9},{9,8},{10,11... | collective-permute-start | bytes 294920 | tf_op jit(solution)/shard_map/ppermute | solution.py:403
  26.8 7.3 %collective-permute-start.8 = (f32[24,1024]{1,0:T(8,128)S(1)}, f32[24,1024]{1,0:T(8,128)S(1)}, u32[]{:S(2)}, u32[]{:S(2)}) collective-permute-start(f32[24,1024]{1,0:T(8,128)S(1)} %shard_map.58.refs_0_), channel_id=1, source_target_pairs={{0,3},{1,2},{2,1},{3,0},{4,7},{5,6},{6,5},{7,4},{8,11},{9,10},{10,... | collective-permute-start | bytes 294920 | tf_op jit(solution)/shard_map/ppermute | solution.py:403
  35.7 1.4 %collective-permute-start.9 = (f32[184,128]{1,0:T(8,128)S(1)}, f32[184,128]{1,0:T(8,128)S(1)}, u32[]{:S(2)}, u32[]{:S(2)}) collective-permute-start(f32[184,128]{1,0:T(8,128)S(1)} %get-tuple-element.47.own_ref), channel_id=1, source_target_pairs={{0,4},{4,0},{8,12},{12,8},{16,20},{20,16},{24,28},{28,24},{1,5},{5... | collective-permute-start | bytes 282632 | tf_op jit(solution)/shard_map/ppermute | solution.py:462
  35.7 4.9 %collective-permute-start.13 = (f32[48,128]{1,0:T(8,128)S(1)}, f32[48,128]{1,0:T(8,128)S(1)}, u32[]{:S(2)}, u32[]{:S(2)}) collective-permute-start(f32[48,128]{1,0:T(8,128)S(1)} %get-tuple-element.43.tiles_ref), channel_id=1, source_target_pairs={{0,28},{4,8},{8,4},{12,16},{16,12},{20,24},{24,20},{28,0},{1,29},{... | collective-permute-start | bytes 73736 | tf_op jit(solution)/shard_map/ppermute | solution.py:463
  37.0 5.3 %collective-permute-start.12 = (f32[136,128]{1,0:T(8,128)S(1)}, f32[136,128]{1,0:T(8,128)S(1)}, u32[]{:S(2)}, u32[]{:S(2)}) collective-permute-start(f32[136,128]{1,0:T(8,128)S(1)} %slice_add_fusion.1), channel_id=1, source_target_pairs={{0,24},{4,28},{8,16},{12,20},{16,8},{20,12},{24,0},{28,4},{1,25},{... | collective-permute-start | bytes 208904 | tf_op jit(solution)/shard_map/ppermute | solution.py:403
  38.6 5.1 %collective-permute-start.10 = (f32[136,128]{1,0:T(8,128)S(1)}, f32[136,128]{1,0:T(8,128)S(1)}, u32[]{:S(2)}, u32[]{:S(2)}) collective-permute-start(f32[136,128]{1,0:T(8,128)S(1)} %slice_add_fusion.1), channel_id=1, source_target_pairs={{0,16},{4,20},{8,24},{12,28},{16,0},{20,4},{24,8},{28,12},{1,17},{... | collective-permute-start | bytes 208904 | tf_op jit(solution)/shard_map/ppermute | solution.py:403
  39.4 4.3 %collective-permute-start.11 = (f32[136,128]{1,0:T(8,128)S(1)}, f32[136,128]{1,0:T(8,128)S(1)}, u32[]{:S(2)}, u32[]{:S(2)}) collective-permute-start(f32[136,128]{1,0:T(8,128)S(1)} %slice_add_fusion.1), channel_id=1, source_target_pairs={{0,8},{4,12},{8,0},{12,4},{16,24},{20,28},{24,16},{28,20},{1,9},{5... | collective-permute-start | bytes 208904 | tf_op jit(solution)/shard_map/ppermute | solution.py:403
  43.8 1.3 %collective-permute-start.14 = (f32[128,128]{1,0:T(8,128)S(1)}, f32[128,128]{1,0:T(8,128)S(1)}, u32[]{:S(2)}, u32[]{:S(2)}) collective-permute-start(f32[128,128]{1,0:T(8,128)S(1)} %slice.50), channel_id=1, source_target_pairs={{0,4},{4,0},{8,12},{12,8},{16,20},{20,16},{24,28},{28,24},{1,5},{5... | collective-permute-start | bytes 196616 | tf_op jit(solution)/shard_map/ppermute | solution.py:490
  45.9 9.7 %collective-permute-start.15 = (f32[24,1024]{1,0:T(8,128)S(1)}, f32[24,1024]{1,0:T(8,128)S(1)}, u32[]{:S(2)}, u32[]{:S(2)}) collective-permute-start(f32[24,1024]{1,0:T(8,128)S(1)} %shard_map.63.refs_0_), channel_id=1, source_target_pairs={{0,2},{1,3},{2,0},{3,1},{4,6},{5,7},{6,4},{7,5},{8,10},{9,11},{10,... | collective-permute-start | bytes 294920 | tf_op jit(solution)/shard_map/ppermute | solution.py:403
  49.3 6.8 %collective-permute-start.16 = (f32[24,1024]{1,0:T(8,128)S(1)}, f32[24,1024]{1,0:T(8,128)S(1)}, u32[]{:S(2)}, u32[]{:S(2)}) collective-permute-start(f32[24,1024]{1,0:T(8,128)S(1)} %shard_map.63.refs_0_), channel_id=1, source_target_pairs={{0,1},{1,0},{2,3},{3,2},{4,5},{5,4},{6,7},{7,6},{8,9},{9,8},{10,11... | collective-permute-start | bytes 294920 | tf_op jit(solution)/shard_map/ppermute | solution.py:403
  49.4 8.0 %collective-permute-start.17 = (f32[24,1024]{1,0:T(8,128)S(1)}, f32[24,1024]{1,0:T(8,128)S(1)}, u32[]{:S(2)}, u32[]{:S(2)}) collective-permute-start(f32[24,1024]{1,0:T(8,128)S(1)} %shard_map.63.refs_0_), channel_id=1, source_target_pairs={{0,3},{1,2},{2,1},{3,0},{4,7},{5,6},{6,5},{7,4},{8,11},{9,10},{10,... | collective-permute-start | bytes 294920 | tf_op jit(solution)/shard_map/ppermute | solution.py:403
  59.0 2.2 %collective-permute-start.18 = (f32[184,128]{1,0:T(8,128)S(1)}, f32[184,128]{1,0:T(8,128)S(1)}, u32[]{:S(2)}, u32[]{:S(2)}) collective-permute-start(f32[184,128]{1,0:T(8,128)S(1)} %get-tuple-element.56.own_ref), channel_id=1, source_target_pairs={{0,4},{4,0},{8,12},{12,8},{16,20},{20,16},{24,28},{28,24},{1,5},{5... | collective-permute-start | bytes 282632 | tf_op jit(solution)/shard_map/ppermute | solution.py:462
  59.1 5.7 %collective-permute-start.22 = (f32[48,128]{1,0:T(8,128)S(1)}, f32[48,128]{1,0:T(8,128)S(1)}, u32[]{:S(2)}, u32[]{:S(2)}) collective-permute-start(f32[48,128]{1,0:T(8,128)S(1)} %get-tuple-element.53.tiles_ref), channel_id=1, source_target_pairs={{0,28},{4,8},{8,4},{12,16},{16,12},{20,24},{24,20},{28,0},{1,29},{... | collective-permute-start | bytes 73736 | tf_op jit(solution)/shard_map/ppermute | solution.py:463
  61.3 5.7 %collective-permute-start.21 = (f32[136,128]{1,0:T(8,128)S(1)}, f32[136,128]{1,0:T(8,128)S(1)}, u32[]{:S(2)}, u32[]{:S(2)}) collective-permute-start(f32[136,128]{1,0:T(8,128)S(1)} %slice_add_fusion), channel_id=1, source_target_pairs={{0,24},{4,28},{8,16},{12,20},{16,8},{20,12},{24,0},{28,4},{1,25},{... | collective-permute-start | bytes 208904 | tf_op jit(solution)/shard_map/ppermute | solution.py:403
  62.5 4.8 %collective-permute-start.19 = (f32[136,128]{1,0:T(8,128)S(1)}, f32[136,128]{1,0:T(8,128)S(1)}, u32[]{:S(2)}, u32[]{:S(2)}) collective-permute-start(f32[136,128]{1,0:T(8,128)S(1)} %slice_add_fusion), channel_id=1, source_target_pairs={{0,16},{4,20},{8,24},{12,28},{16,0},{20,4},{24,8},{28,12},{1,17},{... | collective-permute-start | bytes 208904 | tf_op jit(solution)/shard_map/ppermute | solution.py:403
  63.1 4.3 %collective-permute-start.20 = (f32[136,128]{1,0:T(8,128)S(1)}, f32[136,128]{1,0:T(8,128)S(1)}, u32[]{:S(2)}, u32[]{:S(2)}) collective-permute-start(f32[136,128]{1,0:T(8,128)S(1)} %slice_add_fusion), channel_id=1, source_target_pairs={{0,8},{4,12},{8,0},{12,4},{16,24},{20,28},{24,16},{28,20},{1,9},{5... | collective-permute-start | bytes 208904 | tf_op jit(solution)/shard_map/ppermute | solution.py:403
  67.4 1.3 %collective-permute-start.23 = (f32[128,128]{1,0:T(8,128)S(1)}, f32[128,128]{1,0:T(8,128)S(1)}, u32[]{:S(2)}, u32[]{:S(2)}) collective-permute-start(f32[128,128]{1,0:T(8,128)S(1)} %slice.52), channel_id=1, source_target_pairs={{0,4},{4,0},{8,12},{12,8},{16,20},{20,16},{24,28},{28,24},{1,5},{5... | collective-permute-start | bytes 196616 | tf_op jit(solution)/shard_map/ppermute | solution.py:490
  69.6 8.5 %collective-permute-start.24 = (f32[24,1024]{1,0:T(8,128)S(1)}, f32[24,1024]{1,0:T(8,128)S(1)}, u32[]{:S(2)}, u32[]{:S(2)}) collective-permute-start(f32[24,1024]{1,0:T(8,128)S(1)} %shard_map.68.refs_0_), channel_id=1, source_target_pairs={{0,2},{1,3},{2,0},{3,1},{4,6},{5,7},{6,4},{7,5},{8,10},{9,11},{10,... | collective-permute-start | bytes 294920 | tf_op jit(solution)/shard_map/ppermute | solution.py:403
  72.3 5.9 %collective-permute-start.25 = (f32[24,1024]{1,0:T(8,128)S(1)}, f32[24,1024]{1,0:T(8,128)S(1)}, u32[]{:S(2)}, u32[]{:S(2)}) collective-permute-start(f32[24,1024]{1,0:T(8,128)S(1)} %shard_map.68.refs_0_), channel_id=1, source_target_pairs={{0,1},{1,0},{2,3},{3,2},{4,5},{5,4},{6,7},{7,6},{8,9},{9,8},{10,11... | collective-permute-start | bytes 294920 | tf_op jit(solution)/shard_map/ppermute | solution.py:403
  73.1 8.0 %collective-permute-start.26 = (f32[24,1024]{1,0:T(8,128)S(1)}, f32[24,1024]{1,0:T(8,128)S(1)}, u32[]{:S(2)}, u32[]{:S(2)}) collective-permute-start(f32[24,1024]{1,0:T(8,128)S(1)} %shard_map.68.refs_0_), channel_id=1, source_target_pairs={{0,3},{1,2},{2,1},{3,0},{4,7},{5,6},{6,5},{7,4},{8,11},{9,10},{10,... | collective-permute-start | bytes 294920 | tf_op jit(solution)/shard_map/ppermute | solution.py:403
